TPU v7x, 256 devices: a whole 4x4x8 slice. The times are simulated.
256 devices in a mesh: dp: 32 (over y, x, core), tr: 2 (over z_lo), tc: 4 (over z_hi).
Axes of the slice: x: 4, y: 4, z: 8 (z_hi: 4, z_lo: 2; z = z_hi * 2 + z_lo), core: 2. Of those that a mesh axis runs over, the one named last changes fastest.
Arguments:
- activations: bfloat16 [32768, 3072], P(('dp', 'tc'), 'tr'), may hold values from -24 to 24
- cotangent: bfloat16 [32768, 8192], P(('dp', 'tr'), 'tc'), may hold values from -0.03125 to 0.03125
- master: float32 [2, 1536, 8192], P('tr', ('dp', 'tc')), may hold values from -3 to 3
- moment: float32 [2, 1536, 8192], P('tr', ('dp', 'tc')), may hold values from -2 to 2
- second: float32 [2, 1536, 8192], P('tr', ('dp', 'tc')), may hold values from 0.05 to 2
Outputs:
- new_master: float32 [2, 1536, 8192], P('tr', ('dp', 'tc'))
- new_moment: float32 [2, 1536, 8192], P('tr', ('dp', 'tc'))
- new_second: float32 [2, 1536, 8192], P('tr', ('dp', 'tc'))
All inputs are finite; a program needn't handle non-finite values.
Results may differ from a plain program's by a relative error of at most 0.0003.
Values may be sent and summed in bfloat16 or wider, within the bound.
No kernel may reach another device: no remote copies, remote signals or barrier semaphores. Data moves between devices by JAX's collectives and lax.ppermute only.
A program may use at most 128 MiB of HBM per device.

v0:
```python
import jax
import jax.numpy as jnp
from jax import lax
from jax.sharding import PartitionSpec as P

first_decay = 0.9
second_decay = 0.95
learn_rate = 0.0003
weight_decay = 0.1
epsilon = 1e-08
first_fix = 1.0 - 0.9**10
second_fix = 1.0 - 0.95**10


def shards(activations, cotangent, master, moment, second):
    act_rows = lax.all_gather(activations, "tc", axis=0, tiled=True)
    cot_rows = lax.all_gather(cotangent, "tr", axis=0, tiled=True)
    replicas = lax.axis_size("dp")
    columns = lax.axis_size("tc")
    feature_count = act_rows.shape[1]
    unit_count = cot_rows.shape[1]
    owned = feature_count // (replicas * columns)
    tile = lax.dot_general(
        act_rows, cot_rows, (((0,), (0,)), ((), ())), preferred_element_type=jnp.float32
    )
    tile = tile.reshape(replicas, columns, owned, unit_count)
    moved = lax.all_to_all(tile, "tc", split_axis=1, concat_axis=3, tiled=True)
    grad = lax.psum_scatter(moved, "dp", scatter_dimension=0, tiled=True)
    grad = grad.reshape(1, owned, unit_count * columns)
    new_moment = first_decay * moment + (1.0 - first_decay) * grad
    new_second = second_decay * second + (1.0 - second_decay) * grad * grad
    update = new_moment / first_fix / (jnp.sqrt(new_second / second_fix) + epsilon)
    new_master = master - learn_rate * (update + weight_decay * master)
    return (new_master, new_moment, new_second)


def solution(mesh):
    return jax.shard_map(
        shards,
        mesh=mesh,
        in_specs=(
            P(("dp", "tc"), "tr"),
            P(("dp", "tr"), "tc"),
            P("tr", ("dp", "tc"), None),
            P("tr", ("dp", "tc"), None),
            P("tr", ("dp", "tc"), None),
        ),
        out_specs=(
            P("tr", ("dp", "tc"), None),
            P("tr", ("dp", "tc"), None),
            P("tr", ("dp", "tc"), None),
        ),
        check_vma=False,
    )
```

profile of v0, /device:TPU:6, one launch (start us, length us, event | category | flops | bytes accessed | tf_op | source)
XLA Modules:
  0.0 639.9 jit_solution(1265132735142706624)
XLA Ops:
  7.2 0.0 all-gather.5.cloned.1.call-start
  7.2 0.7 all-gather.5.cloned.1.call-update
  7.9 0.0 all-gather.3.cloned.1.call-start
  7.9 0.7 all-gather.3.cloned.1.call-update
  8.6 0.0 all-reduce.3.cloned.1.call-start
  8.7 65.9 %all-gather.5.cloned.1.call-done = bf16[1024,2048]{1,0:T(8,128)(2,1)} async-done(((bf16[512,2048]{1,0:T(8,128)(2,1)}), bf16[1024,2048]{1,0:T(8,128)(2,1)}) %all-gather.5.cloned.1.call-update) | async-done | bytes 4194320 | tf_op jit(solution)/shard_map/all_gather | solution.py:17
  74.6 65.2 %all-gather.3.cloned.1.call-done = bf16[1024,1536]{1,0:T(8,128)(2,1)} async-done(((bf16[256,1536]{1,0:T(8,128)(2,1)}), bf16[1024,1536]{1,0:T(8,128)(2,1)}) %all-gather.3.cloned.1.call-update) | async-done | bytes 3145744 | tf_op jit(solution)/shard_map/all_gather | solution.py:16
  139.8 12.3 %fusion.2 = f32[1536,2048]{1,0:T(8,128)} fusion(bf16[1024,1536]{1,0:T(8,128)(2,1)} %all-gather.3.cloned.1.call-done, bf16[1024,2048]{1,0:T(8,128)(2,1)} %all-gather.5.cloned.1.call-done), kind=kOutput, calls=%fused_computation.5 | convolution fusion | flops 6442450944 | bytes 19922944 | tf_op jit(solution)/shard_map/dot_general | solution.py:23
  152.1 14.9 %reshape.48 = f32[32,4,12,2048]{3,2,1,0:T(8,128)} reshape(f32[1536,2048]{1,0:T(8,128)} %fusion.2) | data formatting | bytes 25165824 | tf_op jit(solution)/shard_map/reshape | solution.py:26
  167.0 17.6 %copy.10 = f32[32,4,12,2048]{3,0,2,1:T(8,128)} copy(f32[32,4,12,2048]{3,2,1,0:T(8,128)} %reshape.48) | data formatting | bytes 25165824 | tf_op jit(solution)/shard_map/reshape | solution.py:26
  184.5 289.4 %all_to_all.18 = f32[32,4,12,2048]{3,0,2,1:T(8,128)} all-to-all(f32[32,4,12,2048]{3,0,2,1:T(8,128)} %copy.10), channel_id=1, replica_groups=mesh['dp'=32,'tr'=2,'tc'=4] {'tc'}, dimensions={1} | all-to-all | bytes 25165824 | tf_op jit(solution)/shard_map/all_to_all | solution.py:27
  473.9 11.3 %copy.14 = f32[1,4,12,4,8,2048]{5,4,1,3,2,0:T(8,128)} copy(f32[1,4,12,4,8,2048]{5,4,3,2,1,0:T(8,128)} %bitcast.17) | data formatting | bytes 25165824 | tf_op jit(solution)/shard_map/all_to_all | solution.py:27
  485.2 0.0 copy-start.3
  485.2 0.0 copy-start
  485.2 0.0 copy-start.1
  485.2 0.0 copy-start.2
  485.2 0.0 all-reduce.3.cloned.1.call-update
  485.3 0.6 copy-done.3
  485.9 0.7 dynamic-slice
  486.5 141.1 %all-reduce.3.cloned.1.call-done = f32[32,1,12,8192]{3,0,2,1:T(8,128)} async-done(((f32[32,1,12,8192]{3,0,2,1:T(8,128)}), f32[32,1,12,8192]{3,0,2,1:T(8,128)}) %all-reduce.3.cloned.1.call-update) | async-done | bytes 12582928
  627.6 0.0 copy-done
  627.6 0.0 copy-done.1
  627.6 0.0 copy-done.2
  627.6 5.7 multiply_subtract_fusion
Async XLA Ops:
  7.2 67.5 %all-gather.5.cloned.1.call-start = ((), (), s32[]{:S(2)}) async-start(), calls=%async_computation.2 | async-start | bytes 6291456 | tf_op jit(solution)/shard_map/all_gather | solution.py:17
  7.9 131.9 %all-gather.3.cloned.1.call-start = ((), (), s32[]{:S(2)}) async-start(), calls=%async_computation.1 | async-start | bytes 3932160 | tf_op jit(solution)/shard_map/all_gather | solution.py:16
  8.6 619.0 %all-reduce.3.cloned.1.call-start = ((), (), s32[]{:S(2)}) async-start(), calls=%async_computation.3 | async-start | bytes 25165824
  485.2 0.7 copy-start.3
  485.2 142.4 %copy-start = (f32[1,12,8192]{2,0,1:T(1,128)S(1)}, f32[1,12,8192]{2,0,1:T(1,128)}, u32[]{:S(2)}) copy-start(f32[1,12,8192]{2,0,1:T(1,128)} %param.7) | copy-start | bytes 1179652
  485.2 142.4 %copy-start.1 = (f32[1,12,8192]{2,0,1:T(1,128)S(1)}, f32[1,12,8192]{2,0,1:T(1,128)}, u32[]{:S(2)}) copy-start(f32[1,12,8192]{2,0,1:T(1,128)} %param.8) | copy-start | bytes 1179652
  485.2 142.4 %copy-start.2 = (f32[1,12,8192]{2,0,1:T(1,128)S(1)}, f32[1,12,8192]{2,0,1:T(1,128)}, u32[]{:S(2)}) copy-start(f32[1,12,8192]{2,0,1:T(1,128)} %param.9) | copy-start | bytes 1179652
Sparse Core Ops, SparseCore 0:
  9.8 64.7 all-gather.4
  76.4 63.3 all-gather.2
  485.4 142.2 all-reduce.2
where the time goes:
time: 642 us; the launch traced here: 640 us
  blocking collectives  289 us (45%)
  waiting for transfers between devices  274 us (43%)
  local copies, waits for them, and re-layouts  45.1 us (7%)
  between operations  13.8 us (2%)
  matrix products  12.3 us (2%)
    all_to_all x1, blocking collectives, shards(): moved = lax.all_to_all(tile, 'tc', split_axis=1, concat_axis=3, tiled=True)  289 us
    unnamed x4, waiting for transfers between devices  142 us
    all_gather x1, waiting for transfers between devices, shards(): cot_rows = lax.all_gather(cotangent, 'tr', axis=0, tiled=True)  65.9 us
    all_gather x1, waiting for transfers between devices, shards(): act_rows = lax.all_gather(activations, 'tc', axis=0, tiled=True)  65.2 us
    reshape x2, local copies, waits for them, and re-layouts, shards(): tile = tile.reshape(replicas, columns, owned, unit_count)  32.4 us
  transfers between devices with their start and end apart: 3, of which 3 were waited for; matrix products, arithmetic and copies ran while one was open for 0% of the time, Pallas kernels for 0%

commit v1 on v0

v1 whole, which is shorter than its diff:
```python
import jax
import jax.numpy as jnp
from jax import lax
from jax.experimental import pallas as pl
from jax.experimental.pallas import tpu as pltpu
from jax.sharding import PartitionSpec as P

first_decay = 0.9
second_decay = 0.95
learn_rate = 0.0003
weight_decay = 0.1
epsilon = 1e-08
first_fix = 1.0 - 0.9**10
second_fix = 1.0 - 0.95**10

AXES = ("dp", "tr", "tc")
SIDE = 4
ROWS = 48
CHUNKS = (24, 24)


def moves(where):
    pairs = []
    for dp in range(32):
        for tr in range(2):
            for tc in range(4):
                y, x, core, z = where(dp // 8, dp // 2 % 4, dp % 2, 2 * tc + tr)
                to = (y % 4 * 8 + x % 4 * 2 + core % 2, z % 2, z % 8 // 2)
                pairs.append(((dp * 2 + tr) * 4 + tc, (to[0] * 2 + to[1]) * 4 + to[2]))
    return pairs


def step(first, sign):
    def where(y, x, core, z):
        if (core == 0) == first:
            return y, x + sign, core, z
        return y + sign, x, core, z

    return moves(where)


def send(array, pairs):
    return lax.ppermute(array, AXES, pairs)


OTHER_CORE = moves(lambda y, x, core, z: (y, x, 1 - core, z))
PAIR = moves(lambda y, x, core, z: (y, x, core, z ^ 1))


def feature_order(activations):
    dp = lax.axis_index("dp")
    my_y, my_x, core = dp // 8, dp // 2 % 4, dp % 2
    column = lax.broadcasted_iota(jnp.int32, (1, 2 * SIDE * SIDE * ROWS), 1)
    half, rest = column // (SIDE * SIDE * ROWS), column % (SIDE * SIDE * ROWS)
    target = jnp.where(half == 0, core, 1 - core)
    source = jnp.zeros_like(column)
    start = 0
    for rows in CHUNKS:
        size = SIDE * SIDE * rows
        inside = rest - start * SIDE * SIDE
        near, far, row = inside // (SIDE * rows), inside // rows % SIDE, inside % rows
        x = jnp.where(target == 0, my_x + near, my_x + far) % SIDE
        y = jnp.where(target == 0, my_y + far, my_y + near) % SIDE
        feature = (y * SIDE + x) * 2 * ROWS + target * ROWS + start + row
        source = jnp.where((inside >= 0) & (inside < size), feature, source)
        start += rows
    feature = lax.broadcasted_iota(jnp.int32, (activations.shape[1], column.shape[1]), 0)
    chosen = (feature == source).astype(activations.dtype)
    return jnp.dot(activations, chosen, preferred_element_type=jnp.float32).astype(activations.dtype)


def product_kernel(act, own_keep, own_came, far_keep, far_came, plus, minus, add_plus, add_minus, mine):
    tr = lax.axis_index("tr")
    features = act.shape[-1]

    def part(half, replica, cot):
        rows = act[pl.ds(2 * half, 2), 0, replica].reshape(cot.shape[0], features)
        return lax.dot_general(rows, cot[...], (((0,), (0,)), ((), ())), preferred_element_type=jnp.float32)

    total = part(tr, 0, own_keep) + part(1 - tr, 0, own_came)
    total = total + (part(tr, 1, far_keep) + part(1 - tr, 1, far_came))
    total = total.reshape(SIDE, SIDE, 1, features // SIDE**2, total.shape[-1])
    plus[0] = total[2, :2]
    plus[1] = total[1, 2:]
    minus[0] = total[2, 2:]
    minus[1] = total[3, :2]
    add_plus[...] = total[1, :2]
    add_minus[...] = total[3, 2:]
    mine[...] = total[0]


def product(act, cots):
    features, units = act.shape[-1], cots[0].shape[1]
    rows = features // SIDE**2
    whole = pl.BlockSpec(cots[0].shape, lambda i: (0, 0))
    lead = pl.BlockSpec((2, 2, 1, rows, units), lambda i: (0, 0, i, 0, 0))
    pack = pl.BlockSpec((2, 2, 1, rows, units), lambda i: (0, 0, i, 0, 0))
    part = pl.BlockSpec((2, 1, rows, units), lambda i: (0, i, 0, 0))
    full = pl.BlockSpec((SIDE, 1, rows, units), lambda i: (0, i, 0, 0))
    packed = jax.ShapeDtypeStruct((2, 2, 2, rows, units), jnp.float32)
    parted = jax.ShapeDtypeStruct((2, 2, rows, units), jnp.float32)
    return pl.pallas_call(
        product_kernel,
        grid=(2,),
        in_specs=[pl.BlockSpec((4, 1, 2, act.shape[3], features), lambda i: (0, i, 0, 0, 0))] + [whole] * 4,
        out_specs=[lead, pack, part, part, full],
        out_shape=[packed, packed, parted, parted, jax.ShapeDtypeStruct((SIDE, 2, rows, units), jnp.float32)],
        compiler_params=pltpu.CompilerParams(vmem_limit_bytes=40 * 2**20),
        cost_estimate=pl.CostEstimate(
            flops=2 * 2 * features * 4 * cots[0].shape[0] * units, bytes_accessed=12 * 2**20, transcendentals=0
        ),
    )(act, *cots)


def summed(parts):
    plus, minus, add_plus, add_minus, mine = parts
    left = send(plus, step(True, 1))
    right = send(minus, step(True, -1))
    near = send(add_plus + left[0], step(True, 1))
    far = send(add_minus + right[0], step(True, -1))
    low = mine[:2] + right[1] + near
    high = mine[2:] + left[1] + far
    left = send(jnp.stack([high[0, 0], low[1, 1]]), step(False, 1))
    right = send(jnp.stack([high[0, 1], high[1, 0]]), step(False, -1))
    near = send(low[1, 0] + left[0], step(False, 1))
    far = send(high[1, 1] + right[0], step(False, -1))
    return jnp.stack([low[0, 0] + right[1] + near, low[0, 1] + left[1] + far])


def shards(activations, cotangent, master, moment, second):
    tr = lax.axis_index("tr")
    tokens = activations.shape[0]
    units = cotangent.shape[1] // 2
    away = lax.dynamic_slice_in_dim(cotangent, (1 - tr) * units, units, 1)
    own_keep = lax.dynamic_slice_in_dim(cotangent, tr * units, units, 1)
    own_came = send(away, PAIR)
    far_keep = send(own_keep, OTHER_CORE)
    ordered = feature_order(activations)
    half = ordered.shape[1] // 2
    far_act = send(ordered[:, half:], OTHER_CORE)
    both = jnp.stack([ordered[:, :half], far_act])
    gathered = []
    start = 0
    for rows in CHUNKS:
        size = rows * SIDE**2
        block = lax.all_gather(both[:, :, start : start + size], ("tc", "tr"), axis=0)
        gathered.append(block.reshape(4, 2, 2, tokens, size))
        start += size
    far_came = send(own_came, OTHER_CORE)
    cots = (own_keep, own_came, far_keep, far_came)
    sums = [summed(product(block, cots)) for block in gathered]
    rows = jnp.concatenate(sums, axis=1)
    rows = rows.reshape(2, 4, ROWS // 4, units).swapaxes(0, 1).reshape(8, ROWS // 4, units)
    rows = lax.all_to_all(rows, ("tc", "tr"), split_axis=0, concat_axis=0, tiled=True)
    grad = rows.swapaxes(0, 1).reshape(1, ROWS // 4, 8 * units)
    new_moment = first_decay * moment + (1.0 - first_decay) * grad
    new_second = second_decay * second + (1.0 - second_decay) * grad * grad
    update = new_moment / first_fix / (jnp.sqrt(new_second / second_fix) + epsilon)
    new_master = master - learn_rate * (update + weight_decay * master)
    return (new_master, new_moment, new_second)


def solution(mesh):
    state = P("tr", ("dp", "tc"), None)
    return jax.shard_map(
        shards,
        mesh=mesh,
        in_specs=(P(("dp", "tc"), "tr"), P(("dp", "tr"), "tc"), state, state, state),
        out_specs=(state, state, state),
        check_vma=False,
    )
```

time: 642 us -> 205 us (0.32)
  blocking collectives: 289 us -> 17.4 us
  waiting for transfers between devices: 274 us -> 102 us
  starting transfers between devices: 0.11 us -> 29.6 us
  local copies, waits for them, and re-layouts: 45.1 us -> 23 us
  matrix products: 12.3 us -> 1.49 us
  Pallas kernels: 0 us -> 9.14 us
    all_to_all x1, blocking collectives: 289 us -> 17.4 us  [shards(): lax.all_to_all(rows, ('tc', 'tr'), split_axis=0, concat_axis=0, tiled=True)]
    unnamed x4 -> x2, waiting for transfers between devices: 142 us -> 0.03 us
    all_gather x2, waiting for transfers between devices: 131 us -> 49.6 us  [shards(): block = lax.all_gather(both[:, :, start:start + size], ('tc', 'tr'), axis=0)]
    ppermute x0 -> x20, waiting for transfers between devices: none -> 52.6 us  [send(): return lax.ppermute(array, AXES, pairs)]
    reshape x2, local copies, waits for them, and re-layouts: 32.4 us -> 0.25 us  [the longest x1 0.13 us: shards(): rows.reshape(2, 4, ROWS // 4, units).swapaxes(0, 1)]
    ppermute x0 -> x20, starting transfers between devices: none -> 29.6 us  [send(): return lax.ppermute(array, AXES, pairs)]
    unnamed x9 -> x33, local copies, waits for them, and re-layouts: 1.31 us -> 18.5 us
    all_to_all x1 -> x0, local copies, waits for them, and re-layouts: 11.3 us -> none  [shards(): moved = lax.all_to_all(tile, 'tc', split_axis=1, concat_axis=3, tiled=True)]
  transfers between devices with their start and end apart: 3 -> 22, of which waited for: 3 -> 11; matrix products, arithmetic and copies ran while one was open for 0% -> 3% of each run, Pallas kernels for 0% -> 5%
where the time goes in v1:
time: 205 us; the launch traced here: 202 us
  waiting for transfers between devices  102 us (50%)
  starting transfers between devices  29.6 us (14%)
  local copies, waits for them, and re-layouts  23 us (11%)
  blocking collectives  17.4 us (8%)
  between operations  14.4 us (7%)
  Pallas kernels  9.14 us (4%)
  other arithmetic  4.96 us (2%)
    ppermute x20, waiting for transfers between devices, send(): return lax.ppermute(array, AXES, pairs)  52.6 us
    all_gather x2, waiting for transfers between devices, shards(): block = lax.all_gather(both[:, :, start:start + size], ('tc', 'tr'), axis=0)  49.6 us
    ppermute x20, starting transfers between devices, send(): return lax.ppermute(array, AXES, pairs)  29.6 us
    unnamed x33, local copies, waits for them, and re-layouts  18.5 us
    all_to_all x1, blocking collectives, shards(): lax.all_to_all(rows, ('tc', 'tr'), split_axis=0, concat_axis=0, tiled=True)  17.4 us
    pallas_call x2, Pallas kernels, product(): pl.pallas_call(product_kernel, grid=(2,), in_specs=[pl.BlockSpec((4, 1, 2...  9.14 us
  transfers between devices with their start and end apart: 22, of which 11 were waited for; matrix products, arithmetic and copies ran while one was open for 3% of the time, Pallas kernels for 5%

profile of v1, /device:TPU:6, one launch (start us, length us, event | category | flops | bytes accessed | tf_op | source)
XLA Modules:
  0.0 202.3 jit_solution(3400914206659710531)
XLA Ops:
  7.3 0.1 fusion.47
  7.3 1.0 copy-done
  8.3 1.5 fusion.7
  9.8 0.1 slice_bitcast_fusion.8
  9.9 0.1 collective-permute-start
  10.0 1.7 collective-permute-done
  11.7 0.1 fusion.14
  11.7 0.9 copy.29
  12.7 0.0 all-gather.7.cloned.1.call-start
  12.7 0.9 copy.30
  13.7 1.7 constant_dynamic-slice_fusion
  15.4 2.0 collective-permute-start.1
  17.4 36.7 %collective-permute-done.1.own_came = bf16[512,1024]{1,0:T(8,128)(2,1)S(1)} collective-permute-done((bf16[512,1024]{1,0:T(8,128)(2,1)S(1)}, bf16[512,1024]{1,0:T(8,128)(2,1)S(1)}, u32[]{:S(2)}, u32[]{:S(2)}) %collective-permute-start.1) | collective-permute-done | bytes 1048608 | tf_op jit(solution)/shard_map/ppermute | solution.py:43
  54.1 1.0 copy-done.3
  55.1 1.0 copy-done.6
  56.1 0.6 collective-permute-done.3.far_came
  56.7 1.0 copy-done.9
  57.7 17.2 %all-gather.5.cloned.1.call-done = bf16[16,256,384]{2,1,0:T(8,128)(2,1)} async-done(((bf16[2,256,384]{2,1,0:T(8,128)(2,1)}), bf16[16,256,384]{2,1,0:T(8,128)(2,1)}) %all-gather.5.cloned.1.call-update) | async-done | bytes 3145744 | tf_op jit(solution)/shard_map/all_gather | solution.py:146
  74.9 1.9 copy-done.2
  76.7 1.2 copy-done.4
  78.0 1.2 copy-done.7
  79.2 1.2 copy-done.10
  80.4 4.9 %shard_map.76 = (f32[2,2,2,24,1024]{4,3,2,1,0:T(8,128)}, f32[2,2,2,24,1024]{4,3,2,1,0:T(8,128)}, f32[2,2,24,1024]{3,2,1,0:T(8,128)S(1)}, f32[2,2,24,1024]{3,2,1,0:T(8,128)S(1)}, f32[4,2,24,1024]{3,2,1,0:T(8,128)S(1)}) custom-call(bf16[4,2,2,256,384]{4,3,2,1,0:T(8,128)(2,1)S(1)} %bitcast.158, bf16[512,1024]{1,0:T(8,128)(2,1)S(1)} %get-tuple-element.33.own_keep, ...), custom_call_target="tpu_custom_call" | custom-call | flops 3221225472 | bytes 12582912 | tf_op jit(solution)/shard_map/pallas_call | solution.py:102
  85.4 0.8 collective-permute-start.4
  86.2 2.4 %collective-permute-start.5 = (f32[2,2,2,24,1024]{4,3,2,1,0:T(8,128)}, f32[2,2,2,24,1024]{4,3,2,1,0:T(8,128)}, u32[]{:S(2)}, u32[]{:S(2)}) collective-permute-start(f32[2,2,2,24,1024]{4,3,2,1,0:T(8,128)} %get-tuple-element.16), channel_id=1, source_target_pairs={{0,16},{1,17},{2,18},{3,19},{4,20},{5,21},{6,22},{7,23},{8,72},{9,... | collective-permute-start | bytes 2359304 | tf_op jit(solution)/shard_map/ppermute | solution.py:43
  88.6 32.4 %all-gather.7.cloned.1.call-done = bf16[16,256,384]{2,1,0:T(8,128)(2,1)} async-done(((bf16[2,256,384]{2,1,0:T(8,128)(2,1)}), bf16[16,256,384]{2,1,0:T(8,128)(2,1)}) %all-gather.7.cloned.1.call-update) | async-done | bytes 3145744 | tf_op jit(solution)/shard_map/all_gather | solution.py:146
  121.0 1.9 copy-done.1
  122.9 1.2 copy-done.5
  124.2 1.2 copy-done.8
  125.4 1.2 copy-done.11
  126.6 4.2 %shard_map.77 = (f32[2,2,2,24,1024]{4,3,2,1,0:T(8,128)S(1)}, f32[2,2,2,24,1024]{4,3,2,1,0:T(8,128)S(1)}, f32[2,2,24,1024]{3,2,1,0:T(8,128)S(1)}, f32[2,2,24,1024]{3,2,1,0:T(8,128)S(1)}, f32[4,2,24,1024]{3,2,1,0:T(8,128)S(1)}) custom-call(bf16[4,2,2,256,384]{4,3,2,1,0:T(8,128)(2,1)S(1)} %bitcast.157, bf16[512,1024]{1,0:T(8,128)(2,1)S(1)} %get-tuple-element.33.own_keep, ...), custom_call_target="tpu_custom_call" | custom-call | flops 3221225472 | bytes 12582912 | tf_op jit(solution)/shard_map/pallas_call | solution.py:102
  130.8 0.9 collective-permute-start.12
  131.7 2.4 %collective-permute-start.13 = (f32[2,2,2,24,1024]{4,3,2,1,0:T(8,128)S(1)}, f32[2,2,2,24,1024]{4,3,2,1,0:T(8,128)S(1)}, u32[]{:S(2)}, u32[]{:S(2)}) collective-permute-start(f32[2,2,2,24,1024]{4,3,2,1,0:T(8,128)S(1)} %get-tuple-element.21), channel_id=1, source_target_pairs={{0,16},{1,17},{2,18},{3,19},{4,20},{5,21},{6,22},{7,23},{8,72},{9,... | collective-permute-start | bytes 2359304 | tf_op jit(solution)/shard_map/ppermute | solution.py:43
  134.1 1.0 fusion.21
  135.2 0.1 collective-permute-start.7
  135.3 1.0 fusion.24
  136.3 3.5 %collective-permute-start.6 = (f32[2,2,24,1024]{3,2,1,0:T(8,128)S(1)}, f32[2,2,24,1024]{3,2,1,0:T(8,128)S(1)}, u32[]{:S(2)}, u32[]{:S(2)}) collective-permute-start(f32[2,2,24,1024]{3,2,1,0:T(8,128)S(1)} %fusion.24), channel_id=1, source_target_pairs={{0,16},{1,17},{2,18},{3,19},{4,20},{5,21},{6,22},{7,23},{8,72},{9,... | collective-permute-start | bytes 1179656 | tf_op jit(solution)/shard_map/ppermute | solution.py:43
  139.8 4.3 %collective-permute-done.12 = f32[2,2,2,24,1024]{4,3,2,1,0:T(8,128)S(1)} collective-permute-done((f32[2,2,2,24,1024]{4,3,2,1,0:T(8,128)S(1)}, f32[2,2,2,24,1024]{4,3,2,1,0:T(8,128)S(1)}, u32[]{:S(2)}, u32[]{:S(2)}) %collective-permute-start.12) | collective-permute-done | bytes 786464 | tf_op jit(solution)/shard_map/ppermute | solution.py:43
  144.1 0.1 collective-permute-start.15
  144.3 3.3 %collective-permute-start.14 = (f32[2,2,24,1024]{3,2,1,0:T(8,128)S(1)}, f32[2,2,24,1024]{3,2,1,0:T(8,128)S(1)}, u32[]{:S(2)}, u32[]{:S(2)}) collective-permute-start(f32[2,2,24,1024]{3,2,1,0:T(8,128)S(1)} %fusion.18), channel_id=1, source_target_pairs={{0,16},{1,17},{2,18},{3,19},{4,20},{5,21},{6,22},{7,23},{8,72},{9,... | collective-permute-start | bytes 1179656 | tf_op jit(solution)/shard_map/ppermute | solution.py:43
  147.6 0.7 collective-permute-done.7
  148.3 1.3 fusion.26
  149.7 2.8 %collective-permute-start.8 = (f32[2,24,1024]{2,1,0:T(8,128)S(1)}, f32[2,24,1024]{2,1,0:T(8,128)S(1)}, u32[]{:S(2)}, u32[]{:S(2)}) collective-permute-start(f32[2,24,1024]{2,1,0:T(8,128)S(1)} %pad_maximum_fusion.1), channel_id=1, source_target_pairs={{0,192},{1,193},{2,194},{3,195},{4,196},{5,197},{6,198},{7,199},{8... | collective-permute-start | bytes 589832 | tf_op jit(solution)/shard_map/ppermute | solution.py:43
  152.5 0.1 collective-permute-start.9
  152.6 0.6 collective-permute-done.15
  153.2 0.2 fusion.20
  153.4 3.7 %collective-permute-start.16 = (f32[2,24,1024]{2,1,0:T(8,128)S(1)}, f32[2,24,1024]{2,1,0:T(8,128)S(1)}, u32[]{:S(2)}, u32[]{:S(2)}) collective-permute-start(f32[2,24,1024]{2,1,0:T(8,128)S(1)} %pad_maximum_fusion.3), channel_id=1, source_target_pairs={{0,192},{1,193},{2,194},{3,195},{4,196},{5,197},{6,198},{7,199},{8... | collective-permute-start | bytes 589832 | tf_op jit(solution)/shard_map/ppermute | solution.py:43
  157.1 0.1 collective-permute-start.17
  157.3 3.3 %collective-permute-start.11 = (f32[24,1024]{1,0:T(8,128)S(1)}, f32[24,1024]{1,0:T(8,128)S(1)}, u32[]{:S(2)}, u32[]{:S(2)}) collective-permute-start(f32[24,1024]{1,0:T(8,128)S(1)} %fusion.35), channel_id=1, source_target_pairs={{0,192},{1,193},{2,194},{3,195},{4,196},{5,197},{6,198},{7,199},{8... | collective-permute-start | bytes 294920 | tf_op jit(solution)/shard_map/ppermute | solution.py:43
  160.6 3.5 %collective-permute-start.19 = (f32[24,1024]{1,0:T(8,128)S(1)}, f32[24,1024]{1,0:T(8,128)S(1)}, u32[]{:S(2)}, u32[]{:S(2)}) collective-permute-start(f32[24,1024]{1,0:T(8,128)S(1)} %fusion.27), channel_id=1, source_target_pairs={{0,192},{1,193},{2,194},{3,195},{4,196},{5,197},{6,198},{7,199},{8... | collective-permute-start | bytes 294920 | tf_op jit(solution)/shard_map/ppermute | solution.py:43
  164.1 0.1 collective-permute-start.10
  164.2 2.1 %collective-permute-done.19 = f32[24,1024]{1,0:T(8,128)S(1)} collective-permute-done((f32[24,1024]{1,0:T(8,128)S(1)}, f32[24,1024]{1,0:T(8,128)S(1)}, u32[]{:S(2)}, u32[]{:S(2)}) %collective-permute-start.19) | collective-permute-done | bytes 98336 | tf_op jit(solution)/shard_map/ppermute | solution.py:43
  166.4 0.4 collective-permute-start.18
  166.8 3.2 %collective-permute-done.10 = f32[24,1024]{1,0:T(8,128)S(1)} collective-permute-done((f32[24,1024]{1,0:T(8,128)S(1)}, f32[24,1024]{1,0:T(8,128)S(1)}, u32[]{:S(2)}, u32[]{:S(2)}) %collective-permute-start.10) | collective-permute-done | bytes 98336 | tf_op jit(solution)/shard_map/ppermute | solution.py:43
  170.1 2.6 %collective-permute-done.18 = f32[24,1024]{1,0:T(8,128)S(1)} collective-permute-done((f32[24,1024]{1,0:T(8,128)S(1)}, f32[24,1024]{1,0:T(8,128)S(1)}, u32[]{:S(2)}, u32[]{:S(2)}) %collective-permute-start.18) | collective-permute-done | bytes 98336 | tf_op jit(solution)/shard_map/ppermute | solution.py:43
  172.7 0.3 copy.31
  173.0 0.1 copy.41
  173.2 17.4 %all_to_all.5 = f32[8,12,1024]{2,1,0:T(8,128)S(1)} all-to-all(f32[8,12,1024]{2,1,0:T(8,128)S(1)} %bitcast.159), channel_id=1, replica_groups=mesh['dp'=32,'tr'=2,'tc'=4] {'tc','tr'}, dimensions={0} | all-to-all | bytes 786432 | tf_op jit(solution)/shard_map/all_to_all | solution.py:154
  190.6 0.2 copy.34
  190.9 0.1 reshape.347
  191.0 1.0 copy_subtract_fusion
  192.0 1.2 copy.38
  193.1 1.1 copy.39
  194.3 1.1 copy.40
  (51 shorter events, 0.5 us)
Async XLA Ops:
  7.2 1.1 copy-start
  7.2 67.7 %all-gather.5.cloned.1.call-start = ((), (), s32[]{:S(2)}) async-start(), calls=%async_computation.1 | async-start | bytes 3538944 | tf_op jit(solution)/shard_map/all_gather | solution.py:146
  9.9 1.8 collective-permute-start
  12.7 108.4 %all-gather.7.cloned.1.call-start = ((), (), s32[]{:S(2)}) async-start(), calls=%async_computation.2 | async-start | bytes 3538944 | tf_op jit(solution)/shard_map/all_gather | solution.py:146
  15.4 38.7 %collective-permute-start.1 = (bf16[512,1024]{1,0:T(8,128)(2,1)S(1)}, bf16[512,1024]{1,0:T(8,128)(2,1)S(1)}, u32[]{:S(2)}, u32[]{:S(2)}) collective-permute-start(bf16[512,1024]{1,0:T(8,128)(2,1)S(1)} %get-tuple-element.32), channel_id=1, source_target_pairs={{0,4},{1,5},{2,6},{3,7},{4,0},{5,1},{6,2},{7,3},{8,12},{9,13},{10,... | collective-permute-start | bytes 3145736 | tf_op jit(solution)/shard_map/ppermute | solution.py:43
  17.4 37.7 %collective-permute-start.2 = (bf16[512,1024]{1,0:T(8,128)(2,1)S(1)}, bf16[512,1024]{1,0:T(8,128)(2,1)S(1)}, u32[]{:S(2)}, u32[]{:S(2)}) collective-permute-start(bf16[512,1024]{1,0:T(8,128)(2,1)S(1)} %get-tuple-element.33.own_keep), channel_id=1, source_target_pairs={{0,8},{1,9},{2,10},{3,11},{4,12},{5,13},{6,14},{7,15},{8,0},{9,1},... | collective-permute-start | bytes 3145736 | tf_op jit(solution)/shard_map/ppermute | solution.py:43
  54.1 2.7 %collective-permute-start.3 = (bf16[512,1024]{1,0:T(8,128)(2,1)S(1)}, bf16[512,1024]{1,0:T(8,128)(2,1)S(1)}, u32[]{:S(2)}, u32[]{:S(2)}) collective-permute-start(bf16[512,1024]{1,0:T(8,128)(2,1)S(1)} %collective-permute-done.1.own_came), channel_id=1, source_target_pairs={{0,8},{1,9},{2,10},{3,11},{4,12},{5,13},{6,14},{7,15},{8,0},{9,1},... | collective-permute-start | bytes 3145736 | tf_op jit(solution)/shard_map/ppermute | solution.py:43
  54.1 1.0 copy-start.3
  55.1 1.0 copy-start.6
  56.7 1.0 copy-start.9
  74.9 1.9 copy-start.2
  76.7 1.2 copy-start.4
  78.0 1.2 copy-start.7
  79.2 1.2 copy-start.10
  85.4 48.8 %collective-permute-start.4 = (f32[2,2,2,24,1024]{4,3,2,1,0:T(8,128)}, f32[2,2,2,24,1024]{4,3,2,1,0:T(8,128)}, u32[]{:S(2)}, u32[]{:S(2)}) collective-permute-start(f32[2,2,2,24,1024]{4,3,2,1,0:T(8,128)} %get-tuple-element.14), channel_id=1, source_target_pairs={{0,48},{1,49},{2,50},{3,51},{4,52},{5,53},{6,54},{7,55},{8,200},{9... | collective-permute-start | bytes 2359304 | tf_op jit(solution)/shard_map/ppermute | solution.py:43
  86.2 49.1 %collective-permute-start.5 = (f32[2,2,2,24,1024]{4,3,2,1,0:T(8,128)}, f32[2,2,2,24,1024]{4,3,2,1,0:T(8,128)}, u32[]{:S(2)}, u32[]{:S(2)}) collective-permute-start(f32[2,2,2,24,1024]{4,3,2,1,0:T(8,128)} %get-tuple-element.16), channel_id=1, source_target_pairs={{0,16},{1,17},{2,18},{3,19},{4,20},{5,21},{6,22},{7,23},{8,72},{9,... | collective-permute-start | bytes 2359304 | tf_op jit(solution)/shard_map/ppermute | solution.py:43
  121.0 1.9 copy-start.1
  122.9 1.2 copy-start.5
  124.2 1.2 copy-start.8
  125.4 1.2 copy-start.11
  130.8 13.3 %collective-permute-start.12 = (f32[2,2,2,24,1024]{4,3,2,1,0:T(8,128)S(1)}, f32[2,2,2,24,1024]{4,3,2,1,0:T(8,128)S(1)}, u32[]{:S(2)}, u32[]{:S(2)}) collective-permute-start(f32[2,2,2,24,1024]{4,3,2,1,0:T(8,128)S(1)} %get-tuple-element.19), channel_id=1, source_target_pairs={{0,48},{1,49},{2,50},{3,51},{4,52},{5,53},{6,54},{7,55},{8,200},{9... | collective-permute-start | bytes 2359304 | tf_op jit(solution)/shard_map/ppermute | solution.py:43
  131.7 12.5 %collective-permute-start.13 = (f32[2,2,2,24,1024]{4,3,2,1,0:T(8,128)S(1)}, f32[2,2,2,24,1024]{4,3,2,1,0:T(8,128)S(1)}, u32[]{:S(2)}, u32[]{:S(2)}) collective-permute-start(f32[2,2,2,24,1024]{4,3,2,1,0:T(8,128)S(1)} %get-tuple-element.21), channel_id=1, source_target_pairs={{0,16},{1,17},{2,18},{3,19},{4,20},{5,21},{6,22},{7,23},{8,72},{9,... | collective-permute-start | bytes 2359304 | tf_op jit(solution)/shard_map/ppermute | solution.py:43
  135.2 13.1 %collective-permute-start.7 = (f32[2,2,24,1024]{3,2,1,0:T(8,128)S(1)}, f32[2,2,24,1024]{3,2,1,0:T(8,128)S(1)}, u32[]{:S(2)}, u32[]{:S(2)}) collective-permute-start(f32[2,2,24,1024]{3,2,1,0:T(8,128)S(1)} %fusion.21), channel_id=1, source_target_pairs={{0,48},{1,49},{2,50},{3,51},{4,52},{5,53},{6,54},{7,55},{8,200},{9... | collective-permute-start | bytes 1179656 | tf_op jit(solution)/shard_map/ppermute | solution.py:43
  136.3 12.0 %collective-permute-start.6 = (f32[2,2,24,1024]{3,2,1,0:T(8,128)S(1)}, f32[2,2,24,1024]{3,2,1,0:T(8,128)S(1)}, u32[]{:S(2)}, u32[]{:S(2)}) collective-permute-start(f32[2,2,24,1024]{3,2,1,0:T(8,128)S(1)} %fusion.24), channel_id=1, source_target_pairs={{0,16},{1,17},{2,18},{3,19},{4,20},{5,21},{6,22},{7,23},{8,72},{9,... | collective-permute-start | bytes 1179656 | tf_op jit(solution)/shard_map/ppermute | solution.py:43
  144.1 9.1 %collective-permute-start.15 = (f32[2,2,24,1024]{3,2,1,0:T(8,128)S(1)}, f32[2,2,24,1024]{3,2,1,0:T(8,128)S(1)}, u32[]{:S(2)}, u32[]{:S(2)}) collective-permute-start(f32[2,2,24,1024]{3,2,1,0:T(8,128)S(1)} %fusion.15), channel_id=1, source_target_pairs={{0,48},{1,49},{2,50},{3,51},{4,52},{5,53},{6,54},{7,55},{8,200},{9... | collective-permute-start | bytes 1179656 | tf_op jit(solution)/shard_map/ppermute | solution.py:43
  144.3 8.9 %collective-permute-start.14 = (f32[2,2,24,1024]{3,2,1,0:T(8,128)S(1)}, f32[2,2,24,1024]{3,2,1,0:T(8,128)S(1)}, u32[]{:S(2)}, u32[]{:S(2)}) collective-permute-start(f32[2,2,24,1024]{3,2,1,0:T(8,128)S(1)} %fusion.18), channel_id=1, source_target_pairs={{0,16},{1,17},{2,18},{3,19},{4,20},{5,21},{6,22},{7,23},{8,72},{9,... | collective-permute-start | bytes 1179656 | tf_op jit(solution)/shard_map/ppermute | solution.py:43
  149.7 7.6 %collective-permute-start.8 = (f32[2,24,1024]{2,1,0:T(8,128)S(1)}, f32[2,24,1024]{2,1,0:T(8,128)S(1)}, u32[]{:S(2)}, u32[]{:S(2)}) collective-permute-start(f32[2,24,1024]{2,1,0:T(8,128)S(1)} %pad_maximum_fusion.1), channel_id=1, source_target_pairs={{0,192},{1,193},{2,194},{3,195},{4,196},{5,197},{6,198},{7,199},{8... | collective-permute-start | bytes 589832 | tf_op jit(solution)/shard_map/ppermute | solution.py:43
  152.5 11.6 %collective-permute-start.9 = (f32[2,24,1024]{2,1,0:T(8,128)S(1)}, f32[2,24,1024]{2,1,0:T(8,128)S(1)}, u32[]{:S(2)}, u32[]{:S(2)}) collective-permute-start(f32[2,24,1024]{2,1,0:T(8,128)S(1)} %pad_maximum_fusion.2), channel_id=1, source_target_pairs={{0,64},{1,65},{2,66},{3,67},{4,68},{5,69},{6,70},{7,71},{8,24},{9,... | collective-permute-start | bytes 589832 | tf_op jit(solution)/shard_map/ppermute | solution.py:43
  153.4 7.1 %collective-permute-start.16 = (f32[2,24,1024]{2,1,0:T(8,128)S(1)}, f32[2,24,1024]{2,1,0:T(8,128)S(1)}, u32[]{:S(2)}, u32[]{:S(2)}) collective-permute-start(f32[2,24,1024]{2,1,0:T(8,128)S(1)} %pad_maximum_fusion.3), channel_id=1, source_target_pairs={{0,192},{1,193},{2,194},{3,195},{4,196},{5,197},{6,198},{7,199},{8... | collective-permute-start | bytes 589832 | tf_op jit(solution)/shard_map/ppermute | solution.py:43
  157.1 7.1 %collective-permute-start.17 = (f32[2,24,1024]{2,1,0:T(8,128)S(1)}, f32[2,24,1024]{2,1,0:T(8,128)S(1)}, u32[]{:S(2)}, u32[]{:S(2)}) collective-permute-start(f32[2,24,1024]{2,1,0:T(8,128)S(1)} %pad_maximum_fusion.4), channel_id=1, source_target_pairs={{0,64},{1,65},{2,66},{3,67},{4,68},{5,69},{6,70},{7,71},{8,24},{9,... | collective-permute-start | bytes 589832 | tf_op jit(solution)/shard_map/ppermute | solution.py:43
  157.3 6.8 %collective-permute-start.11 = (f32[24,1024]{1,0:T(8,128)S(1)}, f32[24,1024]{1,0:T(8,128)S(1)}, u32[]{:S(2)}, u32[]{:S(2)}) collective-permute-start(f32[24,1024]{1,0:T(8,128)S(1)} %fusion.35), channel_id=1, source_target_pairs={{0,192},{1,193},{2,194},{3,195},{4,196},{5,197},{6,198},{7,199},{8... | collective-permute-start | bytes 294920 | tf_op jit(solution)/shard_map/ppermute | solution.py:43
  160.6 5.7 %collective-permute-start.19 = (f32[24,1024]{1,0:T(8,128)S(1)}, f32[24,1024]{1,0:T(8,128)S(1)}, u32[]{:S(2)}, u32[]{:S(2)}) collective-permute-start(f32[24,1024]{1,0:T(8,128)S(1)} %fusion.27), channel_id=1, source_target_pairs={{0,192},{1,193},{2,194},{3,195},{4,196},{5,197},{6,198},{7,199},{8... | collective-permute-start | bytes 294920 | tf_op jit(solution)/shard_map/ppermute | solution.py:43
  164.1 5.9 %collective-permute-start.10 = (f32[24,1024]{1,0:T(8,128)S(1)}, f32[24,1024]{1,0:T(8,128)S(1)}, u32[]{:S(2)}, u32[]{:S(2)}) collective-permute-start(f32[24,1024]{1,0:T(8,128)S(1)} %get-tuple-element.42), channel_id=1, source_target_pairs={{0,64},{1,65},{2,66},{3,67},{4,68},{5,69},{6,70},{7,71},{8,24},{9,... | collective-permute-start | bytes 294920 | tf_op jit(solution)/shard_map/ppermute | solution.py:43
  166.3 24.6 %copy-start.12 = (f32[1,12,8192]{2,0,1:T(1,128)S(1)}, f32[1,12,8192]{2,0,1:T(1,128)}, u32[]{:S(2)}) copy-start(f32[1,12,8192]{2,0,1:T(1,128)} %param.7) | copy-start | bytes 1179652
  166.4 24.6 %copy-start.13 = (f32[1,12,8192]{2,0,1:T(1,128)S(1)}, f32[1,12,8192]{2,0,1:T(1,128)}, u32[]{:S(2)}) copy-start(f32[1,12,8192]{2,0,1:T(1,128)} %param.8) | copy-start | bytes 1179652
  166.4 24.6 %copy-start.14 = (f32[1,12,8192]{2,0,1:T(1,128)S(1)}, f32[1,12,8192]{2,0,1:T(1,128)}, u32[]{:S(2)}) copy-start(f32[1,12,8192]{2,0,1:T(1,128)} %param.9) | copy-start | bytes 1179652
  166.4 6.3 %collective-permute-start.18 = (f32[24,1024]{1,0:T(8,128)S(1)}, f32[24,1024]{1,0:T(8,128)S(1)}, u32[]{:S(2)}, u32[]{:S(2)}) collective-permute-start(f32[24,1024]{1,0:T(8,128)S(1)} %get-tuple-element.44), channel_id=1, source_target_pairs={{0,64},{1,65},{2,66},{3,67},{4,68},{5,69},{6,70},{7,71},{8,24},{9,... | collective-permute-start | bytes 294920 | tf_op jit(solution)/shard_map/ppermute | solution.py:43
Sparse Core Ops, SparseCore 0:
  12.8 62.0 all-gather.4
  77.2 43.7 all-gather.6

commit v2 on v1

--- a/solution.py
+++ b/solution.py
@@ -105,7 +105,7 @@
         in_specs=[pl.BlockSpec((4, 1, 2, act.shape[3], features), lambda i: (0, i, 0, 0, 0))] + [whole] * 4,
         out_specs=[lead, pack, part, part, full],
         out_shape=[packed, packed, parted, parted, jax.ShapeDtypeStruct((SIDE, 2, rows, units), jnp.float32)],
-        compiler_params=pltpu.CompilerParams(vmem_limit_bytes=40 * 2**20),
+        compiler_params=pltpu.CompilerParams(vmem_limit_bytes=58 * 2**20),
         cost_estimate=pl.CostEstimate(
             flops=2 * 2 * features * 4 * cots[0].shape[0] * units, bytes_accessed=12 * 2**20, transcendentals=0
         ),
@@ -148,16 +148,48 @@
         start += size
     far_came = send(own_came, OTHER_CORE)
     cots = (own_keep, own_came, far_keep, far_came)
-    sums = [summed(product(block, cots)) for block in gathered]
-    rows = jnp.concatenate(sums, axis=1)
-    rows = rows.reshape(2, 4, ROWS // 4, units).swapaxes(0, 1).reshape(8, ROWS // 4, units)
-    rows = lax.all_to_all(rows, ("tc", "tr"), split_axis=0, concat_axis=0, tiled=True)
-    grad = rows.swapaxes(0, 1).reshape(1, ROWS // 4, 8 * units)
-    new_moment = first_decay * moment + (1.0 - first_decay) * grad
-    new_second = second_decay * second + (1.0 - second_decay) * grad * grad
-    update = new_moment / first_fix / (jnp.sqrt(new_second / second_fix) + epsilon)
-    new_master = master - learn_rate * (update + weight_decay * master)
-    return (new_master, new_moment, new_second)
+    sums = []
+    for block in gathered:
+        if sums:
+            block, sums[-1] = lax.optimization_barrier((block, sums[-1]))
+        sums.append(summed(product(block, cots)))
+    rows = jnp.concatenate(sums, axis=1).reshape(2, 4, ROWS // 4, 8, units // 8)
+    return updated(rows, master, moment, second)
+
+
+def updated(rows, master, moment, second):
+    tr, tc = lax.axis_index("tr"), lax.axis_index("tc")
+    keep = lax.dynamic_index_in_dim(rows, tr, 0, keepdims=False)
+    came = send(lax.dynamic_index_in_dim(rows, 1 - tr, 0, keepdims=False), PAIR)
+    both = jnp.stack([keep, came], axis=1)
+    pieces = []
+    for k in range(4):
+        piece = lax.dynamic_index_in_dim(both, (tc + k) % 4, 0, keepdims=False)
+        pieces.append(send(piece, moves(lambda y, x, core, z: (y, x, core, z + 2 * k))) if k else piece)
+    wide = (ROWS // 4, 8 * rows.shape[3], rows.shape[4])
+    flat = [array.reshape(wide) for array in (master, moment, second)]
+    outs = pl.pallas_call(
+        update_kernel,
+        out_shape=[jax.ShapeDtypeStruct(wide, jnp.float32)] * 3,
+        compiler_params=pltpu.CompilerParams(vmem_limit_bytes=16 * 2**20),
+    )(*pieces, *flat)
+    return tuple(out.reshape(master.shape) for out in outs)
+
+
+def update_kernel(piece_0, piece_1, piece_2, piece_3, master, moment, second, new_master, new_moment, new_second):
+    tr, tc = lax.axis_index("tr"), lax.axis_index("tc")
+    for k, piece in enumerate((piece_0, piece_1, piece_2, piece_3)):
+        for came in range(2):
+            owner = 2 * ((tc + 4 - k) % 4) + (1 - tr if came else tr)
+            place = (slice(None), pl.ds(pl.multiple_of(owner * 8, 8), 8), slice(None))
+            grad = piece[came]
+            first = first_decay * moment[place] + (1.0 - first_decay) * grad
+            square = second_decay * second[place] + (1.0 - second_decay) * grad * grad
+            old = master[place]
+            update = first / first_fix / (jnp.sqrt(square / second_fix) + epsilon)
+            new_moment[place] = first
+            new_second[place] = square
+            new_master[place] = old - learn_rate * (update + weight_decay * old)
 
 
 def solution(mesh):

time: 205 us -> 210 us (1.024)
  waiting for transfers between devices: 102 us -> 124 us
  local copies, waits for them, and re-layouts: 23 us -> 5.59 us
  blocking collectives: 17.4 us -> 0 us
  starting transfers between devices: 29.6 us -> 38.5 us
  Pallas kernels: 9.14 us -> 16.4 us
  other arithmetic: 4.96 us -> 7.91 us
    ppermute x20 -> x24, waiting for transfers between devices: 52.6 us -> 105 us  [send(): return lax.ppermute(array, AXES, pairs)]
    all_gather x2, waiting for transfers between devices: 49.6 us -> 18.9 us  [shards(): block = lax.all_gather(both[:, :, start:start + size], ('tc', 'tr'), axis=0)]
    unnamed x33 -> x15, local copies, waits for them, and re-layouts: 18.5 us -> 1.07 us
    all_to_all x1 -> x0, blocking collectives: 17.4 us -> none  [shards(): lax.all_to_all(rows, ('tc', 'tr'), split_axis=0, concat_axis=0, tiled=True)]
    ppermute x20 -> x24, starting transfers between devices: 29.6 us -> 38.4 us  [send(): return lax.ppermute(array, AXES, pairs)]
    pallas_call x2, Pallas kernels: 9.14 us -> 15.1 us  [product(): pl.pallas_call(product_kernel, grid=(2,), in_specs=[pl.BlockSpec((4, 1, 2...]
  transfers between devices with their start and end apart: 22 -> 26, of which waited for: 11 -> 20; matrix products, arithmetic and copies ran while one was open for 3% -> 4% of each run, Pallas kernels for 5% -> 4%
where the time goes in v2:
time: 210 us; the launch traced here: 208 us
  waiting for transfers between devices  124 us (59%)
  starting transfers between devices  38.5 us (18%)
  Pallas kernels  16.4 us (8%)
  between operations  14.4 us (7%)
  other arithmetic  7.91 us (4%)
  local copies, waits for them, and re-layouts  5.59 us (3%)
    ppermute x24, waiting for transfers between devices, send(): return lax.ppermute(array, AXES, pairs)  105 us
    ppermute x24, starting transfers between devices, send(): return lax.ppermute(array, AXES, pairs)  38.4 us
    all_gather x2, waiting for transfers between devices, shards(): block = lax.all_gather(both[:, :, start:start + size], ('tc', 'tr'), axis=0)  18.9 us
    pallas_call x2, Pallas kernels, product(): pl.pallas_call(product_kernel, grid=(2,), in_specs=[pl.BlockSpec((4, 1, 2...  15.1 us
  transfers between devices with their start and end apart: 26, of which 20 were waited for; matrix products, arithmetic and copies ran while one was open for 4% of the time, Pallas kernels for 4%

profile of v2, /device:TPU:6, one launch (start us, length us, event | category | flops | bytes accessed | tf_op | source)
XLA Modules:
  0.0 208.4 jit_solution(9930203709060496337)
XLA Ops:
  7.2 0.0 all-gather.7.cloned.1.call-start
  7.3 0.1 fusion.51
  7.3 1.0 copy-done
  8.3 1.5 fusion.7
  9.8 0.1 fusion.89
  9.9 0.1 collective-permute-start
  10.0 1.7 collective-permute-done
  11.7 0.8 pad_maximum_fusion
  12.5 1.9 copy.19
  14.4 0.0 all-gather.7.cloned.1.call-update
  14.4 0.0 all-gather.5.cloned.1.call-start
  14.5 1.5 constant_dynamic-slice_fusion
  16.0 1.9 collective-permute-start.1
  17.9 0.9 copy.18
  18.9 0.1 collective-permute-start.2
  19.0 35.0 %collective-permute-done.1.own_came = bf16[512,1024]{1,0:T(8,128)(2,1)S(1)} collective-permute-done((bf16[512,1024]{1,0:T(8,128)(2,1)}, bf16[512,1024]{1,0:T(8,128)(2,1)S(1)}, u32[]{:S(2)}, u32[]{:S(2)}) %collective-permute-start.1) | collective-permute-done | bytes 1048608 | tf_op jit(solution)/shard_map/ppermute | solution.py:43
  54.0 2.8 %collective-permute-done.3.far_came = bf16[512,1024]{1,0:T(8,128)(2,1)} collective-permute-done((bf16[512,1024]{1,0:T(8,128)(2,1)S(1)}, bf16[512,1024]{1,0:T(8,128)(2,1)}, u32[]{:S(2)}, u32[]{:S(2)}) %collective-permute-start.3) | collective-permute-done | bytes 1048608 | tf_op jit(solution)/shard_map/ppermute | solution.py:43
  56.7 18.9 %all-gather.7.cloned.1.call-done = bf16[16,256,384]{2,1,0:T(8,128)(2,1)} async-done(((bf16[2,256,384]{2,1,0:T(8,128)(2,1)}), bf16[16,256,384]{2,1,0:T(8,128)(2,1)}) %all-gather.7.cloned.1.call-update) | async-done | bytes 3145744 | tf_op jit(solution)/shard_map/all_gather | solution.py:146
  75.6 7.5 %shard_map.76 = (f32[2,2,2,24,1024]{4,3,2,1,0:T(8,128)}, f32[2,2,2,24,1024]{4,3,2,1,0:T(8,128)}, f32[2,2,24,1024]{3,2,1,0:T(8,128)}, f32[2,2,24,1024]{3,2,1,0:T(8,128)}, f32[4,2,24,1024]{3,2,1,0:T(8,128)}) custom-call(bf16[4,2,2,256,384]{4,3,2,1,0:T(8,128)(2,1)} %bitcast.183, bf16[512,1024]{1,0:T(8,128)(2,1)} %get-tuple-element.43.own_keep, ...), custom_call_target="tpu_custom_call" | custom-call | flops 3221225472 | bytes 12582912 | tf_op jit(solution)/shard_map/pallas_call | solution.py:102
  83.1 0.8 collective-permute-start.4
  84.0 2.4 %collective-permute-start.5 = (f32[2,2,2,24,1024]{4,3,2,1,0:T(8,128)}, f32[2,2,2,24,1024]{4,3,2,1,0:T(8,128)S(1)}, u32[]{:S(2)}, u32[]{:S(2)}) collective-permute-start(f32[2,2,2,24,1024]{4,3,2,1,0:T(8,128)} %get-tuple-element.21), channel_id=1, source_target_pairs={{0,16},{1,17},{2,18},{3,19},{4,20},{5,21},{6,22},{7,23},{8,72},{9,... | collective-permute-start | bytes 2359304 | tf_op jit(solution)/shard_map/ppermute | solution.py:43
  86.4 10.2 %collective-permute-done.4 = f32[2,2,2,24,1024]{4,3,2,1,0:T(8,128)S(1)} collective-permute-done((f32[2,2,2,24,1024]{4,3,2,1,0:T(8,128)}, f32[2,2,2,24,1024]{4,3,2,1,0:T(8,128)S(1)}, u32[]{:S(2)}, u32[]{:S(2)}) %collective-permute-start.4) | collective-permute-done | bytes 786464 | tf_op jit(solution)/shard_map/ppermute | solution.py:43
  96.5 1.0 fusion.17
  97.6 0.1 collective-permute-start.7
  97.7 1.1 fusion.20
  98.7 3.3 %collective-permute-start.6 = (f32[2,2,24,1024]{3,2,1,0:T(8,128)S(1)}, f32[2,2,24,1024]{3,2,1,0:T(8,128)S(1)}, u32[]{:S(2)}, u32[]{:S(2)}) collective-permute-start(f32[2,2,24,1024]{3,2,1,0:T(8,128)S(1)} %fusion.20), channel_id=1, source_target_pairs={{0,16},{1,17},{2,18},{3,19},{4,20},{5,21},{6,22},{7,23},{8,72},{9,... | collective-permute-start | bytes 1179656 | tf_op jit(solution)/shard_map/ppermute | solution.py:43
  102.0 4.6 %collective-permute-done.7 = f32[2,2,24,1024]{3,2,1,0:T(8,128)S(1)} collective-permute-done((f32[2,2,24,1024]{3,2,1,0:T(8,128)S(1)}, f32[2,2,24,1024]{3,2,1,0:T(8,128)S(1)}, u32[]{:S(2)}, u32[]{:S(2)}) %collective-permute-start.7) | collective-permute-done | bytes 393248 | tf_op jit(solution)/shard_map/ppermute | solution.py:43
  106.7 0.7 collective-permute-done.6
  107.3 1.3 fusion.22
  108.7 3.1 %collective-permute-start.8 = (f32[2,24,1024]{2,1,0:T(8,128)S(1)}, f32[2,24,1024]{2,1,0:T(8,128)S(1)}, u32[]{:S(2)}, u32[]{:S(2)}) collective-permute-start(f32[2,24,1024]{2,1,0:T(8,128)S(1)} %pad_maximum_fusion.1), channel_id=1, source_target_pairs={{0,192},{1,193},{2,194},{3,195},{4,196},{5,197},{6,198},{7,199},{8... | collective-permute-start | bytes 589832 | tf_op jit(solution)/shard_map/ppermute | solution.py:43
  111.8 0.1 collective-permute-start.9
  111.9 3.1 %collective-permute-done.8 = f32[2,24,1024]{2,1,0:T(8,128)S(1)} collective-permute-done((f32[2,24,1024]{2,1,0:T(8,128)S(1)}, f32[2,24,1024]{2,1,0:T(8,128)S(1)}, u32[]{:S(2)}, u32[]{:S(2)}) %collective-permute-start.8) | collective-permute-done | bytes 196640 | tf_op jit(solution)/shard_map/ppermute | solution.py:43
  115.0 3.8 %collective-permute-start.11 = (f32[24,1024]{1,0:T(8,128)S(1)}, f32[24,1024]{1,0:T(8,128)S(1)}, u32[]{:S(2)}, u32[]{:S(2)}) collective-permute-start(f32[24,1024]{1,0:T(8,128)S(1)} %fusion.39), channel_id=1, source_target_pairs={{0,192},{1,193},{2,194},{3,195},{4,196},{5,197},{6,198},{7,199},{8... | collective-permute-start | bytes 294920 | tf_op jit(solution)/shard_map/ppermute | solution.py:43
  118.8 2.2 %collective-permute-done.11 = f32[24,1024]{1,0:T(8,128)S(1)} collective-permute-done((f32[24,1024]{1,0:T(8,128)S(1)}, f32[24,1024]{1,0:T(8,128)S(1)}, u32[]{:S(2)}, u32[]{:S(2)}) %collective-permute-start.11) | collective-permute-done | bytes 98336 | tf_op jit(solution)/shard_map/ppermute | solution.py:43
  121.0 0.3 collective-permute-start.10
  121.3 6.2 %collective-permute-done.10 = f32[24,1024]{1,0:T(8,128)S(1)} collective-permute-done((f32[24,1024]{1,0:T(8,128)S(1)}, f32[24,1024]{1,0:T(8,128)S(1)}, u32[]{:S(2)}, u32[]{:S(2)}) %collective-permute-start.10) | collective-permute-done | bytes 98336 | tf_op jit(solution)/shard_map/ppermute | solution.py:43
  127.5 0.0 all-gather.5.cloned.1.call-done
  127.5 7.5 %shard_map.77 = (f32[2,2,2,24,1024]{4,3,2,1,0:T(8,128)}, f32[2,2,2,24,1024]{4,3,2,1,0:T(8,128)}, f32[2,2,24,1024]{3,2,1,0:T(8,128)}, f32[2,2,24,1024]{3,2,1,0:T(8,128)}, f32[4,2,24,1024]{3,2,1,0:T(8,128)}) custom-call(bf16[4,2,2,256,384]{4,3,2,1,0:T(8,128)(2,1)} %bitcast.182, bf16[512,1024]{1,0:T(8,128)(2,1)} %get-tuple-element.43.own_keep, ...), custom_call_target="tpu_custom_call" | custom-call | flops 3221225472 | bytes 12582912 | tf_op jit(solution)/shard_map/pallas_call | solution.py:102
  135.1 3.8 %collective-permute-start.13 = (f32[2,2,2,24,1024]{4,3,2,1,0:T(8,128)}, f32[2,2,2,24,1024]{4,3,2,1,0:T(8,128)S(1)}, u32[]{:S(2)}, u32[]{:S(2)}) collective-permute-start(f32[2,2,2,24,1024]{4,3,2,1,0:T(8,128)} %get-tuple-element.28), channel_id=1, source_target_pairs={{0,16},{1,17},{2,18},{3,19},{4,20},{5,21},{6,22},{7,23},{8,72},{9,... | collective-permute-start | bytes 2359304 | tf_op jit(solution)/shard_map/ppermute | solution.py:43
  138.9 10.1 %collective-permute-done.12 = f32[2,2,2,24,1024]{4,3,2,1,0:T(8,128)S(1)} collective-permute-done((f32[2,2,2,24,1024]{4,3,2,1,0:T(8,128)}, f32[2,2,2,24,1024]{4,3,2,1,0:T(8,128)S(1)}, u32[]{:S(2)}, u32[]{:S(2)}) %collective-permute-start.12) | collective-permute-done | bytes 786464 | tf_op jit(solution)/shard_map/ppermute | solution.py:43
  149.0 1.0 fusion.11
  150.0 0.1 collective-permute-start.15
  150.1 1.0 fusion.14
  151.1 3.3 %collective-permute-start.14 = (f32[2,2,24,1024]{3,2,1,0:T(8,128)S(1)}, f32[2,2,24,1024]{3,2,1,0:T(8,128)S(1)}, u32[]{:S(2)}, u32[]{:S(2)}) collective-permute-start(f32[2,2,24,1024]{3,2,1,0:T(8,128)S(1)} %fusion.14), channel_id=1, source_target_pairs={{0,16},{1,17},{2,18},{3,19},{4,20},{5,21},{6,22},{7,23},{8,72},{9,... | collective-permute-start | bytes 1179656 | tf_op jit(solution)/shard_map/ppermute | solution.py:43
  154.4 4.6 %collective-permute-done.15 = f32[2,2,24,1024]{3,2,1,0:T(8,128)S(1)} collective-permute-done((f32[2,2,24,1024]{3,2,1,0:T(8,128)S(1)}, f32[2,2,24,1024]{3,2,1,0:T(8,128)S(1)}, u32[]{:S(2)}, u32[]{:S(2)}) %collective-permute-start.15) | collective-permute-done | bytes 393248 | tf_op jit(solution)/shard_map/ppermute | solution.py:43
  159.1 0.7 collective-permute-done.14
  159.7 1.3 fusion.16
  161.1 4.2 %collective-permute-start.16 = (f32[2,24,1024]{2,1,0:T(8,128)S(1)}, f32[2,24,1024]{2,1,0:T(8,128)S(1)}, u32[]{:S(2)}, u32[]{:S(2)}) collective-permute-start(f32[2,24,1024]{2,1,0:T(8,128)S(1)} %pad_maximum_fusion.4), channel_id=1, source_target_pairs={{0,192},{1,193},{2,194},{3,195},{4,196},{5,197},{6,198},{7,199},{8... | collective-permute-start | bytes 589832 | tf_op jit(solution)/shard_map/ppermute | solution.py:43
  165.3 0.1 collective-permute-start.17
  165.4 3.1 %collective-permute-done.16 = f32[2,24,1024]{2,1,0:T(8,128)S(1)} collective-permute-done((f32[2,24,1024]{2,1,0:T(8,128)S(1)}, f32[2,24,1024]{2,1,0:T(8,128)S(1)}, u32[]{:S(2)}, u32[]{:S(2)}) %collective-permute-start.16) | collective-permute-done | bytes 196640 | tf_op jit(solution)/shard_map/ppermute | solution.py:43
  168.5 3.8 %collective-permute-start.19 = (f32[24,1024]{1,0:T(8,128)S(1)}, f32[24,1024]{1,0:T(8,128)S(1)}, u32[]{:S(2)}, u32[]{:S(2)}) collective-permute-start(f32[24,1024]{1,0:T(8,128)S(1)} %fusion.31), channel_id=1, source_target_pairs={{0,192},{1,193},{2,194},{3,195},{4,196},{5,197},{6,198},{7,199},{8... | collective-permute-start | bytes 294920 | tf_op jit(solution)/shard_map/ppermute | solution.py:43
  172.3 2.2 %collective-permute-done.19 = f32[24,1024]{1,0:T(8,128)S(1)} collective-permute-done((f32[24,1024]{1,0:T(8,128)S(1)}, f32[24,1024]{1,0:T(8,128)S(1)}, u32[]{:S(2)}, u32[]{:S(2)}) %collective-permute-start.19) | collective-permute-done | bytes 98336 | tf_op jit(solution)/shard_map/ppermute | solution.py:43
  174.5 0.1 collective-permute-start.18
  174.6 6.2 %collective-permute-done.18 = f32[24,1024]{1,0:T(8,128)S(1)} collective-permute-done((f32[24,1024]{1,0:T(8,128)S(1)}, f32[24,1024]{1,0:T(8,128)S(1)}, u32[]{:S(2)}, u32[]{:S(2)}) %collective-permute-start.18) | collective-permute-done | bytes 98336 | tf_op jit(solution)/shard_map/ppermute | solution.py:43
  180.9 0.1 copy.23
  181.0 0.5 collective-permute-start.20
  181.5 7.4 %collective-permute-done.20 = f32[4,12,8,128]{3,2,1,0:T(8,128)S(1)} collective-permute-done((f32[4,12,8,128]{3,2,1,0:T(8,128)S(1)}, f32[4,12,8,128]{3,2,1,0:T(8,128)S(1)}, u32[]{:S(2)}, u32[]{:S(2)}) %collective-permute-start.20) | collective-permute-done | bytes 196640 | tf_op jit(solution)/shard_map/ppermute | solution.py:43
  188.9 1.5 collective-permute-start.21
  190.4 3.1 %collective-permute-start.22 = (f32[2,12,8,128]{3,2,1,0:T(8,128)S(1)}, f32[2,12,8,128]{3,2,1,0:T(8,128)S(1)}, u32[]{:S(2)}, u32[]{:S(2)}) collective-permute-start(f32[2,12,8,128]{3,2,1,0:T(8,128)S(1)} %get-tuple-element.59), channel_id=1, source_target_pairs={{0,2},{1,3},{2,0},{3,1},{4,6},{5,7},{6,4},{7,5},{8,10},{9,11},{10,... | collective-permute-start | bytes 294920 | tf_op jit(solution)/shard_map/ppermute | solution.py:43
  193.5 2.2 %collective-permute-start.23 = (f32[2,12,8,128]{3,2,1,0:T(8,128)S(1)}, f32[2,12,8,128]{3,2,1,0:T(8,128)S(1)}, u32[]{:S(2)}, u32[]{:S(2)}) collective-permute-start(f32[2,12,8,128]{3,2,1,0:T(8,128)S(1)} %get-tuple-element.56), channel_id=1, source_target_pairs={{0,3},{1,0},{2,1},{3,2},{4,7},{5,4},{6,5},{7,6},{8,11},{9,8},{10,9... | collective-permute-start | bytes 294920 | tf_op jit(solution)/shard_map/ppermute | solution.py:43
  195.6 0.1 collective-permute-done.21.piece_1
  195.7 3.3 %collective-permute-done.22.piece_2 = f32[2,12,8,128]{3,2,1,0:T(8,128)S(1)} collective-permute-done((f32[2,12,8,128]{3,2,1,0:T(8,128)S(1)}, f32[2,12,8,128]{3,2,1,0:T(8,128)S(1)}, u32[]{:S(2)}, u32[]{:S(2)}) %collective-permute-start.22) | collective-permute-done | bytes 98336 | tf_op jit(solution)/shard_map/ppermute | solution.py:43
  199.0 1.2 collective-permute-done.23.piece_3
  200.2 1.4 shard_map.78
  (39 shorter events, 0.5 us)
Async XLA Ops:
  7.2 1.1 copy-start
  7.2 68.4 %all-gather.7.cloned.1.call-start = ((), (), s32[]{:S(2)}) async-start(), calls=%async_computation.1 | async-start | bytes 3538944 | tf_op jit(solution)/shard_map/all_gather | solution.py:146
  9.8 4.7 %copy-start.4 = (bf16[512,2048]{1,0:T(8,128)(2,1)S(1)}, bf16[512,2048]{1,0:T(8,128)(2,1)}, u32[]{:S(2)}) copy-start(bf16[512,2048]{1,0:T(8,128)(2,1)} %param.6) | copy-start | bytes 6291460
  9.9 1.8 collective-permute-start
  14.4 113.1 %all-gather.5.cloned.1.call-start = ((), (), s32[]{:S(2)}) async-start(), calls=%async_computation | async-start | bytes 3538944 | tf_op jit(solution)/shard_map/all_gather | solution.py:146
  16.0 37.9 %collective-permute-start.1 = (bf16[512,1024]{1,0:T(8,128)(2,1)}, bf16[512,1024]{1,0:T(8,128)(2,1)S(1)}, u32[]{:S(2)}, u32[]{:S(2)}) collective-permute-start(bf16[512,1024]{1,0:T(8,128)(2,1)} %get-tuple-element.42), channel_id=1, source_target_pairs={{0,4},{1,5},{2,6},{3,7},{4,0},{5,1},{6,2},{7,3},{8,12},{9,13},{10,... | collective-permute-start | bytes 3145736 | tf_op jit(solution)/shard_map/ppermute | solution.py:43
  18.9 35.1 %collective-permute-start.2 = (bf16[512,1024]{1,0:T(8,128)(2,1)}, bf16[512,1024]{1,0:T(8,128)(2,1)S(1)}, u32[]{:S(2)}, u32[]{:S(2)}) collective-permute-start(bf16[512,1024]{1,0:T(8,128)(2,1)} %get-tuple-element.43.own_keep), channel_id=1, source_target_pairs={{0,8},{1,9},{2,10},{3,11},{4,12},{5,13},{6,14},{7,15},{8,0},{9,1},... | collective-permute-start | bytes 3145736 | tf_op jit(solution)/shard_map/ppermute | solution.py:43
  53.9 21.7 %copy-start.5 = (bf16[512,1024]{1,0:T(8,128)(2,1)}, bf16[512,1024]{1,0:T(8,128)(2,1)S(1)}, u32[]{:S(2)}) copy-start(bf16[512,1024]{1,0:T(8,128)(2,1)S(1)} %collective-permute-done.1.own_came) | copy-start | bytes 3145732
  53.9 2.8 %collective-permute-start.3 = (bf16[512,1024]{1,0:T(8,128)(2,1)S(1)}, bf16[512,1024]{1,0:T(8,128)(2,1)}, u32[]{:S(2)}, u32[]{:S(2)}) collective-permute-start(bf16[512,1024]{1,0:T(8,128)(2,1)S(1)} %collective-permute-done.1.own_came), channel_id=1, source_target_pairs={{0,8},{1,9},{2,10},{3,11},{4,12},{5,13},{6,14},{7,15},{8,0},{9,1},... | collective-permute-start | bytes 3145736 | tf_op jit(solution)/shard_map/ppermute | solution.py:43
  54.0 21.7 %copy-start.6 = (bf16[512,1024]{1,0:T(8,128)(2,1)}, bf16[512,1024]{1,0:T(8,128)(2,1)S(1)}, u32[]{:S(2)}) copy-start(bf16[512,1024]{1,0:T(8,128)(2,1)S(1)} %collective-permute-done.2.far_keep) | copy-start | bytes 3145732
  83.1 13.4 %collective-permute-start.4 = (f32[2,2,2,24,1024]{4,3,2,1,0:T(8,128)}, f32[2,2,2,24,1024]{4,3,2,1,0:T(8,128)S(1)}, u32[]{:S(2)}, u32[]{:S(2)}) collective-permute-start(f32[2,2,2,24,1024]{4,3,2,1,0:T(8,128)} %get-tuple-element.19), channel_id=1, source_target_pairs={{0,48},{1,49},{2,50},{3,51},{4,52},{5,53},{6,54},{7,55},{8,200},{9... | collective-permute-start | bytes 2359304 | tf_op jit(solution)/shard_map/ppermute | solution.py:43
  84.0 13.7 %collective-permute-start.5 = (f32[2,2,2,24,1024]{4,3,2,1,0:T(8,128)}, f32[2,2,2,24,1024]{4,3,2,1,0:T(8,128)S(1)}, u32[]{:S(2)}, u32[]{:S(2)}) collective-permute-start(f32[2,2,2,24,1024]{4,3,2,1,0:T(8,128)} %get-tuple-element.21), channel_id=1, source_target_pairs={{0,16},{1,17},{2,18},{3,19},{4,20},{5,21},{6,22},{7,23},{8,72},{9,... | collective-permute-start | bytes 2359304 | tf_op jit(solution)/shard_map/ppermute | solution.py:43
  97.6 9.1 %collective-permute-start.7 = (f32[2,2,24,1024]{3,2,1,0:T(8,128)S(1)}, f32[2,2,24,1024]{3,2,1,0:T(8,128)S(1)}, u32[]{:S(2)}, u32[]{:S(2)}) collective-permute-start(f32[2,2,24,1024]{3,2,1,0:T(8,128)S(1)} %fusion.17), channel_id=1, source_target_pairs={{0,48},{1,49},{2,50},{3,51},{4,52},{5,53},{6,54},{7,55},{8,200},{9... | collective-permute-start | bytes 1179656 | tf_op jit(solution)/shard_map/ppermute | solution.py:43
  98.7 8.6 %collective-permute-start.6 = (f32[2,2,24,1024]{3,2,1,0:T(8,128)S(1)}, f32[2,2,24,1024]{3,2,1,0:T(8,128)S(1)}, u32[]{:S(2)}, u32[]{:S(2)}) collective-permute-start(f32[2,2,24,1024]{3,2,1,0:T(8,128)S(1)} %fusion.20), channel_id=1, source_target_pairs={{0,16},{1,17},{2,18},{3,19},{4,20},{5,21},{6,22},{7,23},{8,72},{9,... | collective-permute-start | bytes 1179656 | tf_op jit(solution)/shard_map/ppermute | solution.py:43
  108.7 6.3 %collective-permute-start.8 = (f32[2,24,1024]{2,1,0:T(8,128)S(1)}, f32[2,24,1024]{2,1,0:T(8,128)S(1)}, u32[]{:S(2)}, u32[]{:S(2)}) collective-permute-start(f32[2,24,1024]{2,1,0:T(8,128)S(1)} %pad_maximum_fusion.1), channel_id=1, source_target_pairs={{0,192},{1,193},{2,194},{3,195},{4,196},{5,197},{6,198},{7,199},{8... | collective-permute-start | bytes 589832 | tf_op jit(solution)/shard_map/ppermute | solution.py:43
  111.8 7.0 %collective-permute-start.9 = (f32[2,24,1024]{2,1,0:T(8,128)S(1)}, f32[2,24,1024]{2,1,0:T(8,128)S(1)}, u32[]{:S(2)}, u32[]{:S(2)}) collective-permute-start(f32[2,24,1024]{2,1,0:T(8,128)S(1)} %pad_maximum_fusion.2), channel_id=1, source_target_pairs={{0,64},{1,65},{2,66},{3,67},{4,68},{5,69},{6,70},{7,71},{8,24},{9,... | collective-permute-start | bytes 589832 | tf_op jit(solution)/shard_map/ppermute | solution.py:43
  115.0 6.0 %collective-permute-start.11 = (f32[24,1024]{1,0:T(8,128)S(1)}, f32[24,1024]{1,0:T(8,128)S(1)}, u32[]{:S(2)}, u32[]{:S(2)}) collective-permute-start(f32[24,1024]{1,0:T(8,128)S(1)} %fusion.39), channel_id=1, source_target_pairs={{0,192},{1,193},{2,194},{3,195},{4,196},{5,197},{6,198},{7,199},{8... | collective-permute-start | bytes 294920 | tf_op jit(solution)/shard_map/ppermute | solution.py:43
  121.0 6.5 %collective-permute-start.10 = (f32[24,1024]{1,0:T(8,128)S(1)}, f32[24,1024]{1,0:T(8,128)S(1)}, u32[]{:S(2)}, u32[]{:S(2)}) collective-permute-start(f32[24,1024]{1,0:T(8,128)S(1)} %get-tuple-element.54), channel_id=1, source_target_pairs={{0,64},{1,65},{2,66},{3,67},{4,68},{5,69},{6,70},{7,71},{8,24},{9,... | collective-permute-start | bytes 294920 | tf_op jit(solution)/shard_map/ppermute | solution.py:43
  135.1 13.9 %collective-permute-start.12 = (f32[2,2,2,24,1024]{4,3,2,1,0:T(8,128)}, f32[2,2,2,24,1024]{4,3,2,1,0:T(8,128)S(1)}, u32[]{:S(2)}, u32[]{:S(2)}) collective-permute-start(f32[2,2,2,24,1024]{4,3,2,1,0:T(8,128)} %get-tuple-element.26), channel_id=1, source_target_pairs={{0,48},{1,49},{2,50},{3,51},{4,52},{5,53},{6,54},{7,55},{8,200},{9... | collective-permute-start | bytes 2359304 | tf_op jit(solution)/shard_map/ppermute | solution.py:43
  135.1 15.0 %collective-permute-start.13 = (f32[2,2,2,24,1024]{4,3,2,1,0:T(8,128)}, f32[2,2,2,24,1024]{4,3,2,1,0:T(8,128)S(1)}, u32[]{:S(2)}, u32[]{:S(2)}) collective-permute-start(f32[2,2,2,24,1024]{4,3,2,1,0:T(8,128)} %get-tuple-element.28), channel_id=1, source_target_pairs={{0,16},{1,17},{2,18},{3,19},{4,20},{5,21},{6,22},{7,23},{8,72},{9,... | collective-permute-start | bytes 2359304 | tf_op jit(solution)/shard_map/ppermute | solution.py:43
  150.0 9.1 %collective-permute-start.15 = (f32[2,2,24,1024]{3,2,1,0:T(8,128)S(1)}, f32[2,2,24,1024]{3,2,1,0:T(8,128)S(1)}, u32[]{:S(2)}, u32[]{:S(2)}) collective-permute-start(f32[2,2,24,1024]{3,2,1,0:T(8,128)S(1)} %fusion.11), channel_id=1, source_target_pairs={{0,48},{1,49},{2,50},{3,51},{4,52},{5,53},{6,54},{7,55},{8,200},{9... | collective-permute-start | bytes 1179656 | tf_op jit(solution)/shard_map/ppermute | solution.py:43
  151.1 8.6 %collective-permute-start.14 = (f32[2,2,24,1024]{3,2,1,0:T(8,128)S(1)}, f32[2,2,24,1024]{3,2,1,0:T(8,128)S(1)}, u32[]{:S(2)}, u32[]{:S(2)}) collective-permute-start(f32[2,2,24,1024]{3,2,1,0:T(8,128)S(1)} %fusion.14), channel_id=1, source_target_pairs={{0,16},{1,17},{2,18},{3,19},{4,20},{5,21},{6,22},{7,23},{8,72},{9,... | collective-permute-start | bytes 1179656 | tf_op jit(solution)/shard_map/ppermute | solution.py:43
  161.0 39.2 %copy-start.1 = (f32[1,12,8192]{2,0,1:T(1,128)S(1)}, f32[1,12,8192]{2,0,1:T(1,128)}, u32[]{:S(2)}) copy-start(f32[1,12,8192]{2,0,1:T(1,128)} %param.7) | copy-start | bytes 1179652
  161.0 39.2 %copy-start.2 = (f32[1,12,8192]{2,0,1:T(1,128)S(1)}, f32[1,12,8192]{2,0,1:T(1,128)}, u32[]{:S(2)}) copy-start(f32[1,12,8192]{2,0,1:T(1,128)} %param.8) | copy-start | bytes 1179652
  161.0 39.1 %copy-start.3 = (f32[1,12,8192]{2,0,1:T(1,128)S(1)}, f32[1,12,8192]{2,0,1:T(1,128)}, u32[]{:S(2)}) copy-start(f32[1,12,8192]{2,0,1:T(1,128)} %param.9) | copy-start | bytes 1179652
  161.1 7.4 %collective-permute-start.16 = (f32[2,24,1024]{2,1,0:T(8,128)S(1)}, f32[2,24,1024]{2,1,0:T(8,128)S(1)}, u32[]{:S(2)}, u32[]{:S(2)}) collective-permute-start(f32[2,24,1024]{2,1,0:T(8,128)S(1)} %pad_maximum_fusion.4), channel_id=1, source_target_pairs={{0,192},{1,193},{2,194},{3,195},{4,196},{5,197},{6,198},{7,199},{8... | collective-permute-start | bytes 589832 | tf_op jit(solution)/shard_map/ppermute | solution.py:43
  165.3 7.0 %collective-permute-start.17 = (f32[2,24,1024]{2,1,0:T(8,128)S(1)}, f32[2,24,1024]{2,1,0:T(8,128)S(1)}, u32[]{:S(2)}, u32[]{:S(2)}) collective-permute-start(f32[2,24,1024]{2,1,0:T(8,128)S(1)} %pad_maximum_fusion.5), channel_id=1, source_target_pairs={{0,64},{1,65},{2,66},{3,67},{4,68},{5,69},{6,70},{7,71},{8,24},{9,... | collective-permute-start | bytes 589832 | tf_op jit(solution)/shard_map/ppermute | solution.py:43
  168.5 6.0 %collective-permute-start.19 = (f32[24,1024]{1,0:T(8,128)S(1)}, f32[24,1024]{1,0:T(8,128)S(1)}, u32[]{:S(2)}, u32[]{:S(2)}) collective-permute-start(f32[24,1024]{1,0:T(8,128)S(1)} %fusion.31), channel_id=1, source_target_pairs={{0,192},{1,193},{2,194},{3,195},{4,196},{5,197},{6,198},{7,199},{8... | collective-permute-start | bytes 294920 | tf_op jit(solution)/shard_map/ppermute | solution.py:43
  174.5 6.3 %collective-permute-start.18 = (f32[24,1024]{1,0:T(8,128)S(1)}, f32[24,1024]{1,0:T(8,128)S(1)}, u32[]{:S(2)}, u32[]{:S(2)}) collective-permute-start(f32[24,1024]{1,0:T(8,128)S(1)} %get-tuple-element.52), channel_id=1, source_target_pairs={{0,64},{1,65},{2,66},{3,67},{4,68},{5,69},{6,70},{7,71},{8,24},{9,... | collective-permute-start | bytes 294920 | tf_op jit(solution)/shard_map/ppermute | solution.py:43
  181.0 7.8 %collective-permute-start.20 = (f32[4,12,8,128]{3,2,1,0:T(8,128)S(1)}, f32[4,12,8,128]{3,2,1,0:T(8,128)S(1)}, u32[]{:S(2)}, u32[]{:S(2)}) collective-permute-start(f32[4,12,8,128]{3,2,1,0:T(8,128)S(1)} %get-tuple-element.60), channel_id=1, source_target_pairs={{0,4},{1,5},{2,6},{3,7},{4,0},{5,1},{6,2},{7,3},{8,12},{9,13},{10,... | collective-permute-start | bytes 589832 | tf_op jit(solution)/shard_map/ppermute | solution.py:43
  188.9 6.8 %collective-permute-start.21 = (f32[2,12,8,128]{3,2,1,0:T(8,128)S(1)}, f32[2,12,8,128]{3,2,1,0:T(8,128)S(1)}, u32[]{:S(2)}, u32[]{:S(2)}) collective-permute-start(f32[2,12,8,128]{3,2,1,0:T(8,128)S(1)} %get-tuple-element.58), channel_id=1, source_target_pairs={{0,1},{1,2},{2,3},{3,0},{4,5},{5,6},{6,7},{7,4},{8,9},{9,10},{10,1... | collective-permute-start | bytes 294920 | tf_op jit(solution)/shard_map/ppermute | solution.py:43
  190.4 8.6 %collective-permute-start.22 = (f32[2,12,8,128]{3,2,1,0:T(8,128)S(1)}, f32[2,12,8,128]{3,2,1,0:T(8,128)S(1)}, u32[]{:S(2)}, u32[]{:S(2)}) collective-permute-start(f32[2,12,8,128]{3,2,1,0:T(8,128)S(1)} %get-tuple-element.59), channel_id=1, source_target_pairs={{0,2},{1,3},{2,0},{3,1},{4,6},{5,7},{6,4},{7,5},{8,10},{9,11},{10,... | collective-permute-start | bytes 294920 | tf_op jit(solution)/shard_map/ppermute | solution.py:43
  193.5 6.7 %collective-permute-start.23 = (f32[2,12,8,128]{3,2,1,0:T(8,128)S(1)}, f32[2,12,8,128]{3,2,1,0:T(8,128)S(1)}, u32[]{:S(2)}, u32[]{:S(2)}) collective-permute-start(f32[2,12,8,128]{3,2,1,0:T(8,128)S(1)} %get-tuple-element.56), channel_id=1, source_target_pairs={{0,3},{1,0},{2,1},{3,2},{4,7},{5,4},{6,5},{7,6},{8,11},{9,8},{10,9... | collective-permute-start | bytes 294920 | tf_op jit(solution)/shard_map/ppermute | solution.py:43
Sparse Core Ops, SparseCore 0:
  14.5 61.0 all-gather.6
  78.0 43.7 all-gather.4

commit v3 on v2

--- a/solution.py
+++ b/solution.py
@@ -30,11 +30,11 @@
     return pairs
 
 
-def step(first, sign):
+def step(first, hop):
     def where(y, x, core, z):
         if (core == 0) == first:
-            return y, x + sign, core, z
-        return y + sign, x, core, z
+            return y, x + hop, core, z
+        return y + hop, x, core, z
 
     return moves(where)
 
@@ -69,62 +69,84 @@
     return jnp.dot(activations, chosen, preferred_element_type=jnp.float32).astype(activations.dtype)
 
 
-def product_kernel(act, own_keep, own_came, far_keep, far_came, plus, minus, add_plus, add_minus, mine):
-    tr = lax.axis_index("tr")
+def product_kernel(pieces, count, *refs):
+    acts, cots = refs[:count], refs[count : count + 4]
+    outs = refs[count + 4 : count + 8]
+    act, cot, act_sem, cot_sem = refs[count + 8 :]
+    tr, tc = lax.axis_index("tr"), lax.axis_index("tc")
     features = act.shape[-1]
-
-    def part(half, replica, cot):
-        rows = act[pl.ds(2 * half, 2), 0, replica].reshape(cot.shape[0], features)
-        return lax.dot_general(rows, cot[...], (((0,), (0,)), ((), ())), preferred_element_type=jnp.float32)
-
-    total = part(tr, 0, own_keep) + part(1 - tr, 0, own_came)
-    total = total + (part(tr, 1, far_keep) + part(1 - tr, 1, far_came))
+    i = pl.program_id(0)
+
+    @pl.when(i == 0)
+    def fetch():
+        copies = []
+        for n, (piece, ref) in enumerate(zip(pieces, acts)):
+            if piece is None:
+                target = act
+            else:
+                z = (2 * tc + tr + 8 + piece[0]) % 8
+                target = act.at[z // 2, z % 2]
+                if piece[1] is not None:
+                    target = target.at[piece[1]]
+            copies.append(pltpu.make_async_copy(ref, target, act_sem.at[n]))
+        late = [pltpu.make_async_copy(ref, cot.at[n], cot_sem.at[n]) for n, ref in enumerate(cots)]
+        for copy in copies + late:
+            copy.start()
+        for copy in copies + late:
+            copy.wait()
+
+    def part(half, replica, n):
+        rows = act[pl.ds(2 * half, 2), i, replica].reshape(cot.shape[1], features)
+        return lax.dot_general(rows, cot[n], (((0,), (0,)), ((), ())), preferred_element_type=jnp.float32)
+
+    total = part(tr, 0, 0) + part(1 - tr, 0, 1)
+    total = total + (part(tr, 1, 2) + part(1 - tr, 1, 3))
     total = total.reshape(SIDE, SIDE, 1, features // SIDE**2, total.shape[-1])
-    plus[0] = total[2, :2]
-    plus[1] = total[1, 2:]
-    minus[0] = total[2, 2:]
-    minus[1] = total[3, :2]
-    add_plus[...] = total[1, :2]
-    add_minus[...] = total[3, 2:]
-    mine[...] = total[0]
-
-
-def product(act, cots):
-    features, units = act.shape[-1], cots[0].shape[1]
+    for near in range(SIDE):
+        outs[near][...] = total[near]
+
+
+def product(acts, pieces, cots):
+    tokens, features = acts[0].shape[-2:]
+    units = cots[0].shape[1]
     rows = features // SIDE**2
-    whole = pl.BlockSpec(cots[0].shape, lambda i: (0, 0))
-    lead = pl.BlockSpec((2, 2, 1, rows, units), lambda i: (0, 0, i, 0, 0))
-    pack = pl.BlockSpec((2, 2, 1, rows, units), lambda i: (0, 0, i, 0, 0))
-    part = pl.BlockSpec((2, 1, rows, units), lambda i: (0, i, 0, 0))
-    full = pl.BlockSpec((SIDE, 1, rows, units), lambda i: (0, i, 0, 0))
-    packed = jax.ShapeDtypeStruct((2, 2, 2, rows, units), jnp.float32)
-    parted = jax.ShapeDtypeStruct((2, 2, rows, units), jnp.float32)
     return pl.pallas_call(
-        product_kernel,
+        lambda *refs: product_kernel(pieces, len(acts), *refs),
         grid=(2,),
-        in_specs=[pl.BlockSpec((4, 1, 2, act.shape[3], features), lambda i: (0, i, 0, 0, 0))] + [whole] * 4,
-        out_specs=[lead, pack, part, part, full],
-        out_shape=[packed, packed, parted, parted, jax.ShapeDtypeStruct((SIDE, 2, rows, units), jnp.float32)],
+        in_specs=[pl.BlockSpec(memory_space=pl.ANY)] * (len(acts) + 4),
+        out_specs=[pl.BlockSpec((SIDE, 1, rows, units), lambda i: (0, i, 0, 0))] * SIDE,
+        out_shape=[jax.ShapeDtypeStruct((SIDE, 2, rows, units), jnp.float32)] * SIDE,
+        scratch_shapes=[
+            pltpu.VMEM((4, 2, 2, tokens, features), acts[0].dtype),
+            pltpu.VMEM((4,) + cots[0].shape, cots[0].dtype),
+            pltpu.SemaphoreType.DMA((len(acts),)),
+            pltpu.SemaphoreType.DMA((4,)),
+        ],
         compiler_params=pltpu.CompilerParams(vmem_limit_bytes=58 * 2**20),
         cost_estimate=pl.CostEstimate(
             flops=2 * 2 * features * 4 * cots[0].shape[0] * units, bytes_accessed=12 * 2**20, transcendentals=0
         ),
-    )(act, *cots)
+    )(*acts, *cots)
+
+
+def gathered_in_ring(own):
+    up, down = moves(lambda y, x, core, z: (y, x, core, z + 1)), moves(lambda y, x, core, z: (y, x, core, z - 1))
+    acts, pieces = [own], [(0, None)]
+    below, above = own, own
+    for hop in range(1, 4):
+        below, above = send(below, up), send(above, down)
+        acts += [below, above]
+        pieces += [(-hop, None), (hop, None)]
+    acts += [send(below[0], up), send(above[1], down)]
+    pieces += [(4, 0), (4, 1)]
+    return acts, pieces
 
 
 def summed(parts):
-    plus, minus, add_plus, add_minus, mine = parts
-    left = send(plus, step(True, 1))
-    right = send(minus, step(True, -1))
-    near = send(add_plus + left[0], step(True, 1))
-    far = send(add_minus + right[0], step(True, -1))
-    low = mine[:2] + right[1] + near
-    high = mine[2:] + left[1] + far
-    left = send(jnp.stack([high[0, 0], low[1, 1]]), step(False, 1))
-    right = send(jnp.stack([high[0, 1], high[1, 0]]), step(False, -1))
-    near = send(low[1, 0] + left[0], step(False, 1))
-    far = send(high[1, 1] + right[0], step(False, -1))
-    return jnp.stack([low[0, 0] + right[1] + near, low[0, 1] + left[1] + far])
+    first = [send(parts[hop], step(True, hop)) for hop in (1, 3, 2)]
+    far = [parts[0][s] + first[0][s] + (first[1][s] + first[2][s]) for s in range(SIDE)]
+    second = [send(far[hop], step(False, hop)) for hop in (1, 3, 2)]
+    return far[0] + second[0] + (second[1] + second[2])
 
 
 def shards(activations, cotangent, master, moment, second):
@@ -139,20 +161,15 @@
     half = ordered.shape[1] // 2
     far_act = send(ordered[:, half:], OTHER_CORE)
     both = jnp.stack([ordered[:, :half], far_act])
-    gathered = []
-    start = 0
-    for rows in CHUNKS:
-        size = rows * SIDE**2
-        block = lax.all_gather(both[:, :, start : start + size], ("tc", "tr"), axis=0)
-        gathered.append(block.reshape(4, 2, 2, tokens, size))
-        start += size
+    size = CHUNKS[0] * SIDE**2
+    whole = lax.all_gather(both[:, :, :size], ("tc", "tr"), axis=0)
+    acts, pieces = gathered_in_ring(both[:, :, size:])
     far_came = send(own_came, OTHER_CORE)
     cots = (own_keep, own_came, far_keep, far_came)
-    sums = []
-    for block in gathered:
-        if sums:
-            block, sums[-1] = lax.optimization_barrier((block, sums[-1]))
-        sums.append(summed(product(block, cots)))
+    sums = [
+        summed(product([whole.reshape(4, 2, 2, tokens, size)], [None], cots)),
+        summed(product(acts, pieces, cots)),
+    ]
     rows = jnp.concatenate(sums, axis=1).reshape(2, 4, ROWS // 4, 8, units // 8)
     return updated(rows, master, moment, second)
 

time: 210 us -> 204 us (0.971)
  waiting for transfers between devices: 124 us -> 106 us
  starting transfers between devices: 38.5 us -> 53.7 us
  local copies, waits for them, and re-layouts: 5.59 us -> 2.05 us
    all_gather x2 -> x1, waiting for transfers between devices: 18.9 us -> 0.01 us  [shards(): whole = lax.all_gather(both[:, :, :size], ('tc', 'tr'), axis=0)]
    ppermute x24 -> x28, starting transfers between devices: 38.4 us -> 53.7 us  [send(): return lax.ppermute(array, AXES, pairs)]
    slice x3 -> x0, local copies, waits for them, and re-layouts: 2.88 us -> none  [the longest x2 2.83 us: shards(): block = lax.all_gather(both[:, :, start:start + size], ('tc', 'tr'), axis=0)]
    add x10 -> x4, other arithmetic: 6.87 us -> 5.54 us  [the longest x2 3.22 us: summed(): parts[0][s] + first[0][s] + (first[1][s] + first[2][s])]
    ppermute x24 -> x28, waiting for transfers between devices: 105 us -> 106 us  [send(): return lax.ppermute(array, AXES, pairs)]
  transfers between devices with their start and end apart: 26 -> 29, of which waited for: 20 -> 15; matrix products, arithmetic and copies ran while one was open for 4% -> 2% of each run, Pallas kernels for 4% -> 8%
where the time goes in v3:
time: 204 us; the launch traced here: 202 us
  waiting for transfers between devices  106 us (52%)
  starting transfers between devices  53.7 us (26%)
  Pallas kernels  17.5 us (9%)
  between operations  14.4 us (7%)
  other arithmetic  6.49 us (3%)
  local copies, waits for them, and re-layouts  2.05 us (1%)
    ppermute x28, waiting for transfers between devices, send(): return lax.ppermute(array, AXES, pairs)  106 us
    ppermute x28, starting transfers between devices, send(): return lax.ppermute(array, AXES, pairs)  53.7 us
    pallas_call x2, Pallas kernels, product(): pl.pallas_call(lambda *refs: product_kernel(pieces, len(acts), *refs), gr...  16.1 us
  transfers between devices with their start and end apart: 29, of which 15 were waited for; matrix products, arithmetic and copies ran while one was open for 2% of the time, Pallas kernels for 8%

profile of v3, /device:TPU:6, one launch (start us, length us, event | category | flops | bytes accessed | tf_op | source)
XLA Modules:
  0.0 201.9 jit_solution(9330469916731540078)
XLA Ops:
  7.2 0.0 copy-start
  7.2 0.0 all-gather.3.cloned.1.call-start
  7.3 0.1 fusion.37
  7.3 1.0 copy-done
  8.3 1.9 fusion.3
  10.2 0.0 copy-start.4
  10.2 0.1 slice_bitcast_fusion
  10.2 0.1 collective-permute-start
  10.3 1.7 collective-permute-done
  12.0 0.8 fusion.4
  12.9 0.0 all-gather.3.cloned.1.call-update
  12.9 0.2 constant_dynamic-slice_fusion
  13.1 2.0 collective-permute-start.1
  15.1 0.1 collective-permute-start.10
  15.3 4.8 %collective-permute-start.11 = (bf16[2,256,384]{2,1,0:T(8,128)(2,1)S(1)}, bf16[2,256,384]{2,1,0:T(8,128)(2,1)S(1)}, u32[]{:S(2)}, u32[]{:S(2)}) collective-permute-start(bf16[2,256,384]{2,1,0:T(8,128)(2,1)S(1)} %get-tuple-element.43.refs_0_), channel_id=1, source_target_pairs={{0,7},{1,4},{2,5},{3,6},{4,0},{5,1},{6,2},{7,3},{8,15},{9,12},{10,... | collective-permute-start | bytes 1179656 | tf_op jit(solution)/shard_map/ppermute | solution.py:43
  20.1 46.1 %collective-permute-done.10.refs_1_ = bf16[2,256,384]{2,1,0:T(8,128)(2,1)S(1)} collective-permute-done((bf16[2,256,384]{2,1,0:T(8,128)(2,1)S(1)}, bf16[2,256,384]{2,1,0:T(8,128)(2,1)S(1)}, u32[]{:S(2)}, u32[]{:S(2)}) %collective-permute-start.10) | collective-permute-done | bytes 393248 | tf_op jit(solution)/shard_map/ppermute | solution.py:43
  66.2 2.5 %collective-permute-start.12 = (bf16[2,256,384]{2,1,0:T(8,128)(2,1)S(1)}, bf16[2,256,384]{2,1,0:T(8,128)(2,1)S(1)}, u32[]{:S(2)}, u32[]{:S(2)}) collective-permute-start(bf16[2,256,384]{2,1,0:T(8,128)(2,1)S(1)} %collective-permute-done.10.refs_1_), channel_id=1, source_target_pairs={{0,4},{1,5},{2,6},{3,7},{4,1},{5,2},{6,3},{7,0},{8,12},{9,13},{10,... | collective-permute-start | bytes 1179656 | tf_op jit(solution)/shard_map/ppermute | solution.py:43
  68.7 0.0 collective-permute-done.11.refs_2_
  68.7 5.3 %collective-permute-start.13 = (bf16[2,256,384]{2,1,0:T(8,128)(2,1)S(1)}, bf16[2,256,384]{2,1,0:T(8,128)(2,1)S(1)}, u32[]{:S(2)}, u32[]{:S(2)}) collective-permute-start(bf16[2,256,384]{2,1,0:T(8,128)(2,1)S(1)} %collective-permute-done.11.refs_2_), channel_id=1, source_target_pairs={{0,7},{1,4},{2,5},{3,6},{4,0},{5,1},{6,2},{7,3},{8,15},{9,12},{10,... | collective-permute-start | bytes 1179656 | tf_op jit(solution)/shard_map/ppermute | solution.py:43
  74.0 13.4 %collective-permute-done.12.refs_3_ = bf16[2,256,384]{2,1,0:T(8,128)(2,1)S(1)} collective-permute-done((bf16[2,256,384]{2,1,0:T(8,128)(2,1)S(1)}, bf16[2,256,384]{2,1,0:T(8,128)(2,1)S(1)}, u32[]{:S(2)}, u32[]{:S(2)}) %collective-permute-start.12) | collective-permute-done | bytes 393248 | tf_op jit(solution)/shard_map/ppermute | solution.py:43
  87.4 0.0 collective-permute-start.14
  87.4 0.5 collective-permute-start.3
  87.9 3.2 %collective-permute-start.15 = (bf16[2,256,384]{2,1,0:T(8,128)(2,1)S(1)}, bf16[2,256,384]{2,1,0:T(8,128)(2,1)S(1)}, u32[]{:S(2)}, u32[]{:S(2)}) collective-permute-start(bf16[2,256,384]{2,1,0:T(8,128)(2,1)S(1)} %collective-permute-done.13.refs_4_), channel_id=1, source_target_pairs={{0,7},{1,4},{2,5},{3,6},{4,0},{5,1},{6,2},{7,3},{8,15},{9,12},{10,... | collective-permute-start | bytes 1179656 | tf_op jit(solution)/shard_map/ppermute | solution.py:43
  91.2 7.8 %collective-permute-done.14.refs_5_ = bf16[2,256,384]{2,1,0:T(8,128)(2,1)S(1)} collective-permute-done((bf16[2,256,384]{2,1,0:T(8,128)(2,1)S(1)}, bf16[2,256,384]{2,1,0:T(8,128)(2,1)S(1)}, u32[]{:S(2)}, u32[]{:S(2)}) %collective-permute-start.14) | collective-permute-done | bytes 393248 | tf_op jit(solution)/shard_map/ppermute | solution.py:43
  99.0 0.1 collective-permute-start.16
  99.1 0.7 collective-permute-done.15.refs_6_
  99.8 3.9 %collective-permute-start.17 = (bf16[256,384]{1,0:T(8,128)(2,1)S(1)}, bf16[256,384]{1,0:T(8,128)(2,1)S(1)}, u32[]{:S(2)}, u32[]{:S(2)}) collective-permute-start(bf16[256,384]{1,0:T(8,128)(2,1)S(1)} %slice_bitcast_fusion.1), channel_id=1, source_target_pairs={{0,7},{1,4},{2,5},{3,6},{4,0},{5,1},{6,2},{7,3},{8,15},{9,12},{10,... | collective-permute-start | bytes 589832 | tf_op jit(solution)/shard_map/ppermute | solution.py:43
  103.8 2.2 %collective-permute-done.16.refs_7_ = bf16[256,384]{1,0:T(8,128)(2,1)S(1)} collective-permute-done((bf16[256,384]{1,0:T(8,128)(2,1)S(1)}, bf16[256,384]{1,0:T(8,128)(2,1)S(1)}, u32[]{:S(2)}, u32[]{:S(2)}) %collective-permute-start.16) | collective-permute-done | bytes 196640 | tf_op jit(solution)/shard_map/ppermute | solution.py:43
  106.0 1.4 collective-permute-done.17.refs_8_
  107.5 0.6 copy-done.18
  108.0 8.1 %shard_map.77 = (f32[4,2,24,1024]{3,2,1,0:T(8,128)}, f32[4,2,24,1024]{3,2,1,0:T(8,128)}, f32[4,2,24,1024]{3,2,1,0:T(8,128)}, f32[4,2,24,1024]{3,2,1,0:T(8,128)}) custom-call(bf16[2,256,384]{2,1,0:T(8,128)(2,1)} %copy-done.8, bf16[2,256,384]{2,1,0:T(8,128)(2,1)} %copy-done.13, bf16[2,256,384]{2,1,0:T(8,128)(2,1)} %copy-done.14, ...), custom_call_target="tpu_custom_call" | custom-call | flops 3221225472 | bytes 12582912 | tf_op jit(solution)/shard_map/pallas_call | solution.py:113
  116.1 0.6 collective-permute-start.18
  116.7 1.5 collective-permute-start.19
  118.2 1.4 collective-permute-start.20
  119.7 8.1 %shard_map.76 = (f32[4,2,24,1024]{3,2,1,0:T(8,128)}, f32[4,2,24,1024]{3,2,1,0:T(8,128)}, f32[4,2,24,1024]{3,2,1,0:T(8,128)}, f32[4,2,24,1024]{3,2,1,0:T(8,128)}) custom-call(bf16[4,2,2,256,384]{4,3,2,1,0:T(8,128)(2,1)} %bitcast.65, bf16[512,1024]{1,0:T(8,128)(2,1)} %copy-done.5, bf16[512,1024]{1,0:T(8,128)(2,1)} %copy-done.11, bf16[512,1024]{1,0:T(8,128)(2,1)} %copy-done.12, ...), custom_call_target="tpu_custom_call" | custom-call | flops 3221225472 | bytes 12582912 | tf_op jit(solution)/shard_map/pallas_call | solution.py:113
  127.8 2.1 %collective-permute-start.4 = (f32[4,2,24,1024]{3,2,1,0:T(8,128)}, f32[4,2,24,1024]{3,2,1,0:T(8,128)}, u32[]{:S(2)}, u32[]{:S(2)}) collective-permute-start(f32[4,2,24,1024]{3,2,1,0:T(8,128)} %get-tuple-element.15), channel_id=1, source_target_pairs={{0,16},{1,17},{2,18},{3,19},{4,20},{5,21},{6,22},{7,23},{8,72},{9,... | collective-permute-start | bytes 2359304 | tf_op jit(solution)/shard_map/ppermute | solution.py:43
  129.9 2.1 %collective-permute-start.6 = (f32[4,2,24,1024]{3,2,1,0:T(8,128)}, f32[4,2,24,1024]{3,2,1,0:T(8,128)}, u32[]{:S(2)}, u32[]{:S(2)}) collective-permute-start(f32[4,2,24,1024]{3,2,1,0:T(8,128)} %get-tuple-element.17), channel_id=1, source_target_pairs={{0,32},{1,33},{2,34},{3,35},{4,36},{5,37},{6,38},{7,39},{8,136},{9... | collective-permute-start | bytes 2359304 | tf_op jit(solution)/shard_map/ppermute | solution.py:43
  132.0 6.7 %collective-permute-done.19 = f32[4,2,24,1024]{3,2,1,0:T(8,128)} collective-permute-done((f32[4,2,24,1024]{3,2,1,0:T(8,128)}, f32[4,2,24,1024]{3,2,1,0:T(8,128)}, u32[]{:S(2)}, u32[]{:S(2)}) %collective-permute-start.19) | collective-permute-done | bytes 786464 | tf_op jit(solution)/shard_map/ppermute | solution.py:43
  138.7 1.5 fusion.6
  140.2 1.6 collective-permute-start.21
  141.8 1.7 collective-permute-start.22
  143.5 4.0 %collective-permute-done.4 = f32[4,2,24,1024]{3,2,1,0:T(8,128)} collective-permute-done((f32[4,2,24,1024]{3,2,1,0:T(8,128)}, f32[4,2,24,1024]{3,2,1,0:T(8,128)}, u32[]{:S(2)}, u32[]{:S(2)}) %collective-permute-start.4) | collective-permute-done | bytes 786464 | tf_op jit(solution)/shard_map/ppermute | solution.py:43
  147.5 5.4 %collective-permute-start.23 = (f32[2,24,1024]{2,1,0:T(8,128)S(1)}, f32[2,24,1024]{2,1,0:T(8,128)S(1)}, u32[]{:S(2)}, u32[]{:S(2)}) collective-permute-start(f32[2,24,1024]{2,1,0:T(8,128)S(1)} %get-tuple-element.37), channel_id=1, source_target_pairs={{0,128},{1,129},{2,130},{3,131},{4,132},{5,133},{6,134},{7,135},{8... | collective-permute-start | bytes 589832 | tf_op jit(solution)/shard_map/ppermute | solution.py:43
  152.9 6.8 %collective-permute-done.5 = f32[4,2,24,1024]{3,2,1,0:T(8,128)} collective-permute-done((f32[4,2,24,1024]{3,2,1,0:T(8,128)}, f32[4,2,24,1024]{3,2,1,0:T(8,128)}, u32[]{:S(2)}, u32[]{:S(2)}) %collective-permute-start.5) | collective-permute-done | bytes 786464 | tf_op jit(solution)/shard_map/ppermute | solution.py:43
  159.8 1.7 fusion.16
  161.5 1.6 collective-permute-start.7
  163.1 1.7 collective-permute-start.8
  164.8 2.0 collective-permute-start.9
  166.8 1.1 fusion.14
  167.9 0.0 copy-start.1
  167.9 0.0 copy-start.2
  167.9 0.0 copy-start.3
  167.9 0.5 collective-permute-done.7
  168.4 0.3 collective-permute-done.8
  168.7 3.2 %collective-permute-done.9 = f32[2,24,1024]{2,1,0:T(8,128)S(1)} collective-permute-done((f32[2,24,1024]{2,1,0:T(8,128)S(1)}, f32[2,24,1024]{2,1,0:T(8,128)S(1)}, u32[]{:S(2)}, u32[]{:S(2)}) %collective-permute-start.9) | collective-permute-done | bytes 196640 | tf_op jit(solution)/shard_map/ppermute | solution.py:43
  171.9 1.2 fusion.24
  173.2 0.1 copy.21
  173.3 0.3 collective-permute-start.24
  173.7 5.6 %collective-permute-done.24 = f32[4,12,8,128]{3,2,1,0:T(8,128)S(1)} collective-permute-done((f32[4,12,8,128]{3,2,1,0:T(8,128)S(1)}, f32[4,12,8,128]{3,2,1,0:T(8,128)S(1)}, u32[]{:S(2)}, u32[]{:S(2)}) %collective-permute-start.24) | collective-permute-done | bytes 196640 | tf_op jit(solution)/shard_map/ppermute | solution.py:43
  179.3 5.3 %collective-permute-start.25 = (f32[2,12,8,128]{3,2,1,0:T(8,128)S(1)}, f32[2,12,8,128]{3,2,1,0:T(8,128)S(1)}, u32[]{:S(2)}, u32[]{:S(2)}) collective-permute-start(f32[2,12,8,128]{3,2,1,0:T(8,128)S(1)} %get-tuple-element.48), channel_id=1, source_target_pairs={{0,1},{1,2},{2,3},{3,0},{4,5},{5,6},{6,7},{7,4},{8,9},{9,10},{10,1... | collective-permute-start | bytes 294920 | tf_op jit(solution)/shard_map/ppermute | solution.py:43
  184.7 3.0 %collective-permute-start.26 = (f32[2,12,8,128]{3,2,1,0:T(8,128)S(1)}, f32[2,12,8,128]{3,2,1,0:T(8,128)S(1)}, u32[]{:S(2)}, u32[]{:S(2)}) collective-permute-start(f32[2,12,8,128]{3,2,1,0:T(8,128)S(1)} %get-tuple-element.49), channel_id=1, source_target_pairs={{0,2},{1,3},{2,0},{3,1},{4,6},{5,7},{6,4},{7,5},{8,10},{9,11},{10,... | collective-permute-start | bytes 294920 | tf_op jit(solution)/shard_map/ppermute | solution.py:43
  187.6 0.7 collective-permute-start.27
  188.3 5.3 %collective-permute-done.26.piece_2 = f32[2,12,8,128]{3,2,1,0:T(8,128)S(1)} collective-permute-done((f32[2,12,8,128]{3,2,1,0:T(8,128)S(1)}, f32[2,12,8,128]{3,2,1,0:T(8,128)S(1)}, u32[]{:S(2)}, u32[]{:S(2)}) %collective-permute-start.26) | collective-permute-done | bytes 98336 | tf_op jit(solution)/shard_map/ppermute | solution.py:43
  193.7 1.4 shard_map.78
  (51 shorter events, 0.2 us)
Async XLA Ops:
  7.2 1.1 copy-start
  7.2 112.5 %all-gather.3.cloned.1.call-start = ((), (), s32[]{:S(2)}) async-start(), calls=%async_computation | async-start | bytes 3538944 | tf_op jit(solution)/shard_map/all_gather | solution.py:165
  10.2 2.7 %copy-start.4 = (bf16[512,2048]{1,0:T(8,128)(2,1)S(1)}, bf16[512,2048]{1,0:T(8,128)(2,1)}, u32[]{:S(2)}) copy-start(bf16[512,2048]{1,0:T(8,128)(2,1)} %param.6) | copy-start | bytes 6291460
  10.2 1.8 collective-permute-start
  12.9 86.1 %copy-start.8 = (bf16[2,256,384]{2,1,0:T(8,128)(2,1)}, bf16[2,256,384]{2,1,0:T(8,128)(2,1)S(1)}, u32[]{:S(2)}) copy-start(bf16[2,256,384]{2,1,0:T(8,128)(2,1)S(1)} %get-tuple-element.43.refs_0_) | copy-start | bytes 1179652
  13.1 94.3 %copy-start.5 = (bf16[512,1024]{1,0:T(8,128)(2,1)}, bf16[512,1024]{1,0:T(8,128)(2,1)S(1)}, u32[]{:S(2)}) copy-start(bf16[512,1024]{1,0:T(8,128)(2,1)S(1)} %get-tuple-element.41.refs_1_.refs_9_) | copy-start | bytes 3145732
  13.1 74.3 %collective-permute-start.1 = (bf16[512,1024]{1,0:T(8,128)(2,1)S(1)}, bf16[512,1024]{1,0:T(8,128)(2,1)S(1)}, u32[]{:S(2)}, u32[]{:S(2)}) collective-permute-start(bf16[512,1024]{1,0:T(8,128)(2,1)S(1)} %get-tuple-element.40), channel_id=1, source_target_pairs={{0,4},{1,5},{2,6},{3,7},{4,0},{5,1},{6,2},{7,3},{8,12},{9,13},{10,... | collective-permute-start | bytes 3145736 | tf_op jit(solution)/shard_map/ppermute | solution.py:43
  15.1 51.0 %collective-permute-start.10 = (bf16[2,256,384]{2,1,0:T(8,128)(2,1)S(1)}, bf16[2,256,384]{2,1,0:T(8,128)(2,1)S(1)}, u32[]{:S(2)}, u32[]{:S(2)}) collective-permute-start(bf16[2,256,384]{2,1,0:T(8,128)(2,1)S(1)} %get-tuple-element.43.refs_0_), channel_id=1, source_target_pairs={{0,4},{1,5},{2,6},{3,7},{4,1},{5,2},{6,3},{7,0},{8,12},{9,13},{10,... | collective-permute-start | bytes 1179656 | tf_op jit(solution)/shard_map/ppermute | solution.py:43
  15.3 53.4 %collective-permute-start.11 = (bf16[2,256,384]{2,1,0:T(8,128)(2,1)S(1)}, bf16[2,256,384]{2,1,0:T(8,128)(2,1)S(1)}, u32[]{:S(2)}, u32[]{:S(2)}) collective-permute-start(bf16[2,256,384]{2,1,0:T(8,128)(2,1)S(1)} %get-tuple-element.43.refs_0_), channel_id=1, source_target_pairs={{0,7},{1,4},{2,5},{3,6},{4,0},{5,1},{6,2},{7,3},{8,15},{9,12},{10,... | collective-permute-start | bytes 1179656 | tf_op jit(solution)/shard_map/ppermute | solution.py:43
  66.2 41.2 %copy-start.13 = (bf16[2,256,384]{2,1,0:T(8,128)(2,1)}, bf16[2,256,384]{2,1,0:T(8,128)(2,1)S(1)}, u32[]{:S(2)}) copy-start(bf16[2,256,384]{2,1,0:T(8,128)(2,1)S(1)} %collective-permute-done.10.refs_1_) | copy-start | bytes 1179652
  66.2 21.2 %collective-permute-start.12 = (bf16[2,256,384]{2,1,0:T(8,128)(2,1)S(1)}, bf16[2,256,384]{2,1,0:T(8,128)(2,1)S(1)}, u32[]{:S(2)}, u32[]{:S(2)}) collective-permute-start(bf16[2,256,384]{2,1,0:T(8,128)(2,1)S(1)} %collective-permute-done.10.refs_1_), channel_id=1, source_target_pairs={{0,4},{1,5},{2,6},{3,7},{4,1},{5,2},{6,3},{7,0},{8,12},{9,13},{10,... | collective-permute-start | bytes 1179656 | tf_op jit(solution)/shard_map/ppermute | solution.py:43
  68.7 38.7 %copy-start.14 = (bf16[2,256,384]{2,1,0:T(8,128)(2,1)}, bf16[2,256,384]{2,1,0:T(8,128)(2,1)S(1)}, u32[]{:S(2)}) copy-start(bf16[2,256,384]{2,1,0:T(8,128)(2,1)S(1)} %collective-permute-done.11.refs_2_) | copy-start | bytes 1179652
  68.7 19.2 %collective-permute-start.13 = (bf16[2,256,384]{2,1,0:T(8,128)(2,1)S(1)}, bf16[2,256,384]{2,1,0:T(8,128)(2,1)S(1)}, u32[]{:S(2)}, u32[]{:S(2)}) collective-permute-start(bf16[2,256,384]{2,1,0:T(8,128)(2,1)S(1)} %collective-permute-done.11.refs_2_), channel_id=1, source_target_pairs={{0,7},{1,4},{2,5},{3,6},{4,0},{5,1},{6,2},{7,3},{8,15},{9,12},{10,... | collective-permute-start | bytes 1179656 | tf_op jit(solution)/shard_map/ppermute | solution.py:43
  87.4 3.8 %copy-start.15 = (bf16[2,256,384]{2,1,0:T(8,128)(2,1)}, bf16[2,256,384]{2,1,0:T(8,128)(2,1)S(1)}, u32[]{:S(2)}) copy-start(bf16[2,256,384]{2,1,0:T(8,128)(2,1)S(1)} %collective-permute-done.12.refs_3_) | copy-start | bytes 1179652
  87.4 11.6 %collective-permute-start.14 = (bf16[2,256,384]{2,1,0:T(8,128)(2,1)S(1)}, bf16[2,256,384]{2,1,0:T(8,128)(2,1)S(1)}, u32[]{:S(2)}, u32[]{:S(2)}) collective-permute-start(bf16[2,256,384]{2,1,0:T(8,128)(2,1)S(1)} %collective-permute-done.12.refs_3_), channel_id=1, source_target_pairs={{0,4},{1,5},{2,6},{3,7},{4,1},{5,2},{6,3},{7,0},{8,12},{9,13},{10,... | collective-permute-start | bytes 1179656 | tf_op jit(solution)/shard_map/ppermute | solution.py:43
  87.4 16.4 %collective-permute-start.2 = (bf16[512,1024]{1,0:T(8,128)(2,1)S(1)}, bf16[512,1024]{1,0:T(8,128)(2,1)S(1)}, u32[]{:S(2)}, u32[]{:S(2)}) collective-permute-start(bf16[512,1024]{1,0:T(8,128)(2,1)S(1)} %get-tuple-element.41.refs_1_.refs_9_), channel_id=1, source_target_pairs={{0,8},{1,9},{2,10},{3,11},{4,12},{5,13},{6,14},{7,15},{8,0},{9,1},... | collective-permute-start | bytes 3145736 | tf_op jit(solution)/shard_map/ppermute | solution.py:43
  87.4 20.0 %copy-start.11 = (bf16[512,1024]{1,0:T(8,128)(2,1)}, bf16[512,1024]{1,0:T(8,128)(2,1)S(1)}, u32[]{:S(2)}) copy-start(bf16[512,1024]{1,0:T(8,128)(2,1)S(1)} %collective-permute-done.1.refs_2_.refs_10_) | copy-start | bytes 3145732
  87.4 20.0 %collective-permute-start.3 = (bf16[512,1024]{1,0:T(8,128)(2,1)S(1)}, bf16[512,1024]{1,0:T(8,128)(2,1)}, u32[]{:S(2)}, u32[]{:S(2)}) collective-permute-start(bf16[512,1024]{1,0:T(8,128)(2,1)S(1)} %collective-permute-done.1.refs_2_.refs_10_), channel_id=1, source_target_pairs={{0,8},{1,9},{2,10},{3,11},{4,12},{5,13},{6,14},{7,15},{8,0},{9,1},... | collective-permute-start | bytes 3145736 | tf_op jit(solution)/shard_map/ppermute | solution.py:43
  87.9 19.5 %copy-start.16 = (bf16[2,256,384]{2,1,0:T(8,128)(2,1)}, bf16[2,256,384]{2,1,0:T(8,128)(2,1)S(1)}, u32[]{:S(2)}) copy-start(bf16[2,256,384]{2,1,0:T(8,128)(2,1)S(1)} %collective-permute-done.13.refs_4_) | copy-start | bytes 1179652
  87.9 11.9 %collective-permute-start.15 = (bf16[2,256,384]{2,1,0:T(8,128)(2,1)S(1)}, bf16[2,256,384]{2,1,0:T(8,128)(2,1)S(1)}, u32[]{:S(2)}, u32[]{:S(2)}) collective-permute-start(bf16[2,256,384]{2,1,0:T(8,128)(2,1)S(1)} %collective-permute-done.13.refs_4_), channel_id=1, source_target_pairs={{0,7},{1,4},{2,5},{3,6},{4,0},{5,1},{6,2},{7,3},{8,15},{9,12},{10,... | collective-permute-start | bytes 1179656 | tf_op jit(solution)/shard_map/ppermute | solution.py:43
  99.0 8.5 %copy-start.9 = (bf16[2,256,384]{2,1,0:T(8,128)(2,1)}, bf16[2,256,384]{2,1,0:T(8,128)(2,1)S(1)}, u32[]{:S(2)}) copy-start(bf16[2,256,384]{2,1,0:T(8,128)(2,1)S(1)} %collective-permute-done.14.refs_5_) | copy-start | bytes 1179652
  99.0 7.0 %collective-permute-start.16 = (bf16[256,384]{1,0:T(8,128)(2,1)S(1)}, bf16[256,384]{1,0:T(8,128)(2,1)S(1)}, u32[]{:S(2)}, u32[]{:S(2)}) collective-permute-start(bf16[256,384]{1,0:T(8,128)(2,1)S(1)} %slice_bitcast_fusion.2), channel_id=1, source_target_pairs={{0,4},{1,5},{2,6},{3,7},{4,1},{5,2},{6,3},{7,0},{8,12},{9,13},{10,... | collective-permute-start | bytes 589832 | tf_op jit(solution)/shard_map/ppermute | solution.py:43
  99.8 7.6 %copy-start.10 = (bf16[2,256,384]{2,1,0:T(8,128)(2,1)}, bf16[2,256,384]{2,1,0:T(8,128)(2,1)S(1)}, u32[]{:S(2)}) copy-start(bf16[2,256,384]{2,1,0:T(8,128)(2,1)S(1)} %collective-permute-done.15.refs_6_) | copy-start | bytes 1179652
  99.8 7.5 %collective-permute-start.17 = (bf16[256,384]{1,0:T(8,128)(2,1)S(1)}, bf16[256,384]{1,0:T(8,128)(2,1)S(1)}, u32[]{:S(2)}, u32[]{:S(2)}) collective-permute-start(bf16[256,384]{1,0:T(8,128)(2,1)S(1)} %slice_bitcast_fusion.1), channel_id=1, source_target_pairs={{0,7},{1,4},{2,5},{3,6},{4,0},{5,1},{6,2},{7,3},{8,15},{9,12},{10,... | collective-permute-start | bytes 589832 | tf_op jit(solution)/shard_map/ppermute | solution.py:43
  103.8 3.6 %copy-start.12 = (bf16[512,1024]{1,0:T(8,128)(2,1)}, bf16[512,1024]{1,0:T(8,128)(2,1)S(1)}, u32[]{:S(2)}) copy-start(bf16[512,1024]{1,0:T(8,128)(2,1)S(1)} %collective-permute-done.2.refs_3_.refs_11_) | copy-start | bytes 3145732
  106.0 1.5 copy-start.17
  107.4 0.7 copy-start.18
  116.1 13.8 %collective-permute-start.18 = (f32[4,2,24,1024]{3,2,1,0:T(8,128)}, f32[4,2,24,1024]{3,2,1,0:T(8,128)S(1)}, u32[]{:S(2)}, u32[]{:S(2)}) collective-permute-start(f32[4,2,24,1024]{3,2,1,0:T(8,128)} %get-tuple-element.19), channel_id=1, source_target_pairs={{0,16},{1,17},{2,18},{3,19},{4,20},{5,21},{6,22},{7,23},{8,72},{9,... | collective-permute-start | bytes 2359304 | tf_op jit(solution)/shard_map/ppermute | solution.py:43
  116.7 21.9 %collective-permute-start.19 = (f32[4,2,24,1024]{3,2,1,0:T(8,128)}, f32[4,2,24,1024]{3,2,1,0:T(8,128)}, u32[]{:S(2)}, u32[]{:S(2)}) collective-permute-start(f32[4,2,24,1024]{3,2,1,0:T(8,128)} %get-tuple-element.20), channel_id=1, source_target_pairs={{0,48},{1,49},{2,50},{3,51},{4,52},{5,53},{6,54},{7,55},{8,200},{9... | collective-permute-start | bytes 2359304 | tf_op jit(solution)/shard_map/ppermute | solution.py:43
  118.2 20.4 %collective-permute-start.20 = (f32[4,2,24,1024]{3,2,1,0:T(8,128)}, f32[4,2,24,1024]{3,2,1,0:T(8,128)}, u32[]{:S(2)}, u32[]{:S(2)}) collective-permute-start(f32[4,2,24,1024]{3,2,1,0:T(8,128)} %get-tuple-element.21), channel_id=1, source_target_pairs={{0,32},{1,33},{2,34},{3,35},{4,36},{5,37},{6,38},{7,39},{8,136},{9... | collective-permute-start | bytes 2359304 | tf_op jit(solution)/shard_map/ppermute | solution.py:43
  119.7 19.0 %copy-start.6 = (f32[4,2,24,1024]{3,2,1,0:T(8,128)S(1)}, f32[4,2,24,1024]{3,2,1,0:T(8,128)}, u32[]{:S(2)}) copy-start(f32[4,2,24,1024]{3,2,1,0:T(8,128)} %get-tuple-element.18) | copy-start | bytes 2359300
  127.7 32.0 %copy-start.7 = (f32[4,2,24,1024]{3,2,1,0:T(8,128)S(1)}, f32[4,2,24,1024]{3,2,1,0:T(8,128)}, u32[]{:S(2)}) copy-start(f32[4,2,24,1024]{3,2,1,0:T(8,128)} %get-tuple-element.14) | copy-start | bytes 2359300
  127.8 19.8 %collective-permute-start.4 = (f32[4,2,24,1024]{3,2,1,0:T(8,128)}, f32[4,2,24,1024]{3,2,1,0:T(8,128)}, u32[]{:S(2)}, u32[]{:S(2)}) collective-permute-start(f32[4,2,24,1024]{3,2,1,0:T(8,128)} %get-tuple-element.15), channel_id=1, source_target_pairs={{0,16},{1,17},{2,18},{3,19},{4,20},{5,21},{6,22},{7,23},{8,72},{9,... | collective-permute-start | bytes 2359304 | tf_op jit(solution)/shard_map/ppermute | solution.py:43
  129.9 29.9 %collective-permute-start.5 = (f32[4,2,24,1024]{3,2,1,0:T(8,128)}, f32[4,2,24,1024]{3,2,1,0:T(8,128)}, u32[]{:S(2)}, u32[]{:S(2)}) collective-permute-start(f32[4,2,24,1024]{3,2,1,0:T(8,128)} %get-tuple-element.16), channel_id=1, source_target_pairs={{0,48},{1,49},{2,50},{3,51},{4,52},{5,53},{6,54},{7,55},{8,200},{9... | collective-permute-start | bytes 2359304 | tf_op jit(solution)/shard_map/ppermute | solution.py:43
  129.9 29.8 %collective-permute-start.6 = (f32[4,2,24,1024]{3,2,1,0:T(8,128)}, f32[4,2,24,1024]{3,2,1,0:T(8,128)}, u32[]{:S(2)}, u32[]{:S(2)}) collective-permute-start(f32[4,2,24,1024]{3,2,1,0:T(8,128)} %get-tuple-element.17), channel_id=1, source_target_pairs={{0,32},{1,33},{2,34},{3,35},{4,36},{5,37},{6,38},{7,39},{8,136},{9... | collective-permute-start | bytes 2359304 | tf_op jit(solution)/shard_map/ppermute | solution.py:43
  140.2 24.6 %collective-permute-start.21 = (f32[2,24,1024]{2,1,0:T(8,128)S(1)}, f32[2,24,1024]{2,1,0:T(8,128)S(1)}, u32[]{:S(2)}, u32[]{:S(2)}) collective-permute-start(f32[2,24,1024]{2,1,0:T(8,128)S(1)} %get-tuple-element.39), channel_id=1, source_target_pairs={{0,64},{1,65},{2,66},{3,67},{4,68},{5,69},{6,70},{7,71},{8,24},{9,... | collective-permute-start | bytes 589832 | tf_op jit(solution)/shard_map/ppermute | solution.py:43
  141.8 25.0 %collective-permute-start.22 = (f32[2,24,1024]{2,1,0:T(8,128)S(1)}, f32[2,24,1024]{2,1,0:T(8,128)S(1)}, u32[]{:S(2)}, u32[]{:S(2)}) collective-permute-start(f32[2,24,1024]{2,1,0:T(8,128)S(1)} %get-tuple-element.38), channel_id=1, source_target_pairs={{0,192},{1,193},{2,194},{3,195},{4,196},{5,197},{6,198},{7,199},{8... | collective-permute-start | bytes 589832 | tf_op jit(solution)/shard_map/ppermute | solution.py:43
  147.5 19.3 %collective-permute-start.23 = (f32[2,24,1024]{2,1,0:T(8,128)S(1)}, f32[2,24,1024]{2,1,0:T(8,128)S(1)}, u32[]{:S(2)}, u32[]{:S(2)}) collective-permute-start(f32[2,24,1024]{2,1,0:T(8,128)S(1)} %get-tuple-element.37), channel_id=1, source_target_pairs={{0,128},{1,129},{2,130},{3,131},{4,132},{5,133},{6,134},{7,135},{8... | collective-permute-start | bytes 589832 | tf_op jit(solution)/shard_map/ppermute | solution.py:43
  161.5 7.0 %collective-permute-start.7 = (f32[2,24,1024]{2,1,0:T(8,128)S(1)}, f32[2,24,1024]{2,1,0:T(8,128)S(1)}, u32[]{:S(2)}, u32[]{:S(2)}) collective-permute-start(f32[2,24,1024]{2,1,0:T(8,128)S(1)} %get-tuple-element.36), channel_id=1, source_target_pairs={{0,64},{1,65},{2,66},{3,67},{4,68},{5,69},{6,70},{7,71},{8,24},{9,... | collective-permute-start | bytes 589832 | tf_op jit(solution)/shard_map/ppermute | solution.py:43
  163.1 5.7 %collective-permute-start.8 = (f32[2,24,1024]{2,1,0:T(8,128)S(1)}, f32[2,24,1024]{2,1,0:T(8,128)S(1)}, u32[]{:S(2)}, u32[]{:S(2)}) collective-permute-start(f32[2,24,1024]{2,1,0:T(8,128)S(1)} %get-tuple-element.35), channel_id=1, source_target_pairs={{0,192},{1,193},{2,194},{3,195},{4,196},{5,197},{6,198},{7,199},{8... | collective-permute-start | bytes 589832 | tf_op jit(solution)/shard_map/ppermute | solution.py:43
  164.8 7.2 %collective-permute-start.9 = (f32[2,24,1024]{2,1,0:T(8,128)S(1)}, f32[2,24,1024]{2,1,0:T(8,128)S(1)}, u32[]{:S(2)}, u32[]{:S(2)}) collective-permute-start(f32[2,24,1024]{2,1,0:T(8,128)S(1)} %get-tuple-element.34), channel_id=1, source_target_pairs={{0,128},{1,129},{2,130},{3,131},{4,132},{5,133},{6,134},{7,135},{8... | collective-permute-start | bytes 589832 | tf_op jit(solution)/shard_map/ppermute | solution.py:43
  167.9 25.8 %copy-start.1 = (f32[1,12,8192]{2,0,1:T(1,128)S(1)}, f32[1,12,8192]{2,0,1:T(1,128)}, u32[]{:S(2)}) copy-start(f32[1,12,8192]{2,0,1:T(1,128)} %param.7) | copy-start | bytes 1179652
  167.9 25.8 %copy-start.2 = (f32[1,12,8192]{2,0,1:T(1,128)S(1)}, f32[1,12,8192]{2,0,1:T(1,128)}, u32[]{:S(2)}) copy-start(f32[1,12,8192]{2,0,1:T(1,128)} %param.8) | copy-start | bytes 1179652
  167.9 25.8 %copy-start.3 = (f32[1,12,8192]{2,0,1:T(1,128)S(1)}, f32[1,12,8192]{2,0,1:T(1,128)}, u32[]{:S(2)}) copy-start(f32[1,12,8192]{2,0,1:T(1,128)} %param.9) | copy-start | bytes 1179652
  173.3 6.0 %collective-permute-start.24 = (f32[4,12,8,128]{3,2,1,0:T(8,128)S(1)}, f32[4,12,8,128]{3,2,1,0:T(8,128)S(1)}, u32[]{:S(2)}, u32[]{:S(2)}) collective-permute-start(f32[4,12,8,128]{3,2,1,0:T(8,128)S(1)} %get-tuple-element.50), channel_id=1, source_target_pairs={{0,4},{1,5},{2,6},{3,7},{4,0},{5,1},{6,2},{7,3},{8,12},{9,13},{10,... | collective-permute-start | bytes 589832 | tf_op jit(solution)/shard_map/ppermute | solution.py:43
  179.3 9.0 %collective-permute-start.25 = (f32[2,12,8,128]{3,2,1,0:T(8,128)S(1)}, f32[2,12,8,128]{3,2,1,0:T(8,128)S(1)}, u32[]{:S(2)}, u32[]{:S(2)}) collective-permute-start(f32[2,12,8,128]{3,2,1,0:T(8,128)S(1)} %get-tuple-element.48), channel_id=1, source_target_pairs={{0,1},{1,2},{2,3},{3,0},{4,5},{5,6},{6,7},{7,4},{8,9},{9,10},{10,1... | collective-permute-start | bytes 294920 | tf_op jit(solution)/shard_map/ppermute | solution.py:43
  184.7 9.0 %collective-permute-start.26 = (f32[2,12,8,128]{3,2,1,0:T(8,128)S(1)}, f32[2,12,8,128]{3,2,1,0:T(8,128)S(1)}, u32[]{:S(2)}, u32[]{:S(2)}) collective-permute-start(f32[2,12,8,128]{3,2,1,0:T(8,128)S(1)} %get-tuple-element.49), channel_id=1, source_target_pairs={{0,2},{1,3},{2,0},{3,1},{4,6},{5,7},{6,4},{7,5},{8,10},{9,11},{10,... | collective-permute-start | bytes 294920 | tf_op jit(solution)/shard_map/ppermute | solution.py:43
  187.6 6.0 %collective-permute-start.27 = (f32[2,12,8,128]{3,2,1,0:T(8,128)S(1)}, f32[2,12,8,128]{3,2,1,0:T(8,128)S(1)}, u32[]{:S(2)}, u32[]{:S(2)}) collective-permute-start(f32[2,12,8,128]{3,2,1,0:T(8,128)S(1)} %get-tuple-element.46), channel_id=1, source_target_pairs={{0,3},{1,0},{2,1},{3,2},{4,7},{5,4},{6,5},{7,6},{8,11},{9,8},{10,9... | collective-permute-start | bytes 294920 | tf_op jit(solution)/shard_map/ppermute | solution.py:43
Sparse Core Ops, SparseCore 0:
  13.0 73.1 all-gather.2

commit v4 on v3

--- a/solution.py
+++ b/solution.py
@@ -16,7 +16,7 @@
 AXES = ("dp", "tr", "tc")
 SIDE = 4
 ROWS = 48
-CHUNKS = (24, 24)
+CHUNKS = (32, 16)
 
 
 def moves(where):
@@ -71,8 +71,8 @@
 
 def product_kernel(pieces, count, *refs):
     acts, cots = refs[:count], refs[count : count + 4]
-    outs = refs[count + 4 : count + 8]
-    act, cot, act_sem, cot_sem = refs[count + 8 :]
+    plus, minus, add_plus, add_minus, mine = refs[count + 4 : count + 9]
+    act, cot, act_sem, cot_sem = refs[count + 9 :]
     tr, tc = lax.axis_index("tr"), lax.axis_index("tc")
     features = act.shape[-1]
     i = pl.program_id(0)
@@ -92,61 +92,85 @@
         late = [pltpu.make_async_copy(ref, cot.at[n], cot_sem.at[n]) for n, ref in enumerate(cots)]
         for copy in copies + late:
             copy.start()
-        for copy in copies + late:
+        for copy in copies:
             copy.wait()
 
     def part(half, replica, n):
+        @pl.when(i == 0)
+        def arrived():
+            pltpu.make_async_copy(cots[n], cot.at[n], cot_sem.at[n]).wait()
+
         rows = act[pl.ds(2 * half, 2), i, replica].reshape(cot.shape[1], features)
         return lax.dot_general(rows, cot[n], (((0,), (0,)), ((), ())), preferred_element_type=jnp.float32)
 
     total = part(tr, 0, 0) + part(1 - tr, 0, 1)
     total = total + (part(tr, 1, 2) + part(1 - tr, 1, 3))
     total = total.reshape(SIDE, SIDE, 1, features // SIDE**2, total.shape[-1])
-    for near in range(SIDE):
-        outs[near][...] = total[near]
+    plus[0] = total[2, :2]
+    plus[1] = total[1, 2:]
+    minus[0] = total[2, 2:]
+    minus[1] = total[3, :2]
+    add_plus[...] = total[1, :2]
+    add_minus[...] = total[3, 2:]
+    mine[...] = total[0]
 
 
 def product(acts, pieces, cots):
     tokens, features = acts[0].shape[-2:]
     units = cots[0].shape[1]
     rows = features // SIDE**2
+    pack = pl.BlockSpec((2, 2, 1, rows, units), lambda i: (0, 0, i, 0, 0))
+    part = pl.BlockSpec((2, 1, rows, units), lambda i: (0, i, 0, 0))
+    full = pl.BlockSpec((SIDE, 1, rows, units), lambda i: (0, i, 0, 0))
+    packed = jax.ShapeDtypeStruct((2, 2, 2, rows, units), jnp.float32)
+    parted = jax.ShapeDtypeStruct((2, 2, rows, units), jnp.float32)
     return pl.pallas_call(
         lambda *refs: product_kernel(pieces, len(acts), *refs),
         grid=(2,),
         in_specs=[pl.BlockSpec(memory_space=pl.ANY)] * (len(acts) + 4),
-        out_specs=[pl.BlockSpec((SIDE, 1, rows, units), lambda i: (0, i, 0, 0))] * SIDE,
-        out_shape=[jax.ShapeDtypeStruct((SIDE, 2, rows, units), jnp.float32)] * SIDE,
+        out_specs=[pack, pack, part, part, full],
+        out_shape=[packed, packed, parted, parted, jax.ShapeDtypeStruct((SIDE, 2, rows, units), jnp.float32)],
         scratch_shapes=[
             pltpu.VMEM((4, 2, 2, tokens, features), acts[0].dtype),
             pltpu.VMEM((4,) + cots[0].shape, cots[0].dtype),
             pltpu.SemaphoreType.DMA((len(acts),)),
             pltpu.SemaphoreType.DMA((4,)),
         ],
-        compiler_params=pltpu.CompilerParams(vmem_limit_bytes=58 * 2**20),
+        compiler_params=pltpu.CompilerParams(vmem_limit_bytes=60 * 2**20),
         cost_estimate=pl.CostEstimate(
             flops=2 * 2 * features * 4 * cots[0].shape[0] * units, bytes_accessed=12 * 2**20, transcendentals=0
         ),
     )(*acts, *cots)
 
 
-def gathered_in_ring(own):
-    up, down = moves(lambda y, x, core, z: (y, x, core, z + 1)), moves(lambda y, x, core, z: (y, x, core, z - 1))
+UP = moves(lambda y, x, core, z: (y, x, core, z + 1))
+DOWN = moves(lambda y, x, core, z: (y, x, core, z - 1))
+
+
+def ring(own):
     acts, pieces = [own], [(0, None)]
     below, above = own, own
     for hop in range(1, 4):
-        below, above = send(below, up), send(above, down)
+        below, above = send(below, UP), send(above, DOWN)
         acts += [below, above]
         pieces += [(-hop, None), (hop, None)]
-    acts += [send(below[0], up), send(above[1], down)]
-    pieces += [(4, 0), (4, 1)]
     return acts, pieces
 
 
+def ring_end(acts, pieces):
+    return acts + [send(acts[-2][0], UP), send(acts[-1][1], DOWN)], pieces + [(4, 0), (4, 1)]
+
+
 def summed(parts):
-    first = [send(parts[hop], step(True, hop)) for hop in (1, 3, 2)]
-    far = [parts[0][s] + first[0][s] + (first[1][s] + first[2][s]) for s in range(SIDE)]
-    second = [send(far[hop], step(False, hop)) for hop in (1, 3, 2)]
-    return far[0] + second[0] + (second[1] + second[2])
+    plus, minus, add_plus, add_minus, mine = parts
+    left = send(plus, step(True, 1))
+    right = send(minus, step(True, -1))
+    near = send(add_plus + left[0], step(True, 1))
+    far = send(add_minus + right[0], step(True, -1))
+    low = [mine[s] + right[1, s] + near[s] for s in range(2)]
+    high = [mine[2 + s] + left[1, s] + far[s] for s in range(2)]
+    came = [send(low[1], step(False, 1)), send(high[1], step(False, -1)), send(high[0], step(False, 2))]
+    return low[0] + came[0] + (came[1] + came[2])
 
 
 def shards(activations, cotangent, master, moment, second):
@@ -155,6 +179,7 @@
     units = cotangent.shape[1] // 2
     away = lax.dynamic_slice_in_dim(cotangent, (1 - tr) * units, units, 1)
     own_keep = lax.dynamic_slice_in_dim(cotangent, tr * units, units, 1)
+    activations, away, own_keep = lax.optimization_barrier((activations, away, own_keep))
     own_came = send(away, PAIR)
     far_keep = send(own_keep, OTHER_CORE)
     ordered = feature_order(activations)
@@ -163,13 +188,14 @@
     both = jnp.stack([ordered[:, :half], far_act])
     size = CHUNKS[0] * SIDE**2
     whole = lax.all_gather(both[:, :, :size], ("tc", "tr"), axis=0)
-    acts, pieces = gathered_in_ring(both[:, :, size:])
+    rest, own_came = lax.optimization_barrier((both[:, :, size:], own_came))
+    acts, pieces = ring(rest)
     far_came = send(own_came, OTHER_CORE)
     cots = (own_keep, own_came, far_keep, far_came)
-    sums = [
-        summed(product([whole.reshape(4, 2, 2, tokens, size)], [None], cots)),
-        summed(product(acts, pieces, cots)),
-    ]
+    parts = product([whole.reshape(4, 2, 2, tokens, size)], [None], cots)
+    acts[-2:], parts = lax.optimization_barrier((acts[-2:], parts))
+    acts, pieces = ring_end(acts, pieces)
+    sums = [summed(parts), summed(product(acts, pieces, cots))]
     rows = jnp.concatenate(sums, axis=1).reshape(2, 4, ROWS // 4, 8, units // 8)
     return updated(rows, master, moment, second)
 

time: 204 us -> 200 us (0.980)
  starting transfers between devices: 53.7 us -> 46.3 us
  local copies, waits for them, and re-layouts: 2.05 us -> 5.31 us
    ppermute x28 -> x30, starting transfers between devices: 53.7 us -> 46.2 us  [send(): return lax.ppermute(array, AXES, pairs)]
    ppermute x28 -> x30, waiting for transfers between devices: 106 us -> 98.6 us  [send(): return lax.ppermute(array, AXES, pairs)]
    all_gather x1, waiting for transfers between devices: 0.01 us -> 6.89 us  [shards(): whole = lax.all_gather(both[:, :, :size], ('tc', 'tr'), axis=0)]
    dynamic_slice x1, local copies, waits for them, and re-layouts: 0.21 us -> 2.78 us  [shards(): own_keep = lax.dynamic_slice_in_dim(cotangent, tr * units, units, 1)]
    add x4 -> x8, other arithmetic: 5.54 us -> 5.34 us  [the longest x2 2.42 us: summed(): return low[0] + came[0] + (came[1] + came[2])]
  transfers between devices with their start and end apart: 29 -> 31, of which waited for: 15 -> 15; matrix products, arithmetic and copies ran while one was open for 2% -> 2% of each run, Pallas kernels for 8% -> 8%
where the time goes in v4:
time: 200 us; the launch traced here: 198 us
  waiting for transfers between devices  105 us (52%)
  starting transfers between devices  46.3 us (23%)
  Pallas kernels  18 us (9%)
  between operations  14.4 us (7%)
  other arithmetic  6.34 us (3%)
  local copies, waits for them, and re-layouts  5.31 us (3%)
  matrix products  2.04 us (1%)
    ppermute x30, waiting for transfers between devices, send(): return lax.ppermute(array, AXES, pairs)  98.6 us
    ppermute x30, starting transfers between devices, send(): return lax.ppermute(array, AXES, pairs)  46.2 us
    pallas_call x2, Pallas kernels, product(): pl.pallas_call(lambda *refs: product_kernel(pieces, len(acts), *refs), gr...  16.7 us
    all_gather x1, waiting for transfers between devices, shards(): whole = lax.all_gather(both[:, :, :size], ('tc', 'tr'), axis=0)  6.89 us
  transfers between devices with their start and end apart: 31, of which 15 were waited for; matrix products, arithmetic and copies ran while one was open for 2% of the time, Pallas kernels for 8%

profile of v4, /device:TPU:6, one launch (start us, length us, event | category | flops | bytes accessed | tf_op | source)
XLA Modules:
  0.0 197.9 jit_solution(14636192225708482677)
XLA Ops:
  7.2 0.0 copy-start
  7.2 0.0 all-gather.3.cloned.1.call-start
  7.3 2.8 %constant_dynamic-slice_fusion = (bf16[512,1024]{1,0:T(8,128)(2,1)S(1)}, bf16[512,1024]{1,0:T(8,128)(2,1)}) fusion(bf16[512,2048]{1,0:T(8,128)(2,1)} %param.6, s32[]{:T(128)S(6)} %select_n.277, s32[]{:T(128)S(6)} %select_n.276), kind=kLoop, calls=%fused_computation.153 | loop fusion | bytes 4194312 | tf_op jit(solution)/shard_map/dynamic_slice | solution.py:181
  10.1 0.1 fusion.39
  10.1 2.0 %fusion.2 = bf16[256,1536]{1,0:T(8,128)(2,1)S(1)} fusion(bf16[256,1536]{1,0:T(8,128)(2,1)S(1)} %copy-done, s32[1536]{0:T(1024)S(1)} %fusion.39), kind=kOutput, calls=%fused_computation.3 | convolution fusion | flops 1210712064 | bytes 1579008 | tf_op jit(solution)/shard_map/dot_general | solution.py:69
  12.2 0.1 slice_bitcast_fusion.2
  12.2 0.1 collective-permute-start
  12.3 1.7 collective-permute-done
  14.1 0.8 pad_maximum_fusion
  14.9 0.0 all-gather.3.cloned.1.call-update
  14.9 2.0 %collective-permute-start.1 = (bf16[512,1024]{1,0:T(8,128)(2,1)}, bf16[512,1024]{1,0:T(8,128)(2,1)S(1)}, u32[]{:S(2)}, u32[]{:S(2)}) collective-permute-start(bf16[512,1024]{1,0:T(8,128)(2,1)} %get-tuple-element.29), channel_id=1, source_target_pairs={{0,4},{1,5},{2,6},{3,7},{4,0},{5,1},{6,2},{7,3},{8,12},{9,13},{10,... | collective-permute-start | bytes 3145736 | tf_op jit(solution)/shard_map/ppermute | solution.py:43
  17.0 34.4 %collective-permute-done.1.refs_2_.refs_10_ = bf16[512,1024]{1,0:T(8,128)(2,1)S(1)} collective-permute-done((bf16[512,1024]{1,0:T(8,128)(2,1)}, bf16[512,1024]{1,0:T(8,128)(2,1)S(1)}, u32[]{:S(2)}, u32[]{:S(2)}) %collective-permute-start.1) | collective-permute-done | bytes 1048608 | tf_op jit(solution)/shard_map/ppermute | solution.py:43
  51.4 2.4 %collective-permute-start.2 = (bf16[2,256,256]{2,1,0:T(8,128)(2,1)S(1)}, bf16[2,256,256]{2,1,0:T(8,128)(2,1)S(1)}, u32[]{:S(2)}, u32[]{:S(2)}) collective-permute-start(bf16[2,256,256]{2,1,0:T(8,128)(2,1)S(1)} %pad_maximum_fusion.2.refs_0_), channel_id=1, source_target_pairs={{0,4},{1,5},{2,6},{3,7},{4,1},{5,2},{6,3},{7,0},{8,12},{9,13},{10,... | collective-permute-start | bytes 786440 | tf_op jit(solution)/shard_map/ppermute | solution.py:43
  53.8 5.3 %collective-permute-start.5 = (bf16[2,256,256]{2,1,0:T(8,128)(2,1)S(1)}, bf16[2,256,256]{2,1,0:T(8,128)(2,1)S(1)}, u32[]{:S(2)}, u32[]{:S(2)}) collective-permute-start(bf16[2,256,256]{2,1,0:T(8,128)(2,1)S(1)} %pad_maximum_fusion.2.refs_0_), channel_id=1, source_target_pairs={{0,7},{1,4},{2,5},{3,6},{4,0},{5,1},{6,2},{7,3},{8,15},{9,12},{10,... | collective-permute-start | bytes 786440 | tf_op jit(solution)/shard_map/ppermute | solution.py:43
  59.1 12.3 %collective-permute-done.2.refs_1_ = bf16[2,256,256]{2,1,0:T(8,128)(2,1)S(1)} collective-permute-done((bf16[2,256,256]{2,1,0:T(8,128)(2,1)S(1)}, bf16[2,256,256]{2,1,0:T(8,128)(2,1)S(1)}, u32[]{:S(2)}, u32[]{:S(2)}) %collective-permute-start.2) | collective-permute-done | bytes 262176 | tf_op jit(solution)/shard_map/ppermute | solution.py:43
  71.4 0.0 copy-start.18
  71.5 3.2 %collective-permute-start.6 = (bf16[2,256,256]{2,1,0:T(8,128)(2,1)S(1)}, bf16[2,256,256]{2,1,0:T(8,128)(2,1)}, u32[]{:S(2)}, u32[]{:S(2)}) collective-permute-start(bf16[2,256,256]{2,1,0:T(8,128)(2,1)S(1)} %collective-permute-done.5.refs_2_), channel_id=1, source_target_pairs={{0,7},{1,4},{2,5},{3,6},{4,0},{5,1},{6,2},{7,3},{8,15},{9,12},{10,... | collective-permute-start | bytes 786440 | tf_op jit(solution)/shard_map/ppermute | solution.py:43
  74.7 12.5 %collective-permute-done.3.refs_3_ = bf16[2,256,256]{2,1,0:T(8,128)(2,1)} collective-permute-done((bf16[2,256,256]{2,1,0:T(8,128)(2,1)S(1)}, bf16[2,256,256]{2,1,0:T(8,128)(2,1)}, u32[]{:S(2)}, u32[]{:S(2)}) %collective-permute-start.3) | collective-permute-done | bytes 262176 | tf_op jit(solution)/shard_map/ppermute | solution.py:43
  87.2 3.2 %collective-permute-start.7 = (bf16[2,256,256]{2,1,0:T(8,128)(2,1)}, bf16[2,256,256]{2,1,0:T(8,128)(2,1)S(1)}, u32[]{:S(2)}, u32[]{:S(2)}) collective-permute-start(bf16[2,256,256]{2,1,0:T(8,128)(2,1)} %collective-permute-done.6.refs_4_), channel_id=1, source_target_pairs={{0,7},{1,4},{2,5},{3,6},{4,0},{5,1},{6,2},{7,3},{8,15},{9,12},{10,... | collective-permute-start | bytes 786440 | tf_op jit(solution)/shard_map/ppermute | solution.py:43
  90.4 1.0 copy-done.15
  91.4 6.9 %all-gather.3.cloned.1.call-done = bf16[16,256,512]{2,1,0:T(8,128)(2,1)} async-done(((bf16[2,256,512]{2,1,0:T(8,128)(2,1)}), bf16[16,256,512]{2,1,0:T(8,128)(2,1)}) %all-gather.3.cloned.1.call-update) | async-done | bytes 4194320 | tf_op jit(solution)/shard_map/all_gather | solution.py:190
  98.3 10.0 %shard_map.76 = (f32[2,2,2,32,1024]{4,3,2,1,0:T(8,128)}, f32[2,2,2,32,1024]{4,3,2,1,0:T(8,128)}, f32[2,2,32,1024]{3,2,1,0:T(8,128)}, f32[2,2,32,1024]{3,2,1,0:T(8,128)}, f32[4,2,32,1024]{3,2,1,0:T(8,128)}) custom-call(bf16[4,2,2,256,512]{4,3,2,1,0:T(8,128)(2,1)} %bitcast.160, bf16[512,1024]{1,0:T(8,128)(2,1)} %copy-done.4, bf16[512,1024]{1,0:T(8,128)(2,1)} %copy-done.14, ...), custom_call_target="tpu_custom_call" | custom-call | flops 4294967296 | bytes 12582912 | tf_op jit(solution)/shard_map/pallas_call | solution.py:127
  108.3 0.1 collective-permute-start.17
  108.4 5.1 %collective-permute-start.18 = (bf16[256,256]{1,0:T(8,128)(2,1)S(1)}, bf16[256,256]{1,0:T(8,128)(2,1)S(1)}, u32[]{:S(2)}, u32[]{:S(2)}) collective-permute-start(bf16[256,256]{1,0:T(8,128)(2,1)S(1)} %slice_bitcast_fusion.21), channel_id=1, source_target_pairs={{0,7},{1,4},{2,5},{3,6},{4,0},{5,1},{6,2},{7,3},{8,15},{9,12},{10,... | collective-permute-start | bytes 393224 | tf_op jit(solution)/shard_map/ppermute | solution.py:43
  113.5 0.5 collective-permute-start.11
  114.0 1.6 collective-permute-start.10
  115.5 1.4 collective-permute-done.17.refs_7_
  116.9 0.6 copy-done.19
  117.6 0.6 copy-done.20
  118.2 6.7 %shard_map.77 = (f32[2,2,2,16,1024]{4,3,2,1,0:T(8,128)}, f32[2,2,2,16,1024]{4,3,2,1,0:T(8,128)}, f32[2,2,16,1024]{3,2,1,0:T(8,128)}, f32[2,2,16,1024]{3,2,1,0:T(8,128)}, f32[4,2,16,1024]{3,2,1,0:T(8,128)}) custom-call(bf16[2,256,256]{2,1,0:T(8,128)(2,1)} %copy-done.11, bf16[2,256,256]{2,1,0:T(8,128)(2,1)} %copy-done.17, bf16[2,256,256]{2,1,0:T(8,128)(2,1)} %copy-done.18, ...), custom_call_target="tpu_custom_call" | custom-call | flops 2147483648 | bytes 12582912 | tf_op jit(solution)/shard_map/pallas_call | solution.py:127
  124.9 0.5 collective-permute-start.20
  125.5 1.6 collective-permute-start.19
  127.1 7.4 %collective-permute-done.20 = f32[2,2,2,16,1024]{4,3,2,1,0:T(8,128)S(1)} collective-permute-done((f32[2,2,2,16,1024]{4,3,2,1,0:T(8,128)}, f32[2,2,2,16,1024]{4,3,2,1,0:T(8,128)S(1)}, u32[]{:S(2)}, u32[]{:S(2)}) %collective-permute-start.20) | collective-permute-done | bytes 524320 | tf_op jit(solution)/shard_map/ppermute | solution.py:43
  134.4 1.0 fusion.6
  135.5 1.8 collective-permute-start.21
  137.2 0.1 fusion.4
  137.3 0.4 collective-permute-start.12
  137.7 0.1 fusion.3
  137.8 1.8 collective-permute-start.14
  139.6 0.4 collective-permute-start.23
  140.0 1.9 collective-permute-done.21
  141.9 9.1 %collective-permute-done.23 = f32[2,2,16,1024]{3,2,1,0:T(8,128)S(1)} collective-permute-done((f32[2,2,16,1024]{3,2,1,0:T(8,128)S(1)}, f32[2,2,16,1024]{3,2,1,0:T(8,128)S(1)}, u32[]{:S(2)}, u32[]{:S(2)}) %collective-permute-start.23) | collective-permute-done | bytes 262176 | tf_op jit(solution)/shard_map/ppermute | solution.py:43
  151.0 0.8 fusion.17
  151.8 1.6 collective-permute-start.22
  153.4 1.7 collective-permute-start.24
  155.0 1.9 collective-permute-start.25
  157.0 0.9 fusion.7
  157.9 0.6 collective-permute-start.13
  158.6 2.6 %collective-permute-start.15 = (f32[2,32,1024]{2,1,0:T(8,128)}, f32[2,32,1024]{2,1,0:T(8,128)}, u32[]{:S(2)}, u32[]{:S(2)}) collective-permute-start(f32[2,32,1024]{2,1,0:T(8,128)} %get-tuple-element.63), channel_id=1, source_target_pairs={{0,192},{1,193},{2,194},{3,195},{4,196},{5,197},{6,198},{7,199},{8... | collective-permute-start | bytes 786440 | tf_op jit(solution)/shard_map/ppermute | solution.py:43
  161.2 0.4 collective-permute-start.16
  161.6 0.3 collective-permute-done.25
  161.8 1.1 fusion.25
  163.0 2.8 %collective-permute-done.13 = f32[2,32,1024]{2,1,0:T(8,128)} collective-permute-done((f32[2,32,1024]{2,1,0:T(8,128)}, f32[2,32,1024]{2,1,0:T(8,128)}, u32[]{:S(2)}, u32[]{:S(2)}) %collective-permute-start.13) | collective-permute-done | bytes 262176 | tf_op jit(solution)/shard_map/ppermute | solution.py:43
  165.8 2.4 %collective-permute-done.15 = f32[2,32,1024]{2,1,0:T(8,128)} collective-permute-done((f32[2,32,1024]{2,1,0:T(8,128)}, f32[2,32,1024]{2,1,0:T(8,128)}, u32[]{:S(2)}, u32[]{:S(2)}) %collective-permute-start.15) | collective-permute-done | bytes 262176 | tf_op jit(solution)/shard_map/ppermute | solution.py:43
  168.2 1.1 collective-permute-done.16
  169.4 1.3 fusion.15
  170.7 0.1 copy.17
  170.8 0.1 collective-permute-start.26
  171.0 6.2 %collective-permute-done.26 = f32[4,12,8,128]{3,2,1,0:T(8,128)S(1)} collective-permute-done((f32[4,12,8,128]{3,2,1,0:T(8,128)S(1)}, f32[4,12,8,128]{3,2,1,0:T(8,128)S(1)}, u32[]{:S(2)}, u32[]{:S(2)}) %collective-permute-start.26) | collective-permute-done | bytes 196640 | tf_op jit(solution)/shard_map/ppermute | solution.py:43
  177.2 3.5 %collective-permute-start.27 = (f32[2,12,8,128]{3,2,1,0:T(8,128)S(1)}, f32[2,12,8,128]{3,2,1,0:T(8,128)S(1)}, u32[]{:S(2)}, u32[]{:S(2)}) collective-permute-start(f32[2,12,8,128]{3,2,1,0:T(8,128)S(1)} %get-tuple-element.74), channel_id=1, source_target_pairs={{0,1},{1,2},{2,3},{3,0},{4,5},{5,6},{6,7},{7,4},{8,9},{9,10},{10,1... | collective-permute-start | bytes 294920 | tf_op jit(solution)/shard_map/ppermute | solution.py:43
  180.7 3.0 %collective-permute-start.28 = (f32[2,12,8,128]{3,2,1,0:T(8,128)S(1)}, f32[2,12,8,128]{3,2,1,0:T(8,128)S(1)}, u32[]{:S(2)}, u32[]{:S(2)}) collective-permute-start(f32[2,12,8,128]{3,2,1,0:T(8,128)S(1)} %get-tuple-element.75), channel_id=1, source_target_pairs={{0,2},{1,3},{2,0},{3,1},{4,6},{5,7},{6,4},{7,5},{8,10},{9,11},{10,... | collective-permute-start | bytes 294920 | tf_op jit(solution)/shard_map/ppermute | solution.py:43
  183.7 1.0 collective-permute-start.29
  184.6 5.0 %collective-permute-done.28.piece_2 = f32[2,12,8,128]{3,2,1,0:T(8,128)S(1)} collective-permute-done((f32[2,12,8,128]{3,2,1,0:T(8,128)S(1)}, f32[2,12,8,128]{3,2,1,0:T(8,128)S(1)}, u32[]{:S(2)}, u32[]{:S(2)}) %collective-permute-start.28) | collective-permute-done | bytes 98336 | tf_op jit(solution)/shard_map/ppermute | solution.py:43
  189.7 1.4 shard_map.78
  (64 shorter events, 0.3 us)
Async XLA Ops:
  7.2 3.0 %copy-start = (bf16[256,1536]{1,0:T(8,128)(2,1)S(1)}, bf16[256,1536]{1,0:T(8,128)(2,1)}, u32[]{:S(2)}) copy-start(bf16[256,1536]{1,0:T(8,128)(2,1)} %param.5) | copy-start | bytes 2359300
  7.2 91.1 %all-gather.3.cloned.1.call-start = ((), (), s32[]{:S(2)}) async-start(), calls=%async_computation | async-start | bytes 4718592 | tf_op jit(solution)/shard_map/all_gather | solution.py:190
  10.1 6.9 %copy-start.4 = (bf16[512,1024]{1,0:T(8,128)(2,1)}, bf16[512,1024]{1,0:T(8,128)(2,1)S(1)}, u32[]{:S(2)}) copy-start(bf16[512,1024]{1,0:T(8,128)(2,1)S(1)} %get-tuple-element.31.refs_1_.refs_9_) | copy-start | bytes 3145732
  12.2 1.8 collective-permute-start
  14.9 36.5 %collective-permute-start.1 = (bf16[512,1024]{1,0:T(8,128)(2,1)}, bf16[512,1024]{1,0:T(8,128)(2,1)S(1)}, u32[]{:S(2)}, u32[]{:S(2)}) collective-permute-start(bf16[512,1024]{1,0:T(8,128)(2,1)} %get-tuple-element.29), channel_id=1, source_target_pairs={{0,4},{1,5},{2,6},{3,7},{4,0},{5,1},{6,2},{7,3},{8,12},{9,13},{10,... | collective-permute-start | bytes 3145736 | tf_op jit(solution)/shard_map/ppermute | solution.py:43
  16.9 73.5 %collective-permute-start.8 = (bf16[512,1024]{1,0:T(8,128)(2,1)S(1)}, bf16[512,1024]{1,0:T(8,128)(2,1)S(1)}, u32[]{:S(2)}, u32[]{:S(2)}) collective-permute-start(bf16[512,1024]{1,0:T(8,128)(2,1)S(1)} %get-tuple-element.31.refs_1_.refs_9_), channel_id=1, source_target_pairs={{0,8},{1,9},{2,10},{3,11},{4,12},{5,13},{6,14},{7,15},{8,0},{9,1},... | collective-permute-start | bytes 3145736 | tf_op jit(solution)/shard_map/ppermute | solution.py:43
  17.0 73.4 %copy-start.11 = (bf16[2,256,256]{2,1,0:T(8,128)(2,1)}, bf16[2,256,256]{2,1,0:T(8,128)(2,1)S(1)}, u32[]{:S(2)}) copy-start(bf16[2,256,256]{2,1,0:T(8,128)(2,1)S(1)} %pad_maximum_fusion.2.refs_0_) | copy-start | bytes 786436
  51.4 39.0 %copy-start.14 = (bf16[512,1024]{1,0:T(8,128)(2,1)}, bf16[512,1024]{1,0:T(8,128)(2,1)S(1)}, u32[]{:S(2)}) copy-start(bf16[512,1024]{1,0:T(8,128)(2,1)S(1)} %collective-permute-done.1.refs_2_.refs_10_) | copy-start | bytes 3145732
  51.4 40.0 %collective-permute-start.9 = (bf16[512,1024]{1,0:T(8,128)(2,1)S(1)}, bf16[512,1024]{1,0:T(8,128)(2,1)S(1)}, u32[]{:S(2)}, u32[]{:S(2)}) collective-permute-start(bf16[512,1024]{1,0:T(8,128)(2,1)S(1)} %collective-permute-done.1.refs_2_.refs_10_), channel_id=1, source_target_pairs={{0,8},{1,9},{2,10},{3,11},{4,12},{5,13},{6,14},{7,15},{8,0},{9,1},... | collective-permute-start | bytes 3145736 | tf_op jit(solution)/shard_map/ppermute | solution.py:43
  51.4 20.0 %collective-permute-start.2 = (bf16[2,256,256]{2,1,0:T(8,128)(2,1)S(1)}, bf16[2,256,256]{2,1,0:T(8,128)(2,1)S(1)}, u32[]{:S(2)}, u32[]{:S(2)}) collective-permute-start(bf16[2,256,256]{2,1,0:T(8,128)(2,1)S(1)} %pad_maximum_fusion.2.refs_0_), channel_id=1, source_target_pairs={{0,4},{1,5},{2,6},{3,7},{4,1},{5,2},{6,3},{7,0},{8,12},{9,13},{10,... | collective-permute-start | bytes 786440 | tf_op jit(solution)/shard_map/ppermute | solution.py:43
  53.8 17.6 %collective-permute-start.5 = (bf16[2,256,256]{2,1,0:T(8,128)(2,1)S(1)}, bf16[2,256,256]{2,1,0:T(8,128)(2,1)S(1)}, u32[]{:S(2)}, u32[]{:S(2)}) collective-permute-start(bf16[2,256,256]{2,1,0:T(8,128)(2,1)S(1)} %pad_maximum_fusion.2.refs_0_), channel_id=1, source_target_pairs={{0,7},{1,4},{2,5},{3,6},{4,0},{5,1},{6,2},{7,3},{8,15},{9,12},{10,... | collective-permute-start | bytes 786440 | tf_op jit(solution)/shard_map/ppermute | solution.py:43
  71.4 3.2 %copy-start.17 = (bf16[2,256,256]{2,1,0:T(8,128)(2,1)}, bf16[2,256,256]{2,1,0:T(8,128)(2,1)S(1)}, u32[]{:S(2)}) copy-start(bf16[2,256,256]{2,1,0:T(8,128)(2,1)S(1)} %collective-permute-done.2.refs_1_) | copy-start | bytes 786436
  71.4 15.7 %collective-permute-start.3 = (bf16[2,256,256]{2,1,0:T(8,128)(2,1)S(1)}, bf16[2,256,256]{2,1,0:T(8,128)(2,1)}, u32[]{:S(2)}, u32[]{:S(2)}) collective-permute-start(bf16[2,256,256]{2,1,0:T(8,128)(2,1)S(1)} %collective-permute-done.2.refs_1_), channel_id=1, source_target_pairs={{0,4},{1,5},{2,6},{3,7},{4,1},{5,2},{6,3},{7,0},{8,12},{9,13},{10,... | collective-permute-start | bytes 786440 | tf_op jit(solution)/shard_map/ppermute | solution.py:43
  71.4 15.7 %copy-start.18 = (bf16[2,256,256]{2,1,0:T(8,128)(2,1)}, bf16[2,256,256]{2,1,0:T(8,128)(2,1)S(1)}, u32[]{:S(2)}) copy-start(bf16[2,256,256]{2,1,0:T(8,128)(2,1)S(1)} %collective-permute-done.5.refs_2_) | copy-start | bytes 786436
  71.5 15.7 %collective-permute-start.6 = (bf16[2,256,256]{2,1,0:T(8,128)(2,1)S(1)}, bf16[2,256,256]{2,1,0:T(8,128)(2,1)}, u32[]{:S(2)}, u32[]{:S(2)}) collective-permute-start(bf16[2,256,256]{2,1,0:T(8,128)(2,1)S(1)} %collective-permute-done.5.refs_2_), channel_id=1, source_target_pairs={{0,7},{1,4},{2,5},{3,6},{4,0},{5,1},{6,2},{7,3},{8,15},{9,12},{10,... | collective-permute-start | bytes 786440 | tf_op jit(solution)/shard_map/ppermute | solution.py:43
  87.1 21.1 %collective-permute-start.4 = (bf16[2,256,256]{2,1,0:T(8,128)(2,1)}, bf16[2,256,256]{2,1,0:T(8,128)(2,1)S(1)}, u32[]{:S(2)}, u32[]{:S(2)}) collective-permute-start(bf16[2,256,256]{2,1,0:T(8,128)(2,1)} %collective-permute-done.3.refs_3_), channel_id=1, source_target_pairs={{0,4},{1,5},{2,6},{3,7},{4,1},{5,2},{6,3},{7,0},{8,12},{9,13},{10,... | collective-permute-start | bytes 786440 | tf_op jit(solution)/shard_map/ppermute | solution.py:43
  87.2 21.1 %collective-permute-start.7 = (bf16[2,256,256]{2,1,0:T(8,128)(2,1)}, bf16[2,256,256]{2,1,0:T(8,128)(2,1)S(1)}, u32[]{:S(2)}, u32[]{:S(2)}) collective-permute-start(bf16[2,256,256]{2,1,0:T(8,128)(2,1)} %collective-permute-done.6.refs_4_), channel_id=1, source_target_pairs={{0,7},{1,4},{2,5},{3,6},{4,0},{5,1},{6,2},{7,3},{8,15},{9,12},{10,... | collective-permute-start | bytes 786440 | tf_op jit(solution)/shard_map/ppermute | solution.py:43
  90.4 1.0 copy-start.15
  91.4 6.9 %copy-start.16 = (bf16[512,1024]{1,0:T(8,128)(2,1)}, bf16[512,1024]{1,0:T(8,128)(2,1)S(1)}, u32[]{:S(2)}) copy-start(bf16[512,1024]{1,0:T(8,128)(2,1)S(1)} %collective-permute-done.9.refs_4_.refs_12_) | copy-start | bytes 3145732
  108.3 5.2 %copy-start.12 = (bf16[2,256,256]{2,1,0:T(8,128)(2,1)}, bf16[2,256,256]{2,1,0:T(8,128)(2,1)S(1)}, u32[]{:S(2)}) copy-start(bf16[2,256,256]{2,1,0:T(8,128)(2,1)S(1)} %collective-permute-done.4.refs_5_) | copy-start | bytes 786436
  108.3 5.2 %copy-start.13 = (bf16[2,256,256]{2,1,0:T(8,128)(2,1)}, bf16[2,256,256]{2,1,0:T(8,128)(2,1)S(1)}, u32[]{:S(2)}) copy-start(bf16[2,256,256]{2,1,0:T(8,128)(2,1)S(1)} %collective-permute-done.7.refs_6_) | copy-start | bytes 786436
  108.3 8.6 %collective-permute-start.17 = (bf16[256,256]{1,0:T(8,128)(2,1)S(1)}, bf16[256,256]{1,0:T(8,128)(2,1)S(1)}, u32[]{:S(2)}, u32[]{:S(2)}) collective-permute-start(bf16[256,256]{1,0:T(8,128)(2,1)S(1)} %slice_bitcast_fusion.22), channel_id=1, source_target_pairs={{0,4},{1,5},{2,6},{3,7},{4,1},{5,2},{6,3},{7,0},{8,12},{9,13},{10,... | collective-permute-start | bytes 393224 | tf_op jit(solution)/shard_map/ppermute | solution.py:43
  108.4 28.8 %copy-start.7 = (f32[2,2,32,1024]{3,2,1,0:T(8,128)S(1)}, f32[2,2,32,1024]{3,2,1,0:T(8,128)}, u32[]{:S(2)}) copy-start(f32[2,2,32,1024]{3,2,1,0:T(8,128)} %get-tuple-element.40) | copy-start | bytes 1572868
  108.4 8.5 %collective-permute-start.18 = (bf16[256,256]{1,0:T(8,128)(2,1)S(1)}, bf16[256,256]{1,0:T(8,128)(2,1)S(1)}, u32[]{:S(2)}, u32[]{:S(2)}) collective-permute-start(bf16[256,256]{1,0:T(8,128)(2,1)S(1)} %slice_bitcast_fusion.21), channel_id=1, source_target_pairs={{0,7},{1,4},{2,5},{3,6},{4,0},{5,1},{6,2},{7,3},{8,15},{9,12},{10,... | collective-permute-start | bytes 393224 | tf_op jit(solution)/shard_map/ppermute | solution.py:43
  113.5 23.7 %collective-permute-start.11 = (f32[2,2,2,32,1024]{4,3,2,1,0:T(8,128)}, f32[2,2,2,32,1024]{4,3,2,1,0:T(8,128)S(1)}, u32[]{:S(2)}, u32[]{:S(2)}) collective-permute-start(f32[2,2,2,32,1024]{4,3,2,1,0:T(8,128)} %get-tuple-element.41), channel_id=1, source_target_pairs={{0,16},{1,17},{2,18},{3,19},{4,20},{5,21},{6,22},{7,23},{8,72},{9,... | collective-permute-start | bytes 3145736 | tf_op jit(solution)/shard_map/ppermute | solution.py:43
  114.0 23.7 %collective-permute-start.10 = (f32[2,2,2,32,1024]{4,3,2,1,0:T(8,128)}, f32[2,2,2,32,1024]{4,3,2,1,0:T(8,128)S(1)}, u32[]{:S(2)}, u32[]{:S(2)}) collective-permute-start(f32[2,2,2,32,1024]{4,3,2,1,0:T(8,128)} %get-tuple-element.39), channel_id=1, source_target_pairs={{0,48},{1,49},{2,50},{3,51},{4,52},{5,53},{6,54},{7,55},{8,200},{9... | collective-permute-start | bytes 3145736 | tf_op jit(solution)/shard_map/ppermute | solution.py:43
  116.9 0.6 copy-start.19
  117.6 0.6 copy-start.20
  124.9 12.7 %copy-start.6 = (f32[2,2,32,1024]{3,2,1,0:T(8,128)S(1)}, f32[2,2,32,1024]{3,2,1,0:T(8,128)}, u32[]{:S(2)}) copy-start(f32[2,2,32,1024]{3,2,1,0:T(8,128)} %get-tuple-element.42) | copy-start | bytes 1572868
  124.9 14.6 %copy-start.10 = (f32[2,2,16,1024]{3,2,1,0:T(8,128)S(1)}, f32[2,2,16,1024]{3,2,1,0:T(8,128)}, u32[]{:S(2)}) copy-start(f32[2,2,16,1024]{3,2,1,0:T(8,128)} %get-tuple-element.49) | copy-start | bytes 786436
  124.9 9.5 %collective-permute-start.20 = (f32[2,2,2,16,1024]{4,3,2,1,0:T(8,128)}, f32[2,2,2,16,1024]{4,3,2,1,0:T(8,128)S(1)}, u32[]{:S(2)}, u32[]{:S(2)}) collective-permute-start(f32[2,2,2,16,1024]{4,3,2,1,0:T(8,128)} %get-tuple-element.48), channel_id=1, source_target_pairs={{0,16},{1,17},{2,18},{3,19},{4,20},{5,21},{6,22},{7,23},{8,72},{9,... | collective-permute-start | bytes 1572872 | tf_op jit(solution)/shard_map/ppermute | solution.py:43
  125.5 14.1 %collective-permute-start.19 = (f32[2,2,2,16,1024]{4,3,2,1,0:T(8,128)}, f32[2,2,2,16,1024]{4,3,2,1,0:T(8,128)S(1)}, u32[]{:S(2)}, u32[]{:S(2)}) collective-permute-start(f32[2,2,2,16,1024]{4,3,2,1,0:T(8,128)} %get-tuple-element.46), channel_id=1, source_target_pairs={{0,48},{1,49},{2,50},{3,51},{4,52},{5,53},{6,54},{7,55},{8,200},{9... | collective-permute-start | bytes 1572872 | tf_op jit(solution)/shard_map/ppermute | solution.py:43
  134.4 16.6 %copy-start.8 = (f32[4,2,16,1024]{3,2,1,0:T(8,128)S(1)}, f32[4,2,16,1024]{3,2,1,0:T(8,128)}, u32[]{:S(2)}) copy-start(f32[4,2,16,1024]{3,2,1,0:T(8,128)} %get-tuple-element.45) | copy-start | bytes 1572868
  135.5 6.4 %collective-permute-start.21 = (f32[2,2,16,1024]{3,2,1,0:T(8,128)S(1)}, f32[2,2,16,1024]{3,2,1,0:T(8,128)S(1)}, u32[]{:S(2)}, u32[]{:S(2)}) collective-permute-start(f32[2,2,16,1024]{3,2,1,0:T(8,128)S(1)} %fusion.6), channel_id=1, source_target_pairs={{0,16},{1,17},{2,18},{3,19},{4,20},{5,21},{6,22},{7,23},{8,72},{9,... | collective-permute-start | bytes 786440 | tf_op jit(solution)/shard_map/ppermute | solution.py:43
  137.3 19.7 %copy-start.5 = (f32[4,2,32,1024]{3,2,1,0:T(8,128)S(1)}, f32[4,2,32,1024]{3,2,1,0:T(8,128)}, u32[]{:S(2)}) copy-start(f32[4,2,32,1024]{3,2,1,0:T(8,128)} %get-tuple-element.38) | copy-start | bytes 3145732
  137.3 19.7 %collective-permute-start.12 = (f32[2,2,32,1024]{3,2,1,0:T(8,128)S(1)}, f32[2,2,32,1024]{3,2,1,0:T(8,128)S(1)}, u32[]{:S(2)}, u32[]{:S(2)}) collective-permute-start(f32[2,2,32,1024]{3,2,1,0:T(8,128)S(1)} %fusion.4), channel_id=1, source_target_pairs={{0,16},{1,17},{2,18},{3,19},{4,20},{5,21},{6,22},{7,23},{8,72},{9,... | collective-permute-start | bytes 1572872 | tf_op jit(solution)/shard_map/ppermute | solution.py:43
  137.8 19.2 %collective-permute-start.14 = (f32[2,2,32,1024]{3,2,1,0:T(8,128)S(1)}, f32[2,2,32,1024]{3,2,1,0:T(8,128)S(1)}, u32[]{:S(2)}, u32[]{:S(2)}) collective-permute-start(f32[2,2,32,1024]{3,2,1,0:T(8,128)S(1)} %fusion.3), channel_id=1, source_target_pairs={{0,48},{1,49},{2,50},{3,51},{4,52},{5,53},{6,54},{7,55},{8,200},{9... | collective-permute-start | bytes 1572872 | tf_op jit(solution)/shard_map/ppermute | solution.py:43
  139.6 11.4 %collective-permute-start.23 = (f32[2,2,16,1024]{3,2,1,0:T(8,128)S(1)}, f32[2,2,16,1024]{3,2,1,0:T(8,128)S(1)}, u32[]{:S(2)}, u32[]{:S(2)}) collective-permute-start(f32[2,2,16,1024]{3,2,1,0:T(8,128)S(1)} %fusion.5), channel_id=1, source_target_pairs={{0,48},{1,49},{2,50},{3,51},{4,52},{5,53},{6,54},{7,55},{8,200},{9... | collective-permute-start | bytes 786440 | tf_op jit(solution)/shard_map/ppermute | solution.py:43
  141.9 15.1 %copy-start.9 = (f32[2,2,16,1024]{3,2,1,0:T(8,128)}, f32[2,2,16,1024]{3,2,1,0:T(8,128)S(1)}, u32[]{:S(2)}) copy-start(f32[2,2,16,1024]{3,2,1,0:T(8,128)S(1)} %collective-permute-done.21) | copy-start | bytes 786436
  151.8 9.4 %collective-permute-start.22 = (f32[2,16,1024]{2,1,0:T(8,128)S(1)}, f32[2,16,1024]{2,1,0:T(8,128)S(1)}, u32[]{:S(2)}, u32[]{:S(2)}) collective-permute-start(f32[2,16,1024]{2,1,0:T(8,128)S(1)} %get-tuple-element.71), channel_id=1, source_target_pairs={{0,64},{1,65},{2,66},{3,67},{4,68},{5,69},{6,70},{7,71},{8,24},{9,... | collective-permute-start | bytes 393224 | tf_op jit(solution)/shard_map/ppermute | solution.py:43
  153.4 8.2 %collective-permute-start.24 = (f32[2,16,1024]{2,1,0:T(8,128)}, f32[2,16,1024]{2,1,0:T(8,128)}, u32[]{:S(2)}, u32[]{:S(2)}) collective-permute-start(f32[2,16,1024]{2,1,0:T(8,128)} %get-tuple-element.67), channel_id=1, source_target_pairs={{0,192},{1,193},{2,194},{3,195},{4,196},{5,197},{6,198},{7,199},{8... | collective-permute-start | bytes 393224 | tf_op jit(solution)/shard_map/ppermute | solution.py:43
  155.0 6.8 %collective-permute-start.25 = (f32[2,16,1024]{2,1,0:T(8,128)}, f32[2,16,1024]{2,1,0:T(8,128)}, u32[]{:S(2)}, u32[]{:S(2)}) collective-permute-start(f32[2,16,1024]{2,1,0:T(8,128)} %get-tuple-element.66), channel_id=1, source_target_pairs={{0,128},{1,129},{2,130},{3,131},{4,132},{5,133},{6,134},{7,135},{8... | collective-permute-start | bytes 393224 | tf_op jit(solution)/shard_map/ppermute | solution.py:43
  157.9 7.9 %collective-permute-start.13 = (f32[2,32,1024]{2,1,0:T(8,128)}, f32[2,32,1024]{2,1,0:T(8,128)}, u32[]{:S(2)}, u32[]{:S(2)}) collective-permute-start(f32[2,32,1024]{2,1,0:T(8,128)} %get-tuple-element.68), channel_id=1, source_target_pairs={{0,64},{1,65},{2,66},{3,67},{4,68},{5,69},{6,70},{7,71},{8,24},{9,... | collective-permute-start | bytes 786440 | tf_op jit(solution)/shard_map/ppermute | solution.py:43
  158.6 9.7 %collective-permute-start.15 = (f32[2,32,1024]{2,1,0:T(8,128)}, f32[2,32,1024]{2,1,0:T(8,128)}, u32[]{:S(2)}, u32[]{:S(2)}) collective-permute-start(f32[2,32,1024]{2,1,0:T(8,128)} %get-tuple-element.63), channel_id=1, source_target_pairs={{0,192},{1,193},{2,194},{3,195},{4,196},{5,197},{6,198},{7,199},{8... | collective-permute-start | bytes 786440 | tf_op jit(solution)/shard_map/ppermute | solution.py:43
  161.2 8.2 %collective-permute-start.16 = (f32[2,32,1024]{2,1,0:T(8,128)}, f32[2,32,1024]{2,1,0:T(8,128)}, u32[]{:S(2)}, u32[]{:S(2)}) collective-permute-start(f32[2,32,1024]{2,1,0:T(8,128)} %get-tuple-element.62), channel_id=1, source_target_pairs={{0,128},{1,129},{2,130},{3,131},{4,132},{5,133},{6,134},{7,135},{8... | collective-permute-start | bytes 786440 | tf_op jit(solution)/shard_map/ppermute | solution.py:43
  163.0 26.7 %copy-start.1 = (f32[1,12,8192]{2,0,1:T(1,128)S(1)}, f32[1,12,8192]{2,0,1:T(1,128)}, u32[]{:S(2)}) copy-start(f32[1,12,8192]{2,0,1:T(1,128)} %param.7) | copy-start | bytes 1179652
  163.0 26.7 %copy-start.2 = (f32[1,12,8192]{2,0,1:T(1,128)S(1)}, f32[1,12,8192]{2,0,1:T(1,128)}, u32[]{:S(2)}) copy-start(f32[1,12,8192]{2,0,1:T(1,128)} %param.8) | copy-start | bytes 1179652
  163.0 26.7 %copy-start.3 = (f32[1,12,8192]{2,0,1:T(1,128)S(1)}, f32[1,12,8192]{2,0,1:T(1,128)}, u32[]{:S(2)}) copy-start(f32[1,12,8192]{2,0,1:T(1,128)} %param.9) | copy-start | bytes 1179652
  170.8 6.3 %collective-permute-start.26 = (f32[4,12,8,128]{3,2,1,0:T(8,128)S(1)}, f32[4,12,8,128]{3,2,1,0:T(8,128)S(1)}, u32[]{:S(2)}, u32[]{:S(2)}) collective-permute-start(f32[4,12,8,128]{3,2,1,0:T(8,128)S(1)} %get-tuple-element.76), channel_id=1, source_target_pairs={{0,4},{1,5},{2,6},{3,7},{4,0},{5,1},{6,2},{7,3},{8,12},{9,13},{10,... | collective-permute-start | bytes 589832 | tf_op jit(solution)/shard_map/ppermute | solution.py:43
  177.2 7.5 %collective-permute-start.27 = (f32[2,12,8,128]{3,2,1,0:T(8,128)S(1)}, f32[2,12,8,128]{3,2,1,0:T(8,128)S(1)}, u32[]{:S(2)}, u32[]{:S(2)}) collective-permute-start(f32[2,12,8,128]{3,2,1,0:T(8,128)S(1)} %get-tuple-element.74), channel_id=1, source_target_pairs={{0,1},{1,2},{2,3},{3,0},{4,5},{5,6},{6,7},{7,4},{8,9},{9,10},{10,1... | collective-permute-start | bytes 294920 | tf_op jit(solution)/shard_map/ppermute | solution.py:43
  180.7 9.0 %collective-permute-start.28 = (f32[2,12,8,128]{3,2,1,0:T(8,128)S(1)}, f32[2,12,8,128]{3,2,1,0:T(8,128)S(1)}, u32[]{:S(2)}, u32[]{:S(2)}) collective-permute-start(f32[2,12,8,128]{3,2,1,0:T(8,128)S(1)} %get-tuple-element.75), channel_id=1, source_target_pairs={{0,2},{1,3},{2,0},{3,1},{4,6},{5,7},{6,4},{7,5},{8,10},{9,11},{10,... | collective-permute-start | bytes 294920 | tf_op jit(solution)/shard_map/ppermute | solution.py:43
  183.7 6.0 %collective-permute-start.29 = (f32[2,12,8,128]{3,2,1,0:T(8,128)S(1)}, f32[2,12,8,128]{3,2,1,0:T(8,128)S(1)}, u32[]{:S(2)}, u32[]{:S(2)}) collective-permute-start(f32[2,12,8,128]{3,2,1,0:T(8,128)S(1)} %get-tuple-element.72), channel_id=1, source_target_pairs={{0,3},{1,0},{2,1},{3,2},{4,7},{5,4},{6,5},{7,6},{8,11},{9,8},{10,9... | collective-permute-start | bytes 294920 | tf_op jit(solution)/shard_map/ppermute | solution.py:43
Sparse Core Ops, SparseCore 0:
  15.0 83.1 all-gather.2

commit v5 on v4

--- a/solution.py
+++ b/solution.py
@@ -16,7 +16,7 @@
 AXES = ("dp", "tr", "tc")
 SIDE = 4
 ROWS = 48
-CHUNKS = (32, 16)
+CHUNKS = (24, 24)
 
 
 def moves(where):
@@ -66,45 +66,59 @@
         start += rows
     feature = lax.broadcasted_iota(jnp.int32, (activations.shape[1], column.shape[1]), 0)
     chosen = (feature == source).astype(activations.dtype)
-    return jnp.dot(activations, chosen, preferred_element_type=jnp.float32).astype(activations.dtype)
-
-
-def product_kernel(pieces, count, *refs):
+    ordered = lax.dot_general(chosen, activations, (((0,), (1,)), ((), ())), preferred_element_type=jnp.float32)
+    return ordered.astype(activations.dtype)
+
+
+def product_kernel(pieces, *refs):
+    count = len(pieces)
     acts, cots = refs[:count], refs[count : count + 4]
     plus, minus, add_plus, add_minus, mine = refs[count + 4 : count + 9]
     act, cot, act_sem, cot_sem = refs[count + 9 :]
     tr, tc = lax.axis_index("tr"), lax.axis_index("tc")
-    features = act.shape[-1]
+    features = act.shape[1]
+    tokens = act.shape[2] // 8
     i = pl.program_id(0)
+
+    def place(n, ref, z, replica):
+        start = pl.multiple_of(replica * 4 * tokens + z // 2 * tokens, tokens)
+        return pltpu.make_async_copy(ref, act.at[z % 2, :, pl.ds(start, tokens)], act_sem.at[n])
+
+    def copies_of(replica):
+        copies = []
+        for piece, ref in zip(pieces, acts):
+            for n in range(8 if piece is None else 1):
+                if piece is not None and piece[1] not in (None, replica):
+                    continue
+                if piece is None:
+                    source, z = ref.at[n, replica], n
+                else:
+                    source = ref.at[replica] if piece[1] is None else ref
+                    z = (2 * tc + tr + 8 + piece[0]) % 8
+                copies.append(place(8 * replica + len(copies), source, z, replica))
+        for came in range(2):
+            half = 1 - tr if came else tr
+            start = pl.multiple_of(replica * 4 * tokens + half * 2 * tokens, 2 * tokens)
+            n = 2 * replica + came
+            copies.append(pltpu.make_async_copy(cots[n], cot.at[pl.ds(start, 2 * tokens)], cot_sem.at[n]))
+        return copies
 
     @pl.when(i == 0)
     def fetch():
-        copies = []
-        for n, (piece, ref) in enumerate(zip(pieces, acts)):
-            if piece is None:
-                target = act
-            else:
-                z = (2 * tc + tr + 8 + piece[0]) % 8
-                target = act.at[z // 2, z % 2]
-                if piece[1] is not None:
-                    target = target.at[piece[1]]
-            copies.append(pltpu.make_async_copy(ref, target, act_sem.at[n]))
-        late = [pltpu.make_async_copy(ref, cot.at[n], cot_sem.at[n]) for n, ref in enumerate(cots)]
-        for copy in copies + late:
+        for copy in copies_of(0) + copies_of(1):
             copy.start()
-        for copy in copies:
-            copy.wait()
-
-    def part(half, replica, n):
+
+    def part(replica):
         @pl.when(i == 0)
         def arrived():
-            pltpu.make_async_copy(cots[n], cot.at[n], cot_sem.at[n]).wait()
-
-        rows = act[pl.ds(2 * half, 2), i, replica].reshape(cot.shape[1], features)
-        return lax.dot_general(rows, cot[n], (((0,), (0,)), ((), ())), preferred_element_type=jnp.float32)
-
-    total = part(tr, 0, 0) + part(1 - tr, 0, 1)
-    total = total + (part(tr, 1, 2) + part(1 - tr, 1, 3))
+            for copy in copies_of(replica):
+                copy.wait()
+
+        depth = slice(replica * 4 * tokens, (replica + 1) * 4 * tokens)
+        return jnp.dot(act[i, :, depth], cot[depth], preferred_element_type=jnp.float32)
+
+    total = part(0)
+    total = total + part(1)
     total = total.reshape(SIDE, SIDE, 1, features // SIDE**2, total.shape[-1])
     plus[0] = total[2, :2]
     plus[1] = total[1, 2:]
@@ -116,7 +130,7 @@
 
 
 def product(acts, pieces, cots):
-    tokens, features = acts[0].shape[-2:]
+    features, tokens = acts[0].shape[-2:]
     units = cots[0].shape[1]
     rows = features // SIDE**2
     pack = pl.BlockSpec((2, 2, 1, rows, units), lambda i: (0, 0, i, 0, 0))
@@ -125,20 +139,20 @@
     packed = jax.ShapeDtypeStruct((2, 2, 2, rows, units), jnp.float32)
     parted = jax.ShapeDtypeStruct((2, 2, rows, units), jnp.float32)
     return pl.pallas_call(
-        lambda *refs: product_kernel(pieces, len(acts), *refs),
+        lambda *refs: product_kernel(pieces, *refs),
         grid=(2,),
         in_specs=[pl.BlockSpec(memory_space=pl.ANY)] * (len(acts) + 4),
         out_specs=[pack, pack, part, part, full],
         out_shape=[packed, packed, parted, parted, jax.ShapeDtypeStruct((SIDE, 2, rows, units), jnp.float32)],
         scratch_shapes=[
-            pltpu.VMEM((4, 2, 2, tokens, features), acts[0].dtype),
-            pltpu.VMEM((4,) + cots[0].shape, cots[0].dtype),
-            pltpu.SemaphoreType.DMA((len(acts),)),
+            pltpu.VMEM((2, features, 8 * tokens), acts[0].dtype),
+            pltpu.VMEM((8 * tokens, units), cots[0].dtype),
+            pltpu.SemaphoreType.DMA((16,)),
             pltpu.SemaphoreType.DMA((4,)),
         ],
         compiler_params=pltpu.CompilerParams(vmem_limit_bytes=60 * 2**20),
         cost_estimate=pl.CostEstimate(
-            flops=2 * 2 * features * 4 * cots[0].shape[0] * units, bytes_accessed=12 * 2**20, transcendentals=0
+            flops=2 * 2 * features * 8 * tokens * units, bytes_accessed=12 * 2**20, transcendentals=0
         ),
     )(*acts, *cots)
 
@@ -175,24 +189,21 @@
 
 def shards(activations, cotangent, master, moment, second):
     tr = lax.axis_index("tr")
-    tokens = activations.shape[0]
     units = cotangent.shape[1] // 2
+    ordered = feature_order(activations)
+    half = ordered.shape[0] // 2
+    both = jnp.stack([ordered[:half], send(ordered[half:], OTHER_CORE)])
     away = lax.dynamic_slice_in_dim(cotangent, (1 - tr) * units, units, 1)
     own_keep = lax.dynamic_slice_in_dim(cotangent, tr * units, units, 1)
-    activations, away, own_keep = lax.optimization_barrier((activations, away, own_keep))
     own_came = send(away, PAIR)
     far_keep = send(own_keep, OTHER_CORE)
-    ordered = feature_order(activations)
-    half = ordered.shape[1] // 2
-    far_act = send(ordered[:, half:], OTHER_CORE)
-    both = jnp.stack([ordered[:, :half], far_act])
     size = CHUNKS[0] * SIDE**2
-    whole = lax.all_gather(both[:, :, :size], ("tc", "tr"), axis=0)
-    rest, own_came = lax.optimization_barrier((both[:, :, size:], own_came))
+    whole = lax.all_gather(both[:, :size], ("tc", "tr"), axis=0)
+    rest, own_came = lax.optimization_barrier((both[:, size:], own_came))
     acts, pieces = ring(rest)
     far_came = send(own_came, OTHER_CORE)
     cots = (own_keep, own_came, far_keep, far_came)
-    parts = product([whole.reshape(4, 2, 2, tokens, size)], [None], cots)
+    parts = product([whole], [None], cots)
     acts[-2:], parts = lax.optimization_barrier((acts[-2:], parts))
     acts, pieces = ring_end(acts, pieces)
     sums = [summed(parts), summed(product(acts, pieces, cots))]

time: 200 us -> 195 us (0.975)
  waiting for transfers between devices: 105 us -> 101 us
  other arithmetic: 6.34 us -> 10.2 us
    all_gather x1, waiting for transfers between devices: 6.89 us -> 0.01 us  [shards(): whole = lax.all_gather(both[:, :size], ('tc', 'tr'), axis=0)]
    dynamic_slice x1, local copies, waits for them, and re-layouts: 2.78 us -> 0.18 us  [shards(): own_keep = lax.dynamic_slice_in_dim(cotangent, tr * units, units, 1)]
    ppermute x30, waiting for transfers between devices: 98.6 us -> 101 us  [send(): return lax.ppermute(array, AXES, pairs)]
    unnamed x43, local copies, waits for them, and re-layouts: 2.42 us -> 4.48 us
  transfers between devices with their start and end apart: 31 -> 31, of which waited for: 15 -> 15; matrix products, arithmetic and copies ran while one was open for 2% -> 4% of each run, Pallas kernels for 8% -> 9%
where the time goes in v5:
time: 195 us
  waiting for transfers between devices  101 us (52%)
  starting transfers between devices  44.7 us (23%)
  Pallas kernels  18.2 us (9%)
  between operations  14.4 us (7%)
  other arithmetic  10.2 us (5%)
  local copies, waits for them, and re-layouts  4.77 us (2%)
    ppermute x30, waiting for transfers between devices, send(): return lax.ppermute(array, AXES, pairs)  101 us
    ppermute x30, starting transfers between devices, send(): return lax.ppermute(array, AXES, pairs)  44.6 us
    pallas_call x2, Pallas kernels, product(): pl.pallas_call(lambda *refs: product_kernel(pieces, *refs), grid=(2,), in...  16.9 us
    unnamed x43, local copies, waits for them, and re-layouts  4.48 us
  transfers between devices with their start and end apart: 31, of which 15 were waited for; matrix products, arithmetic and copies ran while one was open for 4% of the time, Pallas kernels for 9%

profile of v5, /device:TPU:6, one launch (start us, length us, event | category | flops | bytes accessed | tf_op | source)
XLA Modules:
  0.0 194.9 jit_solution(6875356169598265710)
XLA Ops:
  7.3 0.1 fusion.44
  7.3 1.0 copy-done
  8.3 1.5 fusion.4
  9.8 0.1 fusion.82
  9.9 0.1 collective-permute-start
  10.0 1.7 collective-permute-done
  11.7 0.8 pad_maximum_fusion
  12.5 0.2 constant_dynamic-slice_fusion
  12.7 2.0 %collective-permute-start.1 = (bf16[512,1024]{1,0:T(8,128)(2,1)S(1)}, bf16[512,1024]{1,0:T(8,128)(2,1)S(1)}, u32[]{:S(2)}, u32[]{:S(2)}) collective-permute-start(bf16[512,1024]{1,0:T(8,128)(2,1)S(1)} %get-tuple-element.57), channel_id=1, source_target_pairs={{0,4},{1,5},{2,6},{3,7},{4,0},{5,1},{6,2},{7,3},{8,12},{9,13},{10,... | collective-permute-start | bytes 3145736 | tf_op jit(solution)/shard_map/ppermute | solution.py:43
  14.7 34.2 %collective-permute-done.1.refs_2_.refs_10_ = bf16[512,1024]{1,0:T(8,128)(2,1)S(1)} collective-permute-done((bf16[512,1024]{1,0:T(8,128)(2,1)S(1)}, bf16[512,1024]{1,0:T(8,128)(2,1)S(1)}, u32[]{:S(2)}, u32[]{:S(2)}) %collective-permute-start.1) | collective-permute-done | bytes 1048608 | tf_op jit(solution)/shard_map/ppermute | solution.py:43
  48.9 2.5 %collective-permute-start.2 = (bf16[2,384,256]{2,1,0:T(8,128)(2,1)S(1)}, bf16[2,384,256]{2,1,0:T(8,128)(2,1)S(1)}, u32[]{:S(2)}, u32[]{:S(2)}) collective-permute-start(bf16[2,384,256]{2,1,0:T(8,128)(2,1)S(1)} %get-tuple-element.25.refs_0_), channel_id=1, source_target_pairs={{0,4},{1,5},{2,6},{3,7},{4,1},{5,2},{6,3},{7,0},{8,12},{9,13},{10,... | collective-permute-start | bytes 1179656 | tf_op jit(solution)/shard_map/ppermute | solution.py:43
  51.4 5.3 %collective-permute-start.5 = (bf16[2,384,256]{2,1,0:T(8,128)(2,1)S(1)}, bf16[2,384,256]{2,1,0:T(8,128)(2,1)S(1)}, u32[]{:S(2)}, u32[]{:S(2)}) collective-permute-start(bf16[2,384,256]{2,1,0:T(8,128)(2,1)S(1)} %get-tuple-element.25.refs_0_), channel_id=1, source_target_pairs={{0,7},{1,4},{2,5},{3,6},{4,0},{5,1},{6,2},{7,3},{8,15},{9,12},{10,... | collective-permute-start | bytes 1179656 | tf_op jit(solution)/shard_map/ppermute | solution.py:43
  56.7 17.9 %collective-permute-done.2.refs_1_ = bf16[2,384,256]{2,1,0:T(8,128)(2,1)S(1)} collective-permute-done((bf16[2,384,256]{2,1,0:T(8,128)(2,1)S(1)}, bf16[2,384,256]{2,1,0:T(8,128)(2,1)S(1)}, u32[]{:S(2)}, u32[]{:S(2)}) %collective-permute-start.2) | collective-permute-done | bytes 393248 | tf_op jit(solution)/shard_map/ppermute | solution.py:43
  74.6 3.2 %collective-permute-start.6 = (bf16[2,384,256]{2,1,0:T(8,128)(2,1)S(1)}, bf16[2,384,256]{2,1,0:T(8,128)(2,1)S(1)}, u32[]{:S(2)}, u32[]{:S(2)}) collective-permute-start(bf16[2,384,256]{2,1,0:T(8,128)(2,1)S(1)} %collective-permute-done.5.refs_2_), channel_id=1, source_target_pairs={{0,7},{1,4},{2,5},{3,6},{4,0},{5,1},{6,2},{7,3},{8,15},{9,12},{10,... | collective-permute-start | bytes 1179656 | tf_op jit(solution)/shard_map/ppermute | solution.py:43
  77.9 10.5 %collective-permute-done.3.refs_3_ = bf16[2,384,256]{2,1,0:T(8,128)(2,1)S(1)} collective-permute-done((bf16[2,384,256]{2,1,0:T(8,128)(2,1)S(1)}, bf16[2,384,256]{2,1,0:T(8,128)(2,1)S(1)}, u32[]{:S(2)}, u32[]{:S(2)}) %collective-permute-start.3) | collective-permute-done | bytes 393248 | tf_op jit(solution)/shard_map/ppermute | solution.py:43
  88.4 3.3 %collective-permute-start.7 = (bf16[2,384,256]{2,1,0:T(8,128)(2,1)S(1)}, bf16[2,384,256]{2,1,0:T(8,128)(2,1)S(1)}, u32[]{:S(2)}, u32[]{:S(2)}) collective-permute-start(bf16[2,384,256]{2,1,0:T(8,128)(2,1)S(1)} %collective-permute-done.6.refs_4_), channel_id=1, source_target_pairs={{0,7},{1,4},{2,5},{3,6},{4,0},{5,1},{6,2},{7,3},{8,15},{9,12},{10,... | collective-permute-start | bytes 1179656 | tf_op jit(solution)/shard_map/ppermute | solution.py:43
  91.7 1.0 copy-done.14
  92.7 8.4 %shard_map.76 = (f32[2,2,2,24,1024]{4,3,2,1,0:T(8,128)}, f32[2,2,2,24,1024]{4,3,2,1,0:T(8,128)}, f32[2,2,24,1024]{3,2,1,0:T(8,128)}, f32[2,2,24,1024]{3,2,1,0:T(8,128)}, f32[4,2,24,1024]{3,2,1,0:T(8,128)}) custom-call(bf16[8,2,384,256]{3,2,1,0:T(8,128)(2,1)} %bitcast.159, bf16[512,1024]{1,0:T(8,128)(2,1)} %copy-done.5, bf16[512,1024]{1,0:T(8,128)(2,1)} %copy-done.13, ...), custom_call_target="tpu_custom_call" | custom-call | flops 3221225472 | bytes 12582912 | tf_op jit(solution)/shard_map/pallas_call | solution.py:141
  101.2 0.6 collective-permute-start.11
  101.8 0.1 collective-permute-start.17
  101.9 0.1 copy-done.12
  102.0 3.4 %collective-permute-start.18 = (bf16[384,256]{1,0:T(8,128)(2,1)S(1)}, bf16[384,256]{1,0:T(8,128)(2,1)S(1)}, u32[]{:S(2)}, u32[]{:S(2)}) collective-permute-start(bf16[384,256]{1,0:T(8,128)(2,1)S(1)} %slice_bitcast_fusion.21), channel_id=1, source_target_pairs={{0,7},{1,4},{2,5},{3,6},{4,0},{5,1},{6,2},{7,3},{8,15},{9,12},{10,... | collective-permute-start | bytes 589832 | tf_op jit(solution)/shard_map/ppermute | solution.py:43
  105.4 1.5 collective-permute-start.10
  106.9 3.1 %collective-permute-done.17.refs_7_ = bf16[384,256]{1,0:T(8,128)(2,1)S(1)} collective-permute-done((bf16[384,256]{1,0:T(8,128)(2,1)S(1)}, bf16[384,256]{1,0:T(8,128)(2,1)S(1)}, u32[]{:S(2)}, u32[]{:S(2)}) %collective-permute-start.17) | collective-permute-done | bytes 196640 | tf_op jit(solution)/shard_map/ppermute | solution.py:43
  110.0 0.7 copy-done.19
  110.7 0.7 copy-done.20
  111.4 8.4 %shard_map.77 = (f32[2,2,2,24,1024]{4,3,2,1,0:T(8,128)}, f32[2,2,2,24,1024]{4,3,2,1,0:T(8,128)}, f32[2,2,24,1024]{3,2,1,0:T(8,128)}, f32[2,2,24,1024]{3,2,1,0:T(8,128)}, f32[4,2,24,1024]{3,2,1,0:T(8,128)}) custom-call(bf16[2,384,256]{2,1,0:T(8,128)(2,1)} %copy-done.7, bf16[2,384,256]{2,1,0:T(8,128)(2,1)} %copy-done.15, bf16[2,384,256]{2,1,0:T(8,128)(2,1)} %copy-done.16, ...), custom_call_target="tpu_custom_call" | custom-call | flops 3221225472 | bytes 12582912 | tf_op jit(solution)/shard_map/pallas_call | solution.py:141
  119.8 0.6 collective-permute-start.20
  120.4 1.5 collective-permute-start.19
  121.9 0.8 fusion.11
  122.7 1.7 collective-permute-start.12
  124.4 0.8 fusion.10
  125.2 0.3 collective-permute-start.14
  125.6 6.5 %collective-permute-done.20 = f32[2,2,2,24,1024]{4,3,2,1,0:T(8,128)S(1)} collective-permute-done((f32[2,2,2,24,1024]{4,3,2,1,0:T(8,128)}, f32[2,2,2,24,1024]{4,3,2,1,0:T(8,128)S(1)}, u32[]{:S(2)}, u32[]{:S(2)}) %collective-permute-start.20) | collective-permute-done | bytes 786464 | tf_op jit(solution)/shard_map/ppermute | solution.py:43
  132.1 1.8 fusion.9
  133.9 1.7 collective-permute-start.21
  135.6 0.9 copy-done.6
  136.5 0.8 fusion.8
  137.2 0.3 collective-permute-start.23
  137.6 0.5 collective-permute-done.14
  138.1 1.4 fusion.22
  139.5 1.6 collective-permute-start.13
  141.2 1.7 collective-permute-start.15
  142.9 1.8 collective-permute-start.16
  144.7 9.1 %collective-permute-done.23 = f32[2,2,24,1024]{3,2,1,0:T(8,128)S(1)} collective-permute-done((f32[2,2,24,1024]{3,2,1,0:T(8,128)}, f32[2,2,24,1024]{3,2,1,0:T(8,128)S(1)}, u32[]{:S(2)}, u32[]{:S(2)}) %collective-permute-start.23) | collective-permute-done | bytes 393248 | tf_op jit(solution)/shard_map/ppermute | solution.py:43
  153.8 1.4 fusion.12
  155.2 1.6 collective-permute-start.22
  156.8 1.7 collective-permute-start.24
  158.6 1.2 collective-permute-start.25
  159.7 1.1 fusion.30
  160.8 1.4 collective-permute-done.22
  162.2 0.3 collective-permute-done.24
  162.5 3.2 %collective-permute-done.25 = f32[2,24,1024]{2,1,0:T(8,128)S(1)} collective-permute-done((f32[2,24,1024]{2,1,0:T(8,128)S(1)}, f32[2,24,1024]{2,1,0:T(8,128)S(1)}, u32[]{:S(2)}, u32[]{:S(2)}) %collective-permute-start.25) | collective-permute-done | bytes 196640 | tf_op jit(solution)/shard_map/ppermute | solution.py:43
  165.7 1.2 fusion.20
  167.0 0.1 copy.17
  167.1 0.3 collective-permute-start.26
  167.5 6.7 %collective-permute-done.26 = f32[4,12,8,128]{3,2,1,0:T(8,128)S(1)} collective-permute-done((f32[4,12,8,128]{3,2,1,0:T(8,128)S(1)}, f32[4,12,8,128]{3,2,1,0:T(8,128)S(1)}, u32[]{:S(2)}, u32[]{:S(2)}) %collective-permute-start.26) | collective-permute-done | bytes 196640 | tf_op jit(solution)/shard_map/ppermute | solution.py:43
  174.2 1.5 collective-permute-start.27
  175.7 3.5 %collective-permute-start.28 = (f32[2,12,8,128]{3,2,1,0:T(8,128)S(1)}, f32[2,12,8,128]{3,2,1,0:T(8,128)S(1)}, u32[]{:S(2)}, u32[]{:S(2)}) collective-permute-start(f32[2,12,8,128]{3,2,1,0:T(8,128)S(1)} %get-tuple-element.71), channel_id=1, source_target_pairs={{0,2},{1,3},{2,0},{3,1},{4,6},{5,7},{6,4},{7,5},{8,10},{9,11},{10,... | collective-permute-start | bytes 294920 | tf_op jit(solution)/shard_map/ppermute | solution.py:43
  179.1 1.6 collective-permute-start.29
  180.7 1.3 collective-permute-done.27.piece_1
  182.0 2.3 %collective-permute-done.28.piece_2 = f32[2,12,8,128]{3,2,1,0:T(8,128)S(1)} collective-permute-done((f32[2,12,8,128]{3,2,1,0:T(8,128)S(1)}, f32[2,12,8,128]{3,2,1,0:T(8,128)S(1)}, u32[]{:S(2)}, u32[]{:S(2)}) %collective-permute-start.28) | collective-permute-done | bytes 98336 | tf_op jit(solution)/shard_map/ppermute | solution.py:43
  184.3 2.3 %collective-permute-done.29.piece_3 = f32[2,12,8,128]{3,2,1,0:T(8,128)S(1)} collective-permute-done((f32[2,12,8,128]{3,2,1,0:T(8,128)S(1)}, f32[2,12,8,128]{3,2,1,0:T(8,128)S(1)}, u32[]{:S(2)}, u32[]{:S(2)}) %collective-permute-start.29) | collective-permute-done | bytes 98336 | tf_op jit(solution)/shard_map/ppermute | solution.py:43
  186.7 1.4 shard_map.78
  (63 shorter events, 0.3 us)
Async XLA Ops:
  7.2 1.1 copy-start
  7.2 85.5 %all-gather.3.cloned.1.call-start = ((), (), s32[]{:S(2)}) async-start(), calls=%async_computation | async-start | bytes 3538944 | tf_op jit(solution)/shard_map/all_gather | solution.py:201
  9.8 2.7 %copy-start.4 = (bf16[512,2048]{1,0:T(8,128)(2,1)S(1)}, bf16[512,2048]{1,0:T(8,128)(2,1)}, u32[]{:S(2)}) copy-start(bf16[512,2048]{1,0:T(8,128)(2,1)} %param.6) | copy-start | bytes 6291460
  9.9 1.8 collective-permute-start
  12.5 88.6 %copy-start.7 = (bf16[2,384,256]{2,1,0:T(8,128)(2,1)}, bf16[2,384,256]{2,1,0:T(8,128)(2,1)S(1)}, u32[]{:S(2)}) copy-start(bf16[2,384,256]{2,1,0:T(8,128)(2,1)S(1)} %get-tuple-element.25.refs_0_) | copy-start | bytes 1179652
  12.7 2.0 %copy-start.5 = (bf16[512,1024]{1,0:T(8,128)(2,1)}, bf16[512,1024]{1,0:T(8,128)(2,1)S(1)}, u32[]{:S(2)}) copy-start(bf16[512,1024]{1,0:T(8,128)(2,1)S(1)} %get-tuple-element.56.refs_1_.refs_9_) | copy-start | bytes 3145732
  12.7 36.2 %collective-permute-start.1 = (bf16[512,1024]{1,0:T(8,128)(2,1)S(1)}, bf16[512,1024]{1,0:T(8,128)(2,1)S(1)}, u32[]{:S(2)}, u32[]{:S(2)}) collective-permute-start(bf16[512,1024]{1,0:T(8,128)(2,1)S(1)} %get-tuple-element.57), channel_id=1, source_target_pairs={{0,4},{1,5},{2,6},{3,7},{4,0},{5,1},{6,2},{7,3},{8,12},{9,13},{10,... | collective-permute-start | bytes 3145736 | tf_op jit(solution)/shard_map/ppermute | solution.py:43
  14.7 76.9 %collective-permute-start.8 = (bf16[512,1024]{1,0:T(8,128)(2,1)S(1)}, bf16[512,1024]{1,0:T(8,128)(2,1)S(1)}, u32[]{:S(2)}, u32[]{:S(2)}) collective-permute-start(bf16[512,1024]{1,0:T(8,128)(2,1)S(1)} %get-tuple-element.56.refs_1_.refs_9_), channel_id=1, source_target_pairs={{0,8},{1,9},{2,10},{3,11},{4,12},{5,13},{6,14},{7,15},{8,0},{9,1},... | collective-permute-start | bytes 3145736 | tf_op jit(solution)/shard_map/ppermute | solution.py:43
  48.9 42.8 %copy-start.13 = (bf16[512,1024]{1,0:T(8,128)(2,1)}, bf16[512,1024]{1,0:T(8,128)(2,1)S(1)}, u32[]{:S(2)}) copy-start(bf16[512,1024]{1,0:T(8,128)(2,1)S(1)} %collective-permute-done.1.refs_2_.refs_10_) | copy-start | bytes 3145732
  48.9 43.8 %collective-permute-start.9 = (bf16[512,1024]{1,0:T(8,128)(2,1)S(1)}, bf16[512,1024]{1,0:T(8,128)(2,1)}, u32[]{:S(2)}, u32[]{:S(2)}) collective-permute-start(bf16[512,1024]{1,0:T(8,128)(2,1)S(1)} %collective-permute-done.1.refs_2_.refs_10_), channel_id=1, source_target_pairs={{0,8},{1,9},{2,10},{3,11},{4,12},{5,13},{6,14},{7,15},{8,0},{9,1},... | collective-permute-start | bytes 3145736 | tf_op jit(solution)/shard_map/ppermute | solution.py:43
  48.9 25.7 %collective-permute-start.2 = (bf16[2,384,256]{2,1,0:T(8,128)(2,1)S(1)}, bf16[2,384,256]{2,1,0:T(8,128)(2,1)S(1)}, u32[]{:S(2)}, u32[]{:S(2)}) collective-permute-start(bf16[2,384,256]{2,1,0:T(8,128)(2,1)S(1)} %get-tuple-element.25.refs_0_), channel_id=1, source_target_pairs={{0,4},{1,5},{2,6},{3,7},{4,1},{5,2},{6,3},{7,0},{8,12},{9,13},{10,... | collective-permute-start | bytes 1179656 | tf_op jit(solution)/shard_map/ppermute | solution.py:43
  51.4 23.2 %collective-permute-start.5 = (bf16[2,384,256]{2,1,0:T(8,128)(2,1)S(1)}, bf16[2,384,256]{2,1,0:T(8,128)(2,1)S(1)}, u32[]{:S(2)}, u32[]{:S(2)}) collective-permute-start(bf16[2,384,256]{2,1,0:T(8,128)(2,1)S(1)} %get-tuple-element.25.refs_0_), channel_id=1, source_target_pairs={{0,7},{1,4},{2,5},{3,6},{4,0},{5,1},{6,2},{7,3},{8,15},{9,12},{10,... | collective-permute-start | bytes 1179656 | tf_op jit(solution)/shard_map/ppermute | solution.py:43
  74.6 17.0 %copy-start.15 = (bf16[2,384,256]{2,1,0:T(8,128)(2,1)}, bf16[2,384,256]{2,1,0:T(8,128)(2,1)S(1)}, u32[]{:S(2)}) copy-start(bf16[2,384,256]{2,1,0:T(8,128)(2,1)S(1)} %collective-permute-done.2.refs_1_) | copy-start | bytes 1179652
  74.6 13.7 %collective-permute-start.3 = (bf16[2,384,256]{2,1,0:T(8,128)(2,1)S(1)}, bf16[2,384,256]{2,1,0:T(8,128)(2,1)S(1)}, u32[]{:S(2)}, u32[]{:S(2)}) collective-permute-start(bf16[2,384,256]{2,1,0:T(8,128)(2,1)S(1)} %collective-permute-done.2.refs_1_), channel_id=1, source_target_pairs={{0,4},{1,5},{2,6},{3,7},{4,1},{5,2},{6,3},{7,0},{8,12},{9,13},{10,... | collective-permute-start | bytes 1179656 | tf_op jit(solution)/shard_map/ppermute | solution.py:43
  74.6 13.7 %copy-start.16 = (bf16[2,384,256]{2,1,0:T(8,128)(2,1)}, bf16[2,384,256]{2,1,0:T(8,128)(2,1)S(1)}, u32[]{:S(2)}) copy-start(bf16[2,384,256]{2,1,0:T(8,128)(2,1)S(1)} %collective-permute-done.5.refs_2_) | copy-start | bytes 1179652
  74.6 13.7 %collective-permute-start.6 = (bf16[2,384,256]{2,1,0:T(8,128)(2,1)S(1)}, bf16[2,384,256]{2,1,0:T(8,128)(2,1)S(1)}, u32[]{:S(2)}, u32[]{:S(2)}) collective-permute-start(bf16[2,384,256]{2,1,0:T(8,128)(2,1)S(1)} %collective-permute-done.5.refs_2_), channel_id=1, source_target_pairs={{0,7},{1,4},{2,5},{3,6},{4,0},{5,1},{6,2},{7,3},{8,15},{9,12},{10,... | collective-permute-start | bytes 1179656 | tf_op jit(solution)/shard_map/ppermute | solution.py:43
  88.3 13.6 %copy-start.17 = (bf16[2,384,256]{2,1,0:T(8,128)(2,1)}, bf16[2,384,256]{2,1,0:T(8,128)(2,1)S(1)}, u32[]{:S(2)}) copy-start(bf16[2,384,256]{2,1,0:T(8,128)(2,1)S(1)} %collective-permute-done.3.refs_3_) | copy-start | bytes 1179652
  88.3 12.8 %collective-permute-start.4 = (bf16[2,384,256]{2,1,0:T(8,128)(2,1)S(1)}, bf16[2,384,256]{2,1,0:T(8,128)(2,1)S(1)}, u32[]{:S(2)}, u32[]{:S(2)}) collective-permute-start(bf16[2,384,256]{2,1,0:T(8,128)(2,1)S(1)} %collective-permute-done.3.refs_3_), channel_id=1, source_target_pairs={{0,4},{1,5},{2,6},{3,7},{4,1},{5,2},{6,3},{7,0},{8,12},{9,13},{10,... | collective-permute-start | bytes 1179656 | tf_op jit(solution)/shard_map/ppermute | solution.py:43
  88.4 12.8 %copy-start.18 = (bf16[2,384,256]{2,1,0:T(8,128)(2,1)}, bf16[2,384,256]{2,1,0:T(8,128)(2,1)S(1)}, u32[]{:S(2)}) copy-start(bf16[2,384,256]{2,1,0:T(8,128)(2,1)S(1)} %collective-permute-done.6.refs_4_) | copy-start | bytes 1179652
  88.4 12.8 %collective-permute-start.7 = (bf16[2,384,256]{2,1,0:T(8,128)(2,1)S(1)}, bf16[2,384,256]{2,1,0:T(8,128)(2,1)S(1)}, u32[]{:S(2)}, u32[]{:S(2)}) collective-permute-start(bf16[2,384,256]{2,1,0:T(8,128)(2,1)S(1)} %collective-permute-done.6.refs_4_), channel_id=1, source_target_pairs={{0,7},{1,4},{2,5},{3,6},{4,0},{5,1},{6,2},{7,3},{8,15},{9,12},{10,... | collective-permute-start | bytes 1179656 | tf_op jit(solution)/shard_map/ppermute | solution.py:43
  91.7 1.0 copy-start.14
  101.1 0.7 copy-start.11
  101.2 0.9 copy-start.12
  101.2 20.7 %collective-permute-start.11 = (f32[2,2,2,24,1024]{4,3,2,1,0:T(8,128)}, f32[2,2,2,24,1024]{4,3,2,1,0:T(8,128)S(1)}, u32[]{:S(2)}, u32[]{:S(2)}) collective-permute-start(f32[2,2,2,24,1024]{4,3,2,1,0:T(8,128)} %get-tuple-element.35), channel_id=1, source_target_pairs={{0,16},{1,17},{2,18},{3,19},{4,20},{5,21},{6,22},{7,23},{8,72},{9,... | collective-permute-start | bytes 2359304 | tf_op jit(solution)/shard_map/ppermute | solution.py:43
  101.8 8.2 %collective-permute-start.17 = (bf16[384,256]{1,0:T(8,128)(2,1)S(1)}, bf16[384,256]{1,0:T(8,128)(2,1)S(1)}, u32[]{:S(2)}, u32[]{:S(2)}) collective-permute-start(bf16[384,256]{1,0:T(8,128)(2,1)S(1)} %slice_bitcast_fusion.22), channel_id=1, source_target_pairs={{0,4},{1,5},{2,6},{3,7},{4,1},{5,2},{6,3},{7,0},{8,12},{9,13},{10,... | collective-permute-start | bytes 589832 | tf_op jit(solution)/shard_map/ppermute | solution.py:43
  102.0 19.9 %copy-start.9 = (f32[2,2,24,1024]{3,2,1,0:T(8,128)S(1)}, f32[2,2,24,1024]{3,2,1,0:T(8,128)}, u32[]{:S(2)}) copy-start(f32[2,2,24,1024]{3,2,1,0:T(8,128)} %get-tuple-element.34) | copy-start | bytes 1179652
  102.0 22.4 %copy-start.8 = (f32[2,2,24,1024]{3,2,1,0:T(8,128)S(1)}, f32[2,2,24,1024]{3,2,1,0:T(8,128)}, u32[]{:S(2)}) copy-start(f32[2,2,24,1024]{3,2,1,0:T(8,128)} %get-tuple-element.36) | copy-start | bytes 1179652
  102.0 8.0 %collective-permute-start.18 = (bf16[384,256]{1,0:T(8,128)(2,1)S(1)}, bf16[384,256]{1,0:T(8,128)(2,1)S(1)}, u32[]{:S(2)}, u32[]{:S(2)}) collective-permute-start(bf16[384,256]{1,0:T(8,128)(2,1)S(1)} %slice_bitcast_fusion.21), channel_id=1, source_target_pairs={{0,7},{1,4},{2,5},{3,6},{4,0},{5,1},{6,2},{7,3},{8,15},{9,12},{10,... | collective-permute-start | bytes 589832 | tf_op jit(solution)/shard_map/ppermute | solution.py:43
  105.4 19.0 %collective-permute-start.10 = (f32[2,2,2,24,1024]{4,3,2,1,0:T(8,128)}, f32[2,2,2,24,1024]{4,3,2,1,0:T(8,128)S(1)}, u32[]{:S(2)}, u32[]{:S(2)}) collective-permute-start(f32[2,2,2,24,1024]{4,3,2,1,0:T(8,128)} %get-tuple-element.33), channel_id=1, source_target_pairs={{0,48},{1,49},{2,50},{3,51},{4,52},{5,53},{6,54},{7,55},{8,200},{9... | collective-permute-start | bytes 2359304 | tf_op jit(solution)/shard_map/ppermute | solution.py:43
  110.0 0.7 copy-start.19
  110.7 0.7 copy-start.20
  119.8 16.7 %copy-start.10 = (f32[2,2,24,1024]{3,2,1,0:T(8,128)S(1)}, f32[2,2,24,1024]{3,2,1,0:T(8,128)}, u32[]{:S(2)}) copy-start(f32[2,2,24,1024]{3,2,1,0:T(8,128)} %get-tuple-element.43) | copy-start | bytes 1179652
  119.8 12.3 %collective-permute-start.20 = (f32[2,2,2,24,1024]{4,3,2,1,0:T(8,128)}, f32[2,2,2,24,1024]{4,3,2,1,0:T(8,128)S(1)}, u32[]{:S(2)}, u32[]{:S(2)}) collective-permute-start(f32[2,2,2,24,1024]{4,3,2,1,0:T(8,128)} %get-tuple-element.42), channel_id=1, source_target_pairs={{0,16},{1,17},{2,18},{3,19},{4,20},{5,21},{6,22},{7,23},{8,72},{9,... | collective-permute-start | bytes 2359304 | tf_op jit(solution)/shard_map/ppermute | solution.py:43
  120.4 15.2 %collective-permute-start.19 = (f32[2,2,2,24,1024]{4,3,2,1,0:T(8,128)}, f32[2,2,2,24,1024]{4,3,2,1,0:T(8,128)S(1)}, u32[]{:S(2)}, u32[]{:S(2)}) collective-permute-start(f32[2,2,2,24,1024]{4,3,2,1,0:T(8,128)} %get-tuple-element.40), channel_id=1, source_target_pairs={{0,48},{1,49},{2,50},{3,51},{4,52},{5,53},{6,54},{7,55},{8,200},{9... | collective-permute-start | bytes 2359304 | tf_op jit(solution)/shard_map/ppermute | solution.py:43
  122.7 14.8 %collective-permute-start.12 = (f32[2,2,24,1024]{3,2,1,0:T(8,128)}, f32[2,2,24,1024]{3,2,1,0:T(8,128)}, u32[]{:S(2)}, u32[]{:S(2)}) collective-permute-start(f32[2,2,24,1024]{3,2,1,0:T(8,128)} %fusion.11), channel_id=1, source_target_pairs={{0,16},{1,17},{2,18},{3,19},{4,20},{5,21},{6,22},{7,23},{8,72},{9,... | collective-permute-start | bytes 1179656 | tf_op jit(solution)/shard_map/ppermute | solution.py:43
  125.2 12.9 %collective-permute-start.14 = (f32[2,2,24,1024]{3,2,1,0:T(8,128)}, f32[2,2,24,1024]{3,2,1,0:T(8,128)}, u32[]{:S(2)}, u32[]{:S(2)}) collective-permute-start(f32[2,2,24,1024]{3,2,1,0:T(8,128)} %fusion.10), channel_id=1, source_target_pairs={{0,48},{1,49},{2,50},{3,51},{4,52},{5,53},{6,54},{7,55},{8,200},{9... | collective-permute-start | bytes 1179656 | tf_op jit(solution)/shard_map/ppermute | solution.py:43
  133.9 10.8 %collective-permute-start.21 = (f32[2,2,24,1024]{3,2,1,0:T(8,128)}, f32[2,2,24,1024]{3,2,1,0:T(8,128)}, u32[]{:S(2)}, u32[]{:S(2)}) collective-permute-start(f32[2,2,24,1024]{3,2,1,0:T(8,128)} %fusion.9), channel_id=1, source_target_pairs={{0,16},{1,17},{2,18},{3,19},{4,20},{5,21},{6,22},{7,23},{8,72},{9,... | collective-permute-start | bytes 1179656 | tf_op jit(solution)/shard_map/ppermute | solution.py:43
  135.6 0.9 copy-start.6
  137.2 16.6 %collective-permute-start.23 = (f32[2,2,24,1024]{3,2,1,0:T(8,128)}, f32[2,2,24,1024]{3,2,1,0:T(8,128)S(1)}, u32[]{:S(2)}, u32[]{:S(2)}) collective-permute-start(f32[2,2,24,1024]{3,2,1,0:T(8,128)} %fusion.8), channel_id=1, source_target_pairs={{0,48},{1,49},{2,50},{3,51},{4,52},{5,53},{6,54},{7,55},{8,200},{9... | collective-permute-start | bytes 1179656 | tf_op jit(solution)/shard_map/ppermute | solution.py:43
  139.5 19.0 %collective-permute-start.13 = (f32[2,24,1024]{2,1,0:T(8,128)S(1)}, f32[2,24,1024]{2,1,0:T(8,128)S(1)}, u32[]{:S(2)}, u32[]{:S(2)}) collective-permute-start(f32[2,24,1024]{2,1,0:T(8,128)S(1)} %get-tuple-element.62), channel_id=1, source_target_pairs={{0,64},{1,65},{2,66},{3,67},{4,68},{5,69},{6,70},{7,71},{8,24},{9,... | collective-permute-start | bytes 589832 | tf_op jit(solution)/shard_map/ppermute | solution.py:43
  141.2 18.6 %collective-permute-start.15 = (f32[2,24,1024]{2,1,0:T(8,128)S(1)}, f32[2,24,1024]{2,1,0:T(8,128)S(1)}, u32[]{:S(2)}, u32[]{:S(2)}) collective-permute-start(f32[2,24,1024]{2,1,0:T(8,128)S(1)} %get-tuple-element.59), channel_id=1, source_target_pairs={{0,192},{1,193},{2,194},{3,195},{4,196},{5,197},{6,198},{7,199},{8... | collective-permute-start | bytes 589832 | tf_op jit(solution)/shard_map/ppermute | solution.py:43
  142.9 16.9 %collective-permute-start.16 = (f32[2,24,1024]{2,1,0:T(8,128)S(1)}, f32[2,24,1024]{2,1,0:T(8,128)S(1)}, u32[]{:S(2)}, u32[]{:S(2)}) collective-permute-start(f32[2,24,1024]{2,1,0:T(8,128)S(1)} %get-tuple-element.58), channel_id=1, source_target_pairs={{0,128},{1,129},{2,130},{3,131},{4,132},{5,133},{6,134},{7,135},{8... | collective-permute-start | bytes 589832 | tf_op jit(solution)/shard_map/ppermute | solution.py:43
  155.2 31.5 %copy-start.1 = (f32[1,12,8192]{2,0,1:T(1,128)S(1)}, f32[1,12,8192]{2,0,1:T(1,128)}, u32[]{:S(2)}) copy-start(f32[1,12,8192]{2,0,1:T(1,128)} %param.7) | copy-start | bytes 1179652
  155.2 31.4 %copy-start.2 = (f32[1,12,8192]{2,0,1:T(1,128)S(1)}, f32[1,12,8192]{2,0,1:T(1,128)}, u32[]{:S(2)}) copy-start(f32[1,12,8192]{2,0,1:T(1,128)} %param.8) | copy-start | bytes 1179652
  155.2 31.4 %copy-start.3 = (f32[1,12,8192]{2,0,1:T(1,128)S(1)}, f32[1,12,8192]{2,0,1:T(1,128)}, u32[]{:S(2)}) copy-start(f32[1,12,8192]{2,0,1:T(1,128)} %param.9) | copy-start | bytes 1179652
  155.2 7.0 %collective-permute-start.22 = (f32[2,24,1024]{2,1,0:T(8,128)S(1)}, f32[2,24,1024]{2,1,0:T(8,128)S(1)}, u32[]{:S(2)}, u32[]{:S(2)}) collective-permute-start(f32[2,24,1024]{2,1,0:T(8,128)S(1)} %get-tuple-element.63), channel_id=1, source_target_pairs={{0,64},{1,65},{2,66},{3,67},{4,68},{5,69},{6,70},{7,71},{8,24},{9,... | collective-permute-start | bytes 589832 | tf_op jit(solution)/shard_map/ppermute | solution.py:43
  156.8 5.7 %collective-permute-start.24 = (f32[2,24,1024]{2,1,0:T(8,128)S(1)}, f32[2,24,1024]{2,1,0:T(8,128)S(1)}, u32[]{:S(2)}, u32[]{:S(2)}) collective-permute-start(f32[2,24,1024]{2,1,0:T(8,128)S(1)} %get-tuple-element.61), channel_id=1, source_target_pairs={{0,192},{1,193},{2,194},{3,195},{4,196},{5,197},{6,198},{7,199},{8... | collective-permute-start | bytes 589832 | tf_op jit(solution)/shard_map/ppermute | solution.py:43
  158.6 7.2 %collective-permute-start.25 = (f32[2,24,1024]{2,1,0:T(8,128)S(1)}, f32[2,24,1024]{2,1,0:T(8,128)S(1)}, u32[]{:S(2)}, u32[]{:S(2)}) collective-permute-start(f32[2,24,1024]{2,1,0:T(8,128)S(1)} %get-tuple-element.60), channel_id=1, source_target_pairs={{0,128},{1,129},{2,130},{3,131},{4,132},{5,133},{6,134},{7,135},{8... | collective-permute-start | bytes 589832 | tf_op jit(solution)/shard_map/ppermute | solution.py:43
  167.1 7.1 %collective-permute-start.26 = (f32[4,12,8,128]{3,2,1,0:T(8,128)S(1)}, f32[4,12,8,128]{3,2,1,0:T(8,128)S(1)}, u32[]{:S(2)}, u32[]{:S(2)}) collective-permute-start(f32[4,12,8,128]{3,2,1,0:T(8,128)S(1)} %get-tuple-element.72), channel_id=1, source_target_pairs={{0,4},{1,5},{2,6},{3,7},{4,0},{5,1},{6,2},{7,3},{8,12},{9,13},{10,... | collective-permute-start | bytes 589832 | tf_op jit(solution)/shard_map/ppermute | solution.py:43
  174.2 7.9 %collective-permute-start.27 = (f32[2,12,8,128]{3,2,1,0:T(8,128)S(1)}, f32[2,12,8,128]{3,2,1,0:T(8,128)S(1)}, u32[]{:S(2)}, u32[]{:S(2)}) collective-permute-start(f32[2,12,8,128]{3,2,1,0:T(8,128)S(1)} %get-tuple-element.70), channel_id=1, source_target_pairs={{0,1},{1,2},{2,3},{3,0},{4,5},{5,6},{6,7},{7,4},{8,9},{9,10},{10,1... | collective-permute-start | bytes 294920 | tf_op jit(solution)/shard_map/ppermute | solution.py:43
  175.7 8.6 %collective-permute-start.28 = (f32[2,12,8,128]{3,2,1,0:T(8,128)S(1)}, f32[2,12,8,128]{3,2,1,0:T(8,128)S(1)}, u32[]{:S(2)}, u32[]{:S(2)}) collective-permute-start(f32[2,12,8,128]{3,2,1,0:T(8,128)S(1)} %get-tuple-element.71), channel_id=1, source_target_pairs={{0,2},{1,3},{2,0},{3,1},{4,6},{5,7},{6,4},{7,5},{8,10},{9,11},{10,... | collective-permute-start | bytes 294920 | tf_op jit(solution)/shard_map/ppermute | solution.py:43
  179.1 7.5 %collective-permute-start.29 = (f32[2,12,8,128]{3,2,1,0:T(8,128)S(1)}, f32[2,12,8,128]{3,2,1,0:T(8,128)S(1)}, u32[]{:S(2)}, u32[]{:S(2)}) collective-permute-start(f32[2,12,8,128]{3,2,1,0:T(8,128)S(1)} %get-tuple-element.68), channel_id=1, source_target_pairs={{0,3},{1,0},{2,1},{3,2},{4,7},{5,4},{6,5},{7,6},{8,11},{9,8},{10,9... | collective-permute-start | bytes 294920 | tf_op jit(solution)/shard_map/ppermute | solution.py:43
Sparse Core Ops, SparseCore 0:
  12.6 69.5 all-gather.2

commit v6 on v5

v6 whole, which is shorter than its diff:
```python
import jax
import jax.numpy as jnp
from jax import lax
from jax.experimental import pallas as pl
from jax.experimental.pallas import tpu as pltpu
from jax.sharding import PartitionSpec as P

first_decay = 0.9
second_decay = 0.95
learn_rate = 0.0003
weight_decay = 0.1
epsilon = 1e-08
first_fix = 1.0 - 0.9**10
second_fix = 1.0 - 0.95**10

AXES = ("dp", "tr", "tc")
SIDE = 4
ROWS = 48
CHUNKS = (40, 8)


def moves(where):
    pairs = []
    for dp in range(32):
        for tr in range(2):
            for tc in range(4):
                y, x, core, z = where(dp // 8, dp // 2 % 4, dp % 2, 2 * tc + tr)
                to = (y % 4 * 8 + x % 4 * 2 + core % 2, z % 2, z % 8 // 2)
                pairs.append(((dp * 2 + tr) * 4 + tc, (to[0] * 2 + to[1]) * 4 + to[2]))
    return pairs


def step(first, hop):
    def where(y, x, core, z):
        if (core == 0) == first:
            return y, x + hop, core, z
        return y + hop, x, core, z

    return moves(where)


def send(array, pairs):
    return lax.ppermute(array, AXES, pairs)


OTHER_CORE = moves(lambda y, x, core, z: (y, x, 1 - core, z))
PAIR = moves(lambda y, x, core, z: (y, x, core, z ^ 1))


def feature_order(activations):
    dp = lax.axis_index("dp")
    my_y, my_x, core = dp // 8, dp // 2 % 4, dp % 2
    column = lax.broadcasted_iota(jnp.int32, (1, 2 * SIDE * SIDE * ROWS), 1)
    half, rest = column // (SIDE * SIDE * ROWS), column % (SIDE * SIDE * ROWS)
    target = jnp.where(half == 0, core, 1 - core)
    source = jnp.zeros_like(column)
    start = 0
    for rows in CHUNKS:
        size = SIDE * SIDE * rows
        inside = rest - start * SIDE * SIDE
        near, far, row = inside // (SIDE * rows), inside // rows % SIDE, inside % rows
        x = jnp.where(target == 0, my_x + near, my_x + far) % SIDE
        y = jnp.where(target == 0, my_y + far, my_y + near) % SIDE
        feature = (y * SIDE + x) * 2 * ROWS + target * ROWS + start + row
        source = jnp.where((inside >= 0) & (inside < size), feature, source)
        start += rows
    feature = lax.broadcasted_iota(jnp.int32, (activations.shape[1], column.shape[1]), 0)
    chosen = (feature == source).astype(activations.dtype)
    ordered = lax.dot_general(chosen, activations, (((0,), (1,)), ((), ())), preferred_element_type=jnp.float32)
    return ordered.astype(activations.dtype)


def product_kernel(gathered, *refs):
    cots = refs[:4]
    plus, minus, add_plus, add_minus, mine = refs[4:9]
    act, cot, act_sem, cot_sem = refs[9:]
    tr = lax.axis_index("tr")
    features = act.shape[1]
    tokens = act.shape[2] // 8
    i = pl.program_id(0)

    def copies_of(replica):
        copies = []
        for z in range(8):
            window = pl.ds((replica * 4 + z // 2) * tokens, tokens)
            copies.append(
                pltpu.make_async_copy(gathered.at[z, replica], act.at[z % 2, :, window], act_sem.at[8 * replica + z])
            )
        for came in range(2):
            half = 1 - tr if came else tr
            start = pl.multiple_of(replica * 4 * tokens + half * 2 * tokens, 2 * tokens)
            n = 2 * replica + came
            copies.append(pltpu.make_async_copy(cots[n], cot.at[pl.ds(start, 2 * tokens)], cot_sem.at[n]))
        return copies

    @pl.when(i == 0)
    def fetch():
        for copy in copies_of(0) + copies_of(1):
            copy.start()

    def part(replica):
        @pl.when(i == 0)
        def arrived():
            for copy in copies_of(replica):
                copy.wait()

        depth = slice(replica * 4 * tokens, (replica + 1) * 4 * tokens)
        return jnp.dot(act[i, :, depth], cot[depth], preferred_element_type=jnp.float32)

    total = part(0)
    total = total + part(1)
    total = total.reshape(SIDE, SIDE, 1, features // SIDE**2, total.shape[-1])
    plus[0] = total[2, :2]
    plus[1] = total[1, 2:]
    minus[0] = total[2, 2:]
    minus[1] = total[3, :2]
    add_plus[...] = total[1, :2]
    add_minus[...] = total[3, 2:]
    mine[...] = total[0]


def product(gathered, cots):
    features, tokens = gathered.shape[-2:]
    units = cots[0].shape[1]
    rows = features // SIDE**2
    pack = pl.BlockSpec((2, 2, 1, rows, units), lambda i: (0, 0, i, 0, 0))
    part = pl.BlockSpec((2, 1, rows, units), lambda i: (0, i, 0, 0))
    full = pl.BlockSpec((SIDE, 1, rows, units), lambda i: (0, i, 0, 0))
    packed = jax.ShapeDtypeStruct((2, 2, 2, rows, units), jnp.float32)
    parted = jax.ShapeDtypeStruct((2, 2, rows, units), jnp.float32)
    return pl.pallas_call(
        product_kernel,
        grid=(2,),
        in_specs=[pl.BlockSpec(memory_space=pl.ANY)] * 5,
        out_specs=[pack, pack, part, part, full],
        out_shape=[packed, packed, parted, parted, jax.ShapeDtypeStruct((SIDE, 2, rows, units), jnp.float32)],
        scratch_shapes=[
            pltpu.VMEM((2, features, 8 * tokens), gathered.dtype),
            pltpu.VMEM((8 * tokens, units), cots[0].dtype),
            pltpu.SemaphoreType.DMA((16,)),
            pltpu.SemaphoreType.DMA((4,)),
        ],
        compiler_params=pltpu.CompilerParams(vmem_limit_bytes=60 * 2**20),
        cost_estimate=pl.CostEstimate(
            flops=2 * 2 * features * 8 * tokens * units, bytes_accessed=12 * 2**20, transcendentals=0
        ),
    )(gathered, *cots)


def first_round(parts):
    plus, minus, add_plus, add_minus, mine = parts
    left = send(plus, step(True, 1))
    right = send(minus, step(True, -1))
    rest = mine[:2] + right[1], mine[2:] + left[1]
    return (add_plus + left[0], add_minus + right[0]), rest


def second_round(ready, rest):
    near = send(ready[0], step(True, 1))
    far = send(ready[1], step(True, -1))
    low = [rest[0][s] + near[s] for s in range(2)]
    high = [rest[1][s] + far[s] for s in range(2)]
    came = [send(low[1], step(False, 1)), send(high[1], step(False, -1)), send(high[0], step(False, 2))]
    return low[0] + came[0] + (came[1] + came[2])


def shards(activations, cotangent, master, moment, second):
    tr = lax.axis_index("tr")
    units = cotangent.shape[1] // 2
    ordered = feature_order(activations)
    half = ordered.shape[0] // 2
    both = jnp.stack([ordered[:half], send(ordered[half:], OTHER_CORE)])
    away = lax.dynamic_slice_in_dim(cotangent, (1 - tr) * units, units, 1)
    own_keep = lax.dynamic_slice_in_dim(cotangent, tr * units, units, 1)
    own_came = send(away, PAIR)
    far_keep = send(own_keep, OTHER_CORE)
    size = CHUNKS[0] * SIDE**2
    whole = lax.all_gather(both[:, :size], ("tc", "tr"), axis=0)
    last = lax.all_gather(both[:, size:], ("tc", "tr"), axis=0)
    far_came = send(own_came, OTHER_CORE)
    cots = (own_keep, own_came, far_keep, far_came)
    ready, rest = first_round(product(whole, cots))
    last, ready = lax.optimization_barrier((last, ready))
    sums = [second_round(ready, rest), second_round(*first_round(product(last, cots)))]
    rows = jnp.concatenate(sums, axis=1).reshape(2, 4, ROWS // 4, 8, units // 8)
    rows = rows.swapaxes(0, 1).reshape(8, ROWS // 4, 8, units // 8)
    rows = lax.all_to_all(rows, ("tc", "tr"), split_axis=0, concat_axis=0, tiled=True)
    return updated(rows, master, moment, second)


def updated(rows, master, moment, second):
    wide = (rows.shape[1], rows.shape[0] * rows.shape[2], rows.shape[3])
    flat = [array.reshape(wide) for array in (master, moment, second)]
    outs = pl.pallas_call(
        update_kernel,
        out_shape=[jax.ShapeDtypeStruct(wide, jnp.float32)] * 3,
        compiler_params=pltpu.CompilerParams(vmem_limit_bytes=16 * 2**20),
    )(rows, *flat)
    return tuple(out.reshape(master.shape) for out in outs)


def update_kernel(rows, master, moment, second, new_master, new_moment, new_second):
    for z in range(8):
        place = (slice(None), pl.ds(z * 8, 8), slice(None))
        grad = rows[z]
        first = first_decay * moment[place] + (1.0 - first_decay) * grad
        square = second_decay * second[place] + (1.0 - second_decay) * grad * grad
        old = master[place]
        update = first / first_fix / (jnp.sqrt(square / second_fix) + epsilon)
        new_moment[place] = first
        new_second[place] = square
        new_master[place] = old - learn_rate * (update + weight_decay * old)


def solution(mesh):
    state = P("tr", ("dp", "tc"), None)
    return jax.shard_map(
        shards,
        mesh=mesh,
        in_specs=(P(("dp", "tc"), "tr"), P(("dp", "tr"), "tc"), state, state, state),
        out_specs=(state, state, state),
        check_vma=False,
    )
```

time: 195 us -> 203 us (1.041)
  starting transfers between devices: 44.7 us -> 23.5 us
  waiting for transfers between devices: 101 us -> 121 us
  blocking collectives: 0 us -> 16.8 us
  other arithmetic: 10.2 us -> 5.33 us
    all_gather x1, waiting for transfers between devices: 0.01 us -> 36.2 us  [shards(): whole = lax.all_gather(both[:, :size], ('tc', 'tr'), axis=0)]
    ppermute x30 -> x18, waiting for transfers between devices: 101 us -> 75.4 us  [send(): return lax.ppermute(array, AXES, pairs)]
    ppermute x30 -> x18, starting transfers between devices: 44.6 us -> 23.5 us  [send(): return lax.ppermute(array, AXES, pairs)]
    all_to_all x0 -> x1, blocking collectives: none -> 16.8 us  [shards(): lax.all_to_all(rows, ('tc', 'tr'), split_axis=0, concat_axis=0, tiled=True)]
    all_gather x0 -> x1, waiting for transfers between devices: none -> 9.04 us  [shards(): last = lax.all_gather(both[:, size:], ('tc', 'tr'), axis=0)]
    add x8, other arithmetic: 9.3 us -> 3.67 us  [the longest x2 3.41 us: first_round(): rest = (mine[:2] + right[1], mine[2:] + left[1])]
    unnamed x43 -> x11, local copies, waits for them, and re-layouts: 4.48 us -> 1.06 us
  transfers between devices with their start and end apart: 31 -> 20, of which waited for: 15 -> 9; matrix products, arithmetic and copies ran while one was open for 4% -> 3% of each run, Pallas kernels for 9% -> 6%
where the time goes in v6:
time: 203 us
  waiting for transfers between devices  121 us (60%)
  starting transfers between devices  23.5 us (12%)
  Pallas kernels  17.9 us (9%)
  blocking collectives  16.8 us (8%)
  between operations  14.3 us (7%)
  other arithmetic  5.33 us (3%)
  local copies, waits for them, and re-layouts  2.86 us (1%)
    ppermute x18, waiting for transfers between devices, send(): return lax.ppermute(array, AXES, pairs)  75.4 us
    all_gather x1, waiting for transfers between devices, shards(): whole = lax.all_gather(both[:, :size], ('tc', 'tr'), axis=0)  36.2 us
    ppermute x18, starting transfers between devices, send(): return lax.ppermute(array, AXES, pairs)  23.5 us
    all_to_all x1, blocking collectives, shards(): lax.all_to_all(rows, ('tc', 'tr'), split_axis=0, concat_axis=0, tiled=True)  16.8 us
    pallas_call x2, Pallas kernels, product(): pl.pallas_call(product_kernel, grid=(2,), in_specs=[pl.BlockSpec(memory_s...  16.7 us
    all_gather x1, waiting for transfers between devices, shards(): last = lax.all_gather(both[:, size:], ('tc', 'tr'), axis=0)  9.04 us
  transfers between devices with their start and end apart: 20, of which 9 were waited for; matrix products, arithmetic and copies ran while one was open for 3% of the time, Pallas kernels for 6%

profile of v6, /device:TPU:6, one launch (start us, length us, event | category | flops | bytes accessed | tf_op | source)
XLA Modules:
  0.0 203.0 jit_solution(1405055053203746862)
XLA Ops:
  7.2 0.0 copy-start
  7.2 0.0 all-gather.5.cloned.1.call-start
  7.3 0.1 fusion.32
  7.3 1.0 copy-done
  8.3 1.5 fusion.4
  9.8 0.1 slice_bitcast_fusion.4
  9.9 0.1 collective-permute-start
  10.0 1.7 collective-permute-done
  11.7 0.9 fusion.7
  12.6 0.0 all-gather.5.cloned.1.call-update
  12.6 0.0 all-gather.7.cloned.1.call-start
  12.6 1.7 constant_dynamic-slice_fusion
  14.4 0.0 copy-start.4
  14.4 2.0 collective-permute-start.1
  16.4 0.0 collective-permute-start.2
  16.4 35.8 %collective-permute-done.1.refs_1_ = bf16[512,1024]{1,0:T(8,128)(2,1)} collective-permute-done((bf16[512,1024]{1,0:T(8,128)(2,1)S(1)}, bf16[512,1024]{1,0:T(8,128)(2,1)}, u32[]{:S(2)}, u32[]{:S(2)}) %collective-permute-start.1) | collective-permute-done | bytes 1048608 | tf_op jit(solution)/shard_map/ppermute | solution.py:43
  52.1 0.0 collective-permute-start.3
  52.1 0.7 pad_maximum_fusion.1
  52.8 0.0 all-gather.7.cloned.1.call-update
  52.8 0.0 collective-permute-done.2.refs_2_
  52.8 2.3 %collective-permute-done.3.refs_3_ = bf16[512,1024]{1,0:T(8,128)(2,1)} collective-permute-done((bf16[512,1024]{1,0:T(8,128)(2,1)}, bf16[512,1024]{1,0:T(8,128)(2,1)}, u32[]{:S(2)}, u32[]{:S(2)}) %collective-permute-start.3) | collective-permute-done | bytes 1048608 | tf_op jit(solution)/shard_map/ppermute | solution.py:43
  55.1 36.2 %all-gather.5.cloned.1.call-done = bf16[16,640,256]{2,1,0:T(8,128)(2,1)} async-done(((bf16[2,640,256]{2,1,0:T(8,128)(2,1)}), bf16[16,640,256]{2,1,0:T(8,128)(2,1)}) %all-gather.5.cloned.1.call-update) | async-done | bytes 5242896 | tf_op jit(solution)/shard_map/all_gather | solution.py:178
  91.4 11.5 %shard_map.76 = (f32[2,2,2,40,1024]{4,3,2,1,0:T(8,128)}, f32[2,2,2,40,1024]{4,3,2,1,0:T(8,128)}, f32[2,2,40,1024]{3,2,1,0:T(8,128)}, f32[2,2,40,1024]{3,2,1,0:T(8,128)}, f32[4,2,40,1024]{3,2,1,0:T(8,128)}) custom-call(bf16[8,2,640,256]{3,2,1,0:T(8,128)(2,1)} %bitcast.84, bf16[512,1024]{1,0:T(8,128)(2,1)} %copy-done.4, ...), custom_call_target="tpu_custom_call" | custom-call | flops 5368709120 | bytes 12582912 | tf_op jit(solution)/shard_map/pallas_call | solution.py:131
  102.9 0.9 collective-permute-start.4
  103.8 2.4 %collective-permute-start.5 = (f32[2,2,2,40,1024]{4,3,2,1,0:T(8,128)}, f32[2,2,2,40,1024]{4,3,2,1,0:T(8,128)S(1)}, u32[]{:S(2)}, u32[]{:S(2)}) collective-permute-start(f32[2,2,2,40,1024]{4,3,2,1,0:T(8,128)} %get-tuple-element.22), channel_id=1, source_target_pairs={{0,16},{1,17},{2,18},{3,19},{4,20},{5,21},{6,22},{7,23},{8,72},{9,... | collective-permute-start | bytes 3932168 | tf_op jit(solution)/shard_map/ppermute | solution.py:43
  106.2 15.8 %collective-permute-done.4 = f32[2,2,2,40,1024]{4,3,2,1,0:T(8,128)S(1)} collective-permute-done((f32[2,2,2,40,1024]{4,3,2,1,0:T(8,128)}, f32[2,2,2,40,1024]{4,3,2,1,0:T(8,128)S(1)}, u32[]{:S(2)}, u32[]{:S(2)}) %collective-permute-start.4) | collective-permute-done | bytes 1310752 | tf_op jit(solution)/shard_map/ppermute | solution.py:43
  122.0 0.0 collective-permute-done.5
  122.0 2.2 %fusion.8 = (f32[2,2,40,1024]{3,2,1,0:T(8,128)S(1)}, f32[2,2,40,1024]{3,2,1,0:T(8,128)S(1)}, f32[2,2,40,1024]{3,2,1,0:T(8,128)S(1)}, f32[2,2,40,1024]{3,2,1,0:T(8,128)S(1)}) fusion(f32[2,2,2,40,1024]{4,3,2,1,0:T(8,128)S(1)} %collective-permute-done.5, f32[4,2,40,1024]{3,2,1,0:T(8,128)} %get-tuple-element.19, ...), kind=kLoop, calls=%fused_computation.9 | loop fusion | flops 655360 | bytes 7864320 | tf_op jit(solution)/shard_map/add | solution.py:154
  124.2 9.0 %all-gather.7.cloned.1.call-done = bf16[16,128,256]{2,1,0:T(8,128)(2,1)} async-done(((bf16[2,128,256]{2,1,0:T(8,128)(2,1)}), bf16[16,128,256]{2,1,0:T(8,128)(2,1)}) %all-gather.7.cloned.1.call-update) | async-done | bytes 1048592 | tf_op jit(solution)/shard_map/all_gather | solution.py:179
  133.3 5.2 %shard_map.77 = (f32[2,2,2,8,1024]{4,3,2,1,0:T(8,128)}, f32[2,2,2,8,1024]{4,3,2,1,0:T(8,128)}, f32[2,2,8,1024]{3,2,1,0:T(8,128)}, f32[2,2,8,1024]{3,2,1,0:T(8,128)}, f32[4,2,8,1024]{3,2,1,0:T(8,128)}) custom-call(bf16[8,2,128,256]{3,2,1,0:T(8,128)(2,1)} %bitcast.83, bf16[512,1024]{1,0:T(8,128)(2,1)} %copy-done.4, ...), custom_call_target="tpu_custom_call" | custom-call | flops 1073741824 | bytes 12582912 | tf_op jit(solution)/shard_map/pallas_call | solution.py:131
  138.5 1.0 collective-permute-start.11
  139.5 2.4 %collective-permute-start.12 = (f32[2,2,2,8,1024]{4,3,2,1,0:T(8,128)}, f32[2,2,2,8,1024]{4,3,2,1,0:T(8,128)S(1)}, u32[]{:S(2)}, u32[]{:S(2)}) collective-permute-start(f32[2,2,2,8,1024]{4,3,2,1,0:T(8,128)} %get-tuple-element.30), channel_id=1, source_target_pairs={{0,16},{1,17},{2,18},{3,19},{4,20},{5,21},{6,22},{7,23},{8,72},{9,... | collective-permute-start | bytes 786440 | tf_op jit(solution)/shard_map/ppermute | solution.py:43
  141.8 0.0 collective-permute-start.8
  141.8 3.2 %collective-permute-start.6 = (f32[2,2,40,1024]{3,2,1,0:T(8,128)S(1)}, f32[2,2,40,1024]{3,2,1,0:T(8,128)S(1)}, u32[]{:S(2)}, u32[]{:S(2)}) collective-permute-start(f32[2,2,40,1024]{3,2,1,0:T(8,128)S(1)} %get-tuple-element.24), channel_id=1, source_target_pairs={{0,16},{1,17},{2,18},{3,19},{4,20},{5,21},{6,22},{7,23},{8,72},{9,... | collective-permute-start | bytes 1966088 | tf_op jit(solution)/shard_map/ppermute | solution.py:43
  145.1 1.3 collective-permute-done.11
  146.4 0.0 collective-permute-done.12
  146.4 1.2 fusion.19
  147.6 0.3 collective-permute-start.15
  147.9 3.1 %collective-permute-start.13 = (f32[2,2,8,1024]{3,2,1,0:T(8,128)S(1)}, f32[2,2,8,1024]{3,2,1,0:T(8,128)S(1)}, u32[]{:S(2)}, u32[]{:S(2)}) collective-permute-start(f32[2,2,8,1024]{3,2,1,0:T(8,128)S(1)} %get-tuple-element.59), channel_id=1, source_target_pairs={{0,16},{1,17},{2,18},{3,19},{4,20},{5,21},{6,22},{7,23},{8,72},{9,... | collective-permute-start | bytes 393224 | tf_op jit(solution)/shard_map/ppermute | solution.py:43
  151.0 9.8 %collective-permute-done.15 = f32[2,2,8,1024]{3,2,1,0:T(8,128)S(1)} collective-permute-done((f32[2,2,8,1024]{3,2,1,0:T(8,128)S(1)}, f32[2,2,8,1024]{3,2,1,0:T(8,128)S(1)}, u32[]{:S(2)}, u32[]{:S(2)}) %collective-permute-start.15) | collective-permute-done | bytes 131104 | tf_op jit(solution)/shard_map/ppermute | solution.py:43
  160.8 2.3 %collective-permute-start.16 = (f32[2,8,1024]{2,1,0:T(8,128)S(1)}, f32[2,8,1024]{2,1,0:T(8,128)S(1)}, u32[]{:S(2)}, u32[]{:S(2)}) collective-permute-start(f32[2,8,1024]{2,1,0:T(8,128)S(1)} %get-tuple-element.55), channel_id=1, source_target_pairs={{0,192},{1,193},{2,194},{3,195},{4,196},{5,197},{6,198},{7,199},{8... | collective-permute-start | bytes 196616 | tf_op jit(solution)/shard_map/ppermute | solution.py:43
  163.1 1.7 collective-permute-start.17
  164.8 0.0 collective-permute-done.8
  164.8 0.1 fusion.12
  164.9 1.9 collective-permute-start.10
  166.8 0.0 collective-permute-done.6
  166.8 1.7 collective-permute-start.9
  168.6 0.0 collective-permute-done.13
  168.6 0.4 collective-permute-start.7
  169.0 0.0 collective-permute-done.16
  169.0 0.1 collective-permute-start.14
  169.1 0.0 collective-permute-done.17
  169.1 8.7 %collective-permute-done.14 = f32[2,8,1024]{2,1,0:T(8,128)S(1)} collective-permute-done((f32[2,8,1024]{2,1,0:T(8,128)S(1)}, f32[2,8,1024]{2,1,0:T(8,128)S(1)}, u32[]{:S(2)}, u32[]{:S(2)}) %collective-permute-start.14) | collective-permute-done | bytes 65568 | tf_op jit(solution)/shard_map/ppermute | solution.py:43
  177.8 0.0 collective-permute-done.10
  177.8 0.0 collective-permute-done.9
  177.8 0.0 collective-permute-done.7
  177.8 0.1 fusion.17
  177.9 0.0 copy-start.1
  177.9 0.0 copy-start.2
  177.9 0.0 copy-start.3
  178.0 0.1 copy.20
  178.1 16.8 %all_to_all.5.rows = f32[8,12,8,128]{3,2,1,0:T(8,128)S(1)} all-to-all(f32[8,12,8,128]{3,2,1,0:T(8,128)S(1)} %bitcast.82), channel_id=1, replica_groups=mesh['dp'=32,'tr'=2,'tc'=4] {'tc','tr'}, dimensions={0} | all-to-all | bytes 786432 | tf_op jit(solution)/shard_map/all_to_all | solution.py:187
  194.9 0.0 copy-done.3
  194.9 1.2 shard_map.78
  (9 shorter events, 0.1 us)
Async XLA Ops:
  7.2 1.1 copy-start
  7.2 84.2 %all-gather.5.cloned.1.call-start = ((), (), s32[]{:S(2)}) async-start(), calls=%async_computation.1 | async-start | bytes 5898240 | tf_op jit(solution)/shard_map/all_gather | solution.py:178
  9.9 1.8 collective-permute-start
  12.6 120.7 %all-gather.7.cloned.1.call-start = ((), (), s32[]{:S(2)}) async-start(), calls=%async_computation.2 | async-start | bytes 1179648 | tf_op jit(solution)/shard_map/all_gather | solution.py:179
  14.4 77.0 %copy-start.4 = (bf16[512,1024]{1,0:T(8,128)(2,1)}, bf16[512,1024]{1,0:T(8,128)(2,1)S(1)}, u32[]{:S(2)}) copy-start(bf16[512,1024]{1,0:T(8,128)(2,1)S(1)} %get-tuple-element.45.refs_0_) | copy-start | bytes 3145732
  14.4 37.8 %collective-permute-start.1 = (bf16[512,1024]{1,0:T(8,128)(2,1)S(1)}, bf16[512,1024]{1,0:T(8,128)(2,1)}, u32[]{:S(2)}, u32[]{:S(2)}) collective-permute-start(bf16[512,1024]{1,0:T(8,128)(2,1)S(1)} %get-tuple-element.44), channel_id=1, source_target_pairs={{0,4},{1,5},{2,6},{3,7},{4,0},{5,1},{6,2},{7,3},{8,12},{9,13},{10,... | collective-permute-start | bytes 3145736 | tf_op jit(solution)/shard_map/ppermute | solution.py:43
  16.4 36.4 %collective-permute-start.2 = (bf16[512,1024]{1,0:T(8,128)(2,1)S(1)}, bf16[512,1024]{1,0:T(8,128)(2,1)}, u32[]{:S(2)}, u32[]{:S(2)}) collective-permute-start(bf16[512,1024]{1,0:T(8,128)(2,1)S(1)} %get-tuple-element.45.refs_0_), channel_id=1, source_target_pairs={{0,8},{1,9},{2,10},{3,11},{4,12},{5,13},{6,14},{7,15},{8,0},{9,1},... | collective-permute-start | bytes 3145736 | tf_op jit(solution)/shard_map/ppermute | solution.py:43
  52.1 3.0 %collective-permute-start.3 = (bf16[512,1024]{1,0:T(8,128)(2,1)}, bf16[512,1024]{1,0:T(8,128)(2,1)}, u32[]{:S(2)}, u32[]{:S(2)}) collective-permute-start(bf16[512,1024]{1,0:T(8,128)(2,1)} %collective-permute-done.1.refs_1_), channel_id=1, source_target_pairs={{0,8},{1,9},{2,10},{3,11},{4,12},{5,13},{6,14},{7,15},{8,0},{9,1},... | collective-permute-start | bytes 3145736 | tf_op jit(solution)/shard_map/ppermute | solution.py:43
  102.9 19.1 %collective-permute-start.4 = (f32[2,2,2,40,1024]{4,3,2,1,0:T(8,128)}, f32[2,2,2,40,1024]{4,3,2,1,0:T(8,128)S(1)}, u32[]{:S(2)}, u32[]{:S(2)}) collective-permute-start(f32[2,2,2,40,1024]{4,3,2,1,0:T(8,128)} %get-tuple-element.20), channel_id=1, source_target_pairs={{0,48},{1,49},{2,50},{3,51},{4,52},{5,53},{6,54},{7,55},{8,200},{9... | collective-permute-start | bytes 3932168 | tf_op jit(solution)/shard_map/ppermute | solution.py:43
  103.8 18.2 %collective-permute-start.5 = (f32[2,2,2,40,1024]{4,3,2,1,0:T(8,128)}, f32[2,2,2,40,1024]{4,3,2,1,0:T(8,128)S(1)}, u32[]{:S(2)}, u32[]{:S(2)}) collective-permute-start(f32[2,2,2,40,1024]{4,3,2,1,0:T(8,128)} %get-tuple-element.22), channel_id=1, source_target_pairs={{0,16},{1,17},{2,18},{3,19},{4,20},{5,21},{6,22},{7,23},{8,72},{9,... | collective-permute-start | bytes 3932168 | tf_op jit(solution)/shard_map/ppermute | solution.py:43
  138.5 7.9 %collective-permute-start.11 = (f32[2,2,2,8,1024]{4,3,2,1,0:T(8,128)}, f32[2,2,2,8,1024]{4,3,2,1,0:T(8,128)S(1)}, u32[]{:S(2)}, u32[]{:S(2)}) collective-permute-start(f32[2,2,2,8,1024]{4,3,2,1,0:T(8,128)} %get-tuple-element.28), channel_id=1, source_target_pairs={{0,48},{1,49},{2,50},{3,51},{4,52},{5,53},{6,54},{7,55},{8,200},{9... | collective-permute-start | bytes 786440 | tf_op jit(solution)/shard_map/ppermute | solution.py:43
  139.5 6.9 %collective-permute-start.12 = (f32[2,2,2,8,1024]{4,3,2,1,0:T(8,128)}, f32[2,2,2,8,1024]{4,3,2,1,0:T(8,128)S(1)}, u32[]{:S(2)}, u32[]{:S(2)}) collective-permute-start(f32[2,2,2,8,1024]{4,3,2,1,0:T(8,128)} %get-tuple-element.30), channel_id=1, source_target_pairs={{0,16},{1,17},{2,18},{3,19},{4,20},{5,21},{6,22},{7,23},{8,72},{9,... | collective-permute-start | bytes 786440 | tf_op jit(solution)/shard_map/ppermute | solution.py:43
  141.8 23.0 %collective-permute-start.8 = (f32[2,2,40,1024]{3,2,1,0:T(8,128)S(1)}, f32[2,2,40,1024]{3,2,1,0:T(8,128)S(1)}, u32[]{:S(2)}, u32[]{:S(2)}) collective-permute-start(f32[2,2,40,1024]{3,2,1,0:T(8,128)S(1)} %get-tuple-element.25), channel_id=1, source_target_pairs={{0,48},{1,49},{2,50},{3,51},{4,52},{5,53},{6,54},{7,55},{8,200},{9... | collective-permute-start | bytes 1966088 | tf_op jit(solution)/shard_map/ppermute | solution.py:43
  141.8 25.0 %collective-permute-start.6 = (f32[2,2,40,1024]{3,2,1,0:T(8,128)S(1)}, f32[2,2,40,1024]{3,2,1,0:T(8,128)S(1)}, u32[]{:S(2)}, u32[]{:S(2)}) collective-permute-start(f32[2,2,40,1024]{3,2,1,0:T(8,128)S(1)} %get-tuple-element.24), channel_id=1, source_target_pairs={{0,16},{1,17},{2,18},{3,19},{4,20},{5,21},{6,22},{7,23},{8,72},{9,... | collective-permute-start | bytes 1966088 | tf_op jit(solution)/shard_map/ppermute | solution.py:43
  147.6 13.2 %collective-permute-start.15 = (f32[2,2,8,1024]{3,2,1,0:T(8,128)S(1)}, f32[2,2,8,1024]{3,2,1,0:T(8,128)S(1)}, u32[]{:S(2)}, u32[]{:S(2)}) collective-permute-start(f32[2,2,8,1024]{3,2,1,0:T(8,128)S(1)} %get-tuple-element.58), channel_id=1, source_target_pairs={{0,48},{1,49},{2,50},{3,51},{4,52},{5,53},{6,54},{7,55},{8,200},{9... | collective-permute-start | bytes 393224 | tf_op jit(solution)/shard_map/ppermute | solution.py:43
  147.9 20.7 %collective-permute-start.13 = (f32[2,2,8,1024]{3,2,1,0:T(8,128)S(1)}, f32[2,2,8,1024]{3,2,1,0:T(8,128)S(1)}, u32[]{:S(2)}, u32[]{:S(2)}) collective-permute-start(f32[2,2,8,1024]{3,2,1,0:T(8,128)S(1)} %get-tuple-element.59), channel_id=1, source_target_pairs={{0,16},{1,17},{2,18},{3,19},{4,20},{5,21},{6,22},{7,23},{8,72},{9,... | collective-permute-start | bytes 393224 | tf_op jit(solution)/shard_map/ppermute | solution.py:43
  160.8 8.2 %collective-permute-start.16 = (f32[2,8,1024]{2,1,0:T(8,128)S(1)}, f32[2,8,1024]{2,1,0:T(8,128)S(1)}, u32[]{:S(2)}, u32[]{:S(2)}) collective-permute-start(f32[2,8,1024]{2,1,0:T(8,128)S(1)} %get-tuple-element.55), channel_id=1, source_target_pairs={{0,192},{1,193},{2,194},{3,195},{4,196},{5,197},{6,198},{7,199},{8... | collective-permute-start | bytes 196616 | tf_op jit(solution)/shard_map/ppermute | solution.py:43
  163.1 6.0 %collective-permute-start.17 = (f32[2,8,1024]{2,1,0:T(8,128)S(1)}, f32[2,8,1024]{2,1,0:T(8,128)S(1)}, u32[]{:S(2)}, u32[]{:S(2)}) collective-permute-start(f32[2,8,1024]{2,1,0:T(8,128)S(1)} %get-tuple-element.54), channel_id=1, source_target_pairs={{0,128},{1,129},{2,130},{3,131},{4,132},{5,133},{6,134},{7,135},{8... | collective-permute-start | bytes 196616 | tf_op jit(solution)/shard_map/ppermute | solution.py:43
  164.9 12.9 %collective-permute-start.10 = (f32[2,40,1024]{2,1,0:T(8,128)S(1)}, f32[2,40,1024]{2,1,0:T(8,128)S(1)}, u32[]{:S(2)}, u32[]{:S(2)}) collective-permute-start(f32[2,40,1024]{2,1,0:T(8,128)S(1)} %get-tuple-element.46), channel_id=1, source_target_pairs={{0,128},{1,129},{2,130},{3,131},{4,132},{5,133},{6,134},{7,135},{8... | collective-permute-start | bytes 983048 | tf_op jit(solution)/shard_map/ppermute | solution.py:43
  166.8 11.0 %collective-permute-start.9 = (f32[2,40,1024]{2,1,0:T(8,128)S(1)}, f32[2,40,1024]{2,1,0:T(8,128)S(1)}, u32[]{:S(2)}, u32[]{:S(2)}) collective-permute-start(f32[2,40,1024]{2,1,0:T(8,128)S(1)} %get-tuple-element.47), channel_id=1, source_target_pairs={{0,192},{1,193},{2,194},{3,195},{4,196},{5,197},{6,198},{7,199},{8... | collective-permute-start | bytes 983048 | tf_op jit(solution)/shard_map/ppermute | solution.py:43
  168.6 9.2 %collective-permute-start.7 = (f32[2,40,1024]{2,1,0:T(8,128)S(1)}, f32[2,40,1024]{2,1,0:T(8,128)S(1)}, u32[]{:S(2)}, u32[]{:S(2)}) collective-permute-start(f32[2,40,1024]{2,1,0:T(8,128)S(1)} %fusion.14), channel_id=1, source_target_pairs={{0,64},{1,65},{2,66},{3,67},{4,68},{5,69},{6,70},{7,71},{8,24},{9,... | collective-permute-start | bytes 983048 | tf_op jit(solution)/shard_map/ppermute | solution.py:43
  169.0 8.8 %collective-permute-start.14 = (f32[2,8,1024]{2,1,0:T(8,128)S(1)}, f32[2,8,1024]{2,1,0:T(8,128)S(1)}, u32[]{:S(2)}, u32[]{:S(2)}) collective-permute-start(f32[2,8,1024]{2,1,0:T(8,128)S(1)} %fusion.24), channel_id=1, source_target_pairs={{0,64},{1,65},{2,66},{3,67},{4,68},{5,69},{6,70},{7,71},{8,24},{9,... | collective-permute-start | bytes 196616 | tf_op jit(solution)/shard_map/ppermute | solution.py:43
  177.9 17.0 %copy-start.1 = (f32[1,12,8192]{2,0,1:T(1,128)S(1)}, f32[1,12,8192]{2,0,1:T(1,128)}, u32[]{:S(2)}) copy-start(f32[1,12,8192]{2,0,1:T(1,128)} %param.7) | copy-start | bytes 1179652
  177.9 17.0 %copy-start.2 = (f32[1,12,8192]{2,0,1:T(1,128)S(1)}, f32[1,12,8192]{2,0,1:T(1,128)}, u32[]{:S(2)}) copy-start(f32[1,12,8192]{2,0,1:T(1,128)} %param.8) | copy-start | bytes 1179652
  177.9 17.0 %copy-start.3 = (f32[1,12,8192]{2,0,1:T(1,128)S(1)}, f32[1,12,8192]{2,0,1:T(1,128)}, u32[]{:S(2)}) copy-start(f32[1,12,8192]{2,0,1:T(1,128)} %param.9) | copy-start | bytes 1179652
Sparse Core Ops, SparseCore 0:
  12.7 78.6 all-gather.4
  93.7 39.4 all-gather.6

commit v7 on v6

v7 whole, which is shorter than its diff:
```python
import jax
import jax.numpy as jnp
from jax import lax
from jax.experimental import pallas as pl
from jax.experimental.pallas import tpu as pltpu
from jax.sharding import PartitionSpec as P

first_decay = 0.9
second_decay = 0.95
learn_rate = 0.0003
weight_decay = 0.1
epsilon = 1e-08
first_fix = 1.0 - 0.9**10
second_fix = 1.0 - 0.95**10

AXES = ("dp", "tr", "tc")
SIDE = 4
ROWS = 48
GROUP = 4
QUARTER = 4 * ROWS


def moves(where):
    pairs = []
    for dp in range(32):
        for tr in range(2):
            for tc in range(4):
                y, x, core, z = where(dp // 8, dp // 2 % 4, dp % 2, 2 * tc + tr)
                to = (y % 4 * 8 + x % 4 * 2 + core % 2, z % 2, z % 8 // 2)
                pairs.append(((dp * 2 + tr) * 4 + tc, (to[0] * 2 + to[1]) * 4 + to[2]))
    return pairs


def onward(core):
    return 1 - 2 * core


def send(array, pairs):
    return lax.ppermute(array, AXES, pairs)


OTHER_CORE = moves(lambda y, x, core, z: (y, x, 1 - core, z))
PAIR = moves(lambda y, x, core, z: (y, x, core, z ^ 1))
MATE = [moves(lambda y, x, core, z: (y + 2 * (g // 2), x + 2 * (g % 2), core, z)) for g in range(GROUP)]
NEXT_X = moves(lambda y, x, core, z: (y, x + onward(core), core, z))
NEXT_Y = moves(lambda y, x, core, z: (y + onward(core), x, core, z))


def feature_order(activations):
    dp = lax.axis_index("dp")
    my_y, my_x, core = dp // 8, dp // 2 % 4, dp % 2
    column = lax.broadcasted_iota(jnp.int32, (1, 2 * GROUP * QUARTER), 1)
    row, block = column % ROWS, column // ROWS
    far_x, far_y, mate, half = block % 2, block // 2 % 2, block // 4 % GROUP, block // (4 * GROUP)
    target = jnp.where(half == 0, core, 1 - core)
    x = (my_x + 2 * (mate % 2) + far_x * onward(target) + SIDE) % SIDE
    y = (my_y + 2 * (mate // 2) + far_y * onward(target) + SIDE) % SIDE
    source = ((y * SIDE + x) * 2 + target) * ROWS + row
    feature = lax.broadcasted_iota(jnp.int32, (activations.shape[1], column.shape[1]), 0)
    chosen = (feature == source).astype(activations.dtype)
    ordered = lax.dot_general(chosen, activations, (((0,), (1,)), ((), ())), preferred_element_type=jnp.float32)
    return ordered.astype(activations.dtype)


def product_kernel(gathered, *refs):
    cots = refs[: 4 * GROUP]
    a_send, a_keep, b_send, b_keep = refs[4 * GROUP : 4 * GROUP + 4]
    act, cot, act_sem, cot_sem = refs[4 * GROUP + 4 :]
    tr = lax.axis_index("tr")
    replicas, quarter, tokens = gathered.shape[1:]
    depth = 4 * tokens

    def copies_of(replica):
        copies = []
        for z in range(8):
            window = pl.ds(replica * depth + z // 2 * tokens, tokens)
            target = act.at[pl.ds(z % 2 * quarter, quarter), window]
            copies.append(pltpu.make_async_copy(gathered.at[z, replica], target, act_sem.at[8 * replica + z]))
        for came in range(2):
            half = 1 - tr if came else tr
            start = pl.multiple_of(replica * depth + half * 2 * tokens, 2 * tokens)
            n = 2 * replica + came
            copies.append(pltpu.make_async_copy(cots[n], cot.at[pl.ds(start, 2 * tokens)], cot_sem.at[n]))
        return copies

    for replica in range(replicas):
        for copy in copies_of(replica):
            copy.start()
    total = None
    for replica in range(replicas):
        for copy in copies_of(replica):
            copy.wait()
        window = slice(replica * depth, (replica + 1) * depth)
        term = jnp.dot(act[:, window], cot[window], preferred_element_type=jnp.float32)
        total = term if total is None else total + term
    half = total.shape[1] // 2
    total = total.reshape(2, 2, 2, ROWS, 2 * half)
    for far in range(2):
        a_send[far] = total[:, far, 1, :, :half]
        a_keep[far] = total[:, far, 0, :, :half]
        b_send[far] = total[:, 1, far, :, half:]
        b_keep[far] = total[:, 0, far, :, half:]


def product(gathered, cots):
    replicas, quarter, tokens = gathered.shape[1:]
    units = cots[0].shape[1]
    part = jax.ShapeDtypeStruct((2, 2, ROWS, units // 2), jnp.float32)
    return pl.pallas_call(
        product_kernel,
        in_specs=[pl.BlockSpec(memory_space=pl.ANY)] * (1 + len(cots)),
        out_shape=[part] * 4,
        scratch_shapes=[
            pltpu.VMEM((2 * quarter, replicas * 4 * tokens), gathered.dtype),
            pltpu.VMEM((replicas * 4 * tokens, units), cots[0].dtype),
            pltpu.SemaphoreType.DMA((8 * replicas,)),
            pltpu.SemaphoreType.DMA((2 * replicas,)),
        ],
        compiler_params=pltpu.CompilerParams(vmem_limit_bytes=60 * 2**20),
        cost_estimate=pl.CostEstimate(
            flops=2 * 2 * quarter * replicas * 4 * tokens * units, bytes_accessed=28 * 2**20, transcendentals=0
        ),
    )(gathered, *cots)


def shards(activations, cotangent, master, moment, second):
    tr = lax.axis_index("tr")
    units = cotangent.shape[1] // 2
    ordered = feature_order(activations).reshape(2, GROUP, QUARTER, activations.shape[0])
    both = jnp.stack([ordered[0], send(ordered[1], OTHER_CORE)], axis=1)
    shared = jnp.stack([both[0]] + [send(both[g], MATE[g]) for g in (1, 2, 3)])
    away = lax.dynamic_slice_in_dim(cotangent, (1 - tr) * units, units, 1)
    own_keep = lax.dynamic_slice_in_dim(cotangent, tr * units, units, 1)
    own_came = send(away, PAIR)
    early, shared = lax.optimization_barrier((own_keep, shared))
    shared = shared.reshape(2 * GROUP, QUARTER, activations.shape[0])
    gathered = lax.all_gather(shared, ("tc", "tr"), axis=0)
    keep = [own_keep, send(early, MATE[1]), send(early, MATE[2])]
    keep.append(send(keep[1], MATE[2]))
    came = [own_came, send(own_came, MATE[1]), send(own_came, MATE[2])]
    came.append(send(came[2], MATE[1]))
    cots = []
    for g in range(GROUP):
        cots += [keep[g], came[g], send(keep[g], OTHER_CORE), send(came[g], OTHER_CORE)]
    a_send, a_keep, b_send, b_keep = product(gathered, cots)
    a_came, b_came = send(a_send, NEXT_X), send(b_send, NEXT_Y)
    a_last = send(a_keep[1] + a_came[1], NEXT_Y)
    b_last = send(b_keep[1] + b_came[1], NEXT_X)
    rows = jnp.concatenate([a_keep[0] + a_came[0] + a_last, b_keep[0] + b_came[0] + b_last], axis=2)
    rows = rows.reshape(2, 4, ROWS // 4, 8, units // 8)
    rows = rows.swapaxes(0, 1).reshape(8, ROWS // 4, 8, units // 8)
    rows = lax.all_to_all(rows, ("tc", "tr"), split_axis=0, concat_axis=0, tiled=True)
    return updated(rows, master, moment, second)


def updated(rows, master, moment, second):
    wide = (rows.shape[1], rows.shape[0] * rows.shape[2], rows.shape[3])
    flat = [array.reshape(wide) for array in (master, moment, second)]
    outs = pl.pallas_call(
        update_kernel,
        out_shape=[jax.ShapeDtypeStruct(wide, jnp.float32)] * 3,
        compiler_params=pltpu.CompilerParams(vmem_limit_bytes=16 * 2**20),
    )(rows, *flat)
    return tuple(out.reshape(master.shape) for out in outs)


def update_kernel(rows, master, moment, second, new_master, new_moment, new_second):
    for z in range(8):
        place = (slice(None), pl.ds(z * 8, 8), slice(None))
        grad = rows[z]
        first = first_decay * moment[place] + (1.0 - first_decay) * grad
        square = second_decay * second[place] + (1.0 - second_decay) * grad * grad
        old = master[place]
        update = first / first_fix / (jnp.sqrt(square / second_fix) + epsilon)
        new_moment[place] = first
        new_second[place] = square
        new_master[place] = old - learn_rate * (update + weight_decay * old)


def solution(mesh):
    state = P("tr", ("dp", "tc"), None)
    return jax.shard_map(
        shards,
        mesh=mesh,
        in_specs=(P(("dp", "tc"), "tr"), P(("dp", "tr"), "tc"), state, state, state),
        out_specs=(state, state, state),
        check_vma=False,
    )
```

time: 203 us -> 181 us (0.89)
  waiting for transfers between devices: 121 us -> 95.7 us
  blocking collectives: 16.8 us -> 24.4 us
  Pallas kernels: 17.9 us -> 13.6 us
  starting transfers between devices: 23.5 us -> 20.9 us
    all_gather x2 -> x1, waiting for transfers between devices: 45.3 us -> 0.01 us  [shards(): gathered = lax.all_gather(shared, ('tc', 'tr'), axis=0)]
    ppermute x18 -> x23, waiting for transfers between devices: 75.4 us -> 95.6 us  [send(): return lax.ppermute(array, AXES, pairs)]
    all_to_all x1, blocking collectives: 16.8 us -> 24.4 us  [shards(): lax.all_to_all(rows, ('tc', 'tr'), split_axis=0, concat_axis=0, tiled=True)]
    pallas_call x2 -> x1, Pallas kernels: 16.7 us -> 12.4 us  [product(): pl.pallas_call(product_kernel, in_specs=[pl.BlockSpec(memory_space=pl.ANY...]
    ppermute x18 -> x23, starting transfers between devices: 23.5 us -> 20.9 us  [send(): return lax.ppermute(array, AXES, pairs)]
  transfers between devices with their start and end apart: 20 -> 24, of which waited for: 9 -> 13; matrix products, arithmetic and copies ran while one was open for 3% -> 2% of each run, Pallas kernels for 6% -> 0%
where the time goes in v7:
time: 181 us
  waiting for transfers between devices  95.7 us (53%)
  blocking collectives  24.4 us (13%)
  starting transfers between devices  20.9 us (12%)
  between operations  14.3 us (8%)
  Pallas kernels  13.6 us (8%)
  other arithmetic  6.76 us (4%)
  local copies, waits for them, and re-layouts  3.81 us (2%)
    ppermute x23, waiting for transfers between devices, send(): return lax.ppermute(array, AXES, pairs)  95.6 us
    all_to_all x1, blocking collectives, shards(): lax.all_to_all(rows, ('tc', 'tr'), split_axis=0, concat_axis=0, tiled=True)  24.4 us
    ppermute x23, starting transfers between devices, send(): return lax.ppermute(array, AXES, pairs)  20.9 us
    pallas_call x1, Pallas kernels, product(): pl.pallas_call(product_kernel, in_specs=[pl.BlockSpec(memory_space=pl.ANY...  12.4 us
  transfers between devices with their start and end apart: 24, of which 13 were waited for; matrix products, arithmetic and copies ran while one was open for 2% of the time, Pallas kernels for 0%

profile of v7, /device:TPU:6, one launch (start us, length us, event | category | flops | bytes accessed | tf_op | source)
XLA Modules:
  0.0 181.0 jit_solution(12671519672310517009)
XLA Ops:
  7.2 0.0 copy-start
  7.2 0.0 all-gather.2.cloned.1.call-start
  7.3 0.1 fusion.34
  7.3 1.0 copy-done
  8.3 1.5 fusion.4
  9.8 0.1 fusion.53
  9.9 0.1 collective-permute-start
  10.0 1.7 collective-permute-done
  11.7 0.8 fusion.10
  12.5 1.4 collective-permute-start.1
  13.9 4.8 %collective-permute-start.3 = (bf16[2,192,256]{2,1,0:T(8,128)(2,1)}, bf16[2,192,256]{2,1,0:T(8,128)(2,1)}, u32[]{:S(2)}, u32[]{:S(2)}) collective-permute-start(bf16[2,192,256]{2,1,0:T(8,128)(2,1)} %get-tuple-element.34), channel_id=1, source_target_pairs={{0,160},{1,161},{2,162},{3,163},{4,164},{5,165},{6,166},{7,167},{8... | collective-permute-start | bytes 589832 | tf_op jit(solution)/shard_map/ppermute | solution.py:39
  18.6 0.3 collective-permute-start.2
  19.0 1.5 constant_dynamic-slice_fusion
  20.5 1.0 collective-permute-done.1
  21.5 6.7 %collective-permute-done.3 = bf16[2,192,256]{2,1,0:T(8,128)(2,1)} collective-permute-done((bf16[2,192,256]{2,1,0:T(8,128)(2,1)}, bf16[2,192,256]{2,1,0:T(8,128)(2,1)}, u32[]{:S(2)}, u32[]{:S(2)}) %collective-permute-start.3) | collective-permute-done | bytes 196640 | tf_op jit(solution)/shard_map/ppermute | solution.py:39
  28.2 2.7 %collective-permute-done.2 = bf16[2,192,256]{2,1,0:T(8,128)(2,1)} collective-permute-done((bf16[2,192,256]{2,1,0:T(8,128)(2,1)S(1)}, bf16[2,192,256]{2,1,0:T(8,128)(2,1)}, u32[]{:S(2)}, u32[]{:S(2)}) %collective-permute-start.2) | collective-permute-done | bytes 196640 | tf_op jit(solution)/shard_map/ppermute | solution.py:39
  30.8 2.0 %pad_maximum_fusion = bf16[4,2,192,256]{3,2,1,0:T(8,128)(2,1)} fusion(bf16[1,2,192,256]{3,2,1,0:T(8,128)(2,1)} %bitcast.8, bf16[1,2,192,256]{3,2,1,0:T(8,128)(2,1)} %bitcast.6, bf16[1,2,192,256]{3,2,1,0:T(8,128)(2,1)S(1)} %bitcast.55, bf16[1,2,192,256]{3,2,1,0:T(8,128)(2,1)S(1)} %get-tuple-element.32), kind=kLoop, calls=%fused_computation.11 | loop fusion | flops 1179648 | bytes 1572864 | tf_op jit(solution)/shard_map/stack | solution.py:131
  32.9 0.0 all-gather.2.cloned.1.call-update
  32.9 2.0 %collective-permute-start.4 = (bf16[512,1024]{1,0:T(8,128)(2,1)}, bf16[512,1024]{1,0:T(8,128)(2,1)S(1)}, u32[]{:S(2)}, u32[]{:S(2)}) collective-permute-start(bf16[512,1024]{1,0:T(8,128)(2,1)} %get-tuple-element.30), channel_id=1, source_target_pairs={{0,4},{1,5},{2,6},{3,7},{4,0},{5,1},{6,2},{7,3},{8,12},{9,13},{10,... | collective-permute-start | bytes 3145736 | tf_op jit(solution)/shard_map/ppermute | solution.py:39
  34.9 0.3 collective-permute-start.11
  35.2 1.4 collective-permute-start.7
  36.6 33.9 %collective-permute-done.4.refs_1_ = bf16[512,1024]{1,0:T(8,128)(2,1)S(1)} collective-permute-done((bf16[512,1024]{1,0:T(8,128)(2,1)}, bf16[512,1024]{1,0:T(8,128)(2,1)S(1)}, u32[]{:S(2)}, u32[]{:S(2)}) %collective-permute-start.4) | collective-permute-done | bytes 1048608 | tf_op jit(solution)/shard_map/ppermute | solution.py:39
  70.5 1.4 collective-permute-start.8
  71.9 0.0 collective-permute-done.5.refs_2_
  71.9 0.0 collective-permute-start.6
  71.9 0.0 collective-permute-done.11.refs_8_
  71.9 0.5 collective-permute-start.13
  72.4 0.0 collective-permute-done.7.refs_4_
  72.4 3.5 %collective-permute-start.15 = (bf16[512,1024]{1,0:T(8,128)(2,1)S(1)}, bf16[512,1024]{1,0:T(8,128)(2,1)S(1)}, u32[]{:S(2)}, u32[]{:S(2)}) collective-permute-start(bf16[512,1024]{1,0:T(8,128)(2,1)S(1)} %collective-permute-done.7.refs_4_), channel_id=1, source_target_pairs={{0,128},{1,129},{2,130},{3,131},{4,132},{5,133},{6,134},{7,135},{8... | collective-permute-start | bytes 3145736 | tf_op jit(solution)/shard_map/ppermute | solution.py:39
  75.9 22.2 %collective-permute-done.12.refs_9_ = bf16[512,1024]{1,0:T(8,128)(2,1)S(1)} collective-permute-done((bf16[512,1024]{1,0:T(8,128)(2,1)S(1)}, bf16[512,1024]{1,0:T(8,128)(2,1)S(1)}, u32[]{:S(2)}, u32[]{:S(2)}) %collective-permute-start.12) | collective-permute-done | bytes 1048608 | tf_op jit(solution)/shard_map/ppermute | solution.py:39
  98.1 1.4 collective-permute-start.16
  99.5 0.0 collective-permute-done.8.refs_5_
  99.5 0.0 collective-permute-start.9
  99.5 0.0 collective-permute-done.6.refs_3_
  99.5 0.6 collective-permute-start.14
  100.1 0.0 collective-permute-done.13.refs_10_
  100.1 0.1 collective-permute-start.10
  100.2 13.5 %collective-permute-done.15.refs_12_ = bf16[512,1024]{1,0:T(8,128)(2,1)S(1)} collective-permute-done((bf16[512,1024]{1,0:T(8,128)(2,1)S(1)}, bf16[512,1024]{1,0:T(8,128)(2,1)S(1)}, u32[]{:S(2)}, u32[]{:S(2)}) %collective-permute-start.15) | collective-permute-done | bytes 1048608 | tf_op jit(solution)/shard_map/ppermute | solution.py:39
  113.7 0.0 collective-permute-start.17
  113.7 0.7 collective-permute-done.16.refs_13_
  114.4 0.0 collective-permute-start.18
  114.4 0.0 collective-permute-done.9.refs_6_
  114.5 1.8 %collective-permute-done.17.refs_14_ = bf16[512,1024]{1,0:T(8,128)(2,1)S(1)} collective-permute-done((bf16[512,1024]{1,0:T(8,128)(2,1)S(1)}, bf16[512,1024]{1,0:T(8,128)(2,1)S(1)}, u32[]{:S(2)}, u32[]{:S(2)}) %collective-permute-start.17) | collective-permute-done | bytes 1048608 | tf_op jit(solution)/shard_map/ppermute | solution.py:39
  116.4 0.1 copy-done.17
  116.4 1.0 copy-done.18
  117.4 0.5 collective-permute-done.18.refs_15_
  118.0 12.4 %shard_map.76 = (f32[2,2,48,512]{3,2,1,0:T(8,128)}, f32[2,2,48,512]{3,2,1,0:T(8,128)}, f32[2,2,48,512]{3,2,1,0:T(8,128)}, f32[2,2,48,512]{3,2,1,0:T(8,128)}) custom-call(bf16[8,8,192,256]{3,2,1,0:T(8,128)(2,1)} %all-gather.2.cloned.1.call-done.gathered, bf16[512,1024]{1,0:T(8,128)(2,1)} %get-tuple-element.13.refs_0_, bf16[512,1024]{1,0:T(8,128)(2,1)} %copy-done.5, ...), custom_call_target="tpu_custom_call" | custom-call | flops 6442450944 | bytes 29360128 | tf_op jit(solution)/shard_map/pallas_call | solution.py:109
  130.4 0.0 copy-start.1
  130.4 0.0 copy-start.2
  130.4 0.0 copy-start.3
  130.4 0.6 collective-permute-start.19
  131.0 0.4 collective-permute-start.21
  131.4 7.1 %collective-permute-done.19 = f32[2,2,48,512]{3,2,1,0:T(8,128)S(1)} collective-permute-done((f32[2,2,48,512]{3,2,1,0:T(8,128)}, f32[2,2,48,512]{3,2,1,0:T(8,128)S(1)}, u32[]{:S(2)}, u32[]{:S(2)}) %collective-permute-start.19) | collective-permute-done | bytes 393248 | tf_op jit(solution)/shard_map/ppermute | solution.py:39
  138.5 1.0 fusion.16
  139.5 0.6 collective-permute-start.20
  140.0 0.2 collective-permute-done.21
  140.2 1.0 fusion.13
  141.2 1.5 collective-permute-start.22
  142.7 3.7 %collective-permute-done.20 = f32[2,48,512]{2,1,0:T(8,128)S(1)} collective-permute-done((f32[2,48,512]{2,1,0:T(8,128)S(1)}, f32[2,48,512]{2,1,0:T(8,128)S(1)}, u32[]{:S(2)}, u32[]{:S(2)}) %collective-permute-start.20) | collective-permute-done | bytes 196640 | tf_op jit(solution)/shard_map/ppermute | solution.py:39
  146.4 1.0 fusion.18
  147.4 1.0 fusion.15
  148.4 0.1 copy.28
  148.5 24.4 %all_to_all.5.rows = f32[8,12,8,128]{3,2,1,0:T(8,128)S(1)} all-to-all(f32[8,12,8,128]{3,2,1,0:T(8,128)S(1)} %bitcast.51), channel_id=1, replica_groups=mesh['dp'=32,'tr'=2,'tc'=4] {'tc','tr'}, dimensions={0} | all-to-all | bytes 786432 | tf_op jit(solution)/shard_map/all_to_all | solution.py:152
  173.0 1.2 shard_map.77
  (39 shorter events, 0.1 us)
Async XLA Ops:
  7.2 1.1 copy-start
  7.2 110.8 %all-gather.2.cloned.1.call-start = ((), (), s32[]{:S(2)}) async-start(), calls=%async_computation.1 | async-start | bytes 7077888 | tf_op jit(solution)/shard_map/all_gather | solution.py:137
  8.3 10.7 %copy-start.4 = (bf16[512,2048]{1,0:T(8,128)(2,1)S(1)}, bf16[512,2048]{1,0:T(8,128)(2,1)}, u32[]{:S(2)}) copy-start(bf16[512,2048]{1,0:T(8,128)(2,1)} %param.6) | copy-start | bytes 6291460
  9.9 1.8 collective-permute-start
  12.5 9.0 %collective-permute-start.1 = (bf16[2,192,256]{2,1,0:T(8,128)(2,1)}, bf16[2,192,256]{2,1,0:T(8,128)(2,1)S(1)}, u32[]{:S(2)}, u32[]{:S(2)}) collective-permute-start(bf16[2,192,256]{2,1,0:T(8,128)(2,1)} %get-tuple-element.33), channel_id=1, source_target_pairs={{0,32},{1,33},{2,34},{3,35},{4,36},{5,37},{6,38},{7,39},{8,40},{9,... | collective-permute-start | bytes 589832 | tf_op jit(solution)/shard_map/ppermute | solution.py:39
  13.9 14.3 %collective-permute-start.3 = (bf16[2,192,256]{2,1,0:T(8,128)(2,1)}, bf16[2,192,256]{2,1,0:T(8,128)(2,1)}, u32[]{:S(2)}, u32[]{:S(2)}) collective-permute-start(bf16[2,192,256]{2,1,0:T(8,128)(2,1)} %get-tuple-element.34), channel_id=1, source_target_pairs={{0,160},{1,161},{2,162},{3,163},{4,164},{5,165},{6,166},{7,167},{8... | collective-permute-start | bytes 589832 | tf_op jit(solution)/shard_map/ppermute | solution.py:39
  18.6 12.2 %collective-permute-start.2 = (bf16[2,192,256]{2,1,0:T(8,128)(2,1)S(1)}, bf16[2,192,256]{2,1,0:T(8,128)(2,1)}, u32[]{:S(2)}, u32[]{:S(2)}) collective-permute-start(bf16[2,192,256]{2,1,0:T(8,128)(2,1)S(1)} %get-tuple-element.35), channel_id=1, source_target_pairs={{0,128},{1,129},{2,130},{3,131},{4,132},{5,133},{6,134},{7,135},{8... | collective-permute-start | bytes 589832 | tf_op jit(solution)/shard_map/ppermute | solution.py:39
  32.9 37.6 %collective-permute-start.4 = (bf16[512,1024]{1,0:T(8,128)(2,1)}, bf16[512,1024]{1,0:T(8,128)(2,1)S(1)}, u32[]{:S(2)}, u32[]{:S(2)}) collective-permute-start(bf16[512,1024]{1,0:T(8,128)(2,1)} %get-tuple-element.30), channel_id=1, source_target_pairs={{0,4},{1,5},{2,6},{3,7},{4,0},{5,1},{6,2},{7,3},{8,12},{9,13},{10,... | collective-permute-start | bytes 3145736 | tf_op jit(solution)/shard_map/ppermute | solution.py:39
  34.9 37.0 %collective-permute-start.5 = (bf16[512,1024]{1,0:T(8,128)(2,1)}, bf16[512,1024]{1,0:T(8,128)(2,1)S(1)}, u32[]{:S(2)}, u32[]{:S(2)}) collective-permute-start(bf16[512,1024]{1,0:T(8,128)(2,1)} %get-tuple-element.13.refs_0_), channel_id=1, source_target_pairs={{0,8},{1,9},{2,10},{3,11},{4,12},{5,13},{6,14},{7,15},{8,0},{9,1},... | collective-permute-start | bytes 3145736 | tf_op jit(solution)/shard_map/ppermute | solution.py:39
  34.9 37.0 %collective-permute-start.11 = (bf16[512,1024]{1,0:T(8,128)(2,1)}, bf16[512,1024]{1,0:T(8,128)(2,1)S(1)}, u32[]{:S(2)}, u32[]{:S(2)}) collective-permute-start(bf16[512,1024]{1,0:T(8,128)(2,1)} %get-tuple-element.13.refs_0_), channel_id=1, source_target_pairs={{0,128},{1,129},{2,130},{3,131},{4,132},{5,133},{6,134},{7,135},{8... | collective-permute-start | bytes 3145736 | tf_op jit(solution)/shard_map/ppermute | solution.py:39
  35.2 37.2 %collective-permute-start.7 = (bf16[512,1024]{1,0:T(8,128)(2,1)}, bf16[512,1024]{1,0:T(8,128)(2,1)S(1)}, u32[]{:S(2)}, u32[]{:S(2)}) collective-permute-start(bf16[512,1024]{1,0:T(8,128)(2,1)} %get-tuple-element.13.refs_0_), channel_id=1, source_target_pairs={{0,32},{1,33},{2,34},{3,35},{4,36},{5,37},{6,38},{7,39},{8,40},{9,... | collective-permute-start | bytes 3145736 | tf_op jit(solution)/shard_map/ppermute | solution.py:39
  70.5 47.5 %copy-start.5 = (bf16[512,1024]{1,0:T(8,128)(2,1)}, bf16[512,1024]{1,0:T(8,128)(2,1)S(1)}, u32[]{:S(2)}) copy-start(bf16[512,1024]{1,0:T(8,128)(2,1)S(1)} %collective-permute-done.4.refs_1_) | copy-start | bytes 3145732
  70.5 27.6 %collective-permute-start.12 = (bf16[512,1024]{1,0:T(8,128)(2,1)S(1)}, bf16[512,1024]{1,0:T(8,128)(2,1)S(1)}, u32[]{:S(2)}, u32[]{:S(2)}) collective-permute-start(bf16[512,1024]{1,0:T(8,128)(2,1)S(1)} %collective-permute-done.4.refs_1_), channel_id=1, source_target_pairs={{0,128},{1,129},{2,130},{3,131},{4,132},{5,133},{6,134},{7,135},{8... | collective-permute-start | bytes 3145736 | tf_op jit(solution)/shard_map/ppermute | solution.py:39
  70.5 29.0 %collective-permute-start.8 = (bf16[512,1024]{1,0:T(8,128)(2,1)S(1)}, bf16[512,1024]{1,0:T(8,128)(2,1)S(1)}, u32[]{:S(2)}, u32[]{:S(2)}) collective-permute-start(bf16[512,1024]{1,0:T(8,128)(2,1)S(1)} %collective-permute-done.4.refs_1_), channel_id=1, source_target_pairs={{0,32},{1,33},{2,34},{3,35},{4,36},{5,37},{6,38},{7,39},{8,40},{9,... | collective-permute-start | bytes 3145736 | tf_op jit(solution)/shard_map/ppermute | solution.py:39
  71.9 46.1 %copy-start.6 = (bf16[512,1024]{1,0:T(8,128)(2,1)}, bf16[512,1024]{1,0:T(8,128)(2,1)S(1)}, u32[]{:S(2)}) copy-start(bf16[512,1024]{1,0:T(8,128)(2,1)S(1)} %collective-permute-done.5.refs_2_) | copy-start | bytes 3145732
  71.9 27.6 %collective-permute-start.6 = (bf16[512,1024]{1,0:T(8,128)(2,1)S(1)}, bf16[512,1024]{1,0:T(8,128)(2,1)S(1)}, u32[]{:S(2)}, u32[]{:S(2)}) collective-permute-start(bf16[512,1024]{1,0:T(8,128)(2,1)S(1)} %collective-permute-done.4.refs_1_), channel_id=1, source_target_pairs={{0,8},{1,9},{2,10},{3,11},{4,12},{5,13},{6,14},{7,15},{8,0},{9,1},... | collective-permute-start | bytes 3145736 | tf_op jit(solution)/shard_map/ppermute | solution.py:39
  71.9 27.6 %copy-start.7 = (bf16[512,1024]{1,0:T(8,128)(2,1)}, bf16[512,1024]{1,0:T(8,128)(2,1)S(1)}, u32[]{:S(2)}) copy-start(bf16[512,1024]{1,0:T(8,128)(2,1)S(1)} %collective-permute-done.11.refs_8_) | copy-start | bytes 3145732
  71.9 28.2 %collective-permute-start.13 = (bf16[512,1024]{1,0:T(8,128)(2,1)S(1)}, bf16[512,1024]{1,0:T(8,128)(2,1)S(1)}, u32[]{:S(2)}, u32[]{:S(2)}) collective-permute-start(bf16[512,1024]{1,0:T(8,128)(2,1)S(1)} %collective-permute-done.11.refs_8_), channel_id=1, source_target_pairs={{0,8},{1,9},{2,10},{3,11},{4,12},{5,13},{6,14},{7,15},{8,0},{9,1},... | collective-permute-start | bytes 3145736 | tf_op jit(solution)/shard_map/ppermute | solution.py:39
  72.4 27.7 %copy-start.8 = (bf16[512,1024]{1,0:T(8,128)(2,1)}, bf16[512,1024]{1,0:T(8,128)(2,1)S(1)}, u32[]{:S(2)}) copy-start(bf16[512,1024]{1,0:T(8,128)(2,1)S(1)} %collective-permute-done.7.refs_4_) | copy-start | bytes 3145732
  72.4 41.3 %collective-permute-start.15 = (bf16[512,1024]{1,0:T(8,128)(2,1)S(1)}, bf16[512,1024]{1,0:T(8,128)(2,1)S(1)}, u32[]{:S(2)}, u32[]{:S(2)}) collective-permute-start(bf16[512,1024]{1,0:T(8,128)(2,1)S(1)} %collective-permute-done.7.refs_4_), channel_id=1, source_target_pairs={{0,128},{1,129},{2,130},{3,131},{4,132},{5,133},{6,134},{7,135},{8... | collective-permute-start | bytes 3145736 | tf_op jit(solution)/shard_map/ppermute | solution.py:39
  98.1 16.3 %copy-start.9 = (bf16[512,1024]{1,0:T(8,128)(2,1)}, bf16[512,1024]{1,0:T(8,128)(2,1)S(1)}, u32[]{:S(2)}) copy-start(bf16[512,1024]{1,0:T(8,128)(2,1)S(1)} %collective-permute-done.12.refs_9_) | copy-start | bytes 3145732
  98.1 16.3 %collective-permute-start.16 = (bf16[512,1024]{1,0:T(8,128)(2,1)S(1)}, bf16[512,1024]{1,0:T(8,128)(2,1)S(1)}, u32[]{:S(2)}, u32[]{:S(2)}) collective-permute-start(bf16[512,1024]{1,0:T(8,128)(2,1)S(1)} %collective-permute-done.12.refs_9_), channel_id=1, source_target_pairs={{0,32},{1,33},{2,34},{3,35},{4,36},{5,37},{6,38},{7,39},{8,40},{9,... | collective-permute-start | bytes 3145736 | tf_op jit(solution)/shard_map/ppermute | solution.py:39
  99.5 15.0 %copy-start.10 = (bf16[512,1024]{1,0:T(8,128)(2,1)}, bf16[512,1024]{1,0:T(8,128)(2,1)S(1)}, u32[]{:S(2)}) copy-start(bf16[512,1024]{1,0:T(8,128)(2,1)S(1)} %collective-permute-done.8.refs_5_) | copy-start | bytes 3145732
  99.5 15.0 %collective-permute-start.9 = (bf16[512,1024]{1,0:T(8,128)(2,1)S(1)}, bf16[512,1024]{1,0:T(8,128)(2,1)S(1)}, u32[]{:S(2)}, u32[]{:S(2)}) collective-permute-start(bf16[512,1024]{1,0:T(8,128)(2,1)S(1)} %collective-permute-done.7.refs_4_), channel_id=1, source_target_pairs={{0,8},{1,9},{2,10},{3,11},{4,12},{5,13},{6,14},{7,15},{8,0},{9,1},... | collective-permute-start | bytes 3145736 | tf_op jit(solution)/shard_map/ppermute | solution.py:39
  99.5 15.0 %copy-start.11 = (bf16[512,1024]{1,0:T(8,128)(2,1)}, bf16[512,1024]{1,0:T(8,128)(2,1)S(1)}, u32[]{:S(2)}) copy-start(bf16[512,1024]{1,0:T(8,128)(2,1)S(1)} %collective-permute-done.6.refs_3_) | copy-start | bytes 3145732
  99.5 14.9 %collective-permute-start.14 = (bf16[512,1024]{1,0:T(8,128)(2,1)S(1)}, bf16[512,1024]{1,0:T(8,128)(2,1)S(1)}, u32[]{:S(2)}, u32[]{:S(2)}) collective-permute-start(bf16[512,1024]{1,0:T(8,128)(2,1)S(1)} %collective-permute-done.12.refs_9_), channel_id=1, source_target_pairs={{0,8},{1,9},{2,10},{3,11},{4,12},{5,13},{6,14},{7,15},{8,0},{9,1},... | collective-permute-start | bytes 3145736 | tf_op jit(solution)/shard_map/ppermute | solution.py:39
  100.1 16.2 %copy-start.12 = (bf16[512,1024]{1,0:T(8,128)(2,1)}, bf16[512,1024]{1,0:T(8,128)(2,1)S(1)}, u32[]{:S(2)}) copy-start(bf16[512,1024]{1,0:T(8,128)(2,1)S(1)} %collective-permute-done.13.refs_10_) | copy-start | bytes 3145732
  100.1 14.4 %collective-permute-start.10 = (bf16[512,1024]{1,0:T(8,128)(2,1)S(1)}, bf16[512,1024]{1,0:T(8,128)(2,1)S(1)}, u32[]{:S(2)}, u32[]{:S(2)}) collective-permute-start(bf16[512,1024]{1,0:T(8,128)(2,1)S(1)} %collective-permute-done.8.refs_5_), channel_id=1, source_target_pairs={{0,8},{1,9},{2,10},{3,11},{4,12},{5,13},{6,14},{7,15},{8,0},{9,1},... | collective-permute-start | bytes 3145736 | tf_op jit(solution)/shard_map/ppermute | solution.py:39
  113.7 2.7 %copy-start.13 = (bf16[512,1024]{1,0:T(8,128)(2,1)}, bf16[512,1024]{1,0:T(8,128)(2,1)S(1)}, u32[]{:S(2)}) copy-start(bf16[512,1024]{1,0:T(8,128)(2,1)S(1)} %collective-permute-done.15.refs_12_) | copy-start | bytes 3145732
  113.7 2.7 %collective-permute-start.17 = (bf16[512,1024]{1,0:T(8,128)(2,1)S(1)}, bf16[512,1024]{1,0:T(8,128)(2,1)S(1)}, u32[]{:S(2)}, u32[]{:S(2)}) collective-permute-start(bf16[512,1024]{1,0:T(8,128)(2,1)S(1)} %collective-permute-done.15.refs_12_), channel_id=1, source_target_pairs={{0,8},{1,9},{2,10},{3,11},{4,12},{5,13},{6,14},{7,15},{8,0},{9,1},... | collective-permute-start | bytes 3145736 | tf_op jit(solution)/shard_map/ppermute | solution.py:39
  114.4 1.9 %copy-start.14 = (bf16[512,1024]{1,0:T(8,128)(2,1)}, bf16[512,1024]{1,0:T(8,128)(2,1)S(1)}, u32[]{:S(2)}) copy-start(bf16[512,1024]{1,0:T(8,128)(2,1)S(1)} %collective-permute-done.16.refs_13_) | copy-start | bytes 3145732
  114.4 3.5 %collective-permute-start.18 = (bf16[512,1024]{1,0:T(8,128)(2,1)S(1)}, bf16[512,1024]{1,0:T(8,128)(2,1)}, u32[]{:S(2)}, u32[]{:S(2)}) collective-permute-start(bf16[512,1024]{1,0:T(8,128)(2,1)S(1)} %collective-permute-done.16.refs_13_), channel_id=1, source_target_pairs={{0,8},{1,9},{2,10},{3,11},{4,12},{5,13},{6,14},{7,15},{8,0},{9,1},... | collective-permute-start | bytes 3145736 | tf_op jit(solution)/shard_map/ppermute | solution.py:39
  114.4 1.9 %copy-start.15 = (bf16[512,1024]{1,0:T(8,128)(2,1)}, bf16[512,1024]{1,0:T(8,128)(2,1)S(1)}, u32[]{:S(2)}) copy-start(bf16[512,1024]{1,0:T(8,128)(2,1)S(1)} %collective-permute-done.9.refs_6_) | copy-start | bytes 3145732
  114.5 1.9 %copy-start.16 = (bf16[512,1024]{1,0:T(8,128)(2,1)}, bf16[512,1024]{1,0:T(8,128)(2,1)S(1)}, u32[]{:S(2)}) copy-start(bf16[512,1024]{1,0:T(8,128)(2,1)S(1)} %collective-permute-done.14.refs_11_) | copy-start | bytes 3145732
  114.5 1.9 %copy-start.17 = (bf16[512,1024]{1,0:T(8,128)(2,1)}, bf16[512,1024]{1,0:T(8,128)(2,1)S(1)}, u32[]{:S(2)}) copy-start(bf16[512,1024]{1,0:T(8,128)(2,1)S(1)} %collective-permute-done.10.refs_7_) | copy-start | bytes 3145732
  116.4 1.0 copy-start.18
  130.4 42.6 %copy-start.1 = (f32[1,12,8192]{2,0,1:T(1,128)S(1)}, f32[1,12,8192]{2,0,1:T(1,128)}, u32[]{:S(2)}) copy-start(f32[1,12,8192]{2,0,1:T(1,128)} %param.7) | copy-start | bytes 1179652
  130.4 42.6 %copy-start.2 = (f32[1,12,8192]{2,0,1:T(1,128)S(1)}, f32[1,12,8192]{2,0,1:T(1,128)}, u32[]{:S(2)}) copy-start(f32[1,12,8192]{2,0,1:T(1,128)} %param.8) | copy-start | bytes 1179652
  130.4 42.6 %copy-start.3 = (f32[1,12,8192]{2,0,1:T(1,128)S(1)}, f32[1,12,8192]{2,0,1:T(1,128)}, u32[]{:S(2)}) copy-start(f32[1,12,8192]{2,0,1:T(1,128)} %param.9) | copy-start | bytes 1179652
  130.4 8.1 %collective-permute-start.19 = (f32[2,2,48,512]{3,2,1,0:T(8,128)}, f32[2,2,48,512]{3,2,1,0:T(8,128)S(1)}, u32[]{:S(2)}, u32[]{:S(2)}) collective-permute-start(f32[2,2,48,512]{3,2,1,0:T(8,128)} %get-tuple-element.15), channel_id=1, source_target_pairs={{0,16},{1,17},{2,18},{3,19},{4,20},{5,21},{6,22},{7,23},{8,56},{9,... | collective-permute-start | bytes 1179656 | tf_op jit(solution)/shard_map/ppermute | solution.py:39
  131.0 9.2 %collective-permute-start.21 = (f32[2,2,48,512]{3,2,1,0:T(8,128)}, f32[2,2,48,512]{3,2,1,0:T(8,128)S(1)}, u32[]{:S(2)}, u32[]{:S(2)}) collective-permute-start(f32[2,2,48,512]{3,2,1,0:T(8,128)} %get-tuple-element.17), channel_id=1, source_target_pairs={{0,64},{1,65},{2,66},{3,67},{4,68},{5,69},{6,70},{7,71},{8,200},{9... | collective-permute-start | bytes 1179656 | tf_op jit(solution)/shard_map/ppermute | solution.py:39
  139.5 7.0 %collective-permute-start.20 = (f32[2,48,512]{2,1,0:T(8,128)S(1)}, f32[2,48,512]{2,1,0:T(8,128)S(1)}, u32[]{:S(2)}, u32[]{:S(2)}) collective-permute-start(f32[2,48,512]{2,1,0:T(8,128)S(1)} %fusion.16), channel_id=1, source_target_pairs={{0,64},{1,65},{2,66},{3,67},{4,68},{5,69},{6,70},{7,71},{8,200},{9... | collective-permute-start | bytes 589832 | tf_op jit(solution)/shard_map/ppermute | solution.py:39
  141.2 6.2 %collective-permute-start.22 = (f32[2,48,512]{2,1,0:T(8,128)S(1)}, f32[2,48,512]{2,1,0:T(8,128)S(1)}, u32[]{:S(2)}, u32[]{:S(2)}) collective-permute-start(f32[2,48,512]{2,1,0:T(8,128)S(1)} %fusion.13), channel_id=1, source_target_pairs={{0,16},{1,17},{2,18},{3,19},{4,20},{5,21},{6,22},{7,23},{8,56},{9,... | collective-permute-start | bytes 589832 | tf_op jit(solution)/shard_map/ppermute | solution.py:39
Sparse Core Ops, SparseCore 0:
  33.0 84.7 all-gather.1

commit v8 on v7

--- a/solution.py
+++ b/solution.py
@@ -127,21 +127,30 @@
     tr = lax.axis_index("tr")
     units = cotangent.shape[1] // 2
     ordered = feature_order(activations).reshape(2, GROUP, QUARTER, activations.shape[0])
-    both = jnp.stack([ordered[0], send(ordered[1], OTHER_CORE)], axis=1)
+    other = send(ordered[1], OTHER_CORE)
+    tokens = cotangent.shape[0]
+    away = [
+        lax.dynamic_slice(cotangent, (start, (1 - tr) * units), (size, units))
+        for start, size in ((0, tokens * 5 // 8), (tokens * 5 // 8, tokens * 3 // 8))
+    ]
+    own_keep = lax.dynamic_slice_in_dim(cotangent, tr * units, units, 1)
+    other, away, own_keep = lax.optimization_barrier((other, away, own_keep))
+    first_came, last_came = send(away[0], PAIR), send(away[1], PAIR)
+    both = jnp.stack([ordered[0], other], axis=1)
     shared = jnp.stack([both[0]] + [send(both[g], MATE[g]) for g in (1, 2, 3)])
-    away = lax.dynamic_slice_in_dim(cotangent, (1 - tr) * units, units, 1)
-    own_keep = lax.dynamic_slice_in_dim(cotangent, tr * units, units, 1)
-    own_came = send(away, PAIR)
-    early, shared = lax.optimization_barrier((own_keep, shared))
+    far_keep = send(own_keep, OTHER_CORE)
+    early, shared, first_came, far_keep = lax.optimization_barrier((own_keep, shared, first_came, far_keep))
     shared = shared.reshape(2 * GROUP, QUARTER, activations.shape[0])
     gathered = lax.all_gather(shared, ("tc", "tr"), axis=0)
     keep = [own_keep, send(early, MATE[1]), send(early, MATE[2])]
+    came = [(first_came, last_came)] + [[send(part, MATE[g]) for part in (first_came, last_came)] for g in (1, 2)]
+    came = lax.optimization_barrier([jnp.concatenate(parts) for parts in came])
+    keep[1:] = lax.optimization_barrier(keep[1:])
     keep.append(send(keep[1], MATE[2]))
-    came = [own_came, send(own_came, MATE[1]), send(own_came, MATE[2])]
     came.append(send(came[2], MATE[1]))
     cots = []
     for g in range(GROUP):
-        cots += [keep[g], came[g], send(keep[g], OTHER_CORE), send(came[g], OTHER_CORE)]
+        cots += [keep[g], came[g], send(keep[g], OTHER_CORE) if g else far_keep, send(came[g], OTHER_CORE)]
     a_send, a_keep, b_send, b_keep = product(gathered, cots)
     a_came, b_came = send(a_send, NEXT_X), send(b_send, NEXT_Y)
     a_last = send(a_keep[1] + a_came[1], NEXT_Y)

time: 181 us -> 188 us (1.039)
  starting transfers between devices: 20.9 us -> 25.2 us
  waiting for transfers between devices: 95.7 us -> 99.1 us
  blocking collectives: 24.4 us -> 21.8 us
    ppermute x23 -> x26, starting transfers between devices: 20.9 us -> 25.1 us  [send(): return lax.ppermute(array, AXES, pairs)]
    ppermute x23 -> x26, waiting for transfers between devices: 95.6 us -> 99.1 us  [send(): return lax.ppermute(array, AXES, pairs)]
    all_to_all x1, blocking collectives: 24.4 us -> 21.8 us  [shards(): lax.all_to_all(rows, ('tc', 'tr'), split_axis=0, concat_axis=0, tiled=True)]
  transfers between devices with their start and end apart: 24 -> 27, of which waited for: 13 -> 17; matrix products, arithmetic and copies ran while one was open for 2% -> 4% of each run, Pallas kernels for 0% -> 0%
where the time goes in v8:
time: 188 us
  waiting for transfers between devices  99.1 us (53%)
  starting transfers between devices  25.2 us (13%)
  blocking collectives  21.8 us (12%)
  between operations  14.4 us (8%)
  Pallas kernels  13.6 us (7%)
  other arithmetic  6.4 us (3%)
  local copies, waits for them, and re-layouts  4.92 us (3%)
  matrix products  2.74 us (1%)
    ppermute x26, waiting for transfers between devices, send(): return lax.ppermute(array, AXES, pairs)  99.1 us
    ppermute x26, starting transfers between devices, send(): return lax.ppermute(array, AXES, pairs)  25.1 us
    all_to_all x1, blocking collectives, shards(): lax.all_to_all(rows, ('tc', 'tr'), split_axis=0, concat_axis=0, tiled=True)  21.8 us
    pallas_call x1, Pallas kernels, product(): pl.pallas_call(product_kernel, in_specs=[pl.BlockSpec(memory_space=pl.ANY...  12.4 us
  transfers between devices with their start and end apart: 27, of which 17 were waited for; matrix products, arithmetic and copies ran while one was open for 4% of the time, Pallas kernels for 0%

profile of v8, /device:TPU:6, one launch (start us, length us, event | category | flops | bytes accessed | tf_op | source)
XLA Modules:
  0.0 188.1 jit_solution(7939614423094875470)
XLA Ops:
  7.2 0.0 copy-start
  7.2 0.0 all-gather.2.cloned.1.call-start
  7.3 0.1 fusion.34
  7.3 2.7 %fusion.4 = bf16[1536,256]{1,0:T(8,128)(2,1)S(1)} fusion(bf16[256,1536]{1,0:T(8,128)(2,1)} %param.5, s32[1536]{0:T(1024)S(1)} %fusion.34), kind=kOutput, calls=%fused_computation.4 | convolution fusion | flops 1213071360 | bytes 1579008 | tf_op jit(solution)/shard_map/dot_general | solution.py:61
  10.1 0.8 fusion.53
  10.9 0.8 constant_dynamic-slice_fusion
  11.7 0.1 constant_dynamic-slice_fusion.2
  11.7 0.1 constant_dynamic-slice_fusion.1.refs_0_
  11.8 1.1 collective-permute-done
  12.9 0.1 collective-permute-start.5
  13.1 1.9 %collective-permute-start.4 = (bf16[320,1024]{1,0:T(8,128)(2,1)S(1)}, bf16[320,1024]{1,0:T(8,128)(2,1)S(1)}, u32[]{:S(2)}, u32[]{:S(2)}) collective-permute-start(bf16[320,1024]{1,0:T(8,128)(2,1)S(1)} %constant_dynamic-slice_fusion.2), channel_id=1, source_target_pairs={{0,4},{1,5},{2,6},{3,7},{4,0},{5,1},{6,2},{7,3},{8,12},{9,13},{10,... | collective-permute-start | bytes 1966088 | tf_op jit(solution)/shard_map/ppermute | solution.py:39
  15.0 1.1 fusion.10
  16.1 1.5 collective-permute-start.1
  17.6 4.8 %collective-permute-start.3 = (bf16[2,192,256]{2,1,0:T(8,128)(2,1)S(1)}, bf16[2,192,256]{2,1,0:T(8,128)(2,1)S(1)}, u32[]{:S(2)}, u32[]{:S(2)}) collective-permute-start(bf16[2,192,256]{2,1,0:T(8,128)(2,1)S(1)} %get-tuple-element.54), channel_id=1, source_target_pairs={{0,160},{1,161},{2,162},{3,163},{4,164},{5,165},{6,166},{7,167},{8... | collective-permute-start | bytes 589832 | tf_op jit(solution)/shard_map/ppermute | solution.py:39
  22.4 0.3 collective-permute-start.2
  22.7 2.3 %collective-permute-done.1 = bf16[2,192,256]{2,1,0:T(8,128)(2,1)S(1)} collective-permute-done((bf16[2,192,256]{2,1,0:T(8,128)(2,1)S(1)}, bf16[2,192,256]{2,1,0:T(8,128)(2,1)S(1)}, u32[]{:S(2)}, u32[]{:S(2)}) %collective-permute-start.1) | collective-permute-done | bytes 196640 | tf_op jit(solution)/shard_map/ppermute | solution.py:39
  25.0 6.6 %collective-permute-done.3 = bf16[2,192,256]{2,1,0:T(8,128)(2,1)S(1)} collective-permute-done((bf16[2,192,256]{2,1,0:T(8,128)(2,1)S(1)}, bf16[2,192,256]{2,1,0:T(8,128)(2,1)S(1)}, u32[]{:S(2)}, u32[]{:S(2)}) %collective-permute-start.3) | collective-permute-done | bytes 196640 | tf_op jit(solution)/shard_map/ppermute | solution.py:39
  31.5 2.9 %collective-permute-done.2 = bf16[2,192,256]{2,1,0:T(8,128)(2,1)S(1)} collective-permute-done((bf16[2,192,256]{2,1,0:T(8,128)(2,1)S(1)}, bf16[2,192,256]{2,1,0:T(8,128)(2,1)S(1)}, u32[]{:S(2)}, u32[]{:S(2)}) %collective-permute-start.2) | collective-permute-done | bytes 196640 | tf_op jit(solution)/shard_map/ppermute | solution.py:39
  34.4 1.0 pad_maximum_fusion.3
  35.4 0.8 copy-done.8
  36.2 1.0 copy-done.10
  37.2 0.0 all-gather.2.cloned.1.call-update
  37.2 0.4 collective-permute-start.6
  37.6 0.3 collective-permute-start.13
  37.9 1.4 collective-permute-start.12
  39.3 3.2 %collective-permute-start.9 = (bf16[320,1024]{1,0:T(8,128)(2,1)}, bf16[320,1024]{1,0:T(8,128)(2,1)S(1)}, u32[]{:S(2)}, u32[]{:S(2)}) collective-permute-start(bf16[320,1024]{1,0:T(8,128)(2,1)} %copy-done.8), channel_id=1, source_target_pairs={{0,128},{1,129},{2,130},{3,131},{4,132},{5,133},{6,134},{7,135},{8... | collective-permute-start | bytes 1966088 | tf_op jit(solution)/shard_map/ppermute | solution.py:39
  42.5 5.2 %collective-permute-done.6 = bf16[192,1024]{1,0:T(8,128)(2,1)S(1)} collective-permute-done((bf16[192,1024]{1,0:T(8,128)(2,1)}, bf16[192,1024]{1,0:T(8,128)(2,1)S(1)}, u32[]{:S(2)}, u32[]{:S(2)}) %collective-permute-start.6) | collective-permute-done | bytes 393248 | tf_op jit(solution)/shard_map/ppermute | solution.py:39
  47.7 0.1 collective-permute-start.10
  47.8 1.3 collective-permute-start.7
  49.1 36.5 %collective-permute-done.10 = bf16[192,1024]{1,0:T(8,128)(2,1)S(1)} collective-permute-done((bf16[192,1024]{1,0:T(8,128)(2,1)S(1)}, bf16[192,1024]{1,0:T(8,128)(2,1)S(1)}, u32[]{:S(2)}, u32[]{:S(2)}) %collective-permute-start.10) | collective-permute-done | bytes 393248 | tf_op jit(solution)/shard_map/ppermute | solution.py:39
  85.6 1.4 collective-permute-start.8
  87.0 1.2 pad_maximum_fusion.refs_1_
  88.2 0.1 pad_maximum_fusion.2.refs_9_
  88.3 7.9 %collective-permute-done.8 = bf16[192,1024]{1,0:T(8,128)(2,1)S(1)} collective-permute-done((bf16[192,1024]{1,0:T(8,128)(2,1)S(1)}, bf16[192,1024]{1,0:T(8,128)(2,1)S(1)}, u32[]{:S(2)}, u32[]{:S(2)}) %collective-permute-start.8) | collective-permute-done | bytes 393248 | tf_op jit(solution)/shard_map/ppermute | solution.py:39
  96.1 0.1 pad_maximum_fusion.1.refs_5_
  96.2 0.1 collective-permute-start.11
  96.3 0.5 collective-permute-start.15
  96.8 1.4 collective-permute-start.19
  98.3 0.4 collective-permute-start.18
  98.7 0.3 collective-permute-done.11.refs_3_
  99.0 0.3 collective-permute-start.14
  99.3 1.2 collective-permute-done.15.refs_7_
  100.5 0.1 collective-permute-start.16
  100.6 22.9 %collective-permute-done.19.refs_13_ = bf16[512,1024]{1,0:T(8,128)(2,1)S(1)} collective-permute-done((bf16[512,1024]{1,0:T(8,128)(2,1)S(1)}, bf16[512,1024]{1,0:T(8,128)(2,1)S(1)}, u32[]{:S(2)}, u32[]{:S(2)}) %collective-permute-start.19) | collective-permute-done | bytes 1048608 | tf_op jit(solution)/shard_map/ppermute | solution.py:39
  123.5 1.2 collective-permute-done.18.refs_12_
  124.8 1.3 collective-permute-done.21.refs_15_
  126.2 0.2 copy-done.18
  126.4 1.0 copy-done.20
  127.4 0.4 collective-permute-done.20.refs_14_
  127.8 12.4 %shard_map.76 = (f32[2,2,48,512]{3,2,1,0:T(8,128)}, f32[2,2,48,512]{3,2,1,0:T(8,128)}, f32[2,2,48,512]{3,2,1,0:T(8,128)}, f32[2,2,48,512]{3,2,1,0:T(8,128)}) custom-call(bf16[8,8,192,256]{3,2,1,0:T(8,128)(2,1)} %all-gather.2.cloned.1.call-done.gathered, bf16[512,1024]{1,0:T(8,128)(2,1)} %copy-done.4, bf16[512,1024]{1,0:T(8,128)(2,1)} %copy-done.5, ...), custom_call_target="tpu_custom_call" | custom-call | flops 6442450944 | bytes 29360128 | tf_op jit(solution)/shard_map/pallas_call | solution.py:109
  140.2 1.9 %collective-permute-start.22 = (f32[2,2,48,512]{3,2,1,0:T(8,128)}, f32[2,2,48,512]{3,2,1,0:T(8,128)S(1)}, u32[]{:S(2)}, u32[]{:S(2)}) collective-permute-start(f32[2,2,48,512]{3,2,1,0:T(8,128)} %get-tuple-element.37), channel_id=1, source_target_pairs={{0,16},{1,17},{2,18},{3,19},{4,20},{5,21},{6,22},{7,23},{8,56},{9,... | collective-permute-start | bytes 1179656 | tf_op jit(solution)/shard_map/ppermute | solution.py:39
  142.2 0.8 collective-permute-start.24
  142.9 5.4 %collective-permute-done.22 = f32[2,2,48,512]{3,2,1,0:T(8,128)S(1)} collective-permute-done((f32[2,2,48,512]{3,2,1,0:T(8,128)}, f32[2,2,48,512]{3,2,1,0:T(8,128)S(1)}, u32[]{:S(2)}, u32[]{:S(2)}) %collective-permute-start.22) | collective-permute-done | bytes 393248 | tf_op jit(solution)/shard_map/ppermute | solution.py:39
  148.3 1.0 fusion.16
  149.3 0.9 collective-permute-start.23
  150.1 1.2 collective-permute-done.24
  151.3 1.0 fusion.13
  152.3 1.9 %collective-permute-start.25 = (f32[2,48,512]{2,1,0:T(8,128)S(1)}, f32[2,48,512]{2,1,0:T(8,128)S(1)}, u32[]{:S(2)}, u32[]{:S(2)}) collective-permute-start(f32[2,48,512]{2,1,0:T(8,128)S(1)} %fusion.13), channel_id=1, source_target_pairs={{0,16},{1,17},{2,18},{3,19},{4,20},{5,21},{6,22},{7,23},{8,56},{9,... | collective-permute-start | bytes 589832 | tf_op jit(solution)/shard_map/ppermute | solution.py:39
  154.2 2.0 %collective-permute-done.23 = f32[2,48,512]{2,1,0:T(8,128)S(1)} collective-permute-done((f32[2,48,512]{2,1,0:T(8,128)S(1)}, f32[2,48,512]{2,1,0:T(8,128)S(1)}, u32[]{:S(2)}, u32[]{:S(2)}) %collective-permute-start.23) | collective-permute-done | bytes 196640 | tf_op jit(solution)/shard_map/ppermute | solution.py:39
  156.2 1.0 fusion.18
  157.2 0.8 collective-permute-done.25
  158.1 0.1 copy.28
  158.3 21.8 %all_to_all.5.rows = f32[8,12,8,128]{3,2,1,0:T(8,128)S(1)} all-to-all(f32[8,12,8,128]{3,2,1,0:T(8,128)S(1)} %bitcast.51), channel_id=1, replica_groups=mesh['dp'=32,'tr'=2,'tc'=4] {'tc','tr'}, dimensions={0} | all-to-all | bytes 786432 | tf_op jit(solution)/shard_map/all_to_all | solution.py:161
  180.0 1.2 shard_map.77
  (54 shorter events, 0.2 us)
Async XLA Ops:
  7.2 3.7 %copy-start = (bf16[512,2048]{1,0:T(8,128)(2,1)S(1)}, bf16[512,2048]{1,0:T(8,128)(2,1)}, u32[]{:S(2)}) copy-start(bf16[512,2048]{1,0:T(8,128)(2,1)} %param.6) | copy-start | bytes 6291460
  7.2 120.6 %all-gather.2.cloned.1.call-start = ((), (), s32[]{:S(2)}) async-start(), calls=%async_computation.1 | async-start | bytes 7077888 | tf_op jit(solution)/shard_map/all_gather | solution.py:144
  10.9 2.1 %collective-permute-start = (bf16[4,192,256]{2,1,0:T(8,128)(2,1)}, bf16[4,192,256]{2,1,0:T(8,128)(2,1)}, u32[]{:S(2)}, u32[]{:S(2)}) collective-permute-start(bf16[4,192,256]{2,1,0:T(8,128)(2,1)} %bitcast), channel_id=1, source_target_pairs={{0,8},{1,9},{2,10},{3,11},{4,12},{5,13},{6,14},{7,15},{8,0},{9,1},... | collective-permute-start | bytes 1179656 | tf_op jit(solution)/shard_map/ppermute | solution.py:39
  11.8 76.3 %copy-start.4 = (bf16[512,1024]{1,0:T(8,128)(2,1)}, bf16[512,1024]{1,0:T(8,128)(2,1)S(1)}, u32[]{:S(2)}) copy-start(bf16[512,1024]{1,0:T(8,128)(2,1)S(1)} %constant_dynamic-slice_fusion.1.refs_0_) | copy-start | bytes 3145732
  12.9 22.5 %collective-permute-start.5 = (bf16[512,1024]{1,0:T(8,128)(2,1)S(1)}, bf16[512,1024]{1,0:T(8,128)(2,1)S(1)}, u32[]{:S(2)}, u32[]{:S(2)}) collective-permute-start(bf16[512,1024]{1,0:T(8,128)(2,1)S(1)} %constant_dynamic-slice_fusion.1.refs_0_), channel_id=1, source_target_pairs={{0,8},{1,9},{2,10},{3,11},{4,12},{5,13},{6,14},{7,15},{8,0},{9,1},... | collective-permute-start | bytes 3145736 | tf_op jit(solution)/shard_map/ppermute | solution.py:39
  13.1 22.3 %collective-permute-start.4 = (bf16[320,1024]{1,0:T(8,128)(2,1)S(1)}, bf16[320,1024]{1,0:T(8,128)(2,1)S(1)}, u32[]{:S(2)}, u32[]{:S(2)}) collective-permute-start(bf16[320,1024]{1,0:T(8,128)(2,1)S(1)} %constant_dynamic-slice_fusion.2), channel_id=1, source_target_pairs={{0,4},{1,5},{2,6},{3,7},{4,0},{5,1},{6,2},{7,3},{8,12},{9,13},{10,... | collective-permute-start | bytes 1966088 | tf_op jit(solution)/shard_map/ppermute | solution.py:39
  16.1 8.9 %collective-permute-start.1 = (bf16[2,192,256]{2,1,0:T(8,128)(2,1)S(1)}, bf16[2,192,256]{2,1,0:T(8,128)(2,1)S(1)}, u32[]{:S(2)}, u32[]{:S(2)}) collective-permute-start(bf16[2,192,256]{2,1,0:T(8,128)(2,1)S(1)} %get-tuple-element.53), channel_id=1, source_target_pairs={{0,32},{1,33},{2,34},{3,35},{4,36},{5,37},{6,38},{7,39},{8,40},{9,... | collective-permute-start | bytes 589832 | tf_op jit(solution)/shard_map/ppermute | solution.py:39
  17.6 13.9 %collective-permute-start.3 = (bf16[2,192,256]{2,1,0:T(8,128)(2,1)S(1)}, bf16[2,192,256]{2,1,0:T(8,128)(2,1)S(1)}, u32[]{:S(2)}, u32[]{:S(2)}) collective-permute-start(bf16[2,192,256]{2,1,0:T(8,128)(2,1)S(1)} %get-tuple-element.54), channel_id=1, source_target_pairs={{0,160},{1,161},{2,162},{3,163},{4,164},{5,165},{6,166},{7,167},{8... | collective-permute-start | bytes 589832 | tf_op jit(solution)/shard_map/ppermute | solution.py:39
  22.4 12.0 %collective-permute-start.2 = (bf16[2,192,256]{2,1,0:T(8,128)(2,1)S(1)}, bf16[2,192,256]{2,1,0:T(8,128)(2,1)S(1)}, u32[]{:S(2)}, u32[]{:S(2)}) collective-permute-start(bf16[2,192,256]{2,1,0:T(8,128)(2,1)S(1)} %get-tuple-element.55), channel_id=1, source_target_pairs={{0,128},{1,129},{2,130},{3,131},{4,132},{5,133},{6,134},{7,135},{8... | collective-permute-start | bytes 589832 | tf_op jit(solution)/shard_map/ppermute | solution.py:39
  35.4 0.8 copy-start.8
  36.2 1.0 copy-start.10
  37.2 10.5 %collective-permute-start.6 = (bf16[192,1024]{1,0:T(8,128)(2,1)}, bf16[192,1024]{1,0:T(8,128)(2,1)S(1)}, u32[]{:S(2)}, u32[]{:S(2)}) collective-permute-start(bf16[192,1024]{1,0:T(8,128)(2,1)} %constant_dynamic-slice_fusion), channel_id=1, source_target_pairs={{0,4},{1,5},{2,6},{3,7},{4,0},{5,1},{6,2},{7,3},{8,12},{9,13},{10,... | collective-permute-start | bytes 1179656 | tf_op jit(solution)/shard_map/ppermute | solution.py:39
  37.6 60.7 %collective-permute-start.13 = (bf16[512,1024]{1,0:T(8,128)(2,1)S(1)}, bf16[512,1024]{1,0:T(8,128)(2,1)S(1)}, u32[]{:S(2)}, u32[]{:S(2)}) collective-permute-start(bf16[512,1024]{1,0:T(8,128)(2,1)S(1)} %constant_dynamic-slice_fusion.1.refs_0_), channel_id=1, source_target_pairs={{0,128},{1,129},{2,130},{3,131},{4,132},{5,133},{6,134},{7,135},{8... | collective-permute-start | bytes 3145736 | tf_op jit(solution)/shard_map/ppermute | solution.py:39
  37.9 60.3 %collective-permute-start.12 = (bf16[512,1024]{1,0:T(8,128)(2,1)S(1)}, bf16[512,1024]{1,0:T(8,128)(2,1)S(1)}, u32[]{:S(2)}, u32[]{:S(2)}) collective-permute-start(bf16[512,1024]{1,0:T(8,128)(2,1)S(1)} %constant_dynamic-slice_fusion.1.refs_0_), channel_id=1, source_target_pairs={{0,32},{1,33},{2,34},{3,35},{4,36},{5,37},{6,38},{7,39},{8,40},{9,... | collective-permute-start | bytes 3145736 | tf_op jit(solution)/shard_map/ppermute | solution.py:39
  39.3 48.9 %collective-permute-start.9 = (bf16[320,1024]{1,0:T(8,128)(2,1)}, bf16[320,1024]{1,0:T(8,128)(2,1)S(1)}, u32[]{:S(2)}, u32[]{:S(2)}) collective-permute-start(bf16[320,1024]{1,0:T(8,128)(2,1)} %copy-done.8), channel_id=1, source_target_pairs={{0,128},{1,129},{2,130},{3,131},{4,132},{5,133},{6,134},{7,135},{8... | collective-permute-start | bytes 1966088 | tf_op jit(solution)/shard_map/ppermute | solution.py:39
  47.7 37.9 %collective-permute-start.10 = (bf16[192,1024]{1,0:T(8,128)(2,1)S(1)}, bf16[192,1024]{1,0:T(8,128)(2,1)S(1)}, u32[]{:S(2)}, u32[]{:S(2)}) collective-permute-start(bf16[192,1024]{1,0:T(8,128)(2,1)S(1)} %collective-permute-done.6), channel_id=1, source_target_pairs={{0,128},{1,129},{2,130},{3,131},{4,132},{5,133},{6,134},{7,135},{8... | collective-permute-start | bytes 1179656 | tf_op jit(solution)/shard_map/ppermute | solution.py:39
  47.8 48.4 %collective-permute-start.7 = (bf16[320,1024]{1,0:T(8,128)(2,1)}, bf16[320,1024]{1,0:T(8,128)(2,1)S(1)}, u32[]{:S(2)}, u32[]{:S(2)}) collective-permute-start(bf16[320,1024]{1,0:T(8,128)(2,1)} %copy-done.8), channel_id=1, source_target_pairs={{0,32},{1,33},{2,34},{3,35},{4,36},{5,37},{6,38},{7,39},{8,40},{9,... | collective-permute-start | bytes 1966088 | tf_op jit(solution)/shard_map/ppermute | solution.py:39
  85.6 10.6 %collective-permute-start.8 = (bf16[192,1024]{1,0:T(8,128)(2,1)S(1)}, bf16[192,1024]{1,0:T(8,128)(2,1)S(1)}, u32[]{:S(2)}, u32[]{:S(2)}) collective-permute-start(bf16[192,1024]{1,0:T(8,128)(2,1)S(1)} %collective-permute-done.6), channel_id=1, source_target_pairs={{0,32},{1,33},{2,34},{3,35},{4,36},{5,37},{6,38},{7,39},{8,40},{9,... | collective-permute-start | bytes 1179656 | tf_op jit(solution)/shard_map/ppermute | solution.py:39
  88.2 8.1 %copy-start.5 = (bf16[512,1024]{1,0:T(8,128)(2,1)}, bf16[512,1024]{1,0:T(8,128)(2,1)S(1)}, u32[]{:S(2)}) copy-start(bf16[512,1024]{1,0:T(8,128)(2,1)S(1)} %pad_maximum_fusion.refs_1_) | copy-start | bytes 3145732
  88.3 10.7 %copy-start.6 = (bf16[512,1024]{1,0:T(8,128)(2,1)}, bf16[512,1024]{1,0:T(8,128)(2,1)S(1)}, u32[]{:S(2)}) copy-start(bf16[512,1024]{1,0:T(8,128)(2,1)S(1)} %pad_maximum_fusion.2.refs_9_) | copy-start | bytes 3145732
  96.2 28.5 %copy-start.7 = (bf16[512,1024]{1,0:T(8,128)(2,1)}, bf16[512,1024]{1,0:T(8,128)(2,1)S(1)}, u32[]{:S(2)}) copy-start(bf16[512,1024]{1,0:T(8,128)(2,1)S(1)} %pad_maximum_fusion.1.refs_5_) | copy-start | bytes 3145732
  96.2 2.7 %collective-permute-start.11 = (bf16[512,1024]{1,0:T(8,128)(2,1)S(1)}, bf16[512,1024]{1,0:T(8,128)(2,1)S(1)}, u32[]{:S(2)}, u32[]{:S(2)}) collective-permute-start(bf16[512,1024]{1,0:T(8,128)(2,1)S(1)} %pad_maximum_fusion.refs_1_), channel_id=1, source_target_pairs={{0,8},{1,9},{2,10},{3,11},{4,12},{5,13},{6,14},{7,15},{8,0},{9,1},... | collective-permute-start | bytes 3145736 | tf_op jit(solution)/shard_map/ppermute | solution.py:39
  96.3 4.1 %collective-permute-start.15 = (bf16[512,1024]{1,0:T(8,128)(2,1)S(1)}, bf16[512,1024]{1,0:T(8,128)(2,1)S(1)}, u32[]{:S(2)}, u32[]{:S(2)}) collective-permute-start(bf16[512,1024]{1,0:T(8,128)(2,1)S(1)} %pad_maximum_fusion.1.refs_5_), channel_id=1, source_target_pairs={{0,8},{1,9},{2,10},{3,11},{4,12},{5,13},{6,14},{7,15},{8,0},{9,1},... | collective-permute-start | bytes 3145736 | tf_op jit(solution)/shard_map/ppermute | solution.py:39
  96.8 26.7 %collective-permute-start.19 = (bf16[512,1024]{1,0:T(8,128)(2,1)S(1)}, bf16[512,1024]{1,0:T(8,128)(2,1)S(1)}, u32[]{:S(2)}, u32[]{:S(2)}) collective-permute-start(bf16[512,1024]{1,0:T(8,128)(2,1)S(1)} %pad_maximum_fusion.2.refs_9_), channel_id=1, source_target_pairs={{0,32},{1,33},{2,34},{3,35},{4,36},{5,37},{6,38},{7,39},{8,40},{9,... | collective-permute-start | bytes 3145736 | tf_op jit(solution)/shard_map/ppermute | solution.py:39
  98.2 26.5 %copy-start.11 = (bf16[512,1024]{1,0:T(8,128)(2,1)}, bf16[512,1024]{1,0:T(8,128)(2,1)S(1)}, u32[]{:S(2)}) copy-start(bf16[512,1024]{1,0:T(8,128)(2,1)S(1)} %collective-permute-done.13.refs_8_) | copy-start | bytes 3145732
  98.2 26.6 %copy-start.12 = (bf16[512,1024]{1,0:T(8,128)(2,1)}, bf16[512,1024]{1,0:T(8,128)(2,1)S(1)}, u32[]{:S(2)}) copy-start(bf16[512,1024]{1,0:T(8,128)(2,1)S(1)} %collective-permute-done.12.refs_4_) | copy-start | bytes 3145732
  98.3 26.5 %collective-permute-start.18 = (bf16[512,1024]{1,0:T(8,128)(2,1)S(1)}, bf16[512,1024]{1,0:T(8,128)(2,1)S(1)}, u32[]{:S(2)}, u32[]{:S(2)}) collective-permute-start(bf16[512,1024]{1,0:T(8,128)(2,1)S(1)} %collective-permute-done.12.refs_4_), channel_id=1, source_target_pairs={{0,128},{1,129},{2,130},{3,131},{4,132},{5,133},{6,134},{7,135},{8... | collective-permute-start | bytes 3145736 | tf_op jit(solution)/shard_map/ppermute | solution.py:39
  98.7 26.1 %collective-permute-start.17 = (bf16[512,1024]{1,0:T(8,128)(2,1)S(1)}, bf16[512,1024]{1,0:T(8,128)(2,1)S(1)}, u32[]{:S(2)}, u32[]{:S(2)}) collective-permute-start(bf16[512,1024]{1,0:T(8,128)(2,1)S(1)} %pad_maximum_fusion.2.refs_9_), channel_id=1, source_target_pairs={{0,8},{1,9},{2,10},{3,11},{4,12},{5,13},{6,14},{7,15},{8,0},{9,1},... | collective-permute-start | bytes 3145736 | tf_op jit(solution)/shard_map/ppermute | solution.py:39
  99.0 27.2 %copy-start.13 = (bf16[512,1024]{1,0:T(8,128)(2,1)}, bf16[512,1024]{1,0:T(8,128)(2,1)S(1)}, u32[]{:S(2)}) copy-start(bf16[512,1024]{1,0:T(8,128)(2,1)S(1)} %collective-permute-done.11.refs_3_) | copy-start | bytes 3145732
  99.0 25.8 %collective-permute-start.14 = (bf16[512,1024]{1,0:T(8,128)(2,1)S(1)}, bf16[512,1024]{1,0:T(8,128)(2,1)S(1)}, u32[]{:S(2)}, u32[]{:S(2)}) collective-permute-start(bf16[512,1024]{1,0:T(8,128)(2,1)S(1)} %collective-permute-done.12.refs_4_), channel_id=1, source_target_pairs={{0,8},{1,9},{2,10},{3,11},{4,12},{5,13},{6,14},{7,15},{8,0},{9,1},... | collective-permute-start | bytes 3145736 | tf_op jit(solution)/shard_map/ppermute | solution.py:39
  100.5 25.7 %copy-start.14 = (bf16[512,1024]{1,0:T(8,128)(2,1)}, bf16[512,1024]{1,0:T(8,128)(2,1)S(1)}, u32[]{:S(2)}) copy-start(bf16[512,1024]{1,0:T(8,128)(2,1)S(1)} %collective-permute-done.15.refs_7_) | copy-start | bytes 3145732
  100.5 24.3 %collective-permute-start.16 = (bf16[512,1024]{1,0:T(8,128)(2,1)S(1)}, bf16[512,1024]{1,0:T(8,128)(2,1)S(1)}, u32[]{:S(2)}, u32[]{:S(2)}) collective-permute-start(bf16[512,1024]{1,0:T(8,128)(2,1)S(1)} %collective-permute-done.13.refs_8_), channel_id=1, source_target_pairs={{0,8},{1,9},{2,10},{3,11},{4,12},{5,13},{6,14},{7,15},{8,0},{9,1},... | collective-permute-start | bytes 3145736 | tf_op jit(solution)/shard_map/ppermute | solution.py:39
  123.5 2.7 %copy-start.15 = (bf16[512,1024]{1,0:T(8,128)(2,1)}, bf16[512,1024]{1,0:T(8,128)(2,1)S(1)}, u32[]{:S(2)}) copy-start(bf16[512,1024]{1,0:T(8,128)(2,1)S(1)} %collective-permute-done.19.refs_13_) | copy-start | bytes 3145732
  123.5 2.7 %collective-permute-start.21 = (bf16[512,1024]{1,0:T(8,128)(2,1)S(1)}, bf16[512,1024]{1,0:T(8,128)(2,1)S(1)}, u32[]{:S(2)}, u32[]{:S(2)}) collective-permute-start(bf16[512,1024]{1,0:T(8,128)(2,1)S(1)} %collective-permute-done.19.refs_13_), channel_id=1, source_target_pairs={{0,8},{1,9},{2,10},{3,11},{4,12},{5,13},{6,14},{7,15},{8,0},{9,1},... | collective-permute-start | bytes 3145736 | tf_op jit(solution)/shard_map/ppermute | solution.py:39
  124.7 3.1 %copy-start.16 = (bf16[512,1024]{1,0:T(8,128)(2,1)}, bf16[512,1024]{1,0:T(8,128)(2,1)S(1)}, u32[]{:S(2)}) copy-start(bf16[512,1024]{1,0:T(8,128)(2,1)S(1)} %collective-permute-done.18.refs_12_) | copy-start | bytes 3145732
  124.7 3.1 %collective-permute-start.20 = (bf16[512,1024]{1,0:T(8,128)(2,1)S(1)}, bf16[512,1024]{1,0:T(8,128)(2,1)}, u32[]{:S(2)}, u32[]{:S(2)}) collective-permute-start(bf16[512,1024]{1,0:T(8,128)(2,1)S(1)} %collective-permute-done.18.refs_12_), channel_id=1, source_target_pairs={{0,8},{1,9},{2,10},{3,11},{4,12},{5,13},{6,14},{7,15},{8,0},{9,1},... | collective-permute-start | bytes 3145736 | tf_op jit(solution)/shard_map/ppermute | solution.py:39
  124.8 1.4 copy-start.17
  124.8 1.4 copy-start.19
  124.8 1.6 copy-start.18
  126.4 1.0 copy-start.20
  140.2 17.8 %copy-start.9 = (f32[2,2,48,512]{3,2,1,0:T(8,128)S(1)}, f32[2,2,48,512]{3,2,1,0:T(8,128)}, u32[]{:S(2)}) copy-start(f32[2,2,48,512]{3,2,1,0:T(8,128)} %get-tuple-element.38) | copy-start | bytes 1179652
  140.2 8.1 %collective-permute-start.22 = (f32[2,2,48,512]{3,2,1,0:T(8,128)}, f32[2,2,48,512]{3,2,1,0:T(8,128)S(1)}, u32[]{:S(2)}, u32[]{:S(2)}) collective-permute-start(f32[2,2,48,512]{3,2,1,0:T(8,128)} %get-tuple-element.37), channel_id=1, source_target_pairs={{0,16},{1,17},{2,18},{3,19},{4,20},{5,21},{6,22},{7,23},{8,56},{9,... | collective-permute-start | bytes 1179656 | tf_op jit(solution)/shard_map/ppermute | solution.py:39
  142.2 9.2 %collective-permute-start.24 = (f32[2,2,48,512]{3,2,1,0:T(8,128)}, f32[2,2,48,512]{3,2,1,0:T(8,128)S(1)}, u32[]{:S(2)}, u32[]{:S(2)}) collective-permute-start(f32[2,2,48,512]{3,2,1,0:T(8,128)} %get-tuple-element.39), channel_id=1, source_target_pairs={{0,64},{1,65},{2,66},{3,67},{4,68},{5,69},{6,70},{7,71},{8,200},{9... | collective-permute-start | bytes 1179656 | tf_op jit(solution)/shard_map/ppermute | solution.py:39
  149.3 7.0 %collective-permute-start.23 = (f32[2,48,512]{2,1,0:T(8,128)S(1)}, f32[2,48,512]{2,1,0:T(8,128)S(1)}, u32[]{:S(2)}, u32[]{:S(2)}) collective-permute-start(f32[2,48,512]{2,1,0:T(8,128)S(1)} %fusion.16), channel_id=1, source_target_pairs={{0,64},{1,65},{2,66},{3,67},{4,68},{5,69},{6,70},{7,71},{8,200},{9... | collective-permute-start | bytes 589832 | tf_op jit(solution)/shard_map/ppermute | solution.py:39
  152.3 5.7 %collective-permute-start.25 = (f32[2,48,512]{2,1,0:T(8,128)S(1)}, f32[2,48,512]{2,1,0:T(8,128)S(1)}, u32[]{:S(2)}, u32[]{:S(2)}) collective-permute-start(f32[2,48,512]{2,1,0:T(8,128)S(1)} %fusion.13), channel_id=1, source_target_pairs={{0,16},{1,17},{2,18},{3,19},{4,20},{5,21},{6,22},{7,23},{8,56},{9,... | collective-permute-start | bytes 589832 | tf_op jit(solution)/shard_map/ppermute | solution.py:39
  157.2 22.8 %copy-start.1 = (f32[1,12,8192]{2,0,1:T(1,128)S(1)}, f32[1,12,8192]{2,0,1:T(1,128)}, u32[]{:S(2)}) copy-start(f32[1,12,8192]{2,0,1:T(1,128)} %param.7) | copy-start | bytes 1179652
  157.2 22.8 %copy-start.2 = (f32[1,12,8192]{2,0,1:T(1,128)S(1)}, f32[1,12,8192]{2,0,1:T(1,128)}, u32[]{:S(2)}) copy-start(f32[1,12,8192]{2,0,1:T(1,128)} %param.8) | copy-start | bytes 1179652
  157.2 22.8 %copy-start.3 = (f32[1,12,8192]{2,0,1:T(1,128)S(1)}, f32[1,12,8192]{2,0,1:T(1,128)}, u32[]{:S(2)}) copy-start(f32[1,12,8192]{2,0,1:T(1,128)} %param.9) | copy-start | bytes 1179652
Sparse Core Ops, SparseCore 0:
  37.3 74.3 all-gather.1

commit v9 on v8

--- a/solution.py
+++ b/solution.py
@@ -17,6 +17,8 @@
 SIDE = 4
 ROWS = 48
 GROUP = 4
+SOURCES = ((0, 0), (1, 0), (-1, 0), (0, 1))
+OWNERS = ((0, 0), (2, 1), (0, 2), (2, 3))
 QUARTER = 4 * ROWS
 
 
@@ -31,19 +33,14 @@
     return pairs
 
 
-def onward(core):
-    return 1 - 2 * core
-
-
 def send(array, pairs):
     return lax.ppermute(array, AXES, pairs)
 
 
 OTHER_CORE = moves(lambda y, x, core, z: (y, x, 1 - core, z))
 PAIR = moves(lambda y, x, core, z: (y, x, core, z ^ 1))
-MATE = [moves(lambda y, x, core, z: (y + 2 * (g // 2), x + 2 * (g % 2), core, z)) for g in range(GROUP)]
-NEXT_X = moves(lambda y, x, core, z: (y, x + onward(core), core, z))
-NEXT_Y = moves(lambda y, x, core, z: (y + onward(core), x, core, z))
+FEED = [moves(lambda y, x, core, z: (y - dy, x - dx, core, z)) for dx, dy in SOURCES]
+REDUCE = [moves(lambda y, x, core, z: (y + dy, x + dx, core, z)) for dx, dy in OWNERS]
 
 
 def feature_order(activations):
@@ -51,11 +48,13 @@
     my_y, my_x, core = dp // 8, dp // 2 % 4, dp % 2
     column = lax.broadcasted_iota(jnp.int32, (1, 2 * GROUP * QUARTER), 1)
     row, block = column % ROWS, column // ROWS
-    far_x, far_y, mate, half = block % 2, block // 2 % 2, block // 4 % GROUP, block // (4 * GROUP)
+    owner, feed, half = block % 4, block // 4 % GROUP, block // (4 * GROUP)
     target = jnp.where(half == 0, core, 1 - core)
-    x = (my_x + 2 * (mate % 2) + far_x * onward(target) + SIDE) % SIDE
-    y = (my_y + 2 * (mate // 2) + far_y * onward(target) + SIDE) % SIDE
-    source = ((y * SIDE + x) * 2 + target) * ROWS + row
+    x, y = my_x, my_y
+    for index in range(4):
+        x = x + jnp.where(owner == index, OWNERS[index][0], 0) - jnp.where(feed == index, SOURCES[index][0], 0)
+        y = y + jnp.where(owner == index, OWNERS[index][1], 0) - jnp.where(feed == index, SOURCES[index][1], 0)
+    source = (((y + SIDE) % SIDE * SIDE + (x + SIDE) % SIDE) * 2 + target) * ROWS + row
     feature = lax.broadcasted_iota(jnp.int32, (activations.shape[1], column.shape[1]), 0)
     chosen = (feature == source).astype(activations.dtype)
     ordered = lax.dot_general(chosen, activations, (((0,), (1,)), ((), ())), preferred_element_type=jnp.float32)
@@ -64,7 +63,7 @@
 
 def product_kernel(gathered, *refs):
     cots = refs[: 4 * GROUP]
-    a_send, a_keep, b_send, b_keep = refs[4 * GROUP : 4 * GROUP + 4]
+    outs = refs[4 * GROUP : 4 * GROUP + 4]
     act, cot, act_sem, cot_sem = refs[4 * GROUP + 4 :]
     tr = lax.axis_index("tr")
     replicas, quarter, tokens = gathered.shape[1:]
@@ -93,19 +92,15 @@
         window = slice(replica * depth, (replica + 1) * depth)
         term = jnp.dot(act[:, window], cot[window], preferred_element_type=jnp.float32)
         total = term if total is None else total + term
-    half = total.shape[1] // 2
-    total = total.reshape(2, 2, 2, ROWS, 2 * half)
-    for far in range(2):
-        a_send[far] = total[:, far, 1, :, :half]
-        a_keep[far] = total[:, far, 0, :, :half]
-        b_send[far] = total[:, 1, far, :, half:]
-        b_keep[far] = total[:, 0, far, :, half:]
+    total = total.reshape(2, 4, ROWS, total.shape[1])
+    for owner in range(4):
+        outs[owner][...] = total[:, owner]
 
 
 def product(gathered, cots):
     replicas, quarter, tokens = gathered.shape[1:]
     units = cots[0].shape[1]
-    part = jax.ShapeDtypeStruct((2, 2, ROWS, units // 2), jnp.float32)
+    part = jax.ShapeDtypeStruct((2, ROWS, units), jnp.float32)
     return pl.pallas_call(
         product_kernel,
         in_specs=[pl.BlockSpec(memory_space=pl.ANY)] * (1 + len(cots)),
@@ -137,25 +132,20 @@
     other, away, own_keep = lax.optimization_barrier((other, away, own_keep))
     first_came, last_came = send(away[0], PAIR), send(away[1], PAIR)
     both = jnp.stack([ordered[0], other], axis=1)
-    shared = jnp.stack([both[0]] + [send(both[g], MATE[g]) for g in (1, 2, 3)])
+    shared = jnp.stack([both[0]] + [send(both[g], FEED[g]) for g in (1, 2, 3)])
     far_keep = send(own_keep, OTHER_CORE)
     early, shared, first_came, far_keep = lax.optimization_barrier((own_keep, shared, first_came, far_keep))
     shared = shared.reshape(2 * GROUP, QUARTER, activations.shape[0])
     gathered = lax.all_gather(shared, ("tc", "tr"), axis=0)
-    keep = [own_keep, send(early, MATE[1]), send(early, MATE[2])]
-    came = [(first_came, last_came)] + [[send(part, MATE[g]) for part in (first_came, last_came)] for g in (1, 2)]
-    came = lax.optimization_barrier([jnp.concatenate(parts) for parts in came])
-    keep[1:] = lax.optimization_barrier(keep[1:])
-    keep.append(send(keep[1], MATE[2]))
-    came.append(send(came[2], MATE[1]))
+    own_came = jnp.concatenate([first_came, last_came])
+    keep = [own_keep] + [send(early, FEED[g]) for g in (1, 2, 3)]
+    came = [own_came] + [send(own_came, FEED[g]) for g in (1, 2, 3)]
     cots = []
     for g in range(GROUP):
         cots += [keep[g], came[g], send(keep[g], OTHER_CORE) if g else far_keep, send(came[g], OTHER_CORE)]
-    a_send, a_keep, b_send, b_keep = product(gathered, cots)
-    a_came, b_came = send(a_send, NEXT_X), send(b_send, NEXT_Y)
-    a_last = send(a_keep[1] + a_came[1], NEXT_Y)
-    b_last = send(b_keep[1] + b_came[1], NEXT_X)
-    rows = jnp.concatenate([a_keep[0] + a_came[0] + a_last, b_keep[0] + b_came[0] + b_last], axis=2)
+    parts = product(gathered, cots)
+    far = [send(parts[owner], REDUCE[owner]) for owner in (1, 2, 3)]
+    rows = parts[0] + far[0] + (far[1] + far[2])
     rows = rows.reshape(2, 4, ROWS // 4, 8, units // 8)
     rows = rows.swapaxes(0, 1).reshape(8, ROWS // 4, 8, units // 8)
     rows = lax.all_to_all(rows, ("tc", "tr"), split_axis=0, concat_axis=0, tiled=True)

time: 188 us -> 174 us (0.926)
  waiting for transfers between devices: 99.1 us -> 88.1 us
  blocking collectives: 21.8 us -> 18 us
  other arithmetic: 6.4 us -> 3.21 us
  starting transfers between devices: 25.2 us -> 27.5 us
    ppermute x26 -> x23, waiting for transfers between devices: 99.1 us -> 76.9 us  [send(): return lax.ppermute(array, AXES, pairs)]
    all_gather x1, waiting for transfers between devices: 0.01 us -> 11.2 us  [shards(): gathered = lax.all_gather(shared, ('tc', 'tr'), axis=0)]
    all_to_all x1, blocking collectives: 21.8 us -> 18 us  [shards(): lax.all_to_all(rows, ('tc', 'tr'), split_axis=0, concat_axis=0, tiled=True)]
    ppermute x26 -> x23, starting transfers between devices: 25.1 us -> 27.4 us  [send(): return lax.ppermute(array, AXES, pairs)]
  transfers between devices with their start and end apart: 27 -> 24, of which waited for: 17 -> 16; matrix products, arithmetic and copies ran while one was open for 4% -> 2% of each run, Pallas kernels for 0% -> 0%
where the time goes in v9:
time: 174 us; the launch traced here: 173 us
  waiting for transfers between devices  88.1 us (51%)
  starting transfers between devices  27.5 us (16%)
  blocking collectives  18 us (10%)
  between operations  14.3 us (8%)
  Pallas kernels  13.9 us (8%)
  local copies, waits for them, and re-layouts  4.97 us (3%)
  other arithmetic  3.21 us (2%)
  matrix products  2.75 us (2%)
    ppermute x23, waiting for transfers between devices, send(): return lax.ppermute(array, AXES, pairs)  76.9 us
    ppermute x23, starting transfers between devices, send(): return lax.ppermute(array, AXES, pairs)  27.4 us
    all_to_all x1, blocking collectives, shards(): lax.all_to_all(rows, ('tc', 'tr'), split_axis=0, concat_axis=0, tiled=True)  18 us
    pallas_call x1, Pallas kernels, product(): pl.pallas_call(product_kernel, in_specs=[pl.BlockSpec(memory_space=pl.ANY...  12.7 us
    all_gather x1, waiting for transfers between devices, shards(): gathered = lax.all_gather(shared, ('tc', 'tr'), axis=0)  11.2 us
  transfers between devices with their start and end apart: 24, of which 16 were waited for; matrix products, arithmetic and copies ran while one was open for 2% of the time, Pallas kernels for 0%

profile of v9, /device:TPU:6, one launch (start us, length us, event | category | flops | bytes accessed | tf_op | source)
XLA Modules:
  0.0 172.7 jit_solution(1896219512242013349)
XLA Ops:
  7.2 0.0 copy-start
  7.2 0.0 all-gather.2.cloned.1.call-start
  7.3 2.7 %fusion.4 = bf16[1536,256]{1,0:T(8,128)(2,1)S(1)} fusion(bf16[256,1536]{1,0:T(8,128)(2,1)} %param.5, s32[1536]{0:T(1024)S(1)} %fusion.27), kind=kOutput, calls=%fused_computation.4 | convolution fusion | flops 1213071360 | bytes 1579008 | tf_op jit(solution)/shard_map/dot_general | solution.py:60
  10.1 0.8 fusion.34
  10.9 0.0 collective-permute-start
  10.9 0.8 constant_dynamic-slice_fusion
  11.7 0.1 constant_dynamic-slice_fusion.2
  11.7 0.1 constant_dynamic-slice_fusion.1.refs_0_
  11.8 1.1 collective-permute-done
  12.9 0.1 collective-permute-start.5
  13.1 1.9 %collective-permute-start.4 = (bf16[320,1024]{1,0:T(8,128)(2,1)S(1)}, bf16[320,1024]{1,0:T(8,128)(2,1)S(1)}, u32[]{:S(2)}, u32[]{:S(2)}) collective-permute-start(bf16[320,1024]{1,0:T(8,128)(2,1)S(1)} %constant_dynamic-slice_fusion.2), channel_id=1, source_target_pairs={{0,4},{1,5},{2,6},{3,7},{4,0},{5,1},{6,2},{7,3},{8,12},{9,13},{10,... | collective-permute-start | bytes 1966088 | tf_op jit(solution)/shard_map/ppermute | solution.py:37
  15.0 1.1 fusion.10
  16.1 0.9 collective-permute-start.1
  17.0 3.0 %collective-permute-start.3 = (bf16[2,192,256]{2,1,0:T(8,128)(2,1)S(1)}, bf16[2,192,256]{2,1,0:T(8,128)(2,1)S(1)}, u32[]{:S(2)}, u32[]{:S(2)}) collective-permute-start(bf16[2,192,256]{2,1,0:T(8,128)(2,1)S(1)} %get-tuple-element.44), channel_id=1, source_target_pairs={{0,192},{1,193},{2,194},{3,195},{4,196},{5,197},{6,198},{7,199},{8... | collective-permute-start | bytes 589832 | tf_op jit(solution)/shard_map/ppermute | solution.py:37
  20.0 2.4 %collective-permute-start.2 = (bf16[2,192,256]{2,1,0:T(8,128)(2,1)S(1)}, bf16[2,192,256]{2,1,0:T(8,128)(2,1)S(1)}, u32[]{:S(2)}, u32[]{:S(2)}) collective-permute-start(bf16[2,192,256]{2,1,0:T(8,128)(2,1)S(1)} %get-tuple-element.45), channel_id=1, source_target_pairs={{0,16},{1,17},{2,18},{3,19},{4,20},{5,21},{6,22},{7,23},{8,24},{9,... | collective-permute-start | bytes 589832 | tf_op jit(solution)/shard_map/ppermute | solution.py:37
  22.4 1.8 %collective-permute-done.1 = bf16[2,192,256]{2,1,0:T(8,128)(2,1)S(1)} collective-permute-done((bf16[2,192,256]{2,1,0:T(8,128)(2,1)S(1)}, bf16[2,192,256]{2,1,0:T(8,128)(2,1)S(1)}, u32[]{:S(2)}, u32[]{:S(2)}) %collective-permute-start.1) | collective-permute-done | bytes 196640 | tf_op jit(solution)/shard_map/ppermute | solution.py:37
  24.3 0.0 collective-permute-done.3
  24.3 2.1 %collective-permute-done.2 = bf16[2,192,256]{2,1,0:T(8,128)(2,1)S(1)} collective-permute-done((bf16[2,192,256]{2,1,0:T(8,128)(2,1)S(1)}, bf16[2,192,256]{2,1,0:T(8,128)(2,1)S(1)}, u32[]{:S(2)}, u32[]{:S(2)}) %collective-permute-start.2) | collective-permute-done | bytes 196640 | tf_op jit(solution)/shard_map/ppermute | solution.py:37
  26.4 1.0 pad_maximum_fusion
  27.3 2.9 %collective-permute-done.4 = bf16[320,1024]{1,0:T(8,128)(2,1)S(1)} collective-permute-done((bf16[320,1024]{1,0:T(8,128)(2,1)S(1)}, bf16[320,1024]{1,0:T(8,128)(2,1)S(1)}, u32[]{:S(2)}, u32[]{:S(2)}) %collective-permute-start.4) | collective-permute-done | bytes 655392 | tf_op jit(solution)/shard_map/ppermute | solution.py:37
  30.3 0.0 collective-permute-done.5.refs_2_
  30.3 0.9 copy-done.5
  31.1 1.0 copy-done.7
  32.2 0.0 all-gather.2.cloned.1.call-update
  32.2 1.8 %collective-permute-start.6 = (bf16[192,1024]{1,0:T(8,128)(2,1)}, bf16[192,1024]{1,0:T(8,128)(2,1)S(1)}, u32[]{:S(2)}, u32[]{:S(2)}) collective-permute-start(bf16[192,1024]{1,0:T(8,128)(2,1)} %constant_dynamic-slice_fusion), channel_id=1, source_target_pairs={{0,4},{1,5},{2,6},{3,7},{4,0},{5,1},{6,2},{7,3},{8,12},{9,13},{10,... | collective-permute-start | bytes 1179656 | tf_op jit(solution)/shard_map/ppermute | solution.py:37
  34.0 1.1 constant_dynamic-update-slice_fusion.1
  35.1 8.1 %collective-permute-done.6 = bf16[192,1024]{1,0:T(8,128)(2,1)S(1)} collective-permute-done((bf16[192,1024]{1,0:T(8,128)(2,1)}, bf16[192,1024]{1,0:T(8,128)(2,1)S(1)}, u32[]{:S(2)}, u32[]{:S(2)}) %collective-permute-start.6) | collective-permute-done | bytes 393248 | tf_op jit(solution)/shard_map/ppermute | solution.py:37
  43.3 3.1 %collective-permute-start.17 = (bf16[512,1024]{1,0:T(8,128)(2,1)S(1)}, bf16[512,1024]{1,0:T(8,128)(2,1)S(1)}, u32[]{:S(2)}, u32[]{:S(2)}) collective-permute-start(bf16[512,1024]{1,0:T(8,128)(2,1)S(1)} %constant_dynamic-update-slice_fusion.refs_1_), channel_id=1, source_target_pairs={{0,192},{1,193},{2,194},{3,195},{4,196},{5,197},{6,198},{7,199},{8... | collective-permute-start | bytes 3145736 | tf_op jit(solution)/shard_map/ppermute | solution.py:37
  46.4 0.5 collective-permute-start.13
  46.9 1.5 collective-permute-start.9
  48.4 0.0 collective-permute-start.7
  48.4 0.7 collective-permute-start.16
  49.2 20.8 %collective-permute-done.17.refs_13_ = bf16[512,1024]{1,0:T(8,128)(2,1)S(1)} collective-permute-done((bf16[512,1024]{1,0:T(8,128)(2,1)S(1)}, bf16[512,1024]{1,0:T(8,128)(2,1)S(1)}, u32[]{:S(2)}, u32[]{:S(2)}) %collective-permute-start.17) | collective-permute-done | bytes 1048608 | tf_op jit(solution)/shard_map/ppermute | solution.py:37
  70.0 1.3 collective-permute-start.12
  71.3 0.3 collective-permute-done.13.refs_9_
  71.6 0.8 collective-permute-start.8
  72.5 0.0 collective-permute-done.9.refs_5_
  72.5 0.0 collective-permute-start.19
  72.5 0.0 collective-permute-done.7.refs_3_
  72.5 0.5 collective-permute-start.15
  73.0 17.3 %collective-permute-done.16.refs_12_ = bf16[512,1024]{1,0:T(8,128)(2,1)S(1)} collective-permute-done((bf16[512,1024]{1,0:T(8,128)(2,1)S(1)}, bf16[512,1024]{1,0:T(8,128)(2,1)S(1)}, u32[]{:S(2)}, u32[]{:S(2)}) %collective-permute-start.16) | collective-permute-done | bytes 1048608 | tf_op jit(solution)/shard_map/ppermute | solution.py:37
  90.3 0.0 collective-permute-start.11
  90.3 2.2 %collective-permute-done.12.refs_8_ = bf16[512,1024]{1,0:T(8,128)(2,1)S(1)} collective-permute-done((bf16[512,1024]{1,0:T(8,128)(2,1)S(1)}, bf16[512,1024]{1,0:T(8,128)(2,1)S(1)}, u32[]{:S(2)}, u32[]{:S(2)}) %collective-permute-start.12) | collective-permute-done | bytes 1048608 | tf_op jit(solution)/shard_map/ppermute | solution.py:37
  92.5 1.6 collective-permute-done.8.refs_4_
  94.1 0.0 collective-permute-start.14
  94.1 0.6 collective-permute-start.10
  94.7 0.0 collective-permute-done.11.refs_7_
  94.8 0.4 collective-permute-done.18.refs_14_
  95.2 1.7 %collective-permute-done.14.refs_10_ = bf16[512,1024]{1,0:T(8,128)(2,1)S(1)} collective-permute-done((bf16[512,1024]{1,0:T(8,128)(2,1)S(1)}, bf16[512,1024]{1,0:T(8,128)(2,1)S(1)}, u32[]{:S(2)}, u32[]{:S(2)}) %collective-permute-start.14) | collective-permute-done | bytes 1048608 | tf_op jit(solution)/shard_map/ppermute | solution.py:37
  97.0 1.4 collective-permute-done.10.refs_6_
  98.4 11.2 %all-gather.2.cloned.1.call-done.gathered = bf16[8,8,192,256]{3,2,1,0:T(8,128)(2,1)} async-done(((bf16[1,8,192,256]{3,2,1,0:T(8,128)(2,1)}), bf16[8,8,192,256]{3,2,1,0:T(8,128)(2,1)}) %all-gather.2.cloned.1.call-update) | async-done | bytes 6291472 | tf_op jit(solution)/shard_map/all_gather | solution.py:139
  109.6 12.7 %shard_map.76 = (f32[2,48,1024]{2,1,0:T(8,128)}, f32[2,48,1024]{2,1,0:T(8,128)}, f32[2,48,1024]{2,1,0:T(8,128)}, f32[2,48,1024]{2,1,0:T(8,128)}) custom-call(bf16[8,8,192,256]{3,2,1,0:T(8,128)(2,1)} %all-gather.2.cloned.1.call-done.gathered, bf16[512,1024]{1,0:T(8,128)(2,1)} %copy-done.4, bf16[512,1024]{1,0:T(8,128)(2,1)} %copy-done.6, ...), custom_call_target="tpu_custom_call" | custom-call | flops 6442450944 | bytes 29360128 | tf_op jit(solution)/shard_map/pallas_call | solution.py:104
  122.2 0.0 copy-start.1
  122.3 0.0 copy-start.2
  122.3 0.0 copy-start.3
  122.3 2.5 %collective-permute-start.20 = (f32[2,48,1024]{2,1,0:T(8,128)}, f32[2,48,1024]{2,1,0:T(8,128)S(1)}, u32[]{:S(2)}, u32[]{:S(2)}) collective-permute-start(f32[2,48,1024]{2,1,0:T(8,128)} %get-tuple-element.27), channel_id=1, source_target_pairs={{0,96},{1,97},{2,98},{3,99},{4,100},{5,101},{6,102},{7,103},{8,104... | collective-permute-start | bytes 1179656 | tf_op jit(solution)/shard_map/ppermute | solution.py:37
  124.7 2.7 %collective-permute-start.21 = (f32[2,48,1024]{2,1,0:T(8,128)}, f32[2,48,1024]{2,1,0:T(8,128)S(1)}, u32[]{:S(2)}, u32[]{:S(2)}) collective-permute-start(f32[2,48,1024]{2,1,0:T(8,128)} %get-tuple-element.28), channel_id=1, source_target_pairs={{0,128},{1,129},{2,130},{3,131},{4,132},{5,133},{6,134},{7,135},{8... | collective-permute-start | bytes 1179656 | tf_op jit(solution)/shard_map/ppermute | solution.py:37
  127.5 3.0 %collective-permute-start.22 = (f32[2,48,1024]{2,1,0:T(8,128)}, f32[2,48,1024]{2,1,0:T(8,128)S(1)}, u32[]{:S(2)}, u32[]{:S(2)}) collective-permute-start(f32[2,48,1024]{2,1,0:T(8,128)} %get-tuple-element.29), channel_id=1, source_target_pairs={{0,224},{1,225},{2,226},{3,227},{4,228},{5,229},{6,230},{7,231},{8... | collective-permute-start | bytes 1179656 | tf_op jit(solution)/shard_map/ppermute | solution.py:37
  130.4 8.8 %collective-permute-done.20 = f32[2,48,1024]{2,1,0:T(8,128)S(1)} collective-permute-done((f32[2,48,1024]{2,1,0:T(8,128)}, f32[2,48,1024]{2,1,0:T(8,128)S(1)}, u32[]{:S(2)}, u32[]{:S(2)}) %collective-permute-start.20) | collective-permute-done | bytes 393248 | tf_op jit(solution)/shard_map/ppermute | solution.py:37
  139.2 6.2 %collective-permute-done.21 = f32[2,48,1024]{2,1,0:T(8,128)S(1)} collective-permute-done((f32[2,48,1024]{2,1,0:T(8,128)}, f32[2,48,1024]{2,1,0:T(8,128)S(1)}, u32[]{:S(2)}, u32[]{:S(2)}) %collective-permute-start.21) | collective-permute-done | bytes 393248 | tf_op jit(solution)/shard_map/ppermute | solution.py:37
  145.5 1.1 add_add_fusion
  146.5 0.1 copy.28
  146.7 18.0 %all_to_all.5.rows = f32[8,12,8,128]{3,2,1,0:T(8,128)S(1)} all-to-all(f32[8,12,8,128]{3,2,1,0:T(8,128)S(1)} %bitcast.38), channel_id=1, replica_groups=mesh['dp'=32,'tr'=2,'tc'=4] {'tc','tr'}, dimensions={0} | all-to-all | bytes 786432 | tf_op jit(solution)/shard_map/all_to_all | solution.py:151
  164.6 1.2 shard_map.77
  (41 shorter events, 0.2 us)
Async XLA Ops:
  7.2 3.7 %copy-start = (bf16[512,2048]{1,0:T(8,128)(2,1)S(1)}, bf16[512,2048]{1,0:T(8,128)(2,1)}, u32[]{:S(2)}) copy-start(bf16[512,2048]{1,0:T(8,128)(2,1)} %param.6) | copy-start | bytes 6291460
  7.2 102.4 %all-gather.2.cloned.1.call-start = ((), (), s32[]{:S(2)}) async-start(), calls=%async_computation.1 | async-start | bytes 7077888 | tf_op jit(solution)/shard_map/all_gather | solution.py:139
  10.9 2.1 %collective-permute-start = (bf16[4,192,256]{2,1,0:T(8,128)(2,1)}, bf16[4,192,256]{2,1,0:T(8,128)(2,1)}, u32[]{:S(2)}, u32[]{:S(2)}) collective-permute-start(bf16[4,192,256]{2,1,0:T(8,128)(2,1)} %bitcast), channel_id=1, source_target_pairs={{0,8},{1,9},{2,10},{3,11},{4,12},{5,13},{6,14},{7,15},{8,0},{9,1},... | collective-permute-start | bytes 1179656 | tf_op jit(solution)/shard_map/ppermute | solution.py:37
  11.8 59.8 %copy-start.4 = (bf16[512,1024]{1,0:T(8,128)(2,1)}, bf16[512,1024]{1,0:T(8,128)(2,1)S(1)}, u32[]{:S(2)}) copy-start(bf16[512,1024]{1,0:T(8,128)(2,1)S(1)} %constant_dynamic-slice_fusion.1.refs_0_) | copy-start | bytes 3145732
  12.9 17.3 %collective-permute-start.5 = (bf16[512,1024]{1,0:T(8,128)(2,1)S(1)}, bf16[512,1024]{1,0:T(8,128)(2,1)S(1)}, u32[]{:S(2)}, u32[]{:S(2)}) collective-permute-start(bf16[512,1024]{1,0:T(8,128)(2,1)S(1)} %constant_dynamic-slice_fusion.1.refs_0_), channel_id=1, source_target_pairs={{0,8},{1,9},{2,10},{3,11},{4,12},{5,13},{6,14},{7,15},{8,0},{9,1},... | collective-permute-start | bytes 3145736 | tf_op jit(solution)/shard_map/ppermute | solution.py:37
  13.1 17.2 %collective-permute-start.4 = (bf16[320,1024]{1,0:T(8,128)(2,1)S(1)}, bf16[320,1024]{1,0:T(8,128)(2,1)S(1)}, u32[]{:S(2)}, u32[]{:S(2)}) collective-permute-start(bf16[320,1024]{1,0:T(8,128)(2,1)S(1)} %constant_dynamic-slice_fusion.2), channel_id=1, source_target_pairs={{0,4},{1,5},{2,6},{3,7},{4,0},{5,1},{6,2},{7,3},{8,12},{9,13},{10,... | collective-permute-start | bytes 1966088 | tf_op jit(solution)/shard_map/ppermute | solution.py:37
  16.1 8.2 %collective-permute-start.1 = (bf16[2,192,256]{2,1,0:T(8,128)(2,1)S(1)}, bf16[2,192,256]{2,1,0:T(8,128)(2,1)S(1)}, u32[]{:S(2)}, u32[]{:S(2)}) collective-permute-start(bf16[2,192,256]{2,1,0:T(8,128)(2,1)S(1)} %get-tuple-element.43), channel_id=1, source_target_pairs={{0,48},{1,49},{2,50},{3,51},{4,52},{5,53},{6,54},{7,55},{8,56},{9,... | collective-permute-start | bytes 589832 | tf_op jit(solution)/shard_map/ppermute | solution.py:37
  17.0 7.3 %collective-permute-start.3 = (bf16[2,192,256]{2,1,0:T(8,128)(2,1)S(1)}, bf16[2,192,256]{2,1,0:T(8,128)(2,1)S(1)}, u32[]{:S(2)}, u32[]{:S(2)}) collective-permute-start(bf16[2,192,256]{2,1,0:T(8,128)(2,1)S(1)} %get-tuple-element.44), channel_id=1, source_target_pairs={{0,192},{1,193},{2,194},{3,195},{4,196},{5,197},{6,198},{7,199},{8... | collective-permute-start | bytes 589832 | tf_op jit(solution)/shard_map/ppermute | solution.py:37
  20.0 6.3 %collective-permute-start.2 = (bf16[2,192,256]{2,1,0:T(8,128)(2,1)S(1)}, bf16[2,192,256]{2,1,0:T(8,128)(2,1)S(1)}, u32[]{:S(2)}, u32[]{:S(2)}) collective-permute-start(bf16[2,192,256]{2,1,0:T(8,128)(2,1)S(1)} %get-tuple-element.45), channel_id=1, source_target_pairs={{0,16},{1,17},{2,18},{3,19},{4,20},{5,21},{6,22},{7,23},{8,24},{9,... | collective-permute-start | bytes 589832 | tf_op jit(solution)/shard_map/ppermute | solution.py:37
  30.3 0.9 copy-start.5
  31.1 1.0 copy-start.7
  32.2 11.1 %collective-permute-start.6 = (bf16[192,1024]{1,0:T(8,128)(2,1)}, bf16[192,1024]{1,0:T(8,128)(2,1)S(1)}, u32[]{:S(2)}, u32[]{:S(2)}) collective-permute-start(bf16[192,1024]{1,0:T(8,128)(2,1)} %constant_dynamic-slice_fusion), channel_id=1, source_target_pairs={{0,4},{1,5},{2,6},{3,7},{4,0},{5,1},{6,2},{7,3},{8,12},{9,13},{10,... | collective-permute-start | bytes 1179656 | tf_op jit(solution)/shard_map/ppermute | solution.py:37
  43.3 50.8 %copy-start.6 = (bf16[512,1024]{1,0:T(8,128)(2,1)}, bf16[512,1024]{1,0:T(8,128)(2,1)S(1)}, u32[]{:S(2)}) copy-start(bf16[512,1024]{1,0:T(8,128)(2,1)S(1)} %constant_dynamic-update-slice_fusion.refs_1_) | copy-start | bytes 3145732
  43.3 26.7 %collective-permute-start.17 = (bf16[512,1024]{1,0:T(8,128)(2,1)S(1)}, bf16[512,1024]{1,0:T(8,128)(2,1)S(1)}, u32[]{:S(2)}, u32[]{:S(2)}) collective-permute-start(bf16[512,1024]{1,0:T(8,128)(2,1)S(1)} %constant_dynamic-update-slice_fusion.refs_1_), channel_id=1, source_target_pairs={{0,192},{1,193},{2,194},{3,195},{4,196},{5,197},{6,198},{7,199},{8... | collective-permute-start | bytes 3145736 | tf_op jit(solution)/shard_map/ppermute | solution.py:37
  46.4 25.2 %collective-permute-start.13 = (bf16[512,1024]{1,0:T(8,128)(2,1)S(1)}, bf16[512,1024]{1,0:T(8,128)(2,1)S(1)}, u32[]{:S(2)}, u32[]{:S(2)}) collective-permute-start(bf16[512,1024]{1,0:T(8,128)(2,1)S(1)} %constant_dynamic-update-slice_fusion.refs_1_), channel_id=1, source_target_pairs={{0,16},{1,17},{2,18},{3,19},{4,20},{5,21},{6,22},{7,23},{8,24},{9,... | collective-permute-start | bytes 3145736 | tf_op jit(solution)/shard_map/ppermute | solution.py:37
  46.9 25.6 %collective-permute-start.9 = (bf16[512,1024]{1,0:T(8,128)(2,1)S(1)}, bf16[512,1024]{1,0:T(8,128)(2,1)S(1)}, u32[]{:S(2)}, u32[]{:S(2)}) collective-permute-start(bf16[512,1024]{1,0:T(8,128)(2,1)S(1)} %constant_dynamic-update-slice_fusion.refs_1_), channel_id=1, source_target_pairs={{0,48},{1,49},{2,50},{3,51},{4,52},{5,53},{6,54},{7,55},{8,56},{9,... | collective-permute-start | bytes 3145736 | tf_op jit(solution)/shard_map/ppermute | solution.py:37
  48.4 24.1 %collective-permute-start.7 = (bf16[512,1024]{1,0:T(8,128)(2,1)S(1)}, bf16[512,1024]{1,0:T(8,128)(2,1)S(1)}, u32[]{:S(2)}, u32[]{:S(2)}) collective-permute-start(bf16[512,1024]{1,0:T(8,128)(2,1)S(1)} %constant_dynamic-update-slice_fusion.refs_1_), channel_id=1, source_target_pairs={{0,8},{1,9},{2,10},{3,11},{4,12},{5,13},{6,14},{7,15},{8,0},{9,1},... | collective-permute-start | bytes 3145736 | tf_op jit(solution)/shard_map/ppermute | solution.py:37
  48.4 41.9 %collective-permute-start.16 = (bf16[512,1024]{1,0:T(8,128)(2,1)S(1)}, bf16[512,1024]{1,0:T(8,128)(2,1)S(1)}, u32[]{:S(2)}, u32[]{:S(2)}) collective-permute-start(bf16[512,1024]{1,0:T(8,128)(2,1)S(1)} %constant_dynamic-slice_fusion.1.refs_0_), channel_id=1, source_target_pairs={{0,192},{1,193},{2,194},{3,195},{4,196},{5,197},{6,198},{7,199},{8... | collective-permute-start | bytes 3145736 | tf_op jit(solution)/shard_map/ppermute | solution.py:37
  70.0 24.1 %copy-start.8 = (bf16[512,1024]{1,0:T(8,128)(2,1)}, bf16[512,1024]{1,0:T(8,128)(2,1)S(1)}, u32[]{:S(2)}) copy-start(bf16[512,1024]{1,0:T(8,128)(2,1)S(1)} %collective-permute-done.17.refs_13_) | copy-start | bytes 3145732
  70.0 22.5 %collective-permute-start.12 = (bf16[512,1024]{1,0:T(8,128)(2,1)S(1)}, bf16[512,1024]{1,0:T(8,128)(2,1)S(1)}, u32[]{:S(2)}, u32[]{:S(2)}) collective-permute-start(bf16[512,1024]{1,0:T(8,128)(2,1)S(1)} %constant_dynamic-slice_fusion.1.refs_0_), channel_id=1, source_target_pairs={{0,16},{1,17},{2,18},{3,19},{4,20},{5,21},{6,22},{7,23},{8,24},{9,... | collective-permute-start | bytes 3145736 | tf_op jit(solution)/shard_map/ppermute | solution.py:37
  71.6 22.5 %copy-start.9 = (bf16[512,1024]{1,0:T(8,128)(2,1)}, bf16[512,1024]{1,0:T(8,128)(2,1)S(1)}, u32[]{:S(2)}) copy-start(bf16[512,1024]{1,0:T(8,128)(2,1)S(1)} %collective-permute-done.13.refs_9_) | copy-start | bytes 3145732
  71.6 22.5 %collective-permute-start.8 = (bf16[512,1024]{1,0:T(8,128)(2,1)S(1)}, bf16[512,1024]{1,0:T(8,128)(2,1)S(1)}, u32[]{:S(2)}, u32[]{:S(2)}) collective-permute-start(bf16[512,1024]{1,0:T(8,128)(2,1)S(1)} %constant_dynamic-slice_fusion.1.refs_0_), channel_id=1, source_target_pairs={{0,48},{1,49},{2,50},{3,51},{4,52},{5,53},{6,54},{7,55},{8,56},{9,... | collective-permute-start | bytes 3145736 | tf_op jit(solution)/shard_map/ppermute | solution.py:37
  72.5 22.3 %copy-start.10 = (bf16[512,1024]{1,0:T(8,128)(2,1)}, bf16[512,1024]{1,0:T(8,128)(2,1)S(1)}, u32[]{:S(2)}) copy-start(bf16[512,1024]{1,0:T(8,128)(2,1)S(1)} %collective-permute-done.9.refs_5_) | copy-start | bytes 3145732
  72.5 21.6 %collective-permute-start.19 = (bf16[512,1024]{1,0:T(8,128)(2,1)S(1)}, bf16[512,1024]{1,0:T(8,128)(2,1)S(1)}, u32[]{:S(2)}, u32[]{:S(2)}) collective-permute-start(bf16[512,1024]{1,0:T(8,128)(2,1)S(1)} %collective-permute-done.17.refs_13_), channel_id=1, source_target_pairs={{0,8},{1,9},{2,10},{3,11},{4,12},{5,13},{6,14},{7,15},{8,0},{9,1},... | collective-permute-start | bytes 3145736 | tf_op jit(solution)/shard_map/ppermute | solution.py:37
  72.5 22.2 %copy-start.11 = (bf16[512,1024]{1,0:T(8,128)(2,1)}, bf16[512,1024]{1,0:T(8,128)(2,1)S(1)}, u32[]{:S(2)}) copy-start(bf16[512,1024]{1,0:T(8,128)(2,1)S(1)} %collective-permute-done.7.refs_3_) | copy-start | bytes 3145732
  72.5 22.2 %collective-permute-start.15 = (bf16[512,1024]{1,0:T(8,128)(2,1)S(1)}, bf16[512,1024]{1,0:T(8,128)(2,1)S(1)}, u32[]{:S(2)}, u32[]{:S(2)}) collective-permute-start(bf16[512,1024]{1,0:T(8,128)(2,1)S(1)} %collective-permute-done.13.refs_9_), channel_id=1, source_target_pairs={{0,8},{1,9},{2,10},{3,11},{4,12},{5,13},{6,14},{7,15},{8,0},{9,1},... | collective-permute-start | bytes 3145736 | tf_op jit(solution)/shard_map/ppermute | solution.py:37
  90.3 4.9 %copy-start.12 = (bf16[512,1024]{1,0:T(8,128)(2,1)}, bf16[512,1024]{1,0:T(8,128)(2,1)S(1)}, u32[]{:S(2)}) copy-start(bf16[512,1024]{1,0:T(8,128)(2,1)S(1)} %collective-permute-done.16.refs_12_) | copy-start | bytes 3145732
  90.3 4.4 %collective-permute-start.11 = (bf16[512,1024]{1,0:T(8,128)(2,1)S(1)}, bf16[512,1024]{1,0:T(8,128)(2,1)S(1)}, u32[]{:S(2)}, u32[]{:S(2)}) collective-permute-start(bf16[512,1024]{1,0:T(8,128)(2,1)S(1)} %collective-permute-done.9.refs_5_), channel_id=1, source_target_pairs={{0,8},{1,9},{2,10},{3,11},{4,12},{5,13},{6,14},{7,15},{8,0},{9,1},... | collective-permute-start | bytes 3145736 | tf_op jit(solution)/shard_map/ppermute | solution.py:37
  92.5 4.4 %copy-start.13 = (bf16[512,1024]{1,0:T(8,128)(2,1)}, bf16[512,1024]{1,0:T(8,128)(2,1)S(1)}, u32[]{:S(2)}) copy-start(bf16[512,1024]{1,0:T(8,128)(2,1)S(1)} %collective-permute-done.12.refs_8_) | copy-start | bytes 3145732
  92.5 2.7 %collective-permute-start.18 = (bf16[512,1024]{1,0:T(8,128)(2,1)S(1)}, bf16[512,1024]{1,0:T(8,128)(2,1)S(1)}, u32[]{:S(2)}, u32[]{:S(2)}) collective-permute-start(bf16[512,1024]{1,0:T(8,128)(2,1)S(1)} %collective-permute-done.16.refs_12_), channel_id=1, source_target_pairs={{0,8},{1,9},{2,10},{3,11},{4,12},{5,13},{6,14},{7,15},{8,0},{9,1},... | collective-permute-start | bytes 3145736 | tf_op jit(solution)/shard_map/ppermute | solution.py:37
  94.1 2.8 %copy-start.14 = (bf16[512,1024]{1,0:T(8,128)(2,1)}, bf16[512,1024]{1,0:T(8,128)(2,1)S(1)}, u32[]{:S(2)}) copy-start(bf16[512,1024]{1,0:T(8,128)(2,1)S(1)} %collective-permute-done.8.refs_4_) | copy-start | bytes 3145732
  94.1 2.8 %collective-permute-start.14 = (bf16[512,1024]{1,0:T(8,128)(2,1)S(1)}, bf16[512,1024]{1,0:T(8,128)(2,1)S(1)}, u32[]{:S(2)}, u32[]{:S(2)}) collective-permute-start(bf16[512,1024]{1,0:T(8,128)(2,1)S(1)} %collective-permute-done.12.refs_8_), channel_id=1, source_target_pairs={{0,8},{1,9},{2,10},{3,11},{4,12},{5,13},{6,14},{7,15},{8,0},{9,1},... | collective-permute-start | bytes 3145736 | tf_op jit(solution)/shard_map/ppermute | solution.py:37
  94.1 2.8 %copy-start.15 = (bf16[512,1024]{1,0:T(8,128)(2,1)}, bf16[512,1024]{1,0:T(8,128)(2,1)S(1)}, u32[]{:S(2)}) copy-start(bf16[512,1024]{1,0:T(8,128)(2,1)S(1)} %collective-permute-done.19.refs_15_) | copy-start | bytes 3145732
  94.1 4.2 %collective-permute-start.10 = (bf16[512,1024]{1,0:T(8,128)(2,1)S(1)}, bf16[512,1024]{1,0:T(8,128)(2,1)}, u32[]{:S(2)}, u32[]{:S(2)}) collective-permute-start(bf16[512,1024]{1,0:T(8,128)(2,1)S(1)} %collective-permute-done.8.refs_4_), channel_id=1, source_target_pairs={{0,8},{1,9},{2,10},{3,11},{4,12},{5,13},{6,14},{7,15},{8,0},{9,1},... | collective-permute-start | bytes 3145736 | tf_op jit(solution)/shard_map/ppermute | solution.py:37
  94.7 2.2 %copy-start.16 = (bf16[512,1024]{1,0:T(8,128)(2,1)}, bf16[512,1024]{1,0:T(8,128)(2,1)S(1)}, u32[]{:S(2)}) copy-start(bf16[512,1024]{1,0:T(8,128)(2,1)S(1)} %collective-permute-done.15.refs_11_) | copy-start | bytes 3145732
  94.7 2.2 %copy-start.17 = (bf16[512,1024]{1,0:T(8,128)(2,1)}, bf16[512,1024]{1,0:T(8,128)(2,1)S(1)}, u32[]{:S(2)}) copy-start(bf16[512,1024]{1,0:T(8,128)(2,1)S(1)} %collective-permute-done.11.refs_7_) | copy-start | bytes 3145732
  95.2 1.8 %copy-start.18 = (bf16[512,1024]{1,0:T(8,128)(2,1)}, bf16[512,1024]{1,0:T(8,128)(2,1)S(1)}, u32[]{:S(2)}) copy-start(bf16[512,1024]{1,0:T(8,128)(2,1)S(1)} %collective-permute-done.18.refs_14_) | copy-start | bytes 3145732
  97.0 12.6 %copy-start.19 = (bf16[512,1024]{1,0:T(8,128)(2,1)}, bf16[512,1024]{1,0:T(8,128)(2,1)S(1)}, u32[]{:S(2)}) copy-start(bf16[512,1024]{1,0:T(8,128)(2,1)S(1)} %collective-permute-done.14.refs_10_) | copy-start | bytes 3145732
  122.2 42.4 %copy-start.1 = (f32[1,12,8192]{2,0,1:T(1,128)S(1)}, f32[1,12,8192]{2,0,1:T(1,128)}, u32[]{:S(2)}) copy-start(f32[1,12,8192]{2,0,1:T(1,128)} %param.7) | copy-start | bytes 1179652
  122.3 42.4 %copy-start.2 = (f32[1,12,8192]{2,0,1:T(1,128)S(1)}, f32[1,12,8192]{2,0,1:T(1,128)}, u32[]{:S(2)}) copy-start(f32[1,12,8192]{2,0,1:T(1,128)} %param.8) | copy-start | bytes 1179652
  122.3 42.4 %copy-start.3 = (f32[1,12,8192]{2,0,1:T(1,128)S(1)}, f32[1,12,8192]{2,0,1:T(1,128)}, u32[]{:S(2)}) copy-start(f32[1,12,8192]{2,0,1:T(1,128)} %param.9) | copy-start | bytes 1179652
  122.3 16.9 %collective-permute-start.20 = (f32[2,48,1024]{2,1,0:T(8,128)}, f32[2,48,1024]{2,1,0:T(8,128)S(1)}, u32[]{:S(2)}, u32[]{:S(2)}) collective-permute-start(f32[2,48,1024]{2,1,0:T(8,128)} %get-tuple-element.27), channel_id=1, source_target_pairs={{0,96},{1,97},{2,98},{3,99},{4,100},{5,101},{6,102},{7,103},{8,104... | collective-permute-start | bytes 1179656 | tf_op jit(solution)/shard_map/ppermute | solution.py:37
  124.7 20.7 %collective-permute-start.21 = (f32[2,48,1024]{2,1,0:T(8,128)}, f32[2,48,1024]{2,1,0:T(8,128)S(1)}, u32[]{:S(2)}, u32[]{:S(2)}) collective-permute-start(f32[2,48,1024]{2,1,0:T(8,128)} %get-tuple-element.28), channel_id=1, source_target_pairs={{0,128},{1,129},{2,130},{3,131},{4,132},{5,133},{6,134},{7,135},{8... | collective-permute-start | bytes 1179656 | tf_op jit(solution)/shard_map/ppermute | solution.py:37
  127.5 18.0 %collective-permute-start.22 = (f32[2,48,1024]{2,1,0:T(8,128)}, f32[2,48,1024]{2,1,0:T(8,128)S(1)}, u32[]{:S(2)}, u32[]{:S(2)}) collective-permute-start(f32[2,48,1024]{2,1,0:T(8,128)} %get-tuple-element.29), channel_id=1, source_target_pairs={{0,224},{1,225},{2,226},{3,227},{4,228},{5,229},{6,230},{7,231},{8... | collective-permute-start | bytes 1179656 | tf_op jit(solution)/shard_map/ppermute | solution.py:37
Sparse Core Ops, SparseCore 0:
  32.3 77.1 all-gather.1

commit v10 on v9

--- a/solution.py
+++ b/solution.py
@@ -17,6 +17,7 @@
 SIDE = 4
 ROWS = 48
 GROUP = 4
+AHEAD = 3
 SOURCES = ((0, 0), (1, 0), (-1, 0), (0, 1))
 OWNERS = ((0, 0), (2, 1), (0, 2), (2, 3))
 QUARTER = 4 * ROWS
@@ -82,11 +83,16 @@
             copies.append(pltpu.make_async_copy(cots[n], cot.at[pl.ds(start, 2 * tokens)], cot_sem.at[n]))
         return copies
 
-    for replica in range(replicas):
+    def fetch(replica):
         for copy in copies_of(replica):
             copy.start()
+
+    for replica in range(AHEAD):
+        fetch(replica)
     total = None
     for replica in range(replicas):
+        if replica + AHEAD < replicas:
+            fetch(replica + AHEAD)
         for copy in copies_of(replica):
             copy.wait()
         window = slice(replica * depth, (replica + 1) * depth)
@@ -126,15 +132,14 @@
     tokens = cotangent.shape[0]
     away = [
         lax.dynamic_slice(cotangent, (start, (1 - tr) * units), (size, units))
-        for start, size in ((0, tokens * 5 // 8), (tokens * 5 // 8, tokens * 3 // 8))
+        for start, size in ((0, tokens // 2), (tokens // 2, tokens // 2))
     ]
     own_keep = lax.dynamic_slice_in_dim(cotangent, tr * units, units, 1)
     other, away, own_keep = lax.optimization_barrier((other, away, own_keep))
     first_came, last_came = send(away[0], PAIR), send(away[1], PAIR)
     both = jnp.stack([ordered[0], other], axis=1)
     shared = jnp.stack([both[0]] + [send(both[g], FEED[g]) for g in (1, 2, 3)])
-    far_keep = send(own_keep, OTHER_CORE)
-    early, shared, first_came, far_keep = lax.optimization_barrier((own_keep, shared, first_came, far_keep))
+    early, shared, first_came = lax.optimization_barrier((own_keep, shared, first_came))
     shared = shared.reshape(2 * GROUP, QUARTER, activations.shape[0])
     gathered = lax.all_gather(shared, ("tc", "tr"), axis=0)
     own_came = jnp.concatenate([first_came, last_came])
@@ -142,9 +147,10 @@
     came = [own_came] + [send(own_came, FEED[g]) for g in (1, 2, 3)]
     cots = []
     for g in range(GROUP):
-        cots += [keep[g], came[g], send(keep[g], OTHER_CORE) if g else far_keep, send(came[g], OTHER_CORE)]
+        cots += [keep[g], came[g], send(keep[g], OTHER_CORE), send(came[g], OTHER_CORE)]
     parts = product(gathered, cots)
-    far = [send(parts[owner], REDUCE[owner]) for owner in (1, 2, 3)]
+    far = [send(parts[owner], REDUCE[owner]) for owner in (1, 3)]
+    far.append(send(parts[2], REDUCE[2]))
     rows = parts[0] + far[0] + (far[1] + far[2])
     rows = rows.reshape(2, 4, ROWS // 4, 8, units // 8)
     rows = rows.swapaxes(0, 1).reshape(8, ROWS // 4, 8, units // 8)

time: 174 us -> 170 us (0.977)
    all_gather x1, waiting for transfers between devices: 11.2 us -> 8.18 us  [shards(): gathered = lax.all_gather(shared, ('tc', 'tr'), axis=0)]
    unnamed x42, local copies, waits for them, and re-layouts: 3.19 us -> 1.19 us
  transfers between devices with their start and end apart: 24 -> 24, of which waited for: 16 -> 15; matrix products, arithmetic and copies ran while one was open for 2% -> 2% of each run, Pallas kernels for 0% -> 0%
where the time goes in v10:
time: 170 us; the launch traced here: 169 us
  waiting for transfers between devices  86.6 us (51%)
  starting transfers between devices  27.1 us (16%)
  blocking collectives  19.5 us (11%)
  between operations  14.3 us (8%)
  Pallas kernels  13.2 us (8%)
  local copies, waits for them, and re-layouts  4.07 us (2%)
  other arithmetic  3.21 us (2%)
    ppermute x23, waiting for transfers between devices, send(): return lax.ppermute(array, AXES, pairs)  78.4 us
    ppermute x23, starting transfers between devices, send(): return lax.ppermute(array, AXES, pairs)  27.1 us
    all_to_all x1, blocking collectives, shards(): lax.all_to_all(rows, ('tc', 'tr'), split_axis=0, concat_axis=0, tiled=True)  19.5 us
    pallas_call x1, Pallas kernels, product(): pl.pallas_call(product_kernel, in_specs=[pl.BlockSpec(memory_space=pl.ANY...  12 us
    all_gather x1, waiting for transfers between devices, shards(): gathered = lax.all_gather(shared, ('tc', 'tr'), axis=0)  8.18 us
  transfers between devices with their start and end apart: 24, of which 15 were waited for; matrix products, arithmetic and copies ran while one was open for 2% of the time, Pallas kernels for 0%

profile of v10, /device:TPU:6, one launch (start us, length us, event | category | flops | bytes accessed | tf_op | source)
XLA Modules:
  0.0 169.4 jit_solution(15887979576323877507)
XLA Ops:
  7.2 0.0 copy-start
  7.2 0.0 all-gather.2.cloned.1.call-start
  7.3 1.0 copy-done
  8.3 1.5 fusion.4
  9.8 0.8 fusion.34
  10.6 0.0 collective-permute-start
  10.6 1.1 constant_dynamic-slice_fusion.1.refs_0_
  11.7 0.9 constant_dynamic-slice_fusion
  12.6 0.0 collective-permute-done
  12.7 1.9 %collective-permute-start.4 = (bf16[256,1024]{1,0:T(8,128)(2,1)S(1)}, bf16[256,1024]{1,0:T(8,128)(2,1)S(1)}, u32[]{:S(2)}, u32[]{:S(2)}) collective-permute-start(bf16[256,1024]{1,0:T(8,128)(2,1)S(1)} %get-tuple-element.19), channel_id=1, source_target_pairs={{0,4},{1,5},{2,6},{3,7},{4,0},{5,1},{6,2},{7,3},{8,12},{9,13},{10,... | collective-permute-start | bytes 1572872 | tf_op jit(solution)/shard_map/ppermute | solution.py:38
  14.6 1.1 fusion.10
  15.7 0.9 collective-permute-start.1
  16.6 3.0 %collective-permute-start.3 = (bf16[2,192,256]{2,1,0:T(8,128)(2,1)S(1)}, bf16[2,192,256]{2,1,0:T(8,128)(2,1)S(1)}, u32[]{:S(2)}, u32[]{:S(2)}) collective-permute-start(bf16[2,192,256]{2,1,0:T(8,128)(2,1)S(1)} %get-tuple-element.44), channel_id=1, source_target_pairs={{0,192},{1,193},{2,194},{3,195},{4,196},{5,197},{6,198},{7,199},{8... | collective-permute-start | bytes 589832 | tf_op jit(solution)/shard_map/ppermute | solution.py:38
  19.6 2.4 %collective-permute-start.2 = (bf16[2,192,256]{2,1,0:T(8,128)(2,1)S(1)}, bf16[2,192,256]{2,1,0:T(8,128)(2,1)S(1)}, u32[]{:S(2)}, u32[]{:S(2)}) collective-permute-start(bf16[2,192,256]{2,1,0:T(8,128)(2,1)S(1)} %get-tuple-element.45), channel_id=1, source_target_pairs={{0,16},{1,17},{2,18},{3,19},{4,20},{5,21},{6,22},{7,23},{8,24},{9,... | collective-permute-start | bytes 589832 | tf_op jit(solution)/shard_map/ppermute | solution.py:38
  22.0 2.0 %collective-permute-done.1 = bf16[2,192,256]{2,1,0:T(8,128)(2,1)S(1)} collective-permute-done((bf16[2,192,256]{2,1,0:T(8,128)(2,1)S(1)}, bf16[2,192,256]{2,1,0:T(8,128)(2,1)S(1)}, u32[]{:S(2)}, u32[]{:S(2)}) %collective-permute-start.1) | collective-permute-done | bytes 196640 | tf_op jit(solution)/shard_map/ppermute | solution.py:38
  24.0 0.0 collective-permute-done.3
  24.0 2.1 %collective-permute-done.2 = bf16[2,192,256]{2,1,0:T(8,128)(2,1)S(1)} collective-permute-done((bf16[2,192,256]{2,1,0:T(8,128)(2,1)S(1)}, bf16[2,192,256]{2,1,0:T(8,128)(2,1)S(1)}, u32[]{:S(2)}, u32[]{:S(2)}) %collective-permute-start.2) | collective-permute-done | bytes 196640 | tf_op jit(solution)/shard_map/ppermute | solution.py:38
  26.1 1.0 pad_maximum_fusion
  27.0 0.1 collective-permute-done.4
  27.1 0.0 all-gather.2.cloned.1.call-update
  27.2 1.8 %collective-permute-start.5 = (bf16[256,1024]{1,0:T(8,128)(2,1)}, bf16[256,1024]{1,0:T(8,128)(2,1)S(1)}, u32[]{:S(2)}, u32[]{:S(2)}) collective-permute-start(bf16[256,1024]{1,0:T(8,128)(2,1)} %get-tuple-element.22), channel_id=1, source_target_pairs={{0,4},{1,5},{2,6},{3,7},{4,0},{5,1},{6,2},{7,3},{8,12},{9,13},{10,... | collective-permute-start | bytes 1572872 | tf_op jit(solution)/shard_map/ppermute | solution.py:38
  29.0 0.0 collective-permute-start.6
  29.0 12.0 %collective-permute-done.5 = bf16[256,1024]{1,0:T(8,128)(2,1)S(1)} collective-permute-done((bf16[256,1024]{1,0:T(8,128)(2,1)}, bf16[256,1024]{1,0:T(8,128)(2,1)S(1)}, u32[]{:S(2)}, u32[]{:S(2)}) %collective-permute-start.5) | collective-permute-done | bytes 524320 | tf_op jit(solution)/shard_map/ppermute | solution.py:38
  41.1 0.0 copy-start.1
  41.1 0.0 copy-start.2
  41.2 0.0 copy-start.3
  41.2 3.1 %collective-permute-start.17 = (bf16[512,1024]{1,0:T(8,128)(2,1)S(1)}, bf16[512,1024]{1,0:T(8,128)(2,1)S(1)}, u32[]{:S(2)}, u32[]{:S(2)}) collective-permute-start(bf16[512,1024]{1,0:T(8,128)(2,1)S(1)} %constant_dynamic-update-slice_fusion.refs_1_), channel_id=1, source_target_pairs={{0,192},{1,193},{2,194},{3,195},{4,196},{5,197},{6,198},{7,199},{8... | collective-permute-start | bytes 3145736 | tf_op jit(solution)/shard_map/ppermute | solution.py:38
  44.3 0.5 collective-permute-start.13
  44.7 1.5 collective-permute-start.9
  46.3 0.0 collective-permute-start.7
  46.3 0.0 collective-permute-done.6.refs_2_
  46.3 0.8 collective-permute-start.16
  47.1 20.7 %collective-permute-done.17.refs_13_ = bf16[512,1024]{1,0:T(8,128)(2,1)S(1)} collective-permute-done((bf16[512,1024]{1,0:T(8,128)(2,1)S(1)}, bf16[512,1024]{1,0:T(8,128)(2,1)S(1)}, u32[]{:S(2)}, u32[]{:S(2)}) %collective-permute-start.17) | collective-permute-done | bytes 1048608 | tf_op jit(solution)/shard_map/ppermute | solution.py:38
  67.9 1.9 %collective-permute-start.12 = (bf16[512,1024]{1,0:T(8,128)(2,1)S(1)}, bf16[512,1024]{1,0:T(8,128)(2,1)S(1)}, u32[]{:S(2)}, u32[]{:S(2)}) collective-permute-start(bf16[512,1024]{1,0:T(8,128)(2,1)S(1)} %copy-done.5), channel_id=1, source_target_pairs={{0,16},{1,17},{2,18},{3,19},{4,20},{5,21},{6,22},{7,23},{8,24},{9,... | collective-permute-start | bytes 3145736 | tf_op jit(solution)/shard_map/ppermute | solution.py:38
  69.8 0.0 collective-permute-done.13.refs_9_
  69.8 0.5 collective-permute-start.8
  70.3 0.0 collective-permute-done.9.refs_5_
  70.3 0.0 collective-permute-start.19
  70.3 0.0 collective-permute-done.7.refs_3_
  70.4 0.5 collective-permute-start.15
  70.9 17.4 %collective-permute-done.16.refs_12_ = bf16[512,1024]{1,0:T(8,128)(2,1)S(1)} collective-permute-done((bf16[512,1024]{1,0:T(8,128)(2,1)S(1)}, bf16[512,1024]{1,0:T(8,128)(2,1)S(1)}, u32[]{:S(2)}, u32[]{:S(2)}) %collective-permute-start.16) | collective-permute-done | bytes 1048608 | tf_op jit(solution)/shard_map/ppermute | solution.py:38
  88.2 0.0 collective-permute-start.11
  88.2 2.2 %collective-permute-done.12.refs_8_ = bf16[512,1024]{1,0:T(8,128)(2,1)S(1)} collective-permute-done((bf16[512,1024]{1,0:T(8,128)(2,1)S(1)}, bf16[512,1024]{1,0:T(8,128)(2,1)S(1)}, u32[]{:S(2)}, u32[]{:S(2)}) %collective-permute-start.12) | collective-permute-done | bytes 1048608 | tf_op jit(solution)/shard_map/ppermute | solution.py:38
  90.4 0.0 collective-permute-start.18
  90.4 1.6 collective-permute-done.8.refs_4_
  92.1 0.0 collective-permute-start.14
  92.1 0.0 collective-permute-done.19.refs_15_
  92.1 0.6 collective-permute-start.10
  92.7 0.0 collective-permute-done.15.refs_11_
  92.7 0.4 collective-permute-done.18.refs_14_
  93.1 1.8 %collective-permute-done.14.refs_10_ = bf16[512,1024]{1,0:T(8,128)(2,1)S(1)} collective-permute-done((bf16[512,1024]{1,0:T(8,128)(2,1)S(1)}, bf16[512,1024]{1,0:T(8,128)(2,1)S(1)}, u32[]{:S(2)}, u32[]{:S(2)}) %collective-permute-start.14) | collective-permute-done | bytes 1048608 | tf_op jit(solution)/shard_map/ppermute | solution.py:38
  94.9 1.4 collective-permute-done.10.refs_6_
  96.4 8.2 %all-gather.2.cloned.1.call-done.gathered = bf16[8,8,192,256]{3,2,1,0:T(8,128)(2,1)} async-done(((bf16[1,8,192,256]{3,2,1,0:T(8,128)(2,1)}), bf16[8,8,192,256]{3,2,1,0:T(8,128)(2,1)}) %all-gather.2.cloned.1.call-update) | async-done | bytes 6291472 | tf_op jit(solution)/shard_map/all_gather | solution.py:144
  104.5 12.0 %shard_map.76 = (f32[2,48,1024]{2,1,0:T(8,128)}, f32[2,48,1024]{2,1,0:T(8,128)}, f32[2,48,1024]{2,1,0:T(8,128)}, f32[2,48,1024]{2,1,0:T(8,128)}) custom-call(bf16[8,8,192,256]{3,2,1,0:T(8,128)(2,1)} %all-gather.2.cloned.1.call-done.gathered, bf16[512,1024]{1,0:T(8,128)(2,1)} %constant_dynamic-slice_fusion.1.refs_0_, bf16[512,1024]{1,0:T(8,128)(2,1)} %copy-done.6, ...), custom_call_target="tpu_custom_call" | custom-call | flops 6442450944 | bytes 29360128 | tf_op jit(solution)/shard_map/pallas_call | solution.py:110
  116.5 2.5 %collective-permute-start.20 = (f32[2,48,1024]{2,1,0:T(8,128)}, f32[2,48,1024]{2,1,0:T(8,128)S(1)}, u32[]{:S(2)}, u32[]{:S(2)}) collective-permute-start(f32[2,48,1024]{2,1,0:T(8,128)} %get-tuple-element.25), channel_id=1, source_target_pairs={{0,96},{1,97},{2,98},{3,99},{4,100},{5,101},{6,102},{7,103},{8,104... | collective-permute-start | bytes 1179656 | tf_op jit(solution)/shard_map/ppermute | solution.py:38
  119.0 3.3 %collective-permute-start.21 = (f32[2,48,1024]{2,1,0:T(8,128)}, f32[2,48,1024]{2,1,0:T(8,128)S(1)}, u32[]{:S(2)}, u32[]{:S(2)}) collective-permute-start(f32[2,48,1024]{2,1,0:T(8,128)} %get-tuple-element.26), channel_id=1, source_target_pairs={{0,224},{1,225},{2,226},{3,227},{4,228},{5,229},{6,230},{7,231},{8... | collective-permute-start | bytes 1179656 | tf_op jit(solution)/shard_map/ppermute | solution.py:38
  122.3 1.8 %collective-permute-start.22 = (f32[2,48,1024]{2,1,0:T(8,128)}, f32[2,48,1024]{2,1,0:T(8,128)S(1)}, u32[]{:S(2)}, u32[]{:S(2)}) collective-permute-start(f32[2,48,1024]{2,1,0:T(8,128)} %get-tuple-element.27), channel_id=1, source_target_pairs={{0,128},{1,129},{2,130},{3,131},{4,132},{5,133},{6,134},{7,135},{8... | collective-permute-start | bytes 1179656 | tf_op jit(solution)/shard_map/ppermute | solution.py:38
  124.1 8.4 %collective-permute-done.20 = f32[2,48,1024]{2,1,0:T(8,128)S(1)} collective-permute-done((f32[2,48,1024]{2,1,0:T(8,128)}, f32[2,48,1024]{2,1,0:T(8,128)S(1)}, u32[]{:S(2)}, u32[]{:S(2)}) %collective-permute-start.20) | collective-permute-done | bytes 393248 | tf_op jit(solution)/shard_map/ppermute | solution.py:38
  132.5 7.1 %collective-permute-done.21 = f32[2,48,1024]{2,1,0:T(8,128)S(1)} collective-permute-done((f32[2,48,1024]{2,1,0:T(8,128)}, f32[2,48,1024]{2,1,0:T(8,128)S(1)}, u32[]{:S(2)}, u32[]{:S(2)}) %collective-permute-start.21) | collective-permute-done | bytes 393248 | tf_op jit(solution)/shard_map/ppermute | solution.py:38
  139.6 1.1 collective-permute-done.22
  140.7 1.1 add_add_fusion
  141.8 0.1 copy.28
  141.9 19.5 %all_to_all.5.rows = f32[8,12,8,128]{3,2,1,0:T(8,128)S(1)} all-to-all(f32[8,12,8,128]{3,2,1,0:T(8,128)S(1)} %bitcast.38), channel_id=1, replica_groups=mesh['dp'=32,'tr'=2,'tc'=4] {'tc','tr'}, dimensions={0} | all-to-all | bytes 786432 | tf_op jit(solution)/shard_map/all_to_all | solution.py:157
  161.4 1.2 shard_map.77
  (40 shorter events, 0.2 us)
Async XLA Ops:
  7.2 1.1 copy-start
  7.2 97.4 %all-gather.2.cloned.1.call-start = ((), (), s32[]{:S(2)}) async-start(), calls=%async_computation.1 | async-start | bytes 7077888 | tf_op jit(solution)/shard_map/all_gather | solution.py:144
  8.3 2.3 %copy-start.4 = (bf16[512,2048]{1,0:T(8,128)(2,1)S(1)}, bf16[512,2048]{1,0:T(8,128)(2,1)}, u32[]{:S(2)}) copy-start(bf16[512,2048]{1,0:T(8,128)(2,1)} %param.6) | copy-start | bytes 6291460
  10.6 2.1 %collective-permute-start = (bf16[4,192,256]{2,1,0:T(8,128)(2,1)}, bf16[4,192,256]{2,1,0:T(8,128)(2,1)}, u32[]{:S(2)}, u32[]{:S(2)}) collective-permute-start(bf16[4,192,256]{2,1,0:T(8,128)(2,1)} %bitcast), channel_id=1, source_target_pairs={{0,8},{1,9},{2,10},{3,11},{4,12},{5,13},{6,14},{7,15},{8,0},{9,1},... | collective-permute-start | bytes 1179656 | tf_op jit(solution)/shard_map/ppermute | solution.py:38
  12.6 33.7 %copy-start.5 = (bf16[512,1024]{1,0:T(8,128)(2,1)S(1)}, bf16[512,1024]{1,0:T(8,128)(2,1)}, u32[]{:S(2)}) copy-start(bf16[512,1024]{1,0:T(8,128)(2,1)} %constant_dynamic-slice_fusion.1.refs_0_) | copy-start | bytes 3145732
  12.7 14.5 %collective-permute-start.4 = (bf16[256,1024]{1,0:T(8,128)(2,1)S(1)}, bf16[256,1024]{1,0:T(8,128)(2,1)S(1)}, u32[]{:S(2)}, u32[]{:S(2)}) collective-permute-start(bf16[256,1024]{1,0:T(8,128)(2,1)S(1)} %get-tuple-element.19), channel_id=1, source_target_pairs={{0,4},{1,5},{2,6},{3,7},{4,0},{5,1},{6,2},{7,3},{8,12},{9,13},{10,... | collective-permute-start | bytes 1572872 | tf_op jit(solution)/shard_map/ppermute | solution.py:38
  15.7 8.3 %collective-permute-start.1 = (bf16[2,192,256]{2,1,0:T(8,128)(2,1)S(1)}, bf16[2,192,256]{2,1,0:T(8,128)(2,1)S(1)}, u32[]{:S(2)}, u32[]{:S(2)}) collective-permute-start(bf16[2,192,256]{2,1,0:T(8,128)(2,1)S(1)} %get-tuple-element.43), channel_id=1, source_target_pairs={{0,48},{1,49},{2,50},{3,51},{4,52},{5,53},{6,54},{7,55},{8,56},{9,... | collective-permute-start | bytes 589832 | tf_op jit(solution)/shard_map/ppermute | solution.py:38
  16.6 7.4 %collective-permute-start.3 = (bf16[2,192,256]{2,1,0:T(8,128)(2,1)S(1)}, bf16[2,192,256]{2,1,0:T(8,128)(2,1)S(1)}, u32[]{:S(2)}, u32[]{:S(2)}) collective-permute-start(bf16[2,192,256]{2,1,0:T(8,128)(2,1)S(1)} %get-tuple-element.44), channel_id=1, source_target_pairs={{0,192},{1,193},{2,194},{3,195},{4,196},{5,197},{6,198},{7,199},{8... | collective-permute-start | bytes 589832 | tf_op jit(solution)/shard_map/ppermute | solution.py:38
  19.6 6.4 %collective-permute-start.2 = (bf16[2,192,256]{2,1,0:T(8,128)(2,1)S(1)}, bf16[2,192,256]{2,1,0:T(8,128)(2,1)S(1)}, u32[]{:S(2)}, u32[]{:S(2)}) collective-permute-start(bf16[2,192,256]{2,1,0:T(8,128)(2,1)S(1)} %get-tuple-element.45), channel_id=1, source_target_pairs={{0,16},{1,17},{2,18},{3,19},{4,20},{5,21},{6,22},{7,23},{8,24},{9,... | collective-permute-start | bytes 589832 | tf_op jit(solution)/shard_map/ppermute | solution.py:38
  27.2 13.9 %collective-permute-start.5 = (bf16[256,1024]{1,0:T(8,128)(2,1)}, bf16[256,1024]{1,0:T(8,128)(2,1)S(1)}, u32[]{:S(2)}, u32[]{:S(2)}) collective-permute-start(bf16[256,1024]{1,0:T(8,128)(2,1)} %get-tuple-element.22), channel_id=1, source_target_pairs={{0,4},{1,5},{2,6},{3,7},{4,0},{5,1},{6,2},{7,3},{8,12},{9,13},{10,... | collective-permute-start | bytes 1572872 | tf_op jit(solution)/shard_map/ppermute | solution.py:38
  29.0 17.3 %collective-permute-start.6 = (bf16[512,1024]{1,0:T(8,128)(2,1)}, bf16[512,1024]{1,0:T(8,128)(2,1)S(1)}, u32[]{:S(2)}, u32[]{:S(2)}) collective-permute-start(bf16[512,1024]{1,0:T(8,128)(2,1)} %constant_dynamic-slice_fusion.1.refs_0_), channel_id=1, source_target_pairs={{0,8},{1,9},{2,10},{3,11},{4,12},{5,13},{6,14},{7,15},{8,0},{9,1},... | collective-permute-start | bytes 3145736 | tf_op jit(solution)/shard_map/ppermute | solution.py:38
  41.1 50.9 %copy-start.6 = (bf16[512,1024]{1,0:T(8,128)(2,1)}, bf16[512,1024]{1,0:T(8,128)(2,1)S(1)}, u32[]{:S(2)}) copy-start(bf16[512,1024]{1,0:T(8,128)(2,1)S(1)} %constant_dynamic-update-slice_fusion.refs_1_) | copy-start | bytes 3145732
  41.1 120.3 %copy-start.1 = (f32[1,12,8192]{2,0,1:T(1,128)S(1)}, f32[1,12,8192]{2,0,1:T(1,128)}, u32[]{:S(2)}) copy-start(f32[1,12,8192]{2,0,1:T(1,128)} %param.7) | copy-start | bytes 1179652
  41.1 120.2 %copy-start.2 = (f32[1,12,8192]{2,0,1:T(1,128)S(1)}, f32[1,12,8192]{2,0,1:T(1,128)}, u32[]{:S(2)}) copy-start(f32[1,12,8192]{2,0,1:T(1,128)} %param.8) | copy-start | bytes 1179652
  41.2 120.2 %copy-start.3 = (f32[1,12,8192]{2,0,1:T(1,128)S(1)}, f32[1,12,8192]{2,0,1:T(1,128)}, u32[]{:S(2)}) copy-start(f32[1,12,8192]{2,0,1:T(1,128)} %param.9) | copy-start | bytes 1179652
  41.2 26.7 %collective-permute-start.17 = (bf16[512,1024]{1,0:T(8,128)(2,1)S(1)}, bf16[512,1024]{1,0:T(8,128)(2,1)S(1)}, u32[]{:S(2)}, u32[]{:S(2)}) collective-permute-start(bf16[512,1024]{1,0:T(8,128)(2,1)S(1)} %constant_dynamic-update-slice_fusion.refs_1_), channel_id=1, source_target_pairs={{0,192},{1,193},{2,194},{3,195},{4,196},{5,197},{6,198},{7,199},{8... | collective-permute-start | bytes 3145736 | tf_op jit(solution)/shard_map/ppermute | solution.py:38
  44.3 25.5 %collective-permute-start.13 = (bf16[512,1024]{1,0:T(8,128)(2,1)S(1)}, bf16[512,1024]{1,0:T(8,128)(2,1)S(1)}, u32[]{:S(2)}, u32[]{:S(2)}) collective-permute-start(bf16[512,1024]{1,0:T(8,128)(2,1)S(1)} %constant_dynamic-update-slice_fusion.refs_1_), channel_id=1, source_target_pairs={{0,16},{1,17},{2,18},{3,19},{4,20},{5,21},{6,22},{7,23},{8,24},{9,... | collective-permute-start | bytes 3145736 | tf_op jit(solution)/shard_map/ppermute | solution.py:38
  44.7 25.6 %collective-permute-start.9 = (bf16[512,1024]{1,0:T(8,128)(2,1)S(1)}, bf16[512,1024]{1,0:T(8,128)(2,1)S(1)}, u32[]{:S(2)}, u32[]{:S(2)}) collective-permute-start(bf16[512,1024]{1,0:T(8,128)(2,1)S(1)} %constant_dynamic-update-slice_fusion.refs_1_), channel_id=1, source_target_pairs={{0,48},{1,49},{2,50},{3,51},{4,52},{5,53},{6,54},{7,55},{8,56},{9,... | collective-permute-start | bytes 3145736 | tf_op jit(solution)/shard_map/ppermute | solution.py:38
  46.3 24.1 %collective-permute-start.7 = (bf16[512,1024]{1,0:T(8,128)(2,1)S(1)}, bf16[512,1024]{1,0:T(8,128)(2,1)S(1)}, u32[]{:S(2)}, u32[]{:S(2)}) collective-permute-start(bf16[512,1024]{1,0:T(8,128)(2,1)S(1)} %constant_dynamic-update-slice_fusion.refs_1_), channel_id=1, source_target_pairs={{0,8},{1,9},{2,10},{3,11},{4,12},{5,13},{6,14},{7,15},{8,0},{9,1},... | collective-permute-start | bytes 3145736 | tf_op jit(solution)/shard_map/ppermute | solution.py:38
  46.3 45.8 %copy-start.7 = (bf16[512,1024]{1,0:T(8,128)(2,1)}, bf16[512,1024]{1,0:T(8,128)(2,1)S(1)}, u32[]{:S(2)}) copy-start(bf16[512,1024]{1,0:T(8,128)(2,1)S(1)} %collective-permute-done.6.refs_2_) | copy-start | bytes 3145732
  46.3 41.9 %collective-permute-start.16 = (bf16[512,1024]{1,0:T(8,128)(2,1)S(1)}, bf16[512,1024]{1,0:T(8,128)(2,1)S(1)}, u32[]{:S(2)}, u32[]{:S(2)}) collective-permute-start(bf16[512,1024]{1,0:T(8,128)(2,1)S(1)} %copy-done.5), channel_id=1, source_target_pairs={{0,192},{1,193},{2,194},{3,195},{4,196},{5,197},{6,198},{7,199},{8... | collective-permute-start | bytes 3145736 | tf_op jit(solution)/shard_map/ppermute | solution.py:38
  67.9 24.2 %copy-start.8 = (bf16[512,1024]{1,0:T(8,128)(2,1)}, bf16[512,1024]{1,0:T(8,128)(2,1)S(1)}, u32[]{:S(2)}) copy-start(bf16[512,1024]{1,0:T(8,128)(2,1)S(1)} %collective-permute-done.17.refs_13_) | copy-start | bytes 3145732
  67.9 22.6 %collective-permute-start.12 = (bf16[512,1024]{1,0:T(8,128)(2,1)S(1)}, bf16[512,1024]{1,0:T(8,128)(2,1)S(1)}, u32[]{:S(2)}, u32[]{:S(2)}) collective-permute-start(bf16[512,1024]{1,0:T(8,128)(2,1)S(1)} %copy-done.5), channel_id=1, source_target_pairs={{0,16},{1,17},{2,18},{3,19},{4,20},{5,21},{6,22},{7,23},{8,24},{9,... | collective-permute-start | bytes 3145736 | tf_op jit(solution)/shard_map/ppermute | solution.py:38
  69.8 22.9 %copy-start.9 = (bf16[512,1024]{1,0:T(8,128)(2,1)}, bf16[512,1024]{1,0:T(8,128)(2,1)S(1)}, u32[]{:S(2)}) copy-start(bf16[512,1024]{1,0:T(8,128)(2,1)S(1)} %collective-permute-done.13.refs_9_) | copy-start | bytes 3145732
  69.8 22.3 %collective-permute-start.8 = (bf16[512,1024]{1,0:T(8,128)(2,1)S(1)}, bf16[512,1024]{1,0:T(8,128)(2,1)S(1)}, u32[]{:S(2)}, u32[]{:S(2)}) collective-permute-start(bf16[512,1024]{1,0:T(8,128)(2,1)S(1)} %copy-done.5), channel_id=1, source_target_pairs={{0,48},{1,49},{2,50},{3,51},{4,52},{5,53},{6,54},{7,55},{8,56},{9,... | collective-permute-start | bytes 3145736 | tf_op jit(solution)/shard_map/ppermute | solution.py:38
  70.3 22.4 %copy-start.10 = (bf16[512,1024]{1,0:T(8,128)(2,1)}, bf16[512,1024]{1,0:T(8,128)(2,1)S(1)}, u32[]{:S(2)}) copy-start(bf16[512,1024]{1,0:T(8,128)(2,1)S(1)} %collective-permute-done.9.refs_5_) | copy-start | bytes 3145732
  70.3 21.7 %collective-permute-start.19 = (bf16[512,1024]{1,0:T(8,128)(2,1)S(1)}, bf16[512,1024]{1,0:T(8,128)(2,1)S(1)}, u32[]{:S(2)}, u32[]{:S(2)}) collective-permute-start(bf16[512,1024]{1,0:T(8,128)(2,1)S(1)} %collective-permute-done.17.refs_13_), channel_id=1, source_target_pairs={{0,8},{1,9},{2,10},{3,11},{4,12},{5,13},{6,14},{7,15},{8,0},{9,1},... | collective-permute-start | bytes 3145736 | tf_op jit(solution)/shard_map/ppermute | solution.py:38
  70.4 22.4 %copy-start.11 = (bf16[512,1024]{1,0:T(8,128)(2,1)}, bf16[512,1024]{1,0:T(8,128)(2,1)S(1)}, u32[]{:S(2)}) copy-start(bf16[512,1024]{1,0:T(8,128)(2,1)S(1)} %collective-permute-done.7.refs_3_) | copy-start | bytes 3145732
  70.4 22.3 %collective-permute-start.15 = (bf16[512,1024]{1,0:T(8,128)(2,1)S(1)}, bf16[512,1024]{1,0:T(8,128)(2,1)S(1)}, u32[]{:S(2)}, u32[]{:S(2)}) collective-permute-start(bf16[512,1024]{1,0:T(8,128)(2,1)S(1)} %collective-permute-done.13.refs_9_), channel_id=1, source_target_pairs={{0,8},{1,9},{2,10},{3,11},{4,12},{5,13},{6,14},{7,15},{8,0},{9,1},... | collective-permute-start | bytes 3145736 | tf_op jit(solution)/shard_map/ppermute | solution.py:38
  88.2 4.9 %copy-start.12 = (bf16[512,1024]{1,0:T(8,128)(2,1)}, bf16[512,1024]{1,0:T(8,128)(2,1)S(1)}, u32[]{:S(2)}) copy-start(bf16[512,1024]{1,0:T(8,128)(2,1)S(1)} %collective-permute-done.16.refs_12_) | copy-start | bytes 3145732
  88.2 4.5 %collective-permute-start.11 = (bf16[512,1024]{1,0:T(8,128)(2,1)S(1)}, bf16[512,1024]{1,0:T(8,128)(2,1)S(1)}, u32[]{:S(2)}, u32[]{:S(2)}) collective-permute-start(bf16[512,1024]{1,0:T(8,128)(2,1)S(1)} %collective-permute-done.9.refs_5_), channel_id=1, source_target_pairs={{0,8},{1,9},{2,10},{3,11},{4,12},{5,13},{6,14},{7,15},{8,0},{9,1},... | collective-permute-start | bytes 3145736 | tf_op jit(solution)/shard_map/ppermute | solution.py:38
  90.4 4.5 %copy-start.13 = (bf16[512,1024]{1,0:T(8,128)(2,1)}, bf16[512,1024]{1,0:T(8,128)(2,1)S(1)}, u32[]{:S(2)}) copy-start(bf16[512,1024]{1,0:T(8,128)(2,1)S(1)} %collective-permute-done.12.refs_8_) | copy-start | bytes 3145732
  90.4 2.7 %collective-permute-start.18 = (bf16[512,1024]{1,0:T(8,128)(2,1)S(1)}, bf16[512,1024]{1,0:T(8,128)(2,1)S(1)}, u32[]{:S(2)}, u32[]{:S(2)}) collective-permute-start(bf16[512,1024]{1,0:T(8,128)(2,1)S(1)} %collective-permute-done.16.refs_12_), channel_id=1, source_target_pairs={{0,8},{1,9},{2,10},{3,11},{4,12},{5,13},{6,14},{7,15},{8,0},{9,1},... | collective-permute-start | bytes 3145736 | tf_op jit(solution)/shard_map/ppermute | solution.py:38
  92.1 2.8 %copy-start.14 = (bf16[512,1024]{1,0:T(8,128)(2,1)}, bf16[512,1024]{1,0:T(8,128)(2,1)S(1)}, u32[]{:S(2)}) copy-start(bf16[512,1024]{1,0:T(8,128)(2,1)S(1)} %collective-permute-done.8.refs_4_) | copy-start | bytes 3145732
  92.1 2.8 %collective-permute-start.14 = (bf16[512,1024]{1,0:T(8,128)(2,1)S(1)}, bf16[512,1024]{1,0:T(8,128)(2,1)S(1)}, u32[]{:S(2)}, u32[]{:S(2)}) collective-permute-start(bf16[512,1024]{1,0:T(8,128)(2,1)S(1)} %collective-permute-done.12.refs_8_), channel_id=1, source_target_pairs={{0,8},{1,9},{2,10},{3,11},{4,12},{5,13},{6,14},{7,15},{8,0},{9,1},... | collective-permute-start | bytes 3145736 | tf_op jit(solution)/shard_map/ppermute | solution.py:38
  92.1 2.8 %copy-start.15 = (bf16[512,1024]{1,0:T(8,128)(2,1)}, bf16[512,1024]{1,0:T(8,128)(2,1)S(1)}, u32[]{:S(2)}) copy-start(bf16[512,1024]{1,0:T(8,128)(2,1)S(1)} %collective-permute-done.19.refs_15_) | copy-start | bytes 3145732
  92.1 4.2 %collective-permute-start.10 = (bf16[512,1024]{1,0:T(8,128)(2,1)S(1)}, bf16[512,1024]{1,0:T(8,128)(2,1)}, u32[]{:S(2)}, u32[]{:S(2)}) collective-permute-start(bf16[512,1024]{1,0:T(8,128)(2,1)S(1)} %collective-permute-done.8.refs_4_), channel_id=1, source_target_pairs={{0,8},{1,9},{2,10},{3,11},{4,12},{5,13},{6,14},{7,15},{8,0},{9,1},... | collective-permute-start | bytes 3145736 | tf_op jit(solution)/shard_map/ppermute | solution.py:38
  92.7 2.2 %copy-start.16 = (bf16[512,1024]{1,0:T(8,128)(2,1)}, bf16[512,1024]{1,0:T(8,128)(2,1)S(1)}, u32[]{:S(2)}) copy-start(bf16[512,1024]{1,0:T(8,128)(2,1)S(1)} %collective-permute-done.15.refs_11_) | copy-start | bytes 3145732
  92.7 2.2 %copy-start.17 = (bf16[512,1024]{1,0:T(8,128)(2,1)}, bf16[512,1024]{1,0:T(8,128)(2,1)S(1)}, u32[]{:S(2)}) copy-start(bf16[512,1024]{1,0:T(8,128)(2,1)S(1)} %collective-permute-done.11.refs_7_) | copy-start | bytes 3145732
  93.1 1.8 %copy-start.18 = (bf16[512,1024]{1,0:T(8,128)(2,1)}, bf16[512,1024]{1,0:T(8,128)(2,1)S(1)}, u32[]{:S(2)}) copy-start(bf16[512,1024]{1,0:T(8,128)(2,1)S(1)} %collective-permute-done.18.refs_14_) | copy-start | bytes 3145732
  94.9 9.6 %copy-start.19 = (bf16[512,1024]{1,0:T(8,128)(2,1)}, bf16[512,1024]{1,0:T(8,128)(2,1)S(1)}, u32[]{:S(2)}) copy-start(bf16[512,1024]{1,0:T(8,128)(2,1)S(1)} %collective-permute-done.14.refs_10_) | copy-start | bytes 3145732
  116.5 15.9 %collective-permute-start.20 = (f32[2,48,1024]{2,1,0:T(8,128)}, f32[2,48,1024]{2,1,0:T(8,128)S(1)}, u32[]{:S(2)}, u32[]{:S(2)}) collective-permute-start(f32[2,48,1024]{2,1,0:T(8,128)} %get-tuple-element.25), channel_id=1, source_target_pairs={{0,96},{1,97},{2,98},{3,99},{4,100},{5,101},{6,102},{7,103},{8,104... | collective-permute-start | bytes 1179656 | tf_op jit(solution)/shard_map/ppermute | solution.py:38
  119.0 20.6 %collective-permute-start.21 = (f32[2,48,1024]{2,1,0:T(8,128)}, f32[2,48,1024]{2,1,0:T(8,128)S(1)}, u32[]{:S(2)}, u32[]{:S(2)}) collective-permute-start(f32[2,48,1024]{2,1,0:T(8,128)} %get-tuple-element.26), channel_id=1, source_target_pairs={{0,224},{1,225},{2,226},{3,227},{4,228},{5,229},{6,230},{7,231},{8... | collective-permute-start | bytes 1179656 | tf_op jit(solution)/shard_map/ppermute | solution.py:38
  122.3 18.4 %collective-permute-start.22 = (f32[2,48,1024]{2,1,0:T(8,128)}, f32[2,48,1024]{2,1,0:T(8,128)S(1)}, u32[]{:S(2)}, u32[]{:S(2)}) collective-permute-start(f32[2,48,1024]{2,1,0:T(8,128)} %get-tuple-element.27), channel_id=1, source_target_pairs={{0,128},{1,129},{2,130},{3,131},{4,132},{5,133},{6,134},{7,135},{8... | collective-permute-start | bytes 1179656 | tf_op jit(solution)/shard_map/ppermute | solution.py:38
Sparse Core Ops, SparseCore 0:
  27.3 77.1 all-gather.1

commit v11 on v10

--- a/solution.py
+++ b/solution.py
@@ -17,7 +17,8 @@
 SIDE = 4
 ROWS = 48
 GROUP = 4
-AHEAD = 3
+DEPTH = 2
+AHEAD = 2 * DEPTH
 SOURCES = ((0, 0), (1, 0), (-1, 0), (0, 1))
 OWNERS = ((0, 0), (2, 1), (0, 2), (2, 3))
 QUARTER = 4 * ROWS
@@ -44,13 +45,13 @@
 REDUCE = [moves(lambda y, x, core, z: (y + dy, x + dx, core, z)) for dx, dy in OWNERS]
 
 
-def feature_order(activations):
+def feature_order(activations, half):
     dp = lax.axis_index("dp")
     my_y, my_x, core = dp // 8, dp // 2 % 4, dp % 2
-    column = lax.broadcasted_iota(jnp.int32, (1, 2 * GROUP * QUARTER), 1)
+    column = lax.broadcasted_iota(jnp.int32, (1, GROUP * QUARTER), 1)
     row, block = column % ROWS, column // ROWS
-    owner, feed, half = block % 4, block // 4 % GROUP, block // (4 * GROUP)
-    target = jnp.where(half == 0, core, 1 - core)
+    owner, feed = block % 4, block // 4
+    target = 1 - core if half else core
     x, y = my_x, my_y
     for index in range(4):
         x = x + jnp.where(owner == index, OWNERS[index][0], 0) - jnp.where(feed == index, SOURCES[index][0], 0)
@@ -59,7 +60,7 @@
     feature = lax.broadcasted_iota(jnp.int32, (activations.shape[1], column.shape[1]), 0)
     chosen = (feature == source).astype(activations.dtype)
     ordered = lax.dot_general(chosen, activations, (((0,), (1,)), ((), ())), preferred_element_type=jnp.float32)
-    return ordered.astype(activations.dtype)
+    return ordered.astype(activations.dtype).reshape(GROUP, QUARTER, activations.shape[0])
 
 
 def product_kernel(gathered, *refs):
@@ -90,12 +91,13 @@
     for replica in range(AHEAD):
         fetch(replica)
     total = None
-    for replica in range(replicas):
-        if replica + AHEAD < replicas:
-            fetch(replica + AHEAD)
-        for copy in copies_of(replica):
-            copy.wait()
-        window = slice(replica * depth, (replica + 1) * depth)
+    for first in range(0, replicas, DEPTH):
+        for replica in range(first, first + DEPTH):
+            for copy in copies_of(replica):
+                copy.wait()
+        for replica in range(first + AHEAD, min(first + AHEAD + DEPTH, replicas)):
+            fetch(replica)
+        window = slice(first * depth, (first + DEPTH) * depth)
         term = jnp.dot(act[:, window], cot[window], preferred_element_type=jnp.float32)
         total = term if total is None else total + term
     total = total.reshape(2, 4, ROWS, total.shape[1])
@@ -127,17 +129,17 @@
 def shards(activations, cotangent, master, moment, second):
     tr = lax.axis_index("tr")
     units = cotangent.shape[1] // 2
-    ordered = feature_order(activations).reshape(2, GROUP, QUARTER, activations.shape[0])
-    other = send(ordered[1], OTHER_CORE)
+    other = send(feature_order(activations, 1), OTHER_CORE)
+    own = feature_order(activations, 0)
     tokens = cotangent.shape[0]
     away = [
         lax.dynamic_slice(cotangent, (start, (1 - tr) * units), (size, units))
         for start, size in ((0, tokens // 2), (tokens // 2, tokens // 2))
     ]
     own_keep = lax.dynamic_slice_in_dim(cotangent, tr * units, units, 1)
-    other, away, own_keep = lax.optimization_barrier((other, away, own_keep))
+    other, away, own = lax.optimization_barrier((other, away, own))
     first_came, last_came = send(away[0], PAIR), send(away[1], PAIR)
-    both = jnp.stack([ordered[0], other], axis=1)
+    both = jnp.stack([own, other], axis=1)
     shared = jnp.stack([both[0]] + [send(both[g], FEED[g]) for g in (1, 2, 3)])
     early, shared, first_came = lax.optimization_barrier((own_keep, shared, first_came))
     shared = shared.reshape(2 * GROUP, QUARTER, activations.shape[0])

time: 170 us -> 170 us (level)
  waiting for transfers between devices: 86.6 us -> 84.2 us
    ppermute x23, waiting for transfers between devices: 78.4 us -> 75.9 us  [send(): return lax.ppermute(array, AXES, pairs)]
  transfers between devices with their start and end apart: 24 -> 24, of which waited for: 15 -> 14; matrix products, arithmetic and copies ran while one was open for 2% -> 4% of each run, Pallas kernels for 0% -> 0%
where the time goes in v11:
time: 170 us
  waiting for transfers between devices  84.2 us (50%)
  starting transfers between devices  27.1 us (16%)
  blocking collectives  19.2 us (11%)
  Pallas kernels  14.3 us (8%)
  between operations  14.3 us (8%)
  local copies, waits for them, and re-layouts  4.51 us (3%)
  other arithmetic  3.85 us (2%)
  matrix products  2.41 us (1%)
    ppermute x23, waiting for transfers between devices, send(): return lax.ppermute(array, AXES, pairs)  75.9 us
    ppermute x23, starting transfers between devices, send(): return lax.ppermute(array, AXES, pairs)  27.1 us
    all_to_all x1, blocking collectives, shards(): lax.all_to_all(rows, ('tc', 'tr'), split_axis=0, concat_axis=0, tiled=True)  19.2 us
    pallas_call x1, Pallas kernels, product(): pl.pallas_call(product_kernel, in_specs=[pl.BlockSpec(memory_space=pl.ANY...  13.1 us
    all_gather x1, waiting for transfers between devices, shards(): gathered = lax.all_gather(shared, ('tc', 'tr'), axis=0)  8.32 us
  transfers between devices with their start and end apart: 24, of which 14 were waited for; matrix products, arithmetic and copies ran while one was open for 4% of the time, Pallas kernels for 0%

profile of v11, /device:TPU:6, one launch (start us, length us, event | category | flops | bytes accessed | tf_op | source)
XLA Modules:
  0.0 169.9 jit_solution(8410348336122968071)
XLA Ops:
  7.2 0.0 copy-start
  7.2 0.0 all-gather.2.cloned.1.call-start
  7.3 1.0 copy-done
  8.3 1.6 fusion.8
  9.9 0.0 collective-permute-start
  9.9 0.0 copy-done.4
  9.9 1.1 constant_dynamic-slice_fusion
  11.0 0.8 fusion.11
  11.9 0.0 collective-permute-done
  11.9 2.0 %collective-permute-start.4 = (bf16[256,1024]{1,0:T(8,128)(2,1)}, bf16[256,1024]{1,0:T(8,128)(2,1)}, u32[]{:S(2)}, u32[]{:S(2)}) collective-permute-start(bf16[256,1024]{1,0:T(8,128)(2,1)} %get-tuple-element.19), channel_id=1, source_target_pairs={{0,4},{1,5},{2,6},{3,7},{4,0},{5,1},{6,2},{7,3},{8,12},{9,13},{10,... | collective-permute-start | bytes 1572872 | tf_op jit(solution)/shard_map/ppermute | solution.py:39
  13.9 0.8 fusion.17
  14.7 0.8 collective-permute-start.1
  15.5 3.0 %collective-permute-start.3 = (bf16[2,192,256]{2,1,0:T(8,128)(2,1)}, bf16[2,192,256]{2,1,0:T(8,128)(2,1)S(1)}, u32[]{:S(2)}, u32[]{:S(2)}) collective-permute-start(bf16[2,192,256]{2,1,0:T(8,128)(2,1)} %get-tuple-element.44), channel_id=1, source_target_pairs={{0,192},{1,193},{2,194},{3,195},{4,196},{5,197},{6,198},{7,199},{8... | collective-permute-start | bytes 589832 | tf_op jit(solution)/shard_map/ppermute | solution.py:39
  18.5 2.4 %collective-permute-start.2 = (bf16[2,192,256]{2,1,0:T(8,128)(2,1)}, bf16[2,192,256]{2,1,0:T(8,128)(2,1)}, u32[]{:S(2)}, u32[]{:S(2)}) collective-permute-start(bf16[2,192,256]{2,1,0:T(8,128)(2,1)} %get-tuple-element.45), channel_id=1, source_target_pairs={{0,16},{1,17},{2,18},{3,19},{4,20},{5,21},{6,22},{7,23},{8,24},{9,... | collective-permute-start | bytes 589832 | tf_op jit(solution)/shard_map/ppermute | solution.py:39
  20.9 1.1 constant_dynamic-slice_fusion.2.refs_0_
  22.0 1.1 collective-permute-done.1
  23.1 0.0 collective-permute-done.3
  23.1 2.2 %collective-permute-done.2 = bf16[2,192,256]{2,1,0:T(8,128)(2,1)} collective-permute-done((bf16[2,192,256]{2,1,0:T(8,128)(2,1)}, bf16[2,192,256]{2,1,0:T(8,128)(2,1)}, u32[]{:S(2)}, u32[]{:S(2)}) %collective-permute-start.2) | collective-permute-done | bytes 196640 | tf_op jit(solution)/shard_map/ppermute | solution.py:39
  25.3 1.9 %pad_maximum_fusion = bf16[4,2,192,256]{3,2,1,0:T(8,128)(2,1)} fusion(bf16[1,2,192,256]{3,2,1,0:T(8,128)(2,1)S(1)} %bitcast.45, bf16[1,2,192,256]{3,2,1,0:T(8,128)(2,1)} %bitcast.7, bf16[1,2,192,256]{3,2,1,0:T(8,128)(2,1)S(1)} %bitcast.44, bf16[1,2,192,256]{3,2,1,0:T(8,128)(2,1)S(1)} %get-tuple-element.42), kind=kLoop, calls=%fused_computation.16 | loop fusion | flops 1179648 | bytes 1572864 | tf_op jit(solution)/shard_map/stack | solution.py:143
  27.2 0.0 collective-permute-done.4
  27.2 0.0 all-gather.2.cloned.1.call-update
  27.3 1.4 collective-permute-start.5
  28.6 0.0 collective-permute-start.6
  28.6 1.1 constant_dynamic-update-slice_fusion.1
  29.7 10.8 %collective-permute-done.5 = bf16[256,1024]{1,0:T(8,128)(2,1)S(1)} collective-permute-done((bf16[256,1024]{1,0:T(8,128)(2,1)S(1)}, bf16[256,1024]{1,0:T(8,128)(2,1)S(1)}, u32[]{:S(2)}, u32[]{:S(2)}) %collective-permute-start.5) | collective-permute-done | bytes 524320 | tf_op jit(solution)/shard_map/ppermute | solution.py:39
  40.6 3.1 %collective-permute-start.17 = (bf16[512,1024]{1,0:T(8,128)(2,1)S(1)}, bf16[512,1024]{1,0:T(8,128)(2,1)S(1)}, u32[]{:S(2)}, u32[]{:S(2)}) collective-permute-start(bf16[512,1024]{1,0:T(8,128)(2,1)S(1)} %constant_dynamic-update-slice_fusion.refs_1_), channel_id=1, source_target_pairs={{0,192},{1,193},{2,194},{3,195},{4,196},{5,197},{6,198},{7,199},{8... | collective-permute-start | bytes 3145736 | tf_op jit(solution)/shard_map/ppermute | solution.py:39
  43.7 0.8 collective-permute-start.13
  44.4 1.3 collective-permute-start.9
  45.7 0.0 collective-permute-start.7
  45.7 0.0 collective-permute-done.6.refs_2_
  45.7 0.8 collective-permute-start.16
  46.5 20.8 %collective-permute-done.17.refs_13_ = bf16[512,1024]{1,0:T(8,128)(2,1)S(1)} collective-permute-done((bf16[512,1024]{1,0:T(8,128)(2,1)S(1)}, bf16[512,1024]{1,0:T(8,128)(2,1)S(1)}, u32[]{:S(2)}, u32[]{:S(2)}) %collective-permute-start.17) | collective-permute-done | bytes 1048608 | tf_op jit(solution)/shard_map/ppermute | solution.py:39
  67.3 2.6 %collective-permute-start.12 = (bf16[512,1024]{1,0:T(8,128)(2,1)S(1)}, bf16[512,1024]{1,0:T(8,128)(2,1)S(1)}, u32[]{:S(2)}, u32[]{:S(2)}) collective-permute-start(bf16[512,1024]{1,0:T(8,128)(2,1)S(1)} %copy-done.5), channel_id=1, source_target_pairs={{0,16},{1,17},{2,18},{3,19},{4,20},{5,21},{6,22},{7,23},{8,24},{9,... | collective-permute-start | bytes 3145736 | tf_op jit(solution)/shard_map/ppermute | solution.py:39
  70.0 0.0 collective-permute-done.13.refs_9_
  70.0 0.0 collective-permute-start.8
  70.0 0.0 collective-permute-done.9.refs_5_
  70.0 0.3 collective-permute-start.19
  70.3 0.0 collective-permute-done.7.refs_3_
  70.3 0.5 collective-permute-start.15
  70.8 16.9 %collective-permute-done.16.refs_12_ = bf16[512,1024]{1,0:T(8,128)(2,1)S(1)} collective-permute-done((bf16[512,1024]{1,0:T(8,128)(2,1)S(1)}, bf16[512,1024]{1,0:T(8,128)(2,1)S(1)}, u32[]{:S(2)}, u32[]{:S(2)}) %collective-permute-start.16) | collective-permute-done | bytes 1048608 | tf_op jit(solution)/shard_map/ppermute | solution.py:39
  87.7 0.0 collective-permute-start.11
  87.7 2.2 %collective-permute-done.12.refs_8_ = bf16[512,1024]{1,0:T(8,128)(2,1)S(1)} collective-permute-done((bf16[512,1024]{1,0:T(8,128)(2,1)S(1)}, bf16[512,1024]{1,0:T(8,128)(2,1)S(1)}, u32[]{:S(2)}, u32[]{:S(2)}) %collective-permute-start.12) | collective-permute-done | bytes 1048608 | tf_op jit(solution)/shard_map/ppermute | solution.py:39
  89.9 1.7 collective-permute-done.8.refs_4_
  91.6 0.0 collective-permute-done.19.refs_15_
  91.6 0.6 collective-permute-start.10
  92.2 0.0 collective-permute-done.15.refs_11_
  92.2 0.3 collective-permute-done.18.refs_14_
  92.6 1.8 %collective-permute-done.14.refs_10_ = bf16[512,1024]{1,0:T(8,128)(2,1)S(1)} collective-permute-done((bf16[512,1024]{1,0:T(8,128)(2,1)S(1)}, bf16[512,1024]{1,0:T(8,128)(2,1)S(1)}, u32[]{:S(2)}, u32[]{:S(2)}) %collective-permute-start.14) | collective-permute-done | bytes 1048608 | tf_op jit(solution)/shard_map/ppermute | solution.py:39
  94.4 1.4 collective-permute-done.10.refs_6_
  95.8 8.3 %all-gather.2.cloned.1.call-done.gathered = bf16[8,8,192,256]{3,2,1,0:T(8,128)(2,1)} async-done(((bf16[1,8,192,256]{3,2,1,0:T(8,128)(2,1)}), bf16[8,8,192,256]{3,2,1,0:T(8,128)(2,1)}) %all-gather.2.cloned.1.call-update) | async-done | bytes 6291472 | tf_op jit(solution)/shard_map/all_gather | solution.py:146
  104.2 13.1 %shard_map.76 = (f32[2,48,1024]{2,1,0:T(8,128)}, f32[2,48,1024]{2,1,0:T(8,128)}, f32[2,48,1024]{2,1,0:T(8,128)}, f32[2,48,1024]{2,1,0:T(8,128)}) custom-call(bf16[8,8,192,256]{3,2,1,0:T(8,128)(2,1)} %all-gather.2.cloned.1.call-done.gathered, bf16[512,1024]{1,0:T(8,128)(2,1)} %constant_dynamic-slice_fusion.2.refs_0_, bf16[512,1024]{1,0:T(8,128)(2,1)} %copy-done.7, ...), custom_call_target="tpu_custom_call" | custom-call | flops 6442450944 | bytes 29360128 | tf_op jit(solution)/shard_map/pallas_call | solution.py:112
  117.2 0.0 copy-start.1
  117.3 0.0 copy-start.2
  117.3 0.0 copy-start.3
  117.3 2.5 %collective-permute-start.20 = (f32[2,48,1024]{2,1,0:T(8,128)}, f32[2,48,1024]{2,1,0:T(8,128)S(1)}, u32[]{:S(2)}, u32[]{:S(2)}) collective-permute-start(f32[2,48,1024]{2,1,0:T(8,128)} %get-tuple-element.25), channel_id=1, source_target_pairs={{0,96},{1,97},{2,98},{3,99},{4,100},{5,101},{6,102},{7,103},{8,104... | collective-permute-start | bytes 1179656 | tf_op jit(solution)/shard_map/ppermute | solution.py:39
  119.7 3.3 %collective-permute-start.21 = (f32[2,48,1024]{2,1,0:T(8,128)}, f32[2,48,1024]{2,1,0:T(8,128)S(1)}, u32[]{:S(2)}, u32[]{:S(2)}) collective-permute-start(f32[2,48,1024]{2,1,0:T(8,128)} %get-tuple-element.26), channel_id=1, source_target_pairs={{0,224},{1,225},{2,226},{3,227},{4,228},{5,229},{6,230},{7,231},{8... | collective-permute-start | bytes 1179656 | tf_op jit(solution)/shard_map/ppermute | solution.py:39
  123.0 1.8 %collective-permute-start.22 = (f32[2,48,1024]{2,1,0:T(8,128)}, f32[2,48,1024]{2,1,0:T(8,128)S(1)}, u32[]{:S(2)}, u32[]{:S(2)}) collective-permute-start(f32[2,48,1024]{2,1,0:T(8,128)} %get-tuple-element.27), channel_id=1, source_target_pairs={{0,128},{1,129},{2,130},{3,131},{4,132},{5,133},{6,134},{7,135},{8... | collective-permute-start | bytes 1179656 | tf_op jit(solution)/shard_map/ppermute | solution.py:39
  124.8 8.4 %collective-permute-done.20 = f32[2,48,1024]{2,1,0:T(8,128)S(1)} collective-permute-done((f32[2,48,1024]{2,1,0:T(8,128)}, f32[2,48,1024]{2,1,0:T(8,128)S(1)}, u32[]{:S(2)}, u32[]{:S(2)}) %collective-permute-start.20) | collective-permute-done | bytes 393248 | tf_op jit(solution)/shard_map/ppermute | solution.py:39
  133.2 7.1 %collective-permute-done.21 = f32[2,48,1024]{2,1,0:T(8,128)S(1)} collective-permute-done((f32[2,48,1024]{2,1,0:T(8,128)}, f32[2,48,1024]{2,1,0:T(8,128)S(1)}, u32[]{:S(2)}, u32[]{:S(2)}) %collective-permute-start.21) | collective-permute-done | bytes 393248 | tf_op jit(solution)/shard_map/ppermute | solution.py:39
  140.3 1.1 collective-permute-done.22
  141.4 1.1 add_add_fusion
  142.5 0.1 copy.26
  142.6 19.2 %all_to_all.5.rows = f32[8,12,8,128]{3,2,1,0:T(8,128)S(1)} all-to-all(f32[8,12,8,128]{3,2,1,0:T(8,128)S(1)} %bitcast.40), channel_id=1, replica_groups=mesh['dp'=32,'tr'=2,'tc'=4] {'tc','tr'}, dimensions={0} | all-to-all | bytes 786432 | tf_op jit(solution)/shard_map/all_to_all | solution.py:159
  161.8 1.2 shard_map.77
  (42 shorter events, 0.2 us)
Async XLA Ops:
  7.2 1.1 copy-start
  7.2 97.0 %all-gather.2.cloned.1.call-start = ((), (), s32[]{:S(2)}) async-start(), calls=%async_computation.1 | async-start | bytes 7077888 | tf_op jit(solution)/shard_map/all_gather | solution.py:146
  8.3 1.6 copy-start.4
  9.9 2.0 %collective-permute-start = (bf16[4,192,256]{2,1,0:T(8,128)(2,1)}, bf16[4,192,256]{2,1,0:T(8,128)(2,1)S(1)}, u32[]{:S(2)}, u32[]{:S(2)}) collective-permute-start(bf16[4,192,256]{2,1,0:T(8,128)(2,1)} %bitcast), channel_id=1, source_target_pairs={{0,8},{1,9},{2,10},{3,11},{4,12},{5,13},{6,14},{7,15},{8,0},{9,1},... | collective-permute-start | bytes 1179656 | tf_op jit(solution)/shard_map/ppermute | solution.py:39
  11.9 15.4 %collective-permute-start.4 = (bf16[256,1024]{1,0:T(8,128)(2,1)}, bf16[256,1024]{1,0:T(8,128)(2,1)}, u32[]{:S(2)}, u32[]{:S(2)}) collective-permute-start(bf16[256,1024]{1,0:T(8,128)(2,1)} %get-tuple-element.19), channel_id=1, source_target_pairs={{0,4},{1,5},{2,6},{3,7},{4,0},{5,1},{6,2},{7,3},{8,12},{9,13},{10,... | collective-permute-start | bytes 1572872 | tf_op jit(solution)/shard_map/ppermute | solution.py:39
  14.7 8.4 %collective-permute-start.1 = (bf16[2,192,256]{2,1,0:T(8,128)(2,1)}, bf16[2,192,256]{2,1,0:T(8,128)(2,1)S(1)}, u32[]{:S(2)}, u32[]{:S(2)}) collective-permute-start(bf16[2,192,256]{2,1,0:T(8,128)(2,1)} %get-tuple-element.43), channel_id=1, source_target_pairs={{0,48},{1,49},{2,50},{3,51},{4,52},{5,53},{6,54},{7,55},{8,56},{9,... | collective-permute-start | bytes 589832 | tf_op jit(solution)/shard_map/ppermute | solution.py:39
  15.5 7.6 %collective-permute-start.3 = (bf16[2,192,256]{2,1,0:T(8,128)(2,1)}, bf16[2,192,256]{2,1,0:T(8,128)(2,1)S(1)}, u32[]{:S(2)}, u32[]{:S(2)}) collective-permute-start(bf16[2,192,256]{2,1,0:T(8,128)(2,1)} %get-tuple-element.44), channel_id=1, source_target_pairs={{0,192},{1,193},{2,194},{3,195},{4,196},{5,197},{6,198},{7,199},{8... | collective-permute-start | bytes 589832 | tf_op jit(solution)/shard_map/ppermute | solution.py:39
  18.5 6.8 %collective-permute-start.2 = (bf16[2,192,256]{2,1,0:T(8,128)(2,1)}, bf16[2,192,256]{2,1,0:T(8,128)(2,1)}, u32[]{:S(2)}, u32[]{:S(2)}) collective-permute-start(bf16[2,192,256]{2,1,0:T(8,128)(2,1)} %get-tuple-element.45), channel_id=1, source_target_pairs={{0,16},{1,17},{2,18},{3,19},{4,20},{5,21},{6,22},{7,23},{8,24},{9,... | collective-permute-start | bytes 589832 | tf_op jit(solution)/shard_map/ppermute | solution.py:39
  22.0 5.2 %copy-start.6 = (bf16[256,1024]{1,0:T(8,128)(2,1)S(1)}, bf16[256,1024]{1,0:T(8,128)(2,1)}, u32[]{:S(2)}) copy-start(bf16[256,1024]{1,0:T(8,128)(2,1)} %get-tuple-element.22) | copy-start | bytes 1572868
  22.0 6.6 %copy-start.5 = (bf16[512,1024]{1,0:T(8,128)(2,1)S(1)}, bf16[512,1024]{1,0:T(8,128)(2,1)}, u32[]{:S(2)}) copy-start(bf16[512,1024]{1,0:T(8,128)(2,1)} %constant_dynamic-slice_fusion.2.refs_0_) | copy-start | bytes 3145732
  27.3 13.3 %collective-permute-start.5 = (bf16[256,1024]{1,0:T(8,128)(2,1)S(1)}, bf16[256,1024]{1,0:T(8,128)(2,1)S(1)}, u32[]{:S(2)}, u32[]{:S(2)}) collective-permute-start(bf16[256,1024]{1,0:T(8,128)(2,1)S(1)} %copy-done.6), channel_id=1, source_target_pairs={{0,4},{1,5},{2,6},{3,7},{4,0},{5,1},{6,2},{7,3},{8,12},{9,13},{10,... | collective-permute-start | bytes 1572872 | tf_op jit(solution)/shard_map/ppermute | solution.py:39
  28.6 17.1 %collective-permute-start.6 = (bf16[512,1024]{1,0:T(8,128)(2,1)S(1)}, bf16[512,1024]{1,0:T(8,128)(2,1)S(1)}, u32[]{:S(2)}, u32[]{:S(2)}) collective-permute-start(bf16[512,1024]{1,0:T(8,128)(2,1)S(1)} %copy-done.5), channel_id=1, source_target_pairs={{0,8},{1,9},{2,10},{3,11},{4,12},{5,13},{6,14},{7,15},{8,0},{9,1},... | collective-permute-start | bytes 3145736 | tf_op jit(solution)/shard_map/ppermute | solution.py:39
  40.6 63.6 %copy-start.7 = (bf16[512,1024]{1,0:T(8,128)(2,1)}, bf16[512,1024]{1,0:T(8,128)(2,1)S(1)}, u32[]{:S(2)}) copy-start(bf16[512,1024]{1,0:T(8,128)(2,1)S(1)} %constant_dynamic-update-slice_fusion.refs_1_) | copy-start | bytes 3145732
  40.6 26.7 %collective-permute-start.17 = (bf16[512,1024]{1,0:T(8,128)(2,1)S(1)}, bf16[512,1024]{1,0:T(8,128)(2,1)S(1)}, u32[]{:S(2)}, u32[]{:S(2)}) collective-permute-start(bf16[512,1024]{1,0:T(8,128)(2,1)S(1)} %constant_dynamic-update-slice_fusion.refs_1_), channel_id=1, source_target_pairs={{0,192},{1,193},{2,194},{3,195},{4,196},{5,197},{6,198},{7,199},{8... | collective-permute-start | bytes 3145736 | tf_op jit(solution)/shard_map/ppermute | solution.py:39
  43.7 26.3 %collective-permute-start.13 = (bf16[512,1024]{1,0:T(8,128)(2,1)S(1)}, bf16[512,1024]{1,0:T(8,128)(2,1)S(1)}, u32[]{:S(2)}, u32[]{:S(2)}) collective-permute-start(bf16[512,1024]{1,0:T(8,128)(2,1)S(1)} %constant_dynamic-update-slice_fusion.refs_1_), channel_id=1, source_target_pairs={{0,16},{1,17},{2,18},{3,19},{4,20},{5,21},{6,22},{7,23},{8,24},{9,... | collective-permute-start | bytes 3145736 | tf_op jit(solution)/shard_map/ppermute | solution.py:39
  44.4 25.5 %collective-permute-start.9 = (bf16[512,1024]{1,0:T(8,128)(2,1)S(1)}, bf16[512,1024]{1,0:T(8,128)(2,1)S(1)}, u32[]{:S(2)}, u32[]{:S(2)}) collective-permute-start(bf16[512,1024]{1,0:T(8,128)(2,1)S(1)} %constant_dynamic-update-slice_fusion.refs_1_), channel_id=1, source_target_pairs={{0,48},{1,49},{2,50},{3,51},{4,52},{5,53},{6,54},{7,55},{8,56},{9,... | collective-permute-start | bytes 3145736 | tf_op jit(solution)/shard_map/ppermute | solution.py:39
  45.7 24.6 %collective-permute-start.7 = (bf16[512,1024]{1,0:T(8,128)(2,1)S(1)}, bf16[512,1024]{1,0:T(8,128)(2,1)S(1)}, u32[]{:S(2)}, u32[]{:S(2)}) collective-permute-start(bf16[512,1024]{1,0:T(8,128)(2,1)S(1)} %constant_dynamic-update-slice_fusion.refs_1_), channel_id=1, source_target_pairs={{0,8},{1,9},{2,10},{3,11},{4,12},{5,13},{6,14},{7,15},{8,0},{9,1},... | collective-permute-start | bytes 3145736 | tf_op jit(solution)/shard_map/ppermute | solution.py:39
  45.7 45.8 %copy-start.8 = (bf16[512,1024]{1,0:T(8,128)(2,1)}, bf16[512,1024]{1,0:T(8,128)(2,1)S(1)}, u32[]{:S(2)}) copy-start(bf16[512,1024]{1,0:T(8,128)(2,1)S(1)} %collective-permute-done.6.refs_2_) | copy-start | bytes 3145732
  45.7 42.0 %collective-permute-start.16 = (bf16[512,1024]{1,0:T(8,128)(2,1)S(1)}, bf16[512,1024]{1,0:T(8,128)(2,1)S(1)}, u32[]{:S(2)}, u32[]{:S(2)}) collective-permute-start(bf16[512,1024]{1,0:T(8,128)(2,1)S(1)} %copy-done.5), channel_id=1, source_target_pairs={{0,192},{1,193},{2,194},{3,195},{4,196},{5,197},{6,198},{7,199},{8... | collective-permute-start | bytes 3145736 | tf_op jit(solution)/shard_map/ppermute | solution.py:39
  67.3 24.3 %copy-start.9 = (bf16[512,1024]{1,0:T(8,128)(2,1)}, bf16[512,1024]{1,0:T(8,128)(2,1)S(1)}, u32[]{:S(2)}) copy-start(bf16[512,1024]{1,0:T(8,128)(2,1)S(1)} %collective-permute-done.17.refs_13_) | copy-start | bytes 3145732
  67.3 22.6 %collective-permute-start.12 = (bf16[512,1024]{1,0:T(8,128)(2,1)S(1)}, bf16[512,1024]{1,0:T(8,128)(2,1)S(1)}, u32[]{:S(2)}, u32[]{:S(2)}) collective-permute-start(bf16[512,1024]{1,0:T(8,128)(2,1)S(1)} %copy-done.5), channel_id=1, source_target_pairs={{0,16},{1,17},{2,18},{3,19},{4,20},{5,21},{6,22},{7,23},{8,24},{9,... | collective-permute-start | bytes 3145736 | tf_op jit(solution)/shard_map/ppermute | solution.py:39
  70.0 21.6 %copy-start.10 = (bf16[512,1024]{1,0:T(8,128)(2,1)}, bf16[512,1024]{1,0:T(8,128)(2,1)S(1)}, u32[]{:S(2)}) copy-start(bf16[512,1024]{1,0:T(8,128)(2,1)S(1)} %collective-permute-done.13.refs_9_) | copy-start | bytes 3145732
  70.0 21.6 %collective-permute-start.8 = (bf16[512,1024]{1,0:T(8,128)(2,1)S(1)}, bf16[512,1024]{1,0:T(8,128)(2,1)S(1)}, u32[]{:S(2)}, u32[]{:S(2)}) collective-permute-start(bf16[512,1024]{1,0:T(8,128)(2,1)S(1)} %copy-done.5), channel_id=1, source_target_pairs={{0,48},{1,49},{2,50},{3,51},{4,52},{5,53},{6,54},{7,55},{8,56},{9,... | collective-permute-start | bytes 3145736 | tf_op jit(solution)/shard_map/ppermute | solution.py:39
  70.0 22.2 %copy-start.11 = (bf16[512,1024]{1,0:T(8,128)(2,1)}, bf16[512,1024]{1,0:T(8,128)(2,1)S(1)}, u32[]{:S(2)}) copy-start(bf16[512,1024]{1,0:T(8,128)(2,1)S(1)} %collective-permute-done.9.refs_5_) | copy-start | bytes 3145732
  70.0 21.6 %collective-permute-start.19 = (bf16[512,1024]{1,0:T(8,128)(2,1)S(1)}, bf16[512,1024]{1,0:T(8,128)(2,1)S(1)}, u32[]{:S(2)}, u32[]{:S(2)}) collective-permute-start(bf16[512,1024]{1,0:T(8,128)(2,1)S(1)} %collective-permute-done.17.refs_13_), channel_id=1, source_target_pairs={{0,8},{1,9},{2,10},{3,11},{4,12},{5,13},{6,14},{7,15},{8,0},{9,1},... | collective-permute-start | bytes 3145736 | tf_op jit(solution)/shard_map/ppermute | solution.py:39
  70.3 21.9 %copy-start.12 = (bf16[512,1024]{1,0:T(8,128)(2,1)}, bf16[512,1024]{1,0:T(8,128)(2,1)S(1)}, u32[]{:S(2)}) copy-start(bf16[512,1024]{1,0:T(8,128)(2,1)S(1)} %collective-permute-done.7.refs_3_) | copy-start | bytes 3145732
  70.3 21.9 %collective-permute-start.15 = (bf16[512,1024]{1,0:T(8,128)(2,1)S(1)}, bf16[512,1024]{1,0:T(8,128)(2,1)S(1)}, u32[]{:S(2)}, u32[]{:S(2)}) collective-permute-start(bf16[512,1024]{1,0:T(8,128)(2,1)S(1)} %collective-permute-done.13.refs_9_), channel_id=1, source_target_pairs={{0,8},{1,9},{2,10},{3,11},{4,12},{5,13},{6,14},{7,15},{8,0},{9,1},... | collective-permute-start | bytes 3145736 | tf_op jit(solution)/shard_map/ppermute | solution.py:39
  87.7 4.9 %copy-start.13 = (bf16[512,1024]{1,0:T(8,128)(2,1)}, bf16[512,1024]{1,0:T(8,128)(2,1)S(1)}, u32[]{:S(2)}) copy-start(bf16[512,1024]{1,0:T(8,128)(2,1)S(1)} %collective-permute-done.16.refs_12_) | copy-start | bytes 3145732
  87.7 4.5 %collective-permute-start.11 = (bf16[512,1024]{1,0:T(8,128)(2,1)S(1)}, bf16[512,1024]{1,0:T(8,128)(2,1)S(1)}, u32[]{:S(2)}, u32[]{:S(2)}) collective-permute-start(bf16[512,1024]{1,0:T(8,128)(2,1)S(1)} %collective-permute-done.9.refs_5_), channel_id=1, source_target_pairs={{0,8},{1,9},{2,10},{3,11},{4,12},{5,13},{6,14},{7,15},{8,0},{9,1},... | collective-permute-start | bytes 3145736 | tf_op jit(solution)/shard_map/ppermute | solution.py:39
  89.9 4.5 %copy-start.14 = (bf16[512,1024]{1,0:T(8,128)(2,1)}, bf16[512,1024]{1,0:T(8,128)(2,1)S(1)}, u32[]{:S(2)}) copy-start(bf16[512,1024]{1,0:T(8,128)(2,1)S(1)} %collective-permute-done.12.refs_8_) | copy-start | bytes 3145732
  89.9 2.7 %collective-permute-start.18 = (bf16[512,1024]{1,0:T(8,128)(2,1)S(1)}, bf16[512,1024]{1,0:T(8,128)(2,1)S(1)}, u32[]{:S(2)}, u32[]{:S(2)}) collective-permute-start(bf16[512,1024]{1,0:T(8,128)(2,1)S(1)} %collective-permute-done.16.refs_12_), channel_id=1, source_target_pairs={{0,8},{1,9},{2,10},{3,11},{4,12},{5,13},{6,14},{7,15},{8,0},{9,1},... | collective-permute-start | bytes 3145736 | tf_op jit(solution)/shard_map/ppermute | solution.py:39
  91.6 2.8 %copy-start.15 = (bf16[512,1024]{1,0:T(8,128)(2,1)}, bf16[512,1024]{1,0:T(8,128)(2,1)S(1)}, u32[]{:S(2)}) copy-start(bf16[512,1024]{1,0:T(8,128)(2,1)S(1)} %collective-permute-done.8.refs_4_) | copy-start | bytes 3145732
  91.6 2.8 %collective-permute-start.14 = (bf16[512,1024]{1,0:T(8,128)(2,1)S(1)}, bf16[512,1024]{1,0:T(8,128)(2,1)S(1)}, u32[]{:S(2)}, u32[]{:S(2)}) collective-permute-start(bf16[512,1024]{1,0:T(8,128)(2,1)S(1)} %collective-permute-done.12.refs_8_), channel_id=1, source_target_pairs={{0,8},{1,9},{2,10},{3,11},{4,12},{5,13},{6,14},{7,15},{8,0},{9,1},... | collective-permute-start | bytes 3145736 | tf_op jit(solution)/shard_map/ppermute | solution.py:39
  91.6 2.8 %copy-start.16 = (bf16[512,1024]{1,0:T(8,128)(2,1)}, bf16[512,1024]{1,0:T(8,128)(2,1)S(1)}, u32[]{:S(2)}) copy-start(bf16[512,1024]{1,0:T(8,128)(2,1)S(1)} %collective-permute-done.19.refs_15_) | copy-start | bytes 3145732
  91.6 4.2 %collective-permute-start.10 = (bf16[512,1024]{1,0:T(8,128)(2,1)S(1)}, bf16[512,1024]{1,0:T(8,128)(2,1)}, u32[]{:S(2)}, u32[]{:S(2)}) collective-permute-start(bf16[512,1024]{1,0:T(8,128)(2,1)S(1)} %collective-permute-done.8.refs_4_), channel_id=1, source_target_pairs={{0,8},{1,9},{2,10},{3,11},{4,12},{5,13},{6,14},{7,15},{8,0},{9,1},... | collective-permute-start | bytes 3145736 | tf_op jit(solution)/shard_map/ppermute | solution.py:39
  92.2 2.2 %copy-start.17 = (bf16[512,1024]{1,0:T(8,128)(2,1)}, bf16[512,1024]{1,0:T(8,128)(2,1)S(1)}, u32[]{:S(2)}) copy-start(bf16[512,1024]{1,0:T(8,128)(2,1)S(1)} %collective-permute-done.15.refs_11_) | copy-start | bytes 3145732
  92.2 2.2 %copy-start.18 = (bf16[512,1024]{1,0:T(8,128)(2,1)}, bf16[512,1024]{1,0:T(8,128)(2,1)S(1)}, u32[]{:S(2)}) copy-start(bf16[512,1024]{1,0:T(8,128)(2,1)S(1)} %collective-permute-done.11.refs_7_) | copy-start | bytes 3145732
  92.6 1.9 %copy-start.19 = (bf16[512,1024]{1,0:T(8,128)(2,1)}, bf16[512,1024]{1,0:T(8,128)(2,1)S(1)}, u32[]{:S(2)}) copy-start(bf16[512,1024]{1,0:T(8,128)(2,1)S(1)} %collective-permute-done.18.refs_14_) | copy-start | bytes 3145732
  94.4 9.7 %copy-start.20 = (bf16[512,1024]{1,0:T(8,128)(2,1)}, bf16[512,1024]{1,0:T(8,128)(2,1)S(1)}, u32[]{:S(2)}) copy-start(bf16[512,1024]{1,0:T(8,128)(2,1)S(1)} %collective-permute-done.14.refs_10_) | copy-start | bytes 3145732
  117.2 44.6 %copy-start.1 = (f32[1,12,8192]{2,0,1:T(1,128)S(1)}, f32[1,12,8192]{2,0,1:T(1,128)}, u32[]{:S(2)}) copy-start(f32[1,12,8192]{2,0,1:T(1,128)} %param.7) | copy-start | bytes 1179652
  117.3 44.6 %copy-start.2 = (f32[1,12,8192]{2,0,1:T(1,128)S(1)}, f32[1,12,8192]{2,0,1:T(1,128)}, u32[]{:S(2)}) copy-start(f32[1,12,8192]{2,0,1:T(1,128)} %param.8) | copy-start | bytes 1179652
  117.3 44.6 %copy-start.3 = (f32[1,12,8192]{2,0,1:T(1,128)S(1)}, f32[1,12,8192]{2,0,1:T(1,128)}, u32[]{:S(2)}) copy-start(f32[1,12,8192]{2,0,1:T(1,128)} %param.9) | copy-start | bytes 1179652
  117.3 15.9 %collective-permute-start.20 = (f32[2,48,1024]{2,1,0:T(8,128)}, f32[2,48,1024]{2,1,0:T(8,128)S(1)}, u32[]{:S(2)}, u32[]{:S(2)}) collective-permute-start(f32[2,48,1024]{2,1,0:T(8,128)} %get-tuple-element.25), channel_id=1, source_target_pairs={{0,96},{1,97},{2,98},{3,99},{4,100},{5,101},{6,102},{7,103},{8,104... | collective-permute-start | bytes 1179656 | tf_op jit(solution)/shard_map/ppermute | solution.py:39
  119.7 20.6 %collective-permute-start.21 = (f32[2,48,1024]{2,1,0:T(8,128)}, f32[2,48,1024]{2,1,0:T(8,128)S(1)}, u32[]{:S(2)}, u32[]{:S(2)}) collective-permute-start(f32[2,48,1024]{2,1,0:T(8,128)} %get-tuple-element.26), channel_id=1, source_target_pairs={{0,224},{1,225},{2,226},{3,227},{4,228},{5,229},{6,230},{7,231},{8... | collective-permute-start | bytes 1179656 | tf_op jit(solution)/shard_map/ppermute | solution.py:39
  123.0 18.4 %collective-permute-start.22 = (f32[2,48,1024]{2,1,0:T(8,128)}, f32[2,48,1024]{2,1,0:T(8,128)S(1)}, u32[]{:S(2)}, u32[]{:S(2)}) collective-permute-start(f32[2,48,1024]{2,1,0:T(8,128)} %get-tuple-element.27), channel_id=1, source_target_pairs={{0,128},{1,129},{2,130},{3,131},{4,132},{5,133},{6,134},{7,135},{8... | collective-permute-start | bytes 1179656 | tf_op jit(solution)/shard_map/ppermute | solution.py:39
Sparse Core Ops, SparseCore 0:
  27.4 76.7 all-gather.1

commit v12 on v10

--- a/solution.py
+++ b/solution.py
@@ -62,13 +62,14 @@
     return ordered.astype(activations.dtype)
 
 
-def product_kernel(gathered, *refs):
+def product_kernel(first, gathered, *refs):
     cots = refs[: 4 * GROUP]
     outs = refs[4 * GROUP : 4 * GROUP + 4]
     act, cot, act_sem, cot_sem = refs[4 * GROUP + 4 :]
     tr = lax.axis_index("tr")
     replicas, quarter, tokens = gathered.shape[1:]
     depth = 4 * tokens
+    columns = pl.ds(first, cot.shape[1])
 
     def copies_of(replica):
         copies = []
@@ -80,7 +81,7 @@
             half = 1 - tr if came else tr
             start = pl.multiple_of(replica * depth + half * 2 * tokens, 2 * tokens)
             n = 2 * replica + came
-            copies.append(pltpu.make_async_copy(cots[n], cot.at[pl.ds(start, 2 * tokens)], cot_sem.at[n]))
+            copies.append(pltpu.make_async_copy(cots[n].at[:, columns], cot.at[pl.ds(start, 2 * tokens)], cot_sem.at[n]))
         return copies
 
     def fetch(replica):
@@ -103,12 +104,11 @@
         outs[owner][...] = total[:, owner]
 
 
-def product(gathered, cots):
+def product(gathered, cots, first, units):
     replicas, quarter, tokens = gathered.shape[1:]
-    units = cots[0].shape[1]
     part = jax.ShapeDtypeStruct((2, ROWS, units), jnp.float32)
     return pl.pallas_call(
-        product_kernel,
+        lambda *refs: product_kernel(first, *refs),
         in_specs=[pl.BlockSpec(memory_space=pl.ANY)] * (1 + len(cots)),
         out_shape=[part] * 4,
         scratch_shapes=[
@@ -119,7 +119,7 @@
         ],
         compiler_params=pltpu.CompilerParams(vmem_limit_bytes=60 * 2**20),
         cost_estimate=pl.CostEstimate(
-            flops=2 * 2 * quarter * replicas * 4 * tokens * units, bytes_accessed=28 * 2**20, transcendentals=0
+            flops=2 * 2 * quarter * replicas * 4 * tokens * units, bytes_accessed=16 * 2**20, transcendentals=0
         ),
     )(gathered, *cots)
 
@@ -148,11 +148,13 @@
     cots = []
     for g in range(GROUP):
         cots += [keep[g], came[g], send(keep[g], OTHER_CORE), send(came[g], OTHER_CORE)]
-    parts = product(gathered, cots)
-    far = [send(parts[owner], REDUCE[owner]) for owner in (1, 3)]
-    far.append(send(parts[2], REDUCE[2]))
-    rows = parts[0] + far[0] + (far[1] + far[2])
-    rows = rows.reshape(2, 4, ROWS // 4, 8, units // 8)
+    halves = []
+    for first in (0, units // 2):
+        parts = product(gathered, cots, first, units // 2)
+        far = [send(parts[owner], REDUCE[owner]) for owner in (1, 3, 2)]
+        half = parts[0] + far[0] + (far[1] + far[2])
+        halves.append(half.reshape(2, 4, ROWS // 4, 4, units // 8))
+    rows = jnp.concatenate(halves, axis=3)
     rows = rows.swapaxes(0, 1).reshape(8, ROWS // 4, 8, units // 8)
     rows = lax.all_to_all(rows, ("tc", "tr"), split_axis=0, concat_axis=0, tiled=True)
     return updated(rows, master, moment, second)

time: 170 us -> 170 us (level)
  waiting for transfers between devices: 86.6 us -> 74.8 us
  starting transfers between devices: 27.1 us -> 34.5 us
  Pallas kernels: 13.2 us -> 17.1 us
  local copies, waits for them, and re-layouts: 4.07 us -> 6.37 us
    ppermute x23 -> x26, waiting for transfers between devices: 78.4 us -> 67.4 us  [send(): return lax.ppermute(array, AXES, pairs)]
    ppermute x23 -> x26, starting transfers between devices: 27.1 us -> 34.5 us  [send(): return lax.ppermute(array, AXES, pairs)]
    pallas_call x1 -> x2, Pallas kernels: 12 us -> 15.9 us  [product(): pl.pallas_call(lambda *refs: product_kernel(first, *refs), in_specs=[pl.B...]
    unnamed x42 -> x45, local copies, waits for them, and re-layouts: 1.19 us -> 3.15 us
  transfers between devices with their start and end apart: 24 -> 27, of which waited for: 15 -> 15; matrix products, arithmetic and copies ran while one was open for 2% -> 3% of each run, Pallas kernels for 0% -> 5%
where the time goes in v12:
time: 170 us
  waiting for transfers between devices  74.8 us (44%)
  starting transfers between devices  34.5 us (20%)
  blocking collectives  18.1 us (11%)
  Pallas kernels  17.1 us (10%)
  between operations  14.3 us (8%)
  local copies, waits for them, and re-layouts  6.37 us (4%)
  other arithmetic  3.25 us (2%)
    ppermute x26, waiting for transfers between devices, send(): return lax.ppermute(array, AXES, pairs)  67.4 us
    ppermute x26, starting transfers between devices, send(): return lax.ppermute(array, AXES, pairs)  34.5 us
    all_to_all x1, blocking collectives, shards(): lax.all_to_all(rows, ('tc', 'tr'), split_axis=0, concat_axis=0, tiled=True)  18.1 us
    pallas_call x2, Pallas kernels, product(): pl.pallas_call(lambda *refs: product_kernel(first, *refs), in_specs=[pl.B...  15.9 us
    all_gather x1, waiting for transfers between devices, shards(): gathered = lax.all_gather(shared, ('tc', 'tr'), axis=0)  7.38 us
  transfers between devices with their start and end apart: 27, of which 15 were waited for; matrix products, arithmetic and copies ran while one was open for 3% of the time, Pallas kernels for 5%

profile of v12, /device:TPU:6, one launch (start us, length us, event | category | flops | bytes accessed | tf_op | source)
XLA Modules:
  0.0 170.0 jit_solution(7923767006144154688)
XLA Ops:
  7.2 0.0 copy-start
  7.2 0.0 all-gather.2.cloned.1.call-start
  7.3 1.0 copy-done
  8.3 1.5 fusion.4
  9.8 0.8 fusion.34
  10.6 0.9 constant_dynamic-slice_fusion
  11.5 1.3 constant_dynamic-slice_fusion.1.refs_1_
  12.9 2.0 %collective-permute-start.4 = (bf16[256,1024]{1,0:T(8,128)(2,1)S(1)}, bf16[256,1024]{1,0:T(8,128)(2,1)S(1)}, u32[]{:S(2)}, u32[]{:S(2)}) collective-permute-start(bf16[256,1024]{1,0:T(8,128)(2,1)S(1)} %get-tuple-element.23), channel_id=1, source_target_pairs={{0,4},{1,5},{2,6},{3,7},{4,0},{5,1},{6,2},{7,3},{8,12},{9,13},{10,... | collective-permute-start | bytes 1572872 | tf_op jit(solution)/shard_map/ppermute | solution.py:38
  14.9 1.1 fusion.10
  16.0 0.9 collective-permute-start.1
  16.9 2.4 %collective-permute-start.2 = (bf16[2,192,256]{2,1,0:T(8,128)(2,1)S(1)}, bf16[2,192,256]{2,1,0:T(8,128)(2,1)S(1)}, u32[]{:S(2)}, u32[]{:S(2)}) collective-permute-start(bf16[2,192,256]{2,1,0:T(8,128)(2,1)S(1)} %get-tuple-element.53), channel_id=1, source_target_pairs={{0,16},{1,17},{2,18},{3,19},{4,20},{5,21},{6,22},{7,23},{8,24},{9,... | collective-permute-start | bytes 589832 | tf_op jit(solution)/shard_map/ppermute | solution.py:38
  19.3 3.0 %collective-permute-start.3 = (bf16[2,192,256]{2,1,0:T(8,128)(2,1)S(1)}, bf16[2,192,256]{2,1,0:T(8,128)(2,1)S(1)}, u32[]{:S(2)}, u32[]{:S(2)}) collective-permute-start(bf16[2,192,256]{2,1,0:T(8,128)(2,1)S(1)} %get-tuple-element.52), channel_id=1, source_target_pairs={{0,192},{1,193},{2,194},{3,195},{4,196},{5,197},{6,198},{7,199},{8... | collective-permute-start | bytes 589832 | tf_op jit(solution)/shard_map/ppermute | solution.py:38
  22.3 2.0 %collective-permute-done.1 = bf16[2,192,256]{2,1,0:T(8,128)(2,1)S(1)} collective-permute-done((bf16[2,192,256]{2,1,0:T(8,128)(2,1)S(1)}, bf16[2,192,256]{2,1,0:T(8,128)(2,1)S(1)}, u32[]{:S(2)}, u32[]{:S(2)}) %collective-permute-start.1) | collective-permute-done | bytes 196640 | tf_op jit(solution)/shard_map/ppermute | solution.py:38
  24.3 0.0 collective-permute-done.2
  24.3 2.0 %collective-permute-done.3 = bf16[2,192,256]{2,1,0:T(8,128)(2,1)S(1)} collective-permute-done((bf16[2,192,256]{2,1,0:T(8,128)(2,1)S(1)}, bf16[2,192,256]{2,1,0:T(8,128)(2,1)S(1)}, u32[]{:S(2)}, u32[]{:S(2)}) %collective-permute-start.3) | collective-permute-done | bytes 196640 | tf_op jit(solution)/shard_map/ppermute | solution.py:38
  26.3 1.0 pad_maximum_fusion
  27.3 0.2 collective-permute-done.4
  27.5 0.0 all-gather.2.cloned.1.call-update
  27.5 1.8 %collective-permute-start.5 = (bf16[256,1024]{1,0:T(8,128)(2,1)}, bf16[256,1024]{1,0:T(8,128)(2,1)S(1)}, u32[]{:S(2)}, u32[]{:S(2)}) collective-permute-start(bf16[256,1024]{1,0:T(8,128)(2,1)} %get-tuple-element.26), channel_id=1, source_target_pairs={{0,4},{1,5},{2,6},{3,7},{4,0},{5,1},{6,2},{7,3},{8,12},{9,13},{10,... | collective-permute-start | bytes 1572872 | tf_op jit(solution)/shard_map/ppermute | solution.py:38
  29.3 1.1 constant_dynamic-update-slice_fusion.1
  30.4 11.0 %collective-permute-done.5 = bf16[256,1024]{1,0:T(8,128)(2,1)S(1)} collective-permute-done((bf16[256,1024]{1,0:T(8,128)(2,1)}, bf16[256,1024]{1,0:T(8,128)(2,1)S(1)}, u32[]{:S(2)}, u32[]{:S(2)}) %collective-permute-start.5) | collective-permute-done | bytes 524320 | tf_op jit(solution)/shard_map/ppermute | solution.py:38
  41.5 0.9 collective-permute-start.9
  42.4 2.4 %collective-permute-start.13 = (bf16[512,1024]{1,0:T(8,128)(2,1)S(1)}, bf16[512,1024]{1,0:T(8,128)(2,1)S(1)}, u32[]{:S(2)}, u32[]{:S(2)}) collective-permute-start(bf16[512,1024]{1,0:T(8,128)(2,1)S(1)} %constant_dynamic-update-slice_fusion.refs_2_), channel_id=1, source_target_pairs={{0,16},{1,17},{2,18},{3,19},{4,20},{5,21},{6,22},{7,23},{8,24},{9,... | collective-permute-start | bytes 3145736 | tf_op jit(solution)/shard_map/ppermute | solution.py:38
  44.8 3.0 %collective-permute-start.17 = (bf16[512,1024]{1,0:T(8,128)(2,1)S(1)}, bf16[512,1024]{1,0:T(8,128)(2,1)S(1)}, u32[]{:S(2)}, u32[]{:S(2)}) collective-permute-start(bf16[512,1024]{1,0:T(8,128)(2,1)S(1)} %constant_dynamic-update-slice_fusion.refs_2_), channel_id=1, source_target_pairs={{0,192},{1,193},{2,194},{3,195},{4,196},{5,197},{6,198},{7,199},{8... | collective-permute-start | bytes 3145736 | tf_op jit(solution)/shard_map/ppermute | solution.py:38
  47.8 0.1 collective-permute-start.8
  47.9 21.0 %collective-permute-done.9.refs_6_ = bf16[512,1024]{1,0:T(8,128)(2,1)S(1)} collective-permute-done((bf16[512,1024]{1,0:T(8,128)(2,1)S(1)}, bf16[512,1024]{1,0:T(8,128)(2,1)S(1)}, u32[]{:S(2)}, u32[]{:S(2)}) %collective-permute-start.9) | collective-permute-done | bytes 1048608 | tf_op jit(solution)/shard_map/ppermute | solution.py:38
  68.9 0.7 collective-permute-start.12
  69.6 2.4 %collective-permute-start.16 = (bf16[512,1024]{1,0:T(8,128)(2,1)S(1)}, bf16[512,1024]{1,0:T(8,128)(2,1)S(1)}, u32[]{:S(2)}, u32[]{:S(2)}) collective-permute-start(bf16[512,1024]{1,0:T(8,128)(2,1)S(1)} %constant_dynamic-slice_fusion.1.refs_1_), channel_id=1, source_target_pairs={{0,192},{1,193},{2,194},{3,195},{4,196},{5,197},{6,198},{7,199},{8... | collective-permute-start | bytes 3145736 | tf_op jit(solution)/shard_map/ppermute | solution.py:38
  72.0 0.0 collective-permute-done.17.refs_14_
  72.0 0.0 collective-permute-start.11
  72.0 0.0 collective-permute-done.7.refs_4_
  72.0 0.5 collective-permute-start.15
  72.5 16.8 %collective-permute-done.8.refs_5_ = bf16[512,1024]{1,0:T(8,128)(2,1)S(1)} collective-permute-done((bf16[512,1024]{1,0:T(8,128)(2,1)S(1)}, bf16[512,1024]{1,0:T(8,128)(2,1)S(1)}, u32[]{:S(2)}, u32[]{:S(2)}) %collective-permute-start.8) | collective-permute-done | bytes 1048608 | tf_op jit(solution)/shard_map/ppermute | solution.py:38
  89.3 0.0 collective-permute-start.19
  89.3 0.7 collective-permute-done.12.refs_9_
  90.0 0.0 collective-permute-start.10
  90.0 0.7 collective-permute-done.16.refs_13_
  90.8 0.6 collective-permute-start.18
  91.4 0.6 collective-permute-done.19.refs_16_
  91.9 1.5 collective-permute-done.10.refs_7_
  93.4 3.0 %collective-permute-done.14.refs_11_ = bf16[512,1024]{1,0:T(8,128)(2,1)S(1)} collective-permute-done((bf16[512,1024]{1,0:T(8,128)(2,1)S(1)}, bf16[512,1024]{1,0:T(8,128)(2,1)S(1)}, u32[]{:S(2)}, u32[]{:S(2)}) %collective-permute-start.14) | collective-permute-done | bytes 1048608 | tf_op jit(solution)/shard_map/ppermute | solution.py:38
  96.5 1.0 copy-done.18
  97.5 7.4 %all-gather.2.cloned.1.call-done.refs_0_ = bf16[8,8,192,256]{3,2,1,0:T(8,128)(2,1)} async-done(((bf16[1,8,192,256]{3,2,1,0:T(8,128)(2,1)}), bf16[8,8,192,256]{3,2,1,0:T(8,128)(2,1)}) %all-gather.2.cloned.1.call-update) | async-done | bytes 6291472 | tf_op jit(solution)/shard_map/all_gather | solution.py:144
  104.9 8.0 %shard_map.76 = (f32[2,48,512]{2,1,0:T(8,128)}, f32[2,48,512]{2,1,0:T(8,128)}, f32[2,48,512]{2,1,0:T(8,128)}, f32[2,48,512]{2,1,0:T(8,128)}) custom-call(bf16[8,8,192,256]{3,2,1,0:T(8,128)(2,1)} %all-gather.2.cloned.1.call-done.refs_0_, bf16[512,1024]{1,0:T(8,128)(2,1)} %copy-done.4, bf16[512,1024]{1,0:T(8,128)(2,1)} %copy-done.5, ...), custom_call_target="tpu_custom_call" | custom-call | flops 3221225472 | bytes 16777216 | tf_op jit(solution)/shard_map/pallas_call | solution.py:110
  112.8 2.5 %collective-permute-start.20 = (f32[2,48,512]{2,1,0:T(8,128)}, f32[2,48,512]{2,1,0:T(8,128)S(1)}, u32[]{:S(2)}, u32[]{:S(2)}) collective-permute-start(f32[2,48,512]{2,1,0:T(8,128)} %get-tuple-element.29), channel_id=1, source_target_pairs={{0,96},{1,97},{2,98},{3,99},{4,100},{5,101},{6,102},{7,103},{8,104... | collective-permute-start | bytes 589832 | tf_op jit(solution)/shard_map/ppermute | solution.py:38
  115.3 3.3 %collective-permute-start.21 = (f32[2,48,512]{2,1,0:T(8,128)}, f32[2,48,512]{2,1,0:T(8,128)S(1)}, u32[]{:S(2)}, u32[]{:S(2)}) collective-permute-start(f32[2,48,512]{2,1,0:T(8,128)} %get-tuple-element.30), channel_id=1, source_target_pairs={{0,224},{1,225},{2,226},{3,227},{4,228},{5,229},{6,230},{7,231},{8... | collective-permute-start | bytes 589832 | tf_op jit(solution)/shard_map/ppermute | solution.py:38
  118.5 1.8 %collective-permute-start.22 = (f32[2,48,512]{2,1,0:T(8,128)}, f32[2,48,512]{2,1,0:T(8,128)S(1)}, u32[]{:S(2)}, u32[]{:S(2)}) collective-permute-start(f32[2,48,512]{2,1,0:T(8,128)} %get-tuple-element.31), channel_id=1, source_target_pairs={{0,128},{1,129},{2,130},{3,131},{4,132},{5,133},{6,134},{7,135},{8... | collective-permute-start | bytes 589832 | tf_op jit(solution)/shard_map/ppermute | solution.py:38
  120.4 7.9 %shard_map.77 = (f32[2,48,512]{2,1,0:T(8,128)}, f32[2,48,512]{2,1,0:T(8,128)}, f32[2,48,512]{2,1,0:T(8,128)}, f32[2,48,512]{2,1,0:T(8,128)}) custom-call(bf16[8,8,192,256]{3,2,1,0:T(8,128)(2,1)} %all-gather.2.cloned.1.call-done.refs_0_, bf16[512,1024]{1,0:T(8,128)(2,1)} %copy-done.4, bf16[512,1024]{1,0:T(8,128)(2,1)} %copy-done.5, ...), custom_call_target="tpu_custom_call" | custom-call | flops 3221225472 | bytes 16777216 | tf_op jit(solution)/shard_map/pallas_call | solution.py:110
  128.3 0.0 copy-start.1
  128.3 0.0 copy-start.2
  128.3 0.0 copy-start.3
  128.3 1.6 collective-permute-start.23
  129.9 4.2 %collective-permute-start.24 = (f32[2,48,512]{2,1,0:T(8,128)}, f32[2,48,512]{2,1,0:T(8,128)S(1)}, u32[]{:S(2)}, u32[]{:S(2)}) collective-permute-start(f32[2,48,512]{2,1,0:T(8,128)} %get-tuple-element.34), channel_id=1, source_target_pairs={{0,224},{1,225},{2,226},{3,227},{4,228},{5,229},{6,230},{7,231},{8... | collective-permute-start | bytes 589832 | tf_op jit(solution)/shard_map/ppermute | solution.py:38
  134.0 0.5 collective-permute-start.25
  134.6 0.1 add_add_fusion.1
  134.6 0.1 reshape.264
  134.7 5.7 %collective-permute-done.23 = f32[2,48,512]{2,1,0:T(8,128)S(1)} collective-permute-done((f32[2,48,512]{2,1,0:T(8,128)}, f32[2,48,512]{2,1,0:T(8,128)S(1)}, u32[]{:S(2)}, u32[]{:S(2)}) %collective-permute-start.23) | collective-permute-done | bytes 196640 | tf_op jit(solution)/shard_map/ppermute | solution.py:38
  140.4 0.4 collective-permute-done.24
  140.8 1.9 %collective-permute-done.25 = f32[2,48,512]{2,1,0:T(8,128)S(1)} collective-permute-done((f32[2,48,512]{2,1,0:T(8,128)}, f32[2,48,512]{2,1,0:T(8,128)S(1)}, u32[]{:S(2)}, u32[]{:S(2)}) %collective-permute-start.25) | collective-permute-done | bytes 196640 | tf_op jit(solution)/shard_map/ppermute | solution.py:38
  142.6 1.0 add_add_fusion
  143.6 0.1 reshape.265
  143.7 0.1 pad_maximum_fusion.1
  143.8 18.1 %all_to_all.5.rows = f32[8,12,8,128]{3,2,1,0:T(8,128)S(1)} all-to-all(f32[8,12,8,128]{3,2,1,0:T(8,128)S(1)} %bitcast.33), channel_id=1, replica_groups=mesh['dp'=32,'tr'=2,'tc'=4] {'tc','tr'}, dimensions={0} | all-to-all | bytes 786432 | tf_op jit(solution)/shard_map/all_to_all | solution.py:159
  162.0 1.2 shard_map.78
  (54 shorter events, 0.2 us)
Async XLA Ops:
  7.2 1.1 copy-start
  7.2 97.7 %all-gather.2.cloned.1.call-start = ((), (), s32[]{:S(2)}) async-start(), calls=%async_computation.1 | async-start | bytes 7077888 | tf_op jit(solution)/shard_map/all_gather | solution.py:144
  8.3 2.3 %copy-start.19 = (bf16[512,2048]{1,0:T(8,128)(2,1)S(1)}, bf16[512,2048]{1,0:T(8,128)(2,1)}, u32[]{:S(2)}) copy-start(bf16[512,2048]{1,0:T(8,128)(2,1)} %param.6) | copy-start | bytes 6291460
  10.6 2.3 %collective-permute-start = (bf16[4,192,256]{2,1,0:T(8,128)(2,1)}, bf16[4,192,256]{2,1,0:T(8,128)(2,1)}, u32[]{:S(2)}, u32[]{:S(2)}) collective-permute-start(bf16[4,192,256]{2,1,0:T(8,128)(2,1)} %bitcast), channel_id=1, source_target_pairs={{0,8},{1,9},{2,10},{3,11},{4,12},{5,13},{6,14},{7,15},{8,0},{9,1},... | collective-permute-start | bytes 1179656 | tf_op jit(solution)/shard_map/ppermute | solution.py:38
  12.8 92.0 %copy-start.4 = (bf16[512,1024]{1,0:T(8,128)(2,1)}, bf16[512,1024]{1,0:T(8,128)(2,1)S(1)}, u32[]{:S(2)}) copy-start(bf16[512,1024]{1,0:T(8,128)(2,1)S(1)} %constant_dynamic-slice_fusion.1.refs_1_) | copy-start | bytes 3145732
  12.9 14.6 %collective-permute-start.4 = (bf16[256,1024]{1,0:T(8,128)(2,1)S(1)}, bf16[256,1024]{1,0:T(8,128)(2,1)S(1)}, u32[]{:S(2)}, u32[]{:S(2)}) collective-permute-start(bf16[256,1024]{1,0:T(8,128)(2,1)S(1)} %get-tuple-element.23), channel_id=1, source_target_pairs={{0,4},{1,5},{2,6},{3,7},{4,0},{5,1},{6,2},{7,3},{8,12},{9,13},{10,... | collective-permute-start | bytes 1572872 | tf_op jit(solution)/shard_map/ppermute | solution.py:38
  16.0 8.3 %collective-permute-start.1 = (bf16[2,192,256]{2,1,0:T(8,128)(2,1)S(1)}, bf16[2,192,256]{2,1,0:T(8,128)(2,1)S(1)}, u32[]{:S(2)}, u32[]{:S(2)}) collective-permute-start(bf16[2,192,256]{2,1,0:T(8,128)(2,1)S(1)} %get-tuple-element.51), channel_id=1, source_target_pairs={{0,48},{1,49},{2,50},{3,51},{4,52},{5,53},{6,54},{7,55},{8,56},{9,... | collective-permute-start | bytes 589832 | tf_op jit(solution)/shard_map/ppermute | solution.py:38
  16.9 7.4 %collective-permute-start.2 = (bf16[2,192,256]{2,1,0:T(8,128)(2,1)S(1)}, bf16[2,192,256]{2,1,0:T(8,128)(2,1)S(1)}, u32[]{:S(2)}, u32[]{:S(2)}) collective-permute-start(bf16[2,192,256]{2,1,0:T(8,128)(2,1)S(1)} %get-tuple-element.53), channel_id=1, source_target_pairs={{0,16},{1,17},{2,18},{3,19},{4,20},{5,21},{6,22},{7,23},{8,24},{9,... | collective-permute-start | bytes 589832 | tf_op jit(solution)/shard_map/ppermute | solution.py:38
  19.3 7.0 %collective-permute-start.3 = (bf16[2,192,256]{2,1,0:T(8,128)(2,1)S(1)}, bf16[2,192,256]{2,1,0:T(8,128)(2,1)S(1)}, u32[]{:S(2)}, u32[]{:S(2)}) collective-permute-start(bf16[2,192,256]{2,1,0:T(8,128)(2,1)S(1)} %get-tuple-element.52), channel_id=1, source_target_pairs={{0,192},{1,193},{2,194},{3,195},{4,196},{5,197},{6,198},{7,199},{8... | collective-permute-start | bytes 589832 | tf_op jit(solution)/shard_map/ppermute | solution.py:38
  27.5 1.9 %copy-start.20 = (bf16[256,1024]{1,0:T(8,128)(2,1)}, bf16[256,1024]{1,0:T(8,128)(2,1)S(1)}, u32[]{:S(2)}) copy-start(bf16[256,1024]{1,0:T(8,128)(2,1)S(1)} %collective-permute-done.4) | copy-start | bytes 1572868
  27.5 14.0 %collective-permute-start.5 = (bf16[256,1024]{1,0:T(8,128)(2,1)}, bf16[256,1024]{1,0:T(8,128)(2,1)S(1)}, u32[]{:S(2)}, u32[]{:S(2)}) collective-permute-start(bf16[256,1024]{1,0:T(8,128)(2,1)} %get-tuple-element.26), channel_id=1, source_target_pairs={{0,4},{1,5},{2,6},{3,7},{4,0},{5,1},{6,2},{7,3},{8,12},{9,13},{10,... | collective-permute-start | bytes 1572872 | tf_op jit(solution)/shard_map/ppermute | solution.py:38
  29.3 18.5 %collective-permute-start.6 = (bf16[512,1024]{1,0:T(8,128)(2,1)S(1)}, bf16[512,1024]{1,0:T(8,128)(2,1)S(1)}, u32[]{:S(2)}, u32[]{:S(2)}) collective-permute-start(bf16[512,1024]{1,0:T(8,128)(2,1)S(1)} %constant_dynamic-slice_fusion.1.refs_1_), channel_id=1, source_target_pairs={{0,8},{1,9},{2,10},{3,11},{4,12},{5,13},{6,14},{7,15},{8,0},{9,1},... | collective-permute-start | bytes 3145736 | tf_op jit(solution)/shard_map/ppermute | solution.py:38
  41.5 63.4 %copy-start.5 = (bf16[512,1024]{1,0:T(8,128)(2,1)}, bf16[512,1024]{1,0:T(8,128)(2,1)S(1)}, u32[]{:S(2)}) copy-start(bf16[512,1024]{1,0:T(8,128)(2,1)S(1)} %constant_dynamic-update-slice_fusion.refs_2_) | copy-start | bytes 3145732
  41.5 27.4 %collective-permute-start.9 = (bf16[512,1024]{1,0:T(8,128)(2,1)S(1)}, bf16[512,1024]{1,0:T(8,128)(2,1)S(1)}, u32[]{:S(2)}, u32[]{:S(2)}) collective-permute-start(bf16[512,1024]{1,0:T(8,128)(2,1)S(1)} %constant_dynamic-update-slice_fusion.refs_2_), channel_id=1, source_target_pairs={{0,48},{1,49},{2,50},{3,51},{4,52},{5,53},{6,54},{7,55},{8,56},{9,... | collective-permute-start | bytes 3145736 | tf_op jit(solution)/shard_map/ppermute | solution.py:38
  42.4 27.2 %collective-permute-start.13 = (bf16[512,1024]{1,0:T(8,128)(2,1)S(1)}, bf16[512,1024]{1,0:T(8,128)(2,1)S(1)}, u32[]{:S(2)}, u32[]{:S(2)}) collective-permute-start(bf16[512,1024]{1,0:T(8,128)(2,1)S(1)} %constant_dynamic-update-slice_fusion.refs_2_), channel_id=1, source_target_pairs={{0,16},{1,17},{2,18},{3,19},{4,20},{5,21},{6,22},{7,23},{8,24},{9,... | collective-permute-start | bytes 3145736 | tf_op jit(solution)/shard_map/ppermute | solution.py:38
  44.8 27.2 %collective-permute-start.17 = (bf16[512,1024]{1,0:T(8,128)(2,1)S(1)}, bf16[512,1024]{1,0:T(8,128)(2,1)S(1)}, u32[]{:S(2)}, u32[]{:S(2)}) collective-permute-start(bf16[512,1024]{1,0:T(8,128)(2,1)S(1)} %constant_dynamic-update-slice_fusion.refs_2_), channel_id=1, source_target_pairs={{0,192},{1,193},{2,194},{3,195},{4,196},{5,197},{6,198},{7,199},{8... | collective-permute-start | bytes 3145736 | tf_op jit(solution)/shard_map/ppermute | solution.py:38
  47.8 24.2 %collective-permute-start.7 = (bf16[512,1024]{1,0:T(8,128)(2,1)S(1)}, bf16[512,1024]{1,0:T(8,128)(2,1)S(1)}, u32[]{:S(2)}, u32[]{:S(2)}) collective-permute-start(bf16[512,1024]{1,0:T(8,128)(2,1)S(1)} %constant_dynamic-update-slice_fusion.refs_2_), channel_id=1, source_target_pairs={{0,8},{1,9},{2,10},{3,11},{4,12},{5,13},{6,14},{7,15},{8,0},{9,1},... | collective-permute-start | bytes 3145736 | tf_op jit(solution)/shard_map/ppermute | solution.py:38
  47.8 42.9 %copy-start.6 = (bf16[512,1024]{1,0:T(8,128)(2,1)}, bf16[512,1024]{1,0:T(8,128)(2,1)S(1)}, u32[]{:S(2)}) copy-start(bf16[512,1024]{1,0:T(8,128)(2,1)S(1)} %collective-permute-done.6.refs_3_) | copy-start | bytes 3145732
  47.8 41.4 %collective-permute-start.8 = (bf16[512,1024]{1,0:T(8,128)(2,1)S(1)}, bf16[512,1024]{1,0:T(8,128)(2,1)S(1)}, u32[]{:S(2)}, u32[]{:S(2)}) collective-permute-start(bf16[512,1024]{1,0:T(8,128)(2,1)S(1)} %constant_dynamic-slice_fusion.1.refs_1_), channel_id=1, source_target_pairs={{0,48},{1,49},{2,50},{3,51},{4,52},{5,53},{6,54},{7,55},{8,56},{9,... | collective-permute-start | bytes 3145736 | tf_op jit(solution)/shard_map/ppermute | solution.py:38
  68.9 21.9 %copy-start.7 = (bf16[512,1024]{1,0:T(8,128)(2,1)}, bf16[512,1024]{1,0:T(8,128)(2,1)S(1)}, u32[]{:S(2)}) copy-start(bf16[512,1024]{1,0:T(8,128)(2,1)S(1)} %collective-permute-done.9.refs_6_) | copy-start | bytes 3145732
  68.9 21.1 %collective-permute-start.12 = (bf16[512,1024]{1,0:T(8,128)(2,1)S(1)}, bf16[512,1024]{1,0:T(8,128)(2,1)S(1)}, u32[]{:S(2)}, u32[]{:S(2)}) collective-permute-start(bf16[512,1024]{1,0:T(8,128)(2,1)S(1)} %constant_dynamic-slice_fusion.1.refs_1_), channel_id=1, source_target_pairs={{0,16},{1,17},{2,18},{3,19},{4,20},{5,21},{6,22},{7,23},{8,24},{9,... | collective-permute-start | bytes 3145736 | tf_op jit(solution)/shard_map/ppermute | solution.py:38
  69.6 21.2 %copy-start.8 = (bf16[512,1024]{1,0:T(8,128)(2,1)}, bf16[512,1024]{1,0:T(8,128)(2,1)S(1)}, u32[]{:S(2)}) copy-start(bf16[512,1024]{1,0:T(8,128)(2,1)S(1)} %collective-permute-done.13.refs_10_) | copy-start | bytes 3145732
  69.6 21.1 %collective-permute-start.16 = (bf16[512,1024]{1,0:T(8,128)(2,1)S(1)}, bf16[512,1024]{1,0:T(8,128)(2,1)S(1)}, u32[]{:S(2)}, u32[]{:S(2)}) collective-permute-start(bf16[512,1024]{1,0:T(8,128)(2,1)S(1)} %constant_dynamic-slice_fusion.1.refs_1_), channel_id=1, source_target_pairs={{0,192},{1,193},{2,194},{3,195},{4,196},{5,197},{6,198},{7,199},{8... | collective-permute-start | bytes 3145736 | tf_op jit(solution)/shard_map/ppermute | solution.py:38
  72.0 19.4 %copy-start.9 = (bf16[512,1024]{1,0:T(8,128)(2,1)}, bf16[512,1024]{1,0:T(8,128)(2,1)S(1)}, u32[]{:S(2)}) copy-start(bf16[512,1024]{1,0:T(8,128)(2,1)S(1)} %collective-permute-done.17.refs_14_) | copy-start | bytes 3145732
  72.0 18.8 %collective-permute-start.11 = (bf16[512,1024]{1,0:T(8,128)(2,1)S(1)}, bf16[512,1024]{1,0:T(8,128)(2,1)S(1)}, u32[]{:S(2)}, u32[]{:S(2)}) collective-permute-start(bf16[512,1024]{1,0:T(8,128)(2,1)S(1)} %collective-permute-done.9.refs_6_), channel_id=1, source_target_pairs={{0,8},{1,9},{2,10},{3,11},{4,12},{5,13},{6,14},{7,15},{8,0},{9,1},... | collective-permute-start | bytes 3145736 | tf_op jit(solution)/shard_map/ppermute | solution.py:38
  72.0 19.9 %copy-start.10 = (bf16[512,1024]{1,0:T(8,128)(2,1)}, bf16[512,1024]{1,0:T(8,128)(2,1)S(1)}, u32[]{:S(2)}) copy-start(bf16[512,1024]{1,0:T(8,128)(2,1)S(1)} %collective-permute-done.7.refs_4_) | copy-start | bytes 3145732
  72.0 19.3 %collective-permute-start.15 = (bf16[512,1024]{1,0:T(8,128)(2,1)S(1)}, bf16[512,1024]{1,0:T(8,128)(2,1)S(1)}, u32[]{:S(2)}, u32[]{:S(2)}) collective-permute-start(bf16[512,1024]{1,0:T(8,128)(2,1)S(1)} %collective-permute-done.13.refs_10_), channel_id=1, source_target_pairs={{0,8},{1,9},{2,10},{3,11},{4,12},{5,13},{6,14},{7,15},{8,0},{9,1},... | collective-permute-start | bytes 3145736 | tf_op jit(solution)/shard_map/ppermute | solution.py:38
  89.3 4.2 %copy-start.11 = (bf16[512,1024]{1,0:T(8,128)(2,1)}, bf16[512,1024]{1,0:T(8,128)(2,1)S(1)}, u32[]{:S(2)}) copy-start(bf16[512,1024]{1,0:T(8,128)(2,1)S(1)} %collective-permute-done.8.refs_5_) | copy-start | bytes 3145732
  89.3 2.7 %collective-permute-start.19 = (bf16[512,1024]{1,0:T(8,128)(2,1)S(1)}, bf16[512,1024]{1,0:T(8,128)(2,1)S(1)}, u32[]{:S(2)}, u32[]{:S(2)}) collective-permute-start(bf16[512,1024]{1,0:T(8,128)(2,1)S(1)} %collective-permute-done.17.refs_14_), channel_id=1, source_target_pairs={{0,8},{1,9},{2,10},{3,11},{4,12},{5,13},{6,14},{7,15},{8,0},{9,1},... | collective-permute-start | bytes 3145736 | tf_op jit(solution)/shard_map/ppermute | solution.py:38
  90.0 6.4 %copy-start.12 = (bf16[512,1024]{1,0:T(8,128)(2,1)}, bf16[512,1024]{1,0:T(8,128)(2,1)S(1)}, u32[]{:S(2)}) copy-start(bf16[512,1024]{1,0:T(8,128)(2,1)S(1)} %collective-permute-done.12.refs_9_) | copy-start | bytes 3145732
  90.0 3.4 %collective-permute-start.10 = (bf16[512,1024]{1,0:T(8,128)(2,1)S(1)}, bf16[512,1024]{1,0:T(8,128)(2,1)S(1)}, u32[]{:S(2)}, u32[]{:S(2)}) collective-permute-start(bf16[512,1024]{1,0:T(8,128)(2,1)S(1)} %collective-permute-done.8.refs_5_), channel_id=1, source_target_pairs={{0,8},{1,9},{2,10},{3,11},{4,12},{5,13},{6,14},{7,15},{8,0},{9,1},... | collective-permute-start | bytes 3145736 | tf_op jit(solution)/shard_map/ppermute | solution.py:38
  90.7 5.7 %copy-start.13 = (bf16[512,1024]{1,0:T(8,128)(2,1)}, bf16[512,1024]{1,0:T(8,128)(2,1)S(1)}, u32[]{:S(2)}) copy-start(bf16[512,1024]{1,0:T(8,128)(2,1)S(1)} %collective-permute-done.16.refs_13_) | copy-start | bytes 3145732
  90.7 5.7 %collective-permute-start.14 = (bf16[512,1024]{1,0:T(8,128)(2,1)S(1)}, bf16[512,1024]{1,0:T(8,128)(2,1)S(1)}, u32[]{:S(2)}, u32[]{:S(2)}) collective-permute-start(bf16[512,1024]{1,0:T(8,128)(2,1)S(1)} %collective-permute-done.12.refs_9_), channel_id=1, source_target_pairs={{0,8},{1,9},{2,10},{3,11},{4,12},{5,13},{6,14},{7,15},{8,0},{9,1},... | collective-permute-start | bytes 3145736 | tf_op jit(solution)/shard_map/ppermute | solution.py:38
  90.8 5.7 %copy-start.14 = (bf16[512,1024]{1,0:T(8,128)(2,1)}, bf16[512,1024]{1,0:T(8,128)(2,1)S(1)}, u32[]{:S(2)}) copy-start(bf16[512,1024]{1,0:T(8,128)(2,1)S(1)} %collective-permute-done.11.refs_8_) | copy-start | bytes 3145732
  90.8 6.7 %collective-permute-start.18 = (bf16[512,1024]{1,0:T(8,128)(2,1)S(1)}, bf16[512,1024]{1,0:T(8,128)(2,1)}, u32[]{:S(2)}, u32[]{:S(2)}) collective-permute-start(bf16[512,1024]{1,0:T(8,128)(2,1)S(1)} %collective-permute-done.16.refs_13_), channel_id=1, source_target_pairs={{0,8},{1,9},{2,10},{3,11},{4,12},{5,13},{6,14},{7,15},{8,0},{9,1},... | collective-permute-start | bytes 3145736 | tf_op jit(solution)/shard_map/ppermute | solution.py:38
  91.4 5.1 %copy-start.15 = (bf16[512,1024]{1,0:T(8,128)(2,1)}, bf16[512,1024]{1,0:T(8,128)(2,1)S(1)}, u32[]{:S(2)}) copy-start(bf16[512,1024]{1,0:T(8,128)(2,1)S(1)} %collective-permute-done.15.refs_12_) | copy-start | bytes 3145732
  91.9 4.5 %copy-start.16 = (bf16[512,1024]{1,0:T(8,128)(2,1)}, bf16[512,1024]{1,0:T(8,128)(2,1)S(1)}, u32[]{:S(2)}) copy-start(bf16[512,1024]{1,0:T(8,128)(2,1)S(1)} %collective-permute-done.19.refs_16_) | copy-start | bytes 3145732
  93.4 3.0 %copy-start.17 = (bf16[512,1024]{1,0:T(8,128)(2,1)}, bf16[512,1024]{1,0:T(8,128)(2,1)S(1)}, u32[]{:S(2)}) copy-start(bf16[512,1024]{1,0:T(8,128)(2,1)S(1)} %collective-permute-done.10.refs_7_) | copy-start | bytes 3145732
  96.5 1.0 copy-start.18
  112.8 21.2 %collective-permute-start.20 = (f32[2,48,512]{2,1,0:T(8,128)}, f32[2,48,512]{2,1,0:T(8,128)S(1)}, u32[]{:S(2)}, u32[]{:S(2)}) collective-permute-start(f32[2,48,512]{2,1,0:T(8,128)} %get-tuple-element.29), channel_id=1, source_target_pairs={{0,96},{1,97},{2,98},{3,99},{4,100},{5,101},{6,102},{7,103},{8,104... | collective-permute-start | bytes 589832 | tf_op jit(solution)/shard_map/ppermute | solution.py:38
  115.3 19.3 %collective-permute-start.21 = (f32[2,48,512]{2,1,0:T(8,128)}, f32[2,48,512]{2,1,0:T(8,128)S(1)}, u32[]{:S(2)}, u32[]{:S(2)}) collective-permute-start(f32[2,48,512]{2,1,0:T(8,128)} %get-tuple-element.30), channel_id=1, source_target_pairs={{0,224},{1,225},{2,226},{3,227},{4,228},{5,229},{6,230},{7,231},{8... | collective-permute-start | bytes 589832 | tf_op jit(solution)/shard_map/ppermute | solution.py:38
  118.5 16.0 %copy-start.21 = (f32[2,48,512]{2,1,0:T(8,128)S(1)}, f32[2,48,512]{2,1,0:T(8,128)}, u32[]{:S(2)}) copy-start(f32[2,48,512]{2,1,0:T(8,128)} %get-tuple-element.28) | copy-start | bytes 589828
  118.5 16.0 %collective-permute-start.22 = (f32[2,48,512]{2,1,0:T(8,128)}, f32[2,48,512]{2,1,0:T(8,128)S(1)}, u32[]{:S(2)}, u32[]{:S(2)}) collective-permute-start(f32[2,48,512]{2,1,0:T(8,128)} %get-tuple-element.31), channel_id=1, source_target_pairs={{0,128},{1,129},{2,130},{3,131},{4,132},{5,133},{6,134},{7,135},{8... | collective-permute-start | bytes 589832 | tf_op jit(solution)/shard_map/ppermute | solution.py:38
  128.3 33.7 %copy-start.1 = (f32[1,12,8192]{2,0,1:T(1,128)S(1)}, f32[1,12,8192]{2,0,1:T(1,128)}, u32[]{:S(2)}) copy-start(f32[1,12,8192]{2,0,1:T(1,128)} %param.7) | copy-start | bytes 1179652
  128.3 33.7 %copy-start.2 = (f32[1,12,8192]{2,0,1:T(1,128)S(1)}, f32[1,12,8192]{2,0,1:T(1,128)}, u32[]{:S(2)}) copy-start(f32[1,12,8192]{2,0,1:T(1,128)} %param.8) | copy-start | bytes 1179652
  128.3 33.7 %copy-start.3 = (f32[1,12,8192]{2,0,1:T(1,128)S(1)}, f32[1,12,8192]{2,0,1:T(1,128)}, u32[]{:S(2)}) copy-start(f32[1,12,8192]{2,0,1:T(1,128)} %param.9) | copy-start | bytes 1179652
  128.3 12.1 %collective-permute-start.23 = (f32[2,48,512]{2,1,0:T(8,128)}, f32[2,48,512]{2,1,0:T(8,128)S(1)}, u32[]{:S(2)}, u32[]{:S(2)}) collective-permute-start(f32[2,48,512]{2,1,0:T(8,128)} %get-tuple-element.33), channel_id=1, source_target_pairs={{0,96},{1,97},{2,98},{3,99},{4,100},{5,101},{6,102},{7,103},{8,104... | collective-permute-start | bytes 589832 | tf_op jit(solution)/shard_map/ppermute | solution.py:38
  129.9 10.9 %collective-permute-start.24 = (f32[2,48,512]{2,1,0:T(8,128)}, f32[2,48,512]{2,1,0:T(8,128)S(1)}, u32[]{:S(2)}, u32[]{:S(2)}) collective-permute-start(f32[2,48,512]{2,1,0:T(8,128)} %get-tuple-element.34), channel_id=1, source_target_pairs={{0,224},{1,225},{2,226},{3,227},{4,228},{5,229},{6,230},{7,231},{8... | collective-permute-start | bytes 589832 | tf_op jit(solution)/shard_map/ppermute | solution.py:38
  134.0 8.6 %collective-permute-start.25 = (f32[2,48,512]{2,1,0:T(8,128)}, f32[2,48,512]{2,1,0:T(8,128)S(1)}, u32[]{:S(2)}, u32[]{:S(2)}) collective-permute-start(f32[2,48,512]{2,1,0:T(8,128)} %get-tuple-element.35), channel_id=1, source_target_pairs={{0,128},{1,129},{2,130},{3,131},{4,132},{5,133},{6,134},{7,135},{8... | collective-permute-start | bytes 589832 | tf_op jit(solution)/shard_map/ppermute | solution.py:38
Sparse Core Ops, SparseCore 0:
  27.6 77.1 all-gather.1
